TPU v7x, 32 devices: a whole 2x2x4 slice. The times are simulated.
32 devices in a mesh: wide: 16 (over z, y, core), tp: 2 (over x).
Axes of the slice: x: 2, y: 2, z: 4, core: 2. Of those that a mesh axis runs over, the one named last changes fastest.
Arguments:
- clips: bfloat16 [32, 512, 1024], P('wide', 'tp'), may hold values from -6 to 6
- cotangent: bfloat16 [32, 512, 1024], P('wide', 'tp'), may hold values from -6 to 6
- clip_live: int32 [32], P('wide'), may hold values from 0 to 1, as said below
- qkv_weight: bfloat16 [1024, 3, 1024], P('wide', None, 'tp'), may hold values from -0.1875 to 0.1875
- q_bias: float32 [1024], P('tp'), may hold values from -5 to 5
- v_bias: float32 [1024], P('tp'), may hold values from -0.4375 to 0.4375
- proj_weight: bfloat16 [1024, 1024], P('tp', 'wide'), may hold values from -2 to 2
- fc1_weight: bfloat16 [1024, 4096], P('wide', 'tp'), may hold values from -0.1875 to 0.1875
- fc1_bias: float32 [4096], P('tp'), may hold values from -4 to 4
- fc2_weight: bfloat16 [4096, 1024], P('tp', 'wide'), may hold values from -0.09375 to 0.09375
- ln_gains: float32 [2, 1024], replicated, may hold values from 0.25 to 1.75
- ln_biases: float32 [2, 1024], replicated, may hold values from -4 to 4
- out_bias: float32 [2, 1024], replicated, may hold values from -4 to 4
Outputs:
- block_out: bfloat16 [32, 512, 1024], P('wide', 'tp')
- clips_grad: float32 [32, 512, 1024], P('wide', 'tp')
- qkv_grad: float32 [1024, 3, 1024], P('wide', None, 'tp')
- q_bias_grad: float32 [1024], P('tp')
- v_bias_grad: float32 [1024], P('tp')
- proj_grad: float32 [1024, 1024], P('tp', 'wide')
- fc1_grad: float32 [1024, 4096], P('wide', 'tp')
- fc1_bias_grad: float32 [4096], P('tp')
- fc2_grad: float32 [4096, 1024], P('tp', 'wide')
- ln_gains_grad: float32 [2, 1024], replicated
- ln_biases_grad: float32 [2, 1024], replicated
- out_bias_grad: float32 [2, 1024], replicated
Inputs may be any that keep to these rules, and one draw needn't show every extreme that they name: `clip_live`: in each group's 2 consecutive slots the live ones come first; every group has at least one live slot, and some group has all 2 live.
All inputs are finite; a program needn't handle non-finite values.
Results may differ from a plain program's by a relative error of at most 0.015.
The roundings to bfloat16 on the way count: a program that leaves them out, or rounds other values in their place, can miss the bound.
Values may be sent and summed in bfloat16 or wider, within the bound.
No kernel may reach another device: no remote copies, remote signals or barrier semaphores. Data moves between devices by JAX's collectives and lax.ppermute only.
A program may use at most 128 MiB of HBM per device.

v0:
```python
from functools import partial
import math

import jax
import jax.numpy as jnp
from jax import lax
from jax.sharding import PartitionSpec as P

HEAD_DIM = 64


norm_eps = 1e-06
root_half = 1.0 / math.sqrt(2.0)
inv_root_two_pi = 1.0 / math.sqrt(2.0 * math.pi)


def layer_norm(in_rows, gain_row, shift_row):
    row_mean = jnp.mean(in_rows, axis=-1, keepdims=True)
    centred = in_rows - row_mean
    spread = jnp.mean(centred * centred, axis=-1, keepdims=True)
    inverse = lax.rsqrt(spread + norm_eps)
    unit_rows = centred * inverse
    return (unit_rows * gain_row + shift_row, unit_rows, inverse)


def norm_back(grad_rows, unit_rows, inverse, gain_row):
    scaled = grad_rows * gain_row
    mean_one = jnp.mean(scaled, axis=-1, keepdims=True)
    second = jnp.mean(scaled * unit_rows, axis=-1, keepdims=True)
    return inverse * (scaled - mean_one - unit_rows * second)


def contract_last(left_op, right_op):
    return lax.dot_general(
        left_op, right_op, (((1,), (1,)), ((), ())), preferred_element_type=jnp.float32
    )


def contract_first(left_op, right_op):
    return lax.dot_general(
        left_op, right_op, (((0,), (0,)), ((), ())), preferred_element_type=jnp.float32
    )


def attend_block(query, key_rows, value_rows):
    scores = jnp.einsum("qhd,khd->hqk", query, key_rows, preferred_element_type=jnp.float32)
    row_max = jnp.max(scores, axis=-1, keepdims=True)
    weights = jnp.exp(scores - row_max)
    row_sum = jnp.sum(weights, axis=-1, keepdims=True)
    prob_rows = (weights / row_sum).astype(jnp.bfloat16)
    mixed_rows = jnp.einsum(
        "hqk,khd->qhd", prob_rows, value_rows, preferred_element_type=jnp.float32
    )
    return (mixed_rows, row_max[..., 0] + jnp.log(row_sum[..., 0]))


def attend_back(query, grad_rows, log_total, key_rows, value_rows):
    scores = jnp.einsum("qhd,khd->hqk", query, key_rows, preferred_element_type=jnp.float32)
    prob_rows = jnp.exp(scores - log_total[..., None])
    dprobs = jnp.einsum("qhd,khd->hqk", grad_rows, value_rows, preferred_element_type=jnp.float32)
    row_delta = jnp.sum(prob_rows * dprobs, axis=-1, keepdims=True)
    dscores = (prob_rows * (dprobs - row_delta)).astype(jnp.bfloat16)
    dquery = jnp.einsum("hqk,khd->qhd", dscores, key_rows, preferred_element_type=jnp.float32)
    d_keys = jnp.einsum("hqk,qhd->khd", dscores, query, preferred_element_type=jnp.float32)
    dvalues = jnp.einsum(
        "hqk,qhd->khd",
        prob_rows.astype(jnp.bfloat16),
        grad_rows,
        preferred_element_type=jnp.float32,
    )
    return (dquery, d_keys, dvalues)


def per_device(
    clips,
    cotangent,
    clip_live,
    qkv_weight,
    q_bias,
    v_bias,
    proj_weight,
    fc1_weight,
    fc1_bias,
    fc2_weight,
    ln_gains,
    ln_biases,
    out_bias,
):
    tp_count = lax.axis_size("tp")
    wide_count = lax.axis_size("wide")
    slot_count, shard_rows, width = clips.shape
    length = shard_rows * tp_count
    local_cols = qkv_weight.shape[2]
    heads_here = local_cols // HEAD_DIM
    hidden_here = fc1_weight.shape[1]
    q_scale = 1.0 / math.sqrt(HEAD_DIM)
    grad_scale = 1.0 / math.sqrt(wide_count * slot_count * length)
    block_rows = 512
    blocks = length // block_rows
    tp_place = lax.axis_index("tp")
    live_slots = clip_live.astype(jnp.float32)
    qv_bias = jnp.stack([q_bias, v_bias])
    own_weights = (qkv_weight, proj_weight, fc1_weight, fc2_weight)

    def one_slot(state_in, inputs):
        rows_in, cot_in, live_one = inputs
        tied_weights = lax.optimization_barrier((own_weights, rows_in))[0]
        w_qkv, w_proj, w_fc1, w_fc2 = (
            lax.all_gather(tied_weights[0], "wide", axis=0, tiled=True),
            lax.all_gather(tied_weights[1], "wide", axis=1, tiled=True),
            lax.all_gather(tied_weights[2], "wide", axis=0, tiled=True),
            lax.all_gather(tied_weights[3], "wide", axis=1, tiled=True),
        )
        x_rows = rows_in.astype(jnp.float32)
        norm_one, unit_one, inv_one = layer_norm(x_rows, ln_gains[0], ln_biases[0])
        h1_full = lax.all_gather(norm_one.astype(jnp.bfloat16), "tp", axis=0, tiled=True)
        qkv_flat = w_qkv.reshape(width, 3 * local_cols)
        projected = jnp.dot(h1_full, qkv_flat, preferred_element_type=jnp.float32).reshape(
            length, 3, local_cols
        )
        query = (
            ((projected[:, 0] + qv_bias[0]) * q_scale)
            .astype(jnp.bfloat16)
            .reshape(length, heads_here, HEAD_DIM)
        )
        key_rows = projected[:, 1].astype(jnp.bfloat16).reshape(length, heads_here, HEAD_DIM)
        value_rows = (
            (projected[:, 2] + qv_bias[1])
            .astype(jnp.bfloat16)
            .reshape(length, heads_here, HEAD_DIM)
        )
        query_blocks = query.reshape(blocks, block_rows, heads_here, HEAD_DIM)
        mixed_blocks, log_totals = lax.map(
            partial(attend_block, key_rows=key_rows, value_rows=value_rows), query_blocks
        )
        attn_out = mixed_blocks.reshape(length, local_cols).astype(jnp.bfloat16)
        attn_sum = lax.psum_scatter(
            jnp.dot(attn_out, w_proj, preferred_element_type=jnp.float32),
            "tp",
            scatter_dimension=0,
            tiled=True,
        )
        mid_rows = x_rows + attn_sum + out_bias[0]
        norm_two, unit_two, inv_two = layer_norm(mid_rows, ln_gains[1], ln_biases[1])
        h2_full = lax.all_gather(norm_two.astype(jnp.bfloat16), "tp", axis=0, tiled=True)
        pre_act = jnp.dot(h2_full, w_fc1, preferred_element_type=jnp.float32) + fc1_bias
        cdf_part = 0.5 * (1.0 + lax.erf(pre_act * root_half))
        hidden = (pre_act * cdf_part).astype(jnp.bfloat16)
        mlp_sum = lax.psum_scatter(
            jnp.dot(hidden, w_fc2, preferred_element_type=jnp.float32).astype(jnp.bfloat16),
            "tp",
            scatter_dimension=0,
            tiled=True,
        ).astype(jnp.float32)
        block_out = (live_one * (mid_rows + mlp_sum + out_bias[1])).astype(jnp.bfloat16)
        out_grad = live_one * cot_in.astype(jnp.float32)
        out_full = lax.all_gather(out_grad.astype(jnp.bfloat16), "tp", axis=0, tiled=True)
        g_fc2 = contract_first(hidden, out_full)
        act_grad = contract_last(out_full, w_fc2)
        slope = cdf_part + pre_act * jnp.exp(-0.5 * pre_act * pre_act) * inv_root_two_pi
        pre_grad = act_grad * slope
        pre_grad_b = pre_grad.astype(jnp.bfloat16)
        g_fc1 = contract_first(h2_full, pre_grad_b)
        g_fc1b = jnp.sum(pre_grad, axis=0)
        norm_two_grad = lax.psum_scatter(
            contract_last(pre_grad_b, w_fc1), "tp", scatter_dimension=0, tiled=True
        )
        mid_grad = out_grad + norm_back(norm_two_grad, unit_two, inv_two, ln_gains[1])
        attn_full = lax.all_gather(mid_grad.astype(jnp.bfloat16), "tp", axis=0, tiled=True)
        g_proj = contract_first(attn_out, attn_full)
        mixed_grad = (
            contract_last(attn_full, w_proj)
            .astype(jnp.bfloat16)
            .reshape(blocks, block_rows, heads_here, HEAD_DIM)
        )

        def back_block(block_state, pieces):
            query_b, grad_b, lse_b = pieces
            d_query, d_keys, d_values = attend_back(query_b, grad_b, lse_b, key_rows, value_rows)
            return ((block_state[0] + d_keys, block_state[1] + d_values), d_query)

        empty_kv = jnp.zeros((length, heads_here, HEAD_DIM), jnp.float32)
        (key_grad, value_grad), query_grad = lax.scan(
            back_block, (empty_kv, empty_kv), (query_blocks, mixed_grad, log_totals)
        )
        query_grad = query_grad.reshape(length, local_cols) * q_scale
        key_grad = key_grad.reshape(length, local_cols)
        value_grad = value_grad.reshape(length, local_cols)
        g_qvb = jnp.stack([jnp.sum(query_grad, axis=0), jnp.sum(value_grad, axis=0)])
        proj_grads = (
            jnp.stack([query_grad, key_grad, value_grad], axis=1)
            .astype(jnp.bfloat16)
            .reshape(length, 3 * local_cols)
        )
        g_qkv = contract_first(h1_full, proj_grads).reshape(width, 3, local_cols)
        norm_one_grad = lax.psum_scatter(
            contract_last(proj_grads, qkv_flat).astype(jnp.bfloat16),
            "tp",
            scatter_dimension=0,
            tiled=True,
        ).astype(jnp.float32)
        in_grad = mid_grad + norm_back(norm_one_grad, unit_one, inv_one, ln_gains[0])
        gain_part = jnp.stack(
            [jnp.sum(norm_one_grad * unit_one, axis=0), jnp.sum(norm_two_grad * unit_two, axis=0)]
        )
        shift_part = jnp.stack([jnp.sum(norm_one_grad, axis=0), jnp.sum(norm_two_grad, axis=0)])
        bias_part = jnp.stack([jnp.sum(mid_grad, axis=0), jnp.sum(out_grad, axis=0)])
        summed = (
            lax.psum_scatter(
                g_qkv.astype(jnp.bfloat16), "wide", scatter_dimension=0, tiled=True
            ).astype(jnp.float32),
            lax.psum_scatter(
                g_proj.astype(jnp.bfloat16), "wide", scatter_dimension=1, tiled=True
            ).astype(jnp.float32),
            lax.psum_scatter(
                g_fc1.astype(jnp.bfloat16), "wide", scatter_dimension=0, tiled=True
            ).astype(jnp.float32),
            lax.psum_scatter(
                g_fc2.astype(jnp.bfloat16), "wide", scatter_dimension=1, tiled=True
            ).astype(jnp.float32),
        )
        weight_acc = jax.tree.map(jnp.add, state_in[0], summed)
        vector_acc = jax.tree.map(
            jnp.add, state_in[1], (gain_part, shift_part, bias_part, g_qvb, g_fc1b)
        )
        return ((weight_acc, vector_acc), (block_out, in_grad))

    weight_zero = tuple((jnp.zeros(shard_in.shape, jnp.float32) for shard_in in own_weights))
    vector_zero = (
        jnp.zeros((2, width), jnp.float32),
        jnp.zeros((2, width), jnp.float32),
        jnp.zeros((2, width), jnp.float32),
        jnp.zeros((2, local_cols), jnp.float32),
        jnp.zeros((hidden_here,), jnp.float32),
    )
    (weight_sums, vector_acc), (block_out, clips_grad) = lax.scan(
        one_slot, (weight_zero, vector_zero), (clips, cotangent, live_slots)
    )
    gain_acc, shift_acc, bias_acc, qvb_acc, fc1b_acc = vector_acc
    qvb_pad = lax.dynamic_update_slice(
        jnp.zeros((2, width), jnp.float32), qvb_acc, (0, tp_place * local_cols)
    )
    fc1b_pad = lax.dynamic_update_slice(
        jnp.zeros((hidden_here * tp_count,), jnp.float32), fc1b_acc, (tp_place * hidden_here,)
    )
    gain_sum, shift_sum, bias_sum, qvb_sum, fc1b_sum = lax.psum(
        (gain_acc, shift_acc, bias_acc, qvb_pad, fc1b_pad), ("wide", "tp")
    )
    qvb_own = lax.dynamic_slice_in_dim(qvb_sum, tp_place * local_cols, local_cols, 1)
    fc1b_own = lax.dynamic_slice_in_dim(fc1b_sum, tp_place * hidden_here, hidden_here, 0)
    return (
        block_out,
        clips_grad,
        weight_sums[0] * grad_scale,
        qvb_own[0] * grad_scale,
        qvb_own[1] * grad_scale,
        weight_sums[1] * grad_scale,
        weight_sums[2] * grad_scale,
        fc1b_own * grad_scale,
        weight_sums[3] * grad_scale,
        gain_sum * grad_scale,
        shift_sum * grad_scale,
        bias_sum * grad_scale,
    )


def solution(mesh):
    return jax.shard_map(
        per_device,
        mesh=mesh,
        in_specs=(
            P("wide", "tp", None),
            P("wide", "tp", None),
            P("wide"),
            P("wide", None, "tp"),
            P("tp"),
            P("tp"),
            P("tp", "wide"),
            P("wide", "tp"),
            P("tp"),
            P("tp", "wide"),
            P(),
            P(),
            P(),
        ),
        out_specs=(
            P("wide", "tp", None),
            P("wide", "tp", None),
            P("wide", None, "tp"),
            P("tp"),
            P("tp"),
            P("tp", "wide"),
            P("wide", "tp"),
            P("tp"),
            P("tp", "wide"),
            P(),
            P(),
            P(),
        ),
        check_vma=False,
    )
```

profile of v0, /device:TPU:0, one launch (start us, length us, event | category | flops | bytes accessed | tf_op | source)
XLA Modules:
  0.0 1456.9 jit_solution(16137751583045063315)
XLA Ops:
  8.4 1390.2 %while.28 = (s32[]{:T(128)}, f32[64,3,512]{2,0,1:T(8,128)S(1)}, f32[512,64]{0,1:T(8,128)}, f32[64,2048]{1,0:T(8,128)}, f32[2048,64]{0,1:T(8,128)}, /*index=5*/f3...) while((s32[]{:T(128)}, f32[64,3,512]{2,0,1:T(8,128)S(1)}, ...), condition=%wide.region_29.30_spmd.clone, body=%wide.region_0.29_spmd.clone.sunk | while | flops 21024088064 | bytes 454058208 | solution.py:236
  16.9 42.5 %all-gather.11.cloned.1.call-done = bf16[1024,3,512]{2,0,1:T(8,128)(2,1)} async-done(((bf16[64,3,512]{2,0,1:T(8,128)(2,1)}), bf16[1024,3,512]{2,0,1:T(8,128)(2,1)}) %all-gather.11.cloned.1.call-update) | async-done | bytes 3145744 | tf_op jit(solution)/shard_map/while/body/eval_jaxpr/all_gather | solution.py:109
  59.4 4.7 copy.54
  64.1 17.6 %all-gather.13.cloned.1.call-done = bf16[512,1024]{1,0:T(8,128)(2,1)} async-done(((bf16[256,1024]{1,0:T(8,128)(2,1)}), bf16[512,1024]{1,0:T(8,128)(2,1)}) %all-gather.13.cloned.1.call-update) | async-done | bytes 1048592 | tf_op jit(solution)/shard_map/while/body/eval_jaxpr/all_gather | solution.py:116
  92.6 29.2 %all-gather.15.cloned.1.call-done = bf16[512,1024]{0,1:T(8,128)(2,1)} async-done(((bf16[512,64]{0,1:T(8,128)(2,1)}), bf16[512,1024]{0,1:T(8,128)(2,1)}) %all-gather.15.cloned.1.call-update) | async-done | bytes 1048592 | tf_op jit(solution)/shard_map/while/body/eval_jaxpr/all_gather | solution.py:110
  126.4 29.6 %reduce-scatter.9.cloned.1.call-done = f32[256,1024]{1,0:T(8,128)} async-done(((f32[512,1024]{1,0:T(8,128)}), f32[256,1024]{1,0:T(8,128)}) %reduce-scatter.9.cloned.1.call-update) | async-done | bytes 1048592 | tf_op jit(solution)/shard_map/while/body/eval_jaxpr/reduce_scatter | solution.py:137
  164.3 44.6 %all-gather.9.cloned.1.call-done = bf16[1024,2048]{1,0:T(8,128)(2,1)} async-done(((bf16[64,2048]{1,0:T(8,128)(2,1)}), bf16[1024,2048]{1,0:T(8,128)(2,1)}) %all-gather.9.cloned.1.call-update) | async-done | bytes 4194320 | tf_op jit(solution)/shard_map/while/body/eval_jaxpr/all_gather | solution.py:111
  208.9 21.9 %all-gather.17.cloned.1.call-done = bf16[512,1024]{1,0:T(8,128)(2,1)} async-done(((bf16[256,1024]{1,0:T(8,128)(2,1)}), bf16[512,1024]{1,0:T(8,128)(2,1)}) %all-gather.17.cloned.1.call-update) | async-done | bytes 1048592 | tf_op jit(solution)/shard_map/while/body/eval_jaxpr/all_gather | solution.py:145
  230.7 7.9 multiply_convert_fusion.10
  238.6 15.1 %all-gather.19.cloned.1.call-done = bf16[512,1024]{1,0:T(8,128)(2,1)} async-done(((bf16[256,1024]{1,0:T(8,128)(2,1)}), bf16[512,1024]{1,0:T(8,128)(2,1)}) %all-gather.19.cloned.1.call-update) | async-done | bytes 1048592 | tf_op jit(solution)/shard_map/while/body/eval_jaxpr/all_gather | solution.py:157
  253.7 53.0 %all-gather.21.cloned.1.call-done = bf16[2048,1024]{0,1:T(8,128)(2,1)} async-done(((bf16[2048,64]{0,1:T(8,128)(2,1)}), bf16[2048,1024]{0,1:T(8,128)(2,1)}) %all-gather.21.cloned.1.call-update) | async-done | bytes 4194320 | tf_op jit(solution)/shard_map/while/body/eval_jaxpr/all_gather | solution.py:112
  306.7 7.6 fusion.174
  319.4 30.4 %reduce-scatter.11.cloned.1.call-done = f32[256,1024]{1,0:T(8,128)} async-done(((f32[512,1024]{1,0:T(8,128)}), f32[256,1024]{1,0:T(8,128)}) %reduce-scatter.11.cloned.1.call-update) | async-done | bytes 1048592 | tf_op jit(solution)/shard_map/while/body/eval_jaxpr/reduce_scatter | solution.py:165
  357.0 6.2 convolution_convert_fusion.17
  363.3 6.3 convolution_convert_fusion.16
  369.7 6.3 convolution_convert_fusion.15
  384.1 5.2 multiply_reduce_fusion.10
  409.3 5.3 bitcast_convert_fusion.3
  417.9 5.4 convolution_convert_fusion.13
  430.8 46.6 %reduce-scatter.19.cloned.1.call-done = bf16[2048,64]{0,1:T(8,128)(2,1)} async-done(((bf16[2048,1024]{0,1:T(8,128)(2,1)}), bf16[2048,64]{0,1:T(8,128)(2,1)}) %reduce-scatter.19.cloned.1.call-update) | async-done | bytes 262160 | tf_op jit(solution)/shard_map/while/body/eval_jaxpr/reduce_scatter | solution.py:218
  478.5 74.7 %reduce-scatter.17.cloned.1.call-done = bf16[64,2048]{1,0:T(8,128)(2,1)} async-done(((bf16[1024,2048]{1,0:T(8,128)(2,1)}), bf16[64,2048]{1,0:T(8,128)(2,1)}) %reduce-scatter.17.cloned.1.call-update) | async-done | bytes 262160 | tf_op jit(solution)/shard_map/while/body/eval_jaxpr/reduce_scatter | solution.py:215
  555.0 58.1 %reduce-scatter.15.cloned.1.call-done = bf16[512,64]{0,1:T(8,128)(2,1)} async-done(((bf16[512,1024]{0,1:T(8,128)(2,1)}), bf16[512,64]{0,1:T(8,128)(2,1)}) %reduce-scatter.15.cloned.1.call-update) | async-done | bytes 65552 | tf_op jit(solution)/shard_map/while/body/eval_jaxpr/reduce_scatter | solution.py:212
  614.6 20.0 %reduce-scatter.21.cloned.1.call-done = bf16[256,1024]{1,0:T(8,128)(2,1)} async-done(((bf16[512,1024]{1,0:T(8,128)(2,1)}), bf16[256,1024]{1,0:T(8,128)(2,1)}) %reduce-scatter.21.cloned.1.call-update) | async-done | bytes 524304 | tf_op jit(solution)/shard_map/while/body/eval_jaxpr/reduce_scatter | solution.py:196
  640.0 64.5 %reduce-scatter.13.cloned.1.call-done = bf16[64,3,512]{2,0,1:T(8,128)(2,1)} async-done(((bf16[1024,3,512]{2,0,1:T(8,128)(2,1)}), bf16[64,3,512]{2,0,1:T(8,128)(2,1)}) %reduce-scatter.13.cloned.1.call-update) | async-done | bytes 196624 | tf_op jit(solution)/shard_map/while/body/eval_jaxpr/reduce_scatter | solution.py:209
  714.0 38.4 %all-gather.11.cloned.1.call-done = bf16[1024,3,512]{2,0,1:T(8,128)(2,1)} async-done(((bf16[64,3,512]{2,0,1:T(8,128)(2,1)}), bf16[1024,3,512]{2,0,1:T(8,128)(2,1)}) %all-gather.11.cloned.1.call-update) | async-done | bytes 3145744 | tf_op jit(solution)/shard_map/while/body/eval_jaxpr/all_gather | solution.py:109
  752.4 4.7 copy.54
  757.1 17.5 %all-gather.13.cloned.1.call-done = bf16[512,1024]{1,0:T(8,128)(2,1)} async-done(((bf16[256,1024]{1,0:T(8,128)(2,1)}), bf16[512,1024]{1,0:T(8,128)(2,1)}) %all-gather.13.cloned.1.call-update) | async-done | bytes 1048592 | tf_op jit(solution)/shard_map/while/body/eval_jaxpr/all_gather | solution.py:116
  785.5 29.2 %all-gather.15.cloned.1.call-done = bf16[512,1024]{0,1:T(8,128)(2,1)} async-done(((bf16[512,64]{0,1:T(8,128)(2,1)}), bf16[512,1024]{0,1:T(8,128)(2,1)}) %all-gather.15.cloned.1.call-update) | async-done | bytes 1048592 | tf_op jit(solution)/shard_map/while/body/eval_jaxpr/all_gather | solution.py:110
  819.5 29.5 %reduce-scatter.9.cloned.1.call-done = f32[256,1024]{1,0:T(8,128)} async-done(((f32[512,1024]{1,0:T(8,128)}), f32[256,1024]{1,0:T(8,128)}) %reduce-scatter.9.cloned.1.call-update) | async-done | bytes 1048592 | tf_op jit(solution)/shard_map/while/body/eval_jaxpr/reduce_scatter | solution.py:137
  857.0 44.8 %all-gather.9.cloned.1.call-done = bf16[1024,2048]{1,0:T(8,128)(2,1)} async-done(((bf16[64,2048]{1,0:T(8,128)(2,1)}), bf16[1024,2048]{1,0:T(8,128)(2,1)}) %all-gather.9.cloned.1.call-update) | async-done | bytes 4194320 | tf_op jit(solution)/shard_map/while/body/eval_jaxpr/all_gather | solution.py:111
  901.7 22.0 %all-gather.17.cloned.1.call-done = bf16[512,1024]{1,0:T(8,128)(2,1)} async-done(((bf16[256,1024]{1,0:T(8,128)(2,1)}), bf16[512,1024]{1,0:T(8,128)(2,1)}) %all-gather.17.cloned.1.call-update) | async-done | bytes 1048592 | tf_op jit(solution)/shard_map/while/body/eval_jaxpr/all_gather | solution.py:145
  923.8 7.9 multiply_convert_fusion.10
  931.6 15.1 %all-gather.19.cloned.1.call-done = bf16[512,1024]{1,0:T(8,128)(2,1)} async-done(((bf16[256,1024]{1,0:T(8,128)(2,1)}), bf16[512,1024]{1,0:T(8,128)(2,1)}) %all-gather.19.cloned.1.call-update) | async-done | bytes 1048592 | tf_op jit(solution)/shard_map/while/body/eval_jaxpr/all_gather | solution.py:157
  946.7 52.8 %all-gather.21.cloned.1.call-done = bf16[2048,1024]{0,1:T(8,128)(2,1)} async-done(((bf16[2048,64]{0,1:T(8,128)(2,1)}), bf16[2048,1024]{0,1:T(8,128)(2,1)}) %all-gather.21.cloned.1.call-update) | async-done | bytes 4194320 | tf_op jit(solution)/shard_map/while/body/eval_jaxpr/all_gather | solution.py:112
  999.6 7.6 fusion.174
  1012.3 30.4 %reduce-scatter.11.cloned.1.call-done = f32[256,1024]{1,0:T(8,128)} async-done(((f32[512,1024]{1,0:T(8,128)}), f32[256,1024]{1,0:T(8,128)}) %reduce-scatter.11.cloned.1.call-update) | async-done | bytes 1048592 | tf_op jit(solution)/shard_map/while/body/eval_jaxpr/reduce_scatter | solution.py:165
  1049.9 6.2 convolution_convert_fusion.17
  1056.2 6.3 convolution_convert_fusion.16
  1062.6 6.3 convolution_convert_fusion.15
  1077.0 5.2 multiply_reduce_fusion.10
  1102.2 5.3 bitcast_convert_fusion.3
  1110.8 5.4 convolution_convert_fusion.13
  1124.4 45.8 %reduce-scatter.19.cloned.1.call-done = bf16[2048,64]{0,1:T(8,128)(2,1)} async-done(((bf16[2048,1024]{0,1:T(8,128)(2,1)}), bf16[2048,64]{0,1:T(8,128)(2,1)}) %reduce-scatter.19.cloned.1.call-update) | async-done | bytes 262160 | tf_op jit(solution)/shard_map/while/body/eval_jaxpr/reduce_scatter | solution.py:218
  1171.3 74.7 %reduce-scatter.17.cloned.1.call-done = bf16[64,2048]{1,0:T(8,128)(2,1)} async-done(((bf16[1024,2048]{1,0:T(8,128)(2,1)}), bf16[64,2048]{1,0:T(8,128)(2,1)}) %reduce-scatter.17.cloned.1.call-update) | async-done | bytes 262160 | tf_op jit(solution)/shard_map/while/body/eval_jaxpr/reduce_scatter | solution.py:215
  1248.0 57.9 %reduce-scatter.15.cloned.1.call-done = bf16[512,64]{0,1:T(8,128)(2,1)} async-done(((bf16[512,1024]{0,1:T(8,128)(2,1)}), bf16[512,64]{0,1:T(8,128)(2,1)}) %reduce-scatter.15.cloned.1.call-update) | async-done | bytes 65552 | tf_op jit(solution)/shard_map/while/body/eval_jaxpr/reduce_scatter | solution.py:212
  1307.4 20.2 %reduce-scatter.21.cloned.1.call-done = bf16[256,1024]{1,0:T(8,128)(2,1)} async-done(((bf16[512,1024]{1,0:T(8,128)(2,1)}), bf16[256,1024]{1,0:T(8,128)(2,1)}) %reduce-scatter.21.cloned.1.call-update) | async-done | bytes 524304 | tf_op jit(solution)/shard_map/while/body/eval_jaxpr/reduce_scatter | solution.py:196
  1333.0 64.6 %reduce-scatter.13.cloned.1.call-done = bf16[64,3,512]{2,0,1:T(8,128)(2,1)} async-done(((bf16[1024,3,512]{2,0,1:T(8,128)(2,1)}), bf16[64,3,512]{2,0,1:T(8,128)(2,1)}) %reduce-scatter.13.cloned.1.call-update) | async-done | bytes 196624 | tf_op jit(solution)/shard_map/while/body/eval_jaxpr/reduce_scatter | solution.py:209
  1400.3 40.5 %all-reduce = (f32[2,1024]{1,0:T(2,128)S(1)}, f32[4096]{0:T(1024)S(1)}, f32[2,1024]{1,0:T(2,128)S(1)}, f32[2,1024]{1,0:T(2,128)S(1)}, f32[2,1024]{1,0:T(2,128)S(1)}) all-reduce(f32[2,1024]{1,0:T(2,128)S(1)} %constant_dynamic-update-slice_fusion, f32[4096]{0:T(1024)S(1)} %dynamic_update_slice.23, ...), channel_id=1, replica_groups=mesh['wide'=16,'tp'=2] {'wide','tp'}, use_global_device_ids=true, to_apply=%region_30.31 | all-reduce | flops 12288 | bytes 98304 | tf_op jit(solution)/shard_map/psum | solution.py:246
  (316 shorter events, 200.1 us)
Async XLA Ops:
  8.4 51.0 %all-gather.11.cloned.1.call-start = ((), (), s32[]{:S(2)}) async-start(), calls=%async_computation.9 | async-start | bytes 3342336 | tf_op jit(solution)/shard_map/while/body/eval_jaxpr/all_gather | solution.py:109
  9.7 72.0 %all-gather.13.cloned.1.call-start = ((), (), s32[]{:S(2)}) async-start(), calls=%async_computation.10 | async-start | bytes 1572864 | tf_op jit(solution)/shard_map/while/body/eval_jaxpr/all_gather | solution.py:116
  10.1 75.7 %copy-start.20 = (f32[256]{0:T(256)}, f32[256]{0:T(256)S(1)}, u32[]{:S(2)}) copy-start(f32[256]{0:T(256)S(1)} %add_rsqrt_fusion.4) | copy-start | bytes 3076 | tf_op jit(solution)/shard_map/while
  11.7 74.2 %copy-start.10 = (f32[1,1024]{1,0:T(1,128)}, f32[1,1024]{1,0:T(1,128)S(1)}, u32[]{:S(2)}) copy-start(f32[1,1024]{1,0:T(1,128)S(1)} %get-tuple-element.596) | copy-start | bytes 12292 | tf_op jit(solution)/shard_map/while
  12.8 109.1 %all-gather.15.cloned.1.call-start = ((), (), s32[]{:S(2)}) async-start(), calls=%async_computation.11 | async-start | bytes 1114112 | tf_op jit(solution)/shard_map/while/body/eval_jaxpr/all_gather | solution.py:110
  13.5 142.6 %reduce-scatter.9.cloned.1.call-start = ((), (), s32[]{:S(2)}) async-start(), calls=%async_computation.12 | async-start | bytes 3145728 | tf_op jit(solution)/shard_map/while/body/eval_jaxpr/reduce_scatter | solution.py:137
  16.8 69.3 %copy-start.13 = (f32[8,64]{1,0:T(8,128)}, f32[8,64]{1,0:T(8,128)S(1)}, u32[]{:S(2)}) copy-start(f32[8,64]{1,0:T(8,128)S(1)} %add.380) | copy-start | bytes 6148 | tf_op jit(solution)/shard_map/while
  16.9 71.8 %copy-start.19 = (f32[8,64]{1,0:T(8,128)}, f32[8,64]{1,0:T(8,128)S(1)}, u32[]{:S(2)}) copy-start(f32[8,64]{1,0:T(8,128)S(1)} %add.381) | copy-start | bytes 6148 | tf_op jit(solution)/shard_map/while
  125.2 83.7 %all-gather.9.cloned.1.call-start = ((), (), s32[]{:S(2)}) async-start(), calls=%async_computation.8 | async-start | bytes 4456448 | tf_op jit(solution)/shard_map/while/body/eval_jaxpr/all_gather | solution.py:111
  125.8 105.0 %all-gather.17.cloned.1.call-start = ((), (), s32[]{:S(2)}) async-start(), calls=%async_computation.13 | async-start | bytes 1572864 | tf_op jit(solution)/shard_map/while/body/eval_jaxpr/all_gather | solution.py:145
  158.9 94.8 %all-gather.19.cloned.1.call-start = ((), (), s32[]{:S(2)}) async-start(), calls=%async_computation.14 | async-start | bytes 1572864 | tf_op jit(solution)/shard_map/while/body/eval_jaxpr/all_gather | solution.py:157
  163.5 143.2 %all-gather.21.cloned.1.call-start = ((), (), s32[]{:S(2)}) async-start(), calls=%async_computation.15 | async-start | bytes 4456448 | tf_op jit(solution)/shard_map/while/body/eval_jaxpr/all_gather | solution.py:112
  164.2 185.6 %reduce-scatter.11.cloned.1.call-start = ((), (), s32[]{:S(2)}) async-start(), calls=%async_computation.16 | async-start | bytes 3145728 | tf_op jit(solution)/shard_map/while/body/eval_jaxpr/reduce_scatter | solution.py:165
  319.3 59.1 %all-gather.23.cloned.1.call-start = ((), (), s32[]{:S(2)}) async-start(), calls=%async_computation.17 | async-start | bytes 1572864 | tf_op jit(solution)/shard_map/while/body/eval_jaxpr/all_gather | solution.py:169
  357.0 67.7 %reduce-scatter.23.cloned.1.call-start = ((), (), s32[]{:S(2)}) async-start(), calls=%async_computation.23 | async-start | bytes 1572864 | tf_op jit(solution)/shard_map/while/body/eval_jaxpr/reduce_scatter | solution.py:149
  363.3 114.0 %reduce-scatter.19.cloned.1.call-start = ((), (), s32[]{:S(2)}) async-start(), calls=%async_computation.21 | async-start | bytes 4456448 | tf_op jit(solution)/shard_map/while/body/eval_jaxpr/reduce_scatter | solution.py:218
  369.7 183.5 %reduce-scatter.17.cloned.1.call-start = ((), (), s32[]{:S(2)}) async-start(), calls=%async_computation.20 | async-start | bytes 4456448 | tf_op jit(solution)/shard_map/while/body/eval_jaxpr/reduce_scatter | solution.py:215
  376.0 237.1 %reduce-scatter.15.cloned.1.call-start = ((), (), s32[]{:S(2)}) async-start(), calls=%async_computation.19 | async-start | bytes 1114112 | tf_op jit(solution)/shard_map/while/body/eval_jaxpr/reduce_scatter | solution.py:212
  381.6 253.0 %reduce-scatter.21.cloned.1.call-start = ((), (), s32[]{:S(2)}) async-start(), calls=%async_computation.22 | async-start | bytes 1572864 | tf_op jit(solution)/shard_map/while/body/eval_jaxpr/reduce_scatter | solution.py:196
  414.6 289.9 %reduce-scatter.13.cloned.1.call-start = ((), (), s32[]{:S(2)}) async-start(), calls=%async_computation.18 | async-start | bytes 3342336 | tf_op jit(solution)/shard_map/while/body/eval_jaxpr/reduce_scatter | solution.py:209
  423.2 211.4 %copy-start.11 = (f32[1,1024]{1,0:T(1,128)S(1)}, f32[1,1024]{1,0:T(1,128)}, u32[]{:S(2)}) copy-start(f32[1,1024]{1,0:T(1,128)} %copy-done.10) | copy-start | bytes 12292 | tf_op jit(solution)/shard_map/while
  423.2 211.4 %copy-start.16 = (f32[256]{0:T(256)S(1)}, f32[256]{0:T(256)}, u32[]{:S(2)}) copy-start(f32[256]{0:T(256)} %copy-done.15) | copy-start | bytes 3076 | tf_op jit(solution)/shard_map/while
  423.2 213.0 %copy-start.18 = (f32[1024]{0:T(1024)S(1)}, f32[1024]{0:T(1024)}, u32[]{:S(2)}) copy-start(f32[1024]{0:T(1024)} %get-tuple-element.619) | copy-start | bytes 12292 | tf_op jit(solution)/shard_map/while
  423.2 214.3 %copy-start.2 = (f32[256,1024]{1,0:T(8,128)S(1)}, f32[256,1024]{1,0:T(8,128)}, u32[]{:S(2)}) copy-start(f32[256,1024]{1,0:T(8,128)} %copy-done.1) | copy-start | bytes 3145732 | tf_op jit(solution)/shard_map/while
  478.5 227.1 %copy-start.7 = (f32[2048,64]{0,1:T(8,128)}, f32[2048,64]{0,1:T(8,128)S(1)}, u32[]{:S(2)}) copy-start(f32[2048,64]{0,1:T(8,128)S(1)} %select_add_fusion.13) | copy-start | bytes 1572868 | tf_op jit(solution)/shard_map/while
  705.5 46.9 %all-gather.11.cloned.1.call-start = ((), (), s32[]{:S(2)}) async-start(), calls=%async_computation.9 | async-start | bytes 3342336 | tf_op jit(solution)/shard_map/while/body/eval_jaxpr/all_gather | solution.py:109
  706.8 67.8 %all-gather.13.cloned.1.call-start = ((), (), s32[]{:S(2)}) async-start(), calls=%async_computation.10 | async-start | bytes 1572864 | tf_op jit(solution)/shard_map/while/body/eval_jaxpr/all_gather | solution.py:116
  707.2 71.5 %copy-start.20 = (f32[256]{0:T(256)}, f32[256]{0:T(256)S(1)}, u32[]{:S(2)}) copy-start(f32[256]{0:T(256)S(1)} %add_rsqrt_fusion.4) | copy-start | bytes 3076 | tf_op jit(solution)/shard_map/while
  708.8 69.9 %copy-start.10 = (f32[1,1024]{1,0:T(1,128)}, f32[1,1024]{1,0:T(1,128)S(1)}, u32[]{:S(2)}) copy-start(f32[1,1024]{1,0:T(1,128)S(1)} %get-tuple-element.596) | copy-start | bytes 12292 | tf_op jit(solution)/shard_map/while
  709.9 104.8 %all-gather.15.cloned.1.call-start = ((), (), s32[]{:S(2)}) async-start(), calls=%async_computation.11 | async-start | bytes 1114112 | tf_op jit(solution)/shard_map/while/body/eval_jaxpr/all_gather | solution.py:110
  710.6 138.3 %reduce-scatter.9.cloned.1.call-start = ((), (), s32[]{:S(2)}) async-start(), calls=%async_computation.12 | async-start | bytes 3145728 | tf_op jit(solution)/shard_map/while/body/eval_jaxpr/reduce_scatter | solution.py:137
  818.1 83.7 %all-gather.9.cloned.1.call-start = ((), (), s32[]{:S(2)}) async-start(), calls=%async_computation.8 | async-start | bytes 4456448 | tf_op jit(solution)/shard_map/while/body/eval_jaxpr/all_gather | solution.py:111
  818.8 105.0 %all-gather.17.cloned.1.call-start = ((), (), s32[]{:S(2)}) async-start(), calls=%async_computation.13 | async-start | bytes 1572864 | tf_op jit(solution)/shard_map/while/body/eval_jaxpr/all_gather | solution.py:145
  851.8 95.0 %all-gather.19.cloned.1.call-start = ((), (), s32[]{:S(2)}) async-start(), calls=%async_computation.14 | async-start | bytes 1572864 | tf_op jit(solution)/shard_map/while/body/eval_jaxpr/all_gather | solution.py:157
  856.3 143.2 %all-gather.21.cloned.1.call-start = ((), (), s32[]{:S(2)}) async-start(), calls=%async_computation.15 | async-start | bytes 4456448 | tf_op jit(solution)/shard_map/while/body/eval_jaxpr/all_gather | solution.py:112
  856.9 185.8 %reduce-scatter.11.cloned.1.call-start = ((), (), s32[]{:S(2)}) async-start(), calls=%async_computation.16 | async-start | bytes 3145728 | tf_op jit(solution)/shard_map/while/body/eval_jaxpr/reduce_scatter | solution.py:165
  1012.2 59.1 %all-gather.23.cloned.1.call-start = ((), (), s32[]{:S(2)}) async-start(), calls=%async_computation.17 | async-start | bytes 1572864 | tf_op jit(solution)/shard_map/while/body/eval_jaxpr/all_gather | solution.py:169
  1049.9 67.7 %reduce-scatter.23.cloned.1.call-start = ((), (), s32[]{:S(2)}) async-start(), calls=%async_computation.23 | async-start | bytes 1572864 | tf_op jit(solution)/shard_map/while/body/eval_jaxpr/reduce_scatter | solution.py:149
  1056.2 114.0 %reduce-scatter.19.cloned.1.call-start = ((), (), s32[]{:S(2)}) async-start(), calls=%async_computation.21 | async-start | bytes 4456448 | tf_op jit(solution)/shard_map/while/body/eval_jaxpr/reduce_scatter | solution.py:218
  1062.6 183.5 %reduce-scatter.17.cloned.1.call-start = ((), (), s32[]{:S(2)}) async-start(), calls=%async_computation.20 | async-start | bytes 4456448 | tf_op jit(solution)/shard_map/while/body/eval_jaxpr/reduce_scatter | solution.py:215
  1068.9 236.9 %reduce-scatter.15.cloned.1.call-start = ((), (), s32[]{:S(2)}) async-start(), calls=%async_computation.19 | async-start | bytes 1114112 | tf_op jit(solution)/shard_map/while/body/eval_jaxpr/reduce_scatter | solution.py:212
  1074.5 253.1 %reduce-scatter.21.cloned.1.call-start = ((), (), s32[]{:S(2)}) async-start(), calls=%async_computation.22 | async-start | bytes 1572864 | tf_op jit(solution)/shard_map/while/body/eval_jaxpr/reduce_scatter | solution.py:196
  1107.5 290.1 %reduce-scatter.13.cloned.1.call-start = ((), (), s32[]{:S(2)}) async-start(), calls=%async_computation.18 | async-start | bytes 3342336 | tf_op jit(solution)/shard_map/while/body/eval_jaxpr/reduce_scatter | solution.py:209
  1116.1 211.5 %copy-start.11 = (f32[1,1024]{1,0:T(1,128)S(1)}, f32[1,1024]{1,0:T(1,128)}, u32[]{:S(2)}) copy-start(f32[1,1024]{1,0:T(1,128)} %copy-done.10) | copy-start | bytes 12292 | tf_op jit(solution)/shard_map/while
  1116.1 211.5 %copy-start.16 = (f32[256]{0:T(256)S(1)}, f32[256]{0:T(256)}, u32[]{:S(2)}) copy-start(f32[256]{0:T(256)} %copy-done.15) | copy-start | bytes 3076 | tf_op jit(solution)/shard_map/while
  1116.1 213.1 %copy-start.18 = (f32[1024]{0:T(1024)S(1)}, f32[1024]{0:T(1024)}, u32[]{:S(2)}) copy-start(f32[1024]{0:T(1024)} %get-tuple-element.619) | copy-start | bytes 12292 | tf_op jit(solution)/shard_map/while
  1116.2 214.5 %copy-start.2 = (f32[256,1024]{1,0:T(8,128)S(1)}, f32[256,1024]{1,0:T(8,128)}, u32[]{:S(2)}) copy-start(f32[256,1024]{1,0:T(8,128)} %copy-done.1) | copy-start | bytes 3145732 | tf_op jit(solution)/shard_map/while
  1171.3 227.3 %copy-start.7 = (f32[2048,64]{0,1:T(8,128)}, f32[2048,64]{0,1:T(8,128)S(1)}, u32[]{:S(2)}) copy-start(f32[2048,64]{0,1:T(8,128)S(1)} %select_add_fusion.13) | copy-start | bytes 1572868 | tf_op jit(solution)/shard_map/while
  (36 other events, 651.4 us)
Sparse Core Ops, SparseCore 0:
  11.5 47.9 all-gather.10
  61.5 20.0 all-gather.12
  83.8 37.9 all-gather.14
  125.3 30.7 reduce-scatter.8
  158.1 50.7 all-gather.8
  210.9 19.7 all-gather.16
  232.3 21.2 all-gather.18
  256.1 50.5 all-gather.20
  319.4 30.3 reduce-scatter.10
  357.1 21.2 all-gather.22
  380.7 20.3 reduce-scatter.22
  404.8 72.5 reduce-scatter.18
  481.7 71.4 reduce-scatter.16
  556.7 56.3 reduce-scatter.14
  615.3 19.3 reduce-scatter.20
  638.3 66.1 reduce-scatter.12
  708.3 44.1 all-gather.10
  754.4 20.0 all-gather.12
  776.7 37.9 all-gather.14
  818.2 30.7 reduce-scatter.8
  851.1 50.5 all-gather.8
  903.9 19.7 all-gather.16
  925.4 21.2 all-gather.18
  949.0 50.5 all-gather.20
  1012.3 30.3 reduce-scatter.10
  1050.0 21.2 all-gather.22
  1073.4 20.3 reduce-scatter.22
  1097.6 72.5 reduce-scatter.18
  1174.6 71.4 reduce-scatter.16
  1249.5 56.3 reduce-scatter.14
  1308.2 19.3 reduce-scatter.20
  1331.4 66.1 reduce-scatter.12
where the time goes:
time: 1460 us
  waiting for transfers between devices  1100 us (75%)
  matrix products  161 us (11%)
  other arithmetic  94 us (6%)
  local copies, waits for them, and re-layouts  45.6 us (3%)
  blocking collectives  40.5 us (3%)
  between operations  14.8 us (1%)
    reduce_scatter x2, waiting for transfers between devices, one_slot(): lax.psum_scatter(g_fc1.astype(jnp.bfloat16), 'wide', scatter_dimension=0,...  149 us
    reduce_scatter x2, waiting for transfers between devices, one_slot(): lax.psum_scatter(g_qkv.astype(jnp.bfloat16), 'wide', scatter_dimension=0,...  129 us
    reduce_scatter x2, waiting for transfers between devices, one_slot(): lax.psum_scatter(g_proj.astype(jnp.bfloat16), 'wide', scatter_dimension=1...  116 us
    all_gather x2, waiting for transfers between devices, one_slot(): lax.all_gather(tied_weights[3], 'wide', axis=1, tiled=True)  106 us
    reduce_scatter x2, waiting for transfers between devices, one_slot(): lax.psum_scatter(g_fc2.astype(jnp.bfloat16), 'wide', scatter_dimension=1,...  92.4 us
    all_gather x2, waiting for transfers between devices, one_slot(): lax.all_gather(tied_weights[2], 'wide', axis=0, tiled=True)  89.4 us
    all_gather x2, waiting for transfers between devices, one_slot(): lax.all_gather(tied_weights[0], 'wide', axis=0, tiled=True)  80.9 us
    reduce_scatter x2, waiting for transfers between devices, one_slot(): lax.psum_scatter(contract_last(pre_grad_b, w_fc1), 'tp', scatter_dimensio...  60.9 us
  transfers between devices with their start and end apart: 32, of which 30 were waited for; matrix products, arithmetic and copies ran while one was open for 16% of the time, Pallas kernels for 0%

commit v1 on v0

--- a/solution.py
+++ b/solution.py
@@ -4,6 +4,8 @@
 import jax
 import jax.numpy as jnp
 from jax import lax
+from jax.experimental import pallas as pl
+from jax.experimental.pallas import tpu as pltpu
 from jax.sharding import PartitionSpec as P
 
 HEAD_DIM = 64
@@ -71,7 +73,7 @@
     return (dquery, d_keys, dvalues)
 
 
-def per_device(
+def shared_slots(
     clips,
     cotangent,
     clip_live,
@@ -264,9 +266,392 @@
     )
 
 
+AXES = ("wide", "tp")
+PAIR = 128
+
+
+def fits_own_slot(mesh):
+    return mesh.shape["tp"] == 2 and mesh.shape["wide"] % 4 == 0
+
+
+def nt_dot(left_op, right_op):
+    return lax.dot_general(
+        left_op, right_op, (((1,), (1,)), ((), ())), preferred_element_type=jnp.float32
+    )
+
+
+def nn_dot(left_op, right_op):
+    return lax.dot_general(
+        left_op, right_op, (((1,), (0,)), ((), ())), preferred_element_type=jnp.float32
+    )
+
+
+def attend_kernel(q_ref, k_ref, v_ref, o_ref, lse_ref):
+    pair = pl.program_id(0)
+    rows = q_ref.shape[0]
+    lanes = lax.broadcasted_iota(jnp.int32, (rows, PAIR), 1)
+    keys = k_ref[...]
+    values = v_ref[...]
+    total = jnp.zeros((rows, PAIR), jnp.float32)
+    for half in range(2):
+        mask = (lanes // HEAD_DIM) == half
+        query = jnp.where(mask, q_ref[...], jnp.zeros_like(keys))
+        scores = nt_dot(query, keys)
+        row_max = jnp.max(scores, axis=-1, keepdims=True)
+        weights = jnp.exp(scores - row_max)
+        row_sum = jnp.sum(weights, axis=-1, keepdims=True)
+        probs = (weights * (1.0 / row_sum)).astype(jnp.bfloat16)
+        mixed = nn_dot(probs, values)
+        total = jnp.where(mask, mixed, total)
+        lse = row_max + jnp.log(row_sum)
+        lse_ref[...] = jnp.where(lanes == 2 * pair + half, lse, lse_ref[...])
+    o_ref[...] = total.astype(jnp.bfloat16)
+
+
+def attend_fwd(query, keys, values):
+    length, width = query.shape
+    block = pl.BlockSpec((length, PAIR), lambda i: (0, i))
+    return pl.pallas_call(
+        attend_kernel,
+        grid=(width // PAIR,),
+        in_specs=[block, block, block],
+        out_specs=[block, pl.BlockSpec((length, PAIR), lambda i: (0, 0))],
+        out_shape=[
+            jax.ShapeDtypeStruct((length, width), jnp.bfloat16),
+            jax.ShapeDtypeStruct((length, PAIR), jnp.float32),
+        ],
+        compiler_params=pltpu.CompilerParams(vmem_limit_bytes=40 * 1024 * 1024),
+        cost_estimate=pl.CostEstimate(
+            flops=8 * length * length * width,
+            bytes_accessed=8 * length * width,
+            transcendentals=length * length * (width // HEAD_DIM),
+        ),
+        name="attend_fwd",
+    )(query, keys, values)
+
+
+def attend_back_kernel(q_ref, k_ref, v_ref, g_ref, lse_ref, dq_ref, dk_ref, dv_ref, qs_ref, vs_ref):
+    pair = pl.program_id(0)
+    rows = q_ref.shape[0]
+    lanes = lax.broadcasted_iota(jnp.int32, (rows, PAIR), 1)
+    query = q_ref[...]
+    keys = k_ref[...]
+    values = v_ref[...]
+    grads = g_ref[...]
+    blank = jnp.zeros_like(keys)
+    keys_t = keys.T
+    dq_t = jnp.zeros((PAIR, rows), jnp.float32)
+    dk = jnp.zeros((rows, PAIR), jnp.float32)
+    dv = jnp.zeros((rows, PAIR), jnp.float32)
+    for half in range(2):
+        mask = (lanes // HEAD_DIM) == half
+        scores_t = nt_dot(jnp.where(mask, keys, blank), query)
+        lse = lse_ref[pl.ds(2 * pair + half, 1), :]
+        probs_t = jnp.exp(scores_t - lse)
+        dprobs_t = nt_dot(jnp.where(mask, values, blank), grads)
+        delta = jnp.sum(probs_t * dprobs_t, axis=0, keepdims=True)
+        ds_t = (probs_t * (dprobs_t - delta)).astype(jnp.bfloat16)
+        dv = jnp.where(mask, nn_dot(probs_t.astype(jnp.bfloat16), grads), dv)
+        dk = jnp.where(mask, nn_dot(ds_t, query), dk)
+        sub = lax.broadcasted_iota(jnp.int32, (PAIR, rows), 0)
+        dq_t = jnp.where((sub // HEAD_DIM) == half, nn_dot(keys_t, ds_t), dq_t)
+    dq = dq_t.T * (1.0 / math.sqrt(HEAD_DIM))
+    dq_ref[...] = dq.astype(jnp.bfloat16)
+    dk_ref[...] = dk.astype(jnp.bfloat16)
+    dv_ref[...] = dv.astype(jnp.bfloat16)
+    qs_ref[...] = jnp.sum(dq, axis=0, keepdims=True)
+    vs_ref[...] = jnp.sum(dv, axis=0, keepdims=True)
+
+
+def attend_bwd(query, keys, values, grads, lse_rows):
+    length, width = query.shape
+    block = pl.BlockSpec((length, PAIR), lambda i: (0, i))
+    row = pl.BlockSpec((1, PAIR), lambda i: (0, i))
+    shape = jax.ShapeDtypeStruct((length, width), jnp.bfloat16)
+    sums = jax.ShapeDtypeStruct((1, width), jnp.float32)
+    return pl.pallas_call(
+        attend_back_kernel,
+        grid=(width // PAIR,),
+        in_specs=[block] * 4 + [pl.BlockSpec((PAIR, length), lambda i: (0, 0))],
+        out_specs=[block] * 3 + [row] * 2,
+        out_shape=[shape] * 3 + [sums] * 2,
+        compiler_params=pltpu.CompilerParams(vmem_limit_bytes=40 * 1024 * 1024),
+        cost_estimate=pl.CostEstimate(
+            flops=20 * length * length * width,
+            bytes_accessed=14 * length * width,
+            transcendentals=length * length * (width // HEAD_DIM),
+        ),
+        name="attend_bwd",
+    )(query, keys, values, grads, lse_rows)
+
+
+class Links:
+    def __init__(self):
+        self.nz = lax.axis_size("wide") // 4
+        self.across = self.table(lambda z, y, c, x: (z, y, c, 1 - x))
+        self.beside = self.table(lambda z, y, c, x: (z, 1 - y, c, x))
+        self.twin = self.table(lambda z, y, c, x: (z, y, 1 - c, x))
+
+    def table(self, source):
+        pairs = []
+        for z in range(self.nz):
+            for y in range(2):
+                for c in range(2):
+                    for x in range(2):
+                        zs, ys, cs, xs = source(z, y, c, x)
+                        pairs.append(
+                            (((zs * 2 + ys) * 2 + cs) * 2 + xs, ((z * 2 + y) * 2 + c) * 2 + x)
+                        )
+        return pairs
+
+    def from_z(self, rows, step):
+        shift = self.table(lambda z, y, c, x: ((z + step) % self.nz, y, c, x))
+        return lax.ppermute(rows, AXES, shift)
+
+    def x(self, rows):
+        return lax.ppermute(rows, AXES, self.across)
+
+    def y(self, rows):
+        return lax.ppermute(rows, AXES, self.beside)
+
+    def c(self, rows):
+        return lax.ppermute(rows, AXES, self.twin)
+
+
+def gather_chunk(links, shard):
+    along = jnp.concatenate([shard] + [links.from_z(shard, k) for k in range(1, links.nz)], axis=0)
+    half = along.shape[0] // 2
+    by_x = links.x(along)
+    by_y = links.y(along)
+    far_a = links.x(by_y[:half])
+    far_b = links.y(by_x[half:])
+    mine = (along, by_x, by_y, far_a, far_b)
+    other = tuple(links.c(piece) for piece in mine)
+    own_half = jnp.concatenate([along, by_y, other[0], other[2]], axis=0)
+    far_half = jnp.concatenate(
+        [by_x, far_a, far_b, other[1], other[3], other[4]], axis=0
+    )
+    return own_half, far_half
+
+
+def scatter_chunk(links, make_piece, rows_all):
+    half_rows = rows_all // 2
+    quarter = rows_all // 4
+    sent = [make_piece(half_rows, half_rows, kx, None) for kx in range(2)]
+    got = [links.c(piece) for piece in sent]
+    keep = {
+        (kx, ky): make_piece(ky * quarter, quarter, kx, got[kx][ky * quarter : (ky + 1) * quarter])
+        for kx, ky in ((1, 1), (1, 0), (0, 1), (0, 0))
+    }
+    mid = quarter // 2
+    f32 = jnp.float32
+    far_a = links.x(keep[1, 1][:mid])
+    far_b = links.y(keep[1, 1][mid:])
+    out_y = (
+        keep[0, 1]
+        .astype(f32)
+        .at[:mid]
+        .add(far_a.astype(f32))
+        .astype(jnp.bfloat16)
+    )
+    out_x = (
+        keep[1, 0]
+        .astype(f32)
+        .at[mid:]
+        .add(far_b.astype(f32))
+        .astype(jnp.bfloat16)
+    )
+    total = (
+        keep[0, 0].astype(f32) + links.x(out_x).astype(f32) + links.y(out_y).astype(f32)
+    )
+    shard_rows = quarter // links.nz
+    total_b = total.astype(jnp.bfloat16)
+    final = total[:shard_rows]
+    for k in range(1, links.nz):
+        block = total_b[k * shard_rows : (k + 1) * shard_rows]
+        back = links.from_z(block, links.nz - k)
+        final = final + back.astype(f32)
+    return final
+
+
+def own_slot(
+    clips,
+    cotangent,
+    clip_live,
+    qkv_weight,
+    q_bias,
+    v_bias,
+    proj_weight,
+    fc1_weight,
+    fc1_bias,
+    fc2_weight,
+    ln_gains,
+    ln_biases,
+    out_bias,
+):
+    f32 = jnp.float32
+    bf16 = jnp.bfloat16
+    links = Links()
+    slot_count, shard_rows, width = clips.shape
+    wide_count = lax.axis_size("wide")
+    length = 2 * shard_rows
+    block = qkv_weight.shape[0]
+    heads_cols = qkv_weight.shape[2]
+    hidden_here = fc1_weight.shape[1]
+    q_scale = 1.0 / math.sqrt(HEAD_DIM)
+    grad_scale = 1.0 / math.sqrt(wide_count * slot_count * length)
+    wide_at = lax.axis_index("wide")
+    t = lax.axis_index("tp")
+    z_at, y_at, c_at = wide_at // 4, (wide_at // 2) % 2, wide_at % 2
+
+    spot = jnp.arange(width)
+    rel = spot // block
+    kc, ky, kz = rel // (2 * links.nz), (rel // links.nz) % 2, rel % links.nz
+    source = (((z_at + kz) % links.nz * 2 + (y_at ^ ky)) * 2 + (c_at ^ kc)) * block + spot % block
+    order = spot[:, None] == source[None, :]
+    order_b = order.astype(bf16)
+    exact = partial(jnp.dot, precision=lax.Precision.HIGHEST)
+    order_f = order.astype(f32)
+
+    pick = lambda both, at: lax.dynamic_index_in_dim(both, at, 0, keepdims=False)
+    sent_rows = jnp.concatenate([pick(clips, 1 - t), pick(cotangent, 1 - t)], axis=0)
+    got_rows = links.x(sent_rows)
+    live = pick(clip_live, t).astype(f32)
+    x_b = jnp.concatenate([pick(clips, t), got_rows[:shard_rows]], axis=0)
+    cot_b = jnp.concatenate([pick(cotangent, t), got_rows[shard_rows:]], axis=0)
+    x_rows = nn_dot(x_b, order_b)
+    cot_rows = nn_dot(cot_b, order_b)
+    vectors = exact(jnp.concatenate([ln_gains, ln_biases, out_bias], axis=0), order_f)
+    gains, shifts, outs = vectors[0:2], vectors[2:4], vectors[4:6]
+    far_small = jnp.concatenate([q_bias, v_bias, fc1_bias])[None]
+    far_small = links.x(far_small)[0]
+    q_biases = (q_bias, far_small[:heads_cols])
+    v_biases = (v_bias, far_small[heads_cols : 2 * heads_cols])
+    fc1_biases = (fc1_bias, far_small[2 * heads_cols :])
+
+    chunk_one = jnp.concatenate([qkv_weight.reshape(block, 3 * heads_cols), proj_weight.T], axis=1)
+    w_one = gather_chunk(links, chunk_one)
+    w_fc1 = gather_chunk(links, fc1_weight)
+    w_fc2 = gather_chunk(links, fc2_weight.T)
+    qkv_cols = 3 * heads_cols
+    w_qkv = [w[:, :qkv_cols] for w in w_one]
+    w_proj = [w[:, qkv_cols:] for w in w_one]
+
+    norm_one, unit_one, inv_one = layer_norm(x_rows, gains[0], shifts[0])
+    h1 = norm_one.astype(bf16)
+    queries, keys, values = [], [], []
+    for kx in range(2):
+        projected = nn_dot(h1, w_qkv[kx])
+        queries.append(((projected[:, :heads_cols] + q_biases[kx]) * q_scale).astype(bf16))
+        keys.append(projected[:, heads_cols : 2 * heads_cols].astype(bf16))
+        values.append((projected[:, 2 * heads_cols :] + v_biases[kx]).astype(bf16))
+    query, key_rows, value_rows = (jnp.concatenate(part, axis=1) for part in (queries, keys, values))
+    attn_out, lse = attend_fwd(query, key_rows, value_rows)
+    halves = lambda rows, size: (rows[:, :size], rows[:, size:])
+    attn_halves = halves(attn_out, heads_cols)
+    mid_rows = (
+        x_rows + nt_dot(attn_halves[0], w_proj[0]) + nt_dot(attn_halves[1], w_proj[1]) + outs[0]
+    )
+    norm_two, unit_two, inv_two = layer_norm(mid_rows, gains[1], shifts[1])
+    h2 = norm_two.astype(bf16)
+    hidden, slope = [], []
+    for kx in range(2):
+        pre_act = nn_dot(h2, w_fc1[kx]) + fc1_biases[kx]
+        cdf_part = 0.5 * (1.0 + lax.erf(pre_act * root_half))
+        hidden.append((pre_act * cdf_part).astype(bf16))
+        slope.append(cdf_part + pre_act * jnp.exp(-0.5 * pre_act * pre_act) * inv_root_two_pi)
+    out_grad = live * cot_rows
+    e_b = out_grad.astype(bf16)
+
+    def fc2_piece(first, count, kx, extra):
+        piece = contract_first(e_b[:, first : first + count], hidden[kx])
+        return (piece if extra is None else piece + extra.astype(f32)).astype(bf16)
+
+    g_fc2 = scatter_chunk(links, fc2_piece, width)
+    mlp_sum = nt_dot(hidden[0], w_fc2[0]) + nt_dot(hidden[1], w_fc2[1])
+    block_out = (live * (mid_rows + mlp_sum + outs[1])).astype(bf16)
+    pre_grad = [nn_dot(e_b, w_fc2[kx]) * slope[kx] for kx in range(2)]
+    pre_grad_b = [rows.astype(bf16) for rows in pre_grad]
+    g_fc1b = [jnp.sum(rows, axis=0) for rows in pre_grad]
+
+    def fc1_piece(first, count, kx, extra):
+        piece = contract_first(h2[:, first : first + count], pre_grad_b[kx])
+        return (piece if extra is None else piece + extra.astype(f32)).astype(bf16)
+
+    g_fc1 = scatter_chunk(links, fc1_piece, width)
+    norm_two_grad = nt_dot(pre_grad_b[0], w_fc1[0]) + nt_dot(pre_grad_b[1], w_fc1[1])
+    mid_grad = out_grad + norm_back(norm_two_grad, unit_two, inv_two, gains[1])
+    da_b = mid_grad.astype(bf16)
+    mixed_grad = jnp.concatenate([nn_dot(da_b, w_proj[kx]) for kx in range(2)], axis=1).astype(bf16)
+    dq, dk, dv, q_sums, v_sums = attend_bwd(query, key_rows, value_rows, mixed_grad, lse.T)
+    parts = [halves(rows, heads_cols) for rows in (dq, dk, dv)]
+    one_sides = [jnp.concatenate([p[kx] for p in parts], axis=1) for kx in range(2)]
+
+    def one_piece(first, count, kx, extra):
+        cols = slice(first, first + count)
+        piece = jnp.concatenate(
+            [
+                contract_first(h1[:, cols], one_sides[kx]),
+                contract_first(da_b[:, cols], attn_halves[kx]),
+            ],
+            axis=1,
+        )
+        return (piece if extra is None else piece + extra.astype(f32)).astype(bf16)
+
+    g_one = scatter_chunk(links, one_piece, width)
+    norm_one_grad = nt_dot(one_sides[0], w_qkv[0]) + nt_dot(one_sides[1], w_qkv[1])
+    in_grad = mid_grad + norm_back(norm_one_grad, unit_one, inv_one, gains[0])
+
+    sums = jnp.stack(
+        [
+            jnp.sum(norm_one_grad * unit_one, axis=0),
+            jnp.sum(norm_two_grad * unit_two, axis=0),
+            jnp.sum(norm_one_grad, axis=0),
+            jnp.sum(norm_two_grad, axis=0),
+            jnp.sum(mid_grad, axis=0),
+            jnp.sum(out_grad, axis=0),
+        ]
+    )
+    sums = lax.dot_general(
+        sums, order_f, (((1,), (1,)), ((), ())), precision=lax.Precision.HIGHEST
+    )
+    placed = lambda near, far: jnp.where(
+        t == 0, jnp.concatenate([near, far]), jnp.concatenate([far, near])
+    )
+    q_all = placed(*(q_sums[0, :heads_cols], q_sums[0, heads_cols:]))
+    v_all = placed(*(v_sums[0, :heads_cols], v_sums[0, heads_cols:]))
+    fc1b_all = placed(*g_fc1b)
+    sums, q_all, v_all, fc1b_all = lax.psum((sums, q_all, v_all, fc1b_all), AXES)
+    own = lambda full, size: lax.dynamic_slice_in_dim(full, t * size, size, 0) * grad_scale
+
+    def back_home(rows_rel):
+        rows = lax.dot_general(
+            rows_rel.astype(bf16), order_b, (((1,), (1,)), ((), ())), preferred_element_type=f32
+        ).astype(bf16)
+        got = links.x(rows[shard_rows:])
+        near = rows[:shard_rows]
+        return jnp.where(t == 0, jnp.stack([near, got]), jnp.stack([got, near]))
+
+    return (
+        back_home(block_out),
+        back_home(in_grad).astype(f32),
+        g_one[:, :qkv_cols].reshape(block, 3, heads_cols) * grad_scale,
+        own(q_all, heads_cols),
+        own(v_all, heads_cols),
+        g_one[:, qkv_cols:].T * grad_scale,
+        g_fc1 * grad_scale,
+        own(fc1b_all, hidden_here),
+        g_fc2.T * grad_scale,
+        sums[0:2] * grad_scale,
+        sums[2:4] * grad_scale,
+        sums[4:6] * grad_scale,
+    )
+
+
 def solution(mesh):
+    body = own_slot if fits_own_slot(mesh) else shared_slots
     return jax.shard_map(
-        per_device,
+        body,
         mesh=mesh,
         in_specs=(
             P("wide", "tp", None),

time: 1460 us -> 586 us (0.40)
  waiting for transfers between devices: 1100 us -> 224 us
  starting transfers between devices: 1.32 us -> 112 us
  other arithmetic: 94 us -> 25.3 us
  matrix products: 161 us -> 106 us
  Pallas kernels: 0 us -> 28.4 us
    reduce_scatter x16 -> x0, waiting for transfers between devices: 647 us -> none  [the longest x2 149 us: one_slot(): lax.psum_scatter(g_fc1.astype(jnp.bfloat16), 'wide', scatter_dimension=0,...]
    all_gather x16 -> x0, waiting for transfers between devices: 447 us -> none  [the longest x2 106 us: one_slot(): lax.all_gather(tied_weights[3], 'wide', axis=1, tiled=True)]
    ppermute x0 -> x67, waiting for transfers between devices: none -> 224 us  [the longest x16 152 us: x(): return lax.ppermute(rows, AXES, self.across)]
    ppermute x0 -> x67, starting transfers between devices: none -> 112 us  [the longest x18 72.1 us: from_z(): return lax.ppermute(rows, AXES, shift)]
    dot_general x28 -> x21, matrix products: 119 us -> 64.6 us  [the longest x10 30.9 us: nn_dot(): lax.dot_general(left_op, right_op, (((1,), (0,)), ((), ())), preferred_el...]
    pallas_call x0 -> x2, Pallas kernels: none -> 28.4 us  [the longest x1 16.6 us: attend_bwd(): pl.pallas_call(attend_back_kernel, grid=(width // PAIR,), in_specs=[block...]
    reduce_sum x14 -> x1, other arithmetic: 27.9 us -> 0.96 us  [own_slot(): jnp.sum(mid_grad, axis=0)]
    unnamed x0 -> x164, local copies, waits for them, and re-layouts: none -> 23.9 us
  transfers between devices with their start and end apart: 32 -> 67, of which waited for: 30 -> 20; matrix products, arithmetic and copies ran while one was open for 16% -> 16% of each run, Pallas kernels for 0% -> 2%
where the time goes in v1:
time: 586 us; the launch traced here: 582 us
  waiting for transfers between devices  224 us (38%)
  starting transfers between devices  112 us (19%)
  matrix products  106 us (18%)
  blocking collectives  47.7 us (8%)
  local copies, waits for them, and re-layouts  35.9 us (6%)
  Pallas kernels  28.4 us (5%)
  other arithmetic  25.3 us (4%)
    ppermute x16, waiting for transfers between devices, x(): return lax.ppermute(rows, AXES, self.across)  152 us
    ppermute x18, starting transfers between devices, from_z(): return lax.ppermute(rows, AXES, shift)  72.1 us
    ppermute x12, waiting for transfers between devices, y(): return lax.ppermute(rows, AXES, self.beside)  48.1 us
    psum x1, blocking collectives, own_slot(): lax.psum((sums, q_all, v_all, fc1b_all), AXES)  47.7 us
    dot_general x24, matrix products, contract_first(): lax.dot_general(left_op, right_op, (((0,), (0,)), ((), ())), preferred_el...  41.7 us
    dot_general x10, matrix products, nn_dot(): lax.dot_general(left_op, right_op, (((1,), (0,)), ((), ())), preferred_el...  30.9 us
    unnamed x164, local copies, waits for them, and re-layouts  23.9 us
    ppermute x18, waiting for transfers between devices, from_z(): return lax.ppermute(rows, AXES, shift)  23.8 us
  transfers between devices with their start and end apart: 67, of which 20 were waited for; matrix products, arithmetic and copies ran while one was open for 16% of the time, Pallas kernels for 2%

profile of v1, /device:TPU:0, one launch (start us, length us, event | category | flops | bytes accessed | tf_op | source)
XLA Modules:
  0.0 582.2 jit_solution(2530017524180099964)
XLA Ops:
  0.7 3.1 collective-permute-start.22
  3.8 2.6 collective-permute-start.21
  19.9 2.8 collective-permute-start.14
  22.6 13.7 %collective-permute-start.16 = (bf16[64,2048]{1,0:T(8,128)(2,1)S(1)}, bf16[64,2048]{1,0:T(8,128)(2,1)S(1)}, u32[]{:S(2)}, u32[]{:S(2)}) collective-permute-start(bf16[64,2048]{1,0:T(8,128)(2,1)S(1)} %copy-done.50), channel_id=1, source_target_pairs={{24,0},{25,1},{26,2},{27,3},{28,4},{29,5},{30,6},{31,7},{0,8},{1,9... | collective-permute-start | bytes 786440 | tf_op jit(solution)/shard_map/ppermute | solution.py:409
  37.1 6.2 %collective-permute-start.1 = (bf16[64,2048]{1,0:T(8,128)(2,1)}, bf16[64,2048]{1,0:T(8,128)(2,1)S(1)}, u32[]{:S(2)}, u32[]{:S(2)}) collective-permute-start(bf16[64,2048]{1,0:T(8,128)(2,1)} %get-tuple-element.192), channel_id=1, source_target_pairs={{8,0},{9,1},{10,2},{11,3},{12,4},{13,5},{14,6},{15,7},{16,8},{17,9... | collective-permute-start | bytes 786440 | tf_op jit(solution)/shard_map/ppermute | solution.py:409
  43.4 20.5 %collective-permute-start.3 = (bf16[64,2048]{1,0:T(8,128)(2,1)}, bf16[64,2048]{1,0:T(8,128)(2,1)S(1)}, u32[]{:S(2)}, u32[]{:S(2)}) collective-permute-start(bf16[64,2048]{1,0:T(8,128)(2,1)} %get-tuple-element.192), channel_id=1, source_target_pairs={{24,0},{25,1},{26,2},{27,3},{28,4},{29,5},{30,6},{31,7},{0,8},{1,9... | collective-permute-start | bytes 786440 | tf_op jit(solution)/shard_map/ppermute | solution.py:409
  74.9 17.3 %collective-permute-done = bf16[512,1024]{1,0:T(8,128)(2,1)S(1)} collective-permute-done((bf16[512,1024]{1,0:T(8,128)(2,1)S(1)}, bf16[512,1024]{1,0:T(8,128)(2,1)S(1)}, u32[]{:S(2)}, u32[]{:S(2)}) %collective-permute-start) | collective-permute-done | bytes 1048608 | tf_op jit(solution)/shard_map/ppermute | solution.py:412
  98.4 16.3 %collective-permute-done.32 = bf16[256,2048]{1,0:T(8,128)(2,1)S(1)} collective-permute-done((bf16[256,2048]{1,0:T(8,128)(2,1)S(1)}, bf16[256,2048]{1,0:T(8,128)(2,1)S(1)}, u32[]{:S(2)}, u32[]{:S(2)}) %collective-permute-start.32) | collective-permute-done | bytes 1048608 | tf_op jit(solution)/shard_map/ppermute | solution.py:412
  116.3 20.9 %collective-permute-done.7 = bf16[256,2048]{1,0:T(8,128)(2,1)S(1)} collective-permute-done((bf16[256,2048]{1,0:T(8,128)(2,1)S(1)}, bf16[256,2048]{1,0:T(8,128)(2,1)S(1)}, u32[]{:S(2)}, u32[]{:S(2)}) %collective-permute-start.7) | collective-permute-done | bytes 1048608 | tf_op jit(solution)/shard_map/ppermute | solution.py:412
  137.2 21.0 %collective-permute-done.26 = bf16[256,2048]{1,0:T(8,128)(2,1)S(1)} collective-permute-done((bf16[256,2048]{1,0:T(8,128)(2,1)S(1)}, bf16[256,2048]{1,0:T(8,128)(2,1)S(1)}, u32[]{:S(2)}, u32[]{:S(2)}) %collective-permute-start.26) | collective-permute-done | bytes 1048608 | tf_op jit(solution)/shard_map/ppermute | solution.py:412
  166.2 18.2 %collective-permute-done.17 = bf16[256,2048]{1,0:T(8,128)(2,1)S(1)} collective-permute-done((bf16[256,2048]{1,0:T(8,128)(2,1)S(1)}, bf16[256,2048]{1,0:T(8,128)(2,1)S(1)}, u32[]{:S(2)}, u32[]{:S(2)}) %collective-permute-start.17) | collective-permute-done | bytes 1048608 | tf_op jit(solution)/shard_map/ppermute | solution.py:415
  188.3 7.3 %collective-permute-done.34 = bf16[128,2048]{1,0:T(8,128)(2,1)S(1)} collective-permute-done((bf16[128,2048]{1,0:T(8,128)(2,1)S(1)}, bf16[128,2048]{1,0:T(8,128)(2,1)S(1)}, u32[]{:S(2)}, u32[]{:S(2)}) %collective-permute-start.34) | collective-permute-done | bytes 524320 | tf_op jit(solution)/shard_map/ppermute | solution.py:415
  195.6 3.6 collective-permute-done.8
  199.3 7.6 %collective-permute-done.9 = bf16[128,2048]{1,0:T(8,128)(2,1)S(1)} collective-permute-done((bf16[128,2048]{1,0:T(8,128)(2,1)S(1)}, bf16[128,2048]{1,0:T(8,128)(2,1)S(1)}, u32[]{:S(2)}, u32[]{:S(2)}) %collective-permute-start.9) | collective-permute-done | bytes 524320 | tf_op jit(solution)/shard_map/ppermute | solution.py:415
  207.5 8.3 %collective-permute-done.28 = bf16[128,2048]{1,0:T(8,128)(2,1)S(1)} collective-permute-done((bf16[128,2048]{1,0:T(8,128)(2,1)S(1)}, bf16[128,2048]{1,0:T(8,128)(2,1)S(1)}, u32[]{:S(2)}, u32[]{:S(2)}) %collective-permute-start.28) | collective-permute-done | bytes 524320 | tf_op jit(solution)/shard_map/ppermute | solution.py:415
  227.3 11.8 %attend_fwd.1 = (bf16[512,1024]{1,0:T(8,128)(2,1)S(1)}, f32[512,128]{1,0:T(8,128)S(1)}) custom-call(bf16[512,1024]{1,0:T(8,128)(2,1)S(1)} %pad_maximum_fusion.6.q_ref, bf16[512,1024]{1,0:T(8,128)(2,1)S(1)} %pad_maximum_fusion.7.k_ref, bf16[512,1024]{1,0:T(8,128)(2,1)S(1)} %pad_maximum_fusion.8.v_ref), custom_call_target="tpu_custom_call" | custom-call | flops 2147483648 | bytes 4194304 | tf_op jit(solution)/shard_map/attend_fwd/pallas_call | solution.py:314
  243.2 4.3 multiply_convert_fusion
  248.4 7.0 %fusion.180 = (f32[2048]{0:T(1024)S(1)}, bf16[512,2048]{1,0:T(8,128)(2,1)S(1)}) fusion(f32[512,2048]{1,0:T(8,128)} %get-tuple-element.219, f32[2048]{0:T(1024)S(1)} %bitcast.110, bf16[512,1024]{1,0:T(8,128)(2,1)S(1)} %get-tuple-element.213, bf16[1024,2048]{1,0:T(8,128)(2,1)} %constant_dynamic-update-slice_fusion.37), kind=kOutput, calls=%fused_computation.334 | convolution fusion | flops 2160064512 | bytes 11550720 | tf_op jit(solution)/shard_map/dot_general | solution.py:284
  255.4 2.4 fusion.198
  257.8 2.6 convolution_convert_fusion.4
  260.4 3.7 fusion.197
  264.1 2.6 convolution_convert_fusion.2
  266.8 4.7 multiply_convert_fusion.1
  271.5 5.5 fusion.179
  277.0 3.0 multiply_reduce_fusion
  292.9 16.6 %attend_bwd.1 = (bf16[512,1024]{1,0:T(8,128)(2,1)S(1)}, bf16[512,1024]{1,0:T(8,128)(2,1)S(1)}, bf16[512,1024]{1,0:T(8,128)(2,1)S(1)}, f32[1,1024]{1,0:T(1,128)S(1)}, f32[1,1024]{1,0:T(1,128)S(1)}) custom-call(bf16[512,1024]{1,0:T(8,128)(2,1)S(1)} %copy-done.1, bf16[512,1024]{1,0:T(8,128)(2,1)S(1)} %pad_maximum_fusion.7.k_ref, ...), custom_call_target="tpu_custom_call" | custom-call | flops 5368709120 | bytes 7340032 | tf_op jit(solution)/shard_map/attend_bwd/pallas_call | solution.py:372
  318.1 3.2 fusion.16
  323.1 2.2 convolution_convert_fusion
  327.7 2.6 convolution_convert_fusion.3
  330.3 8.0 %fusion.37 = bf16[512,1024]{1,0:T(8,128)(2,1)} fusion(s32[1024]{0:T(1024)S(1)} %fusion.162, f32[512,1024]{1,0:T(8,128)S(1)} %copy-done.4, f32[512,1024]{1,0:T(8,128)} %fusion.197, bf16[512,2048]{1,0:T(8,128)(2,1)} %get-tuple-element.220, bf16[1024,2048]{1,0:T(8,128)(2,1)} %constant_dynamic-update-slice_fusion.24, f32[1024]{0:T(1024)S(1)} %bitcast.119, f32[]{:T(128)} %bitcast), kind=kOutput, calls=%fused_computation.86 | convolution fusion | flops 3225419776 | bytes 11542532 | tf_op jit(solution)/shard_map/dot_general | solution.py:628
  338.3 2.4 slice_bitcast_fusion.1
  342.2 5.5 multiply_reduce_fusion.1
  347.7 2.3 fusion.38
  352.9 47.7 %all-reduce = (f32[1024]{0:T(1024)S(1)}, f32[1024]{0:T(1024)S(1)}, f32[4096]{0:T(1024)S(1)}, f32[6,1024]{1,0:T(8,128)S(1)}) all-reduce(f32[1024]{0:T(1024)S(1)} %maximum_select_fusion.3, f32[1024]{0:T(1024)S(1)} %maximum_select_fusion.4, f32[4096]{0:T(1024)S(1)} %maximum_select_fusion.2, ...), channel_id=1, replica_groups=mesh['wide'=16,'tp'=2] {'wide','tp'}, use_global_device_ids=true, to_apply=%region_8.9 | all-reduce | flops 12288 | bytes 98304 | tf_op jit(solution)/shard_map/psum | solution.py:624
  401.3 2.2 collective-permute-start.39
  411.9 2.6 convolution_convert_fusion.5
  415.0 2.4 maximum_select_fusion
  442.5 6.1 %collective-permute-done.51 = bf16[128,2048]{1,0:T(8,128)(2,1)S(1)} collective-permute-done((bf16[128,2048]{1,0:T(8,128)(2,1)S(1)}, bf16[128,2048]{1,0:T(8,128)(2,1)S(1)}, u32[]{:S(2)}, u32[]{:S(2)}) %collective-permute-start.51) | collective-permute-done | bytes 524320 | tf_op jit(solution)/shard_map/ppermute | solution.py:415
  451.5 6.4 %collective-permute-done.53 = bf16[128,2048]{1,0:T(8,128)(2,1)S(1)} collective-permute-done((bf16[128,2048]{1,0:T(8,128)(2,1)S(1)}, bf16[128,2048]{1,0:T(8,128)(2,1)S(1)}, u32[]{:S(2)}, u32[]{:S(2)}) %collective-permute-start.53) | collective-permute-done | bytes 524320 | tf_op jit(solution)/shard_map/ppermute | solution.py:412
  462.1 7.0 %collective-permute-done.44 = bf16[128,2048]{1,0:T(8,128)(2,1)S(1)} collective-permute-done((bf16[128,2048]{1,0:T(8,128)(2,1)S(1)}, bf16[128,2048]{1,0:T(8,128)(2,1)S(1)}, u32[]{:S(2)}, u32[]{:S(2)}) %collective-permute-start.44) | collective-permute-done | bytes 524320 | tf_op jit(solution)/shard_map/ppermute | solution.py:412
  469.9 21.7 %collective-permute-done.61 = bf16[256,2048]{1,0:T(8,128)(2,1)S(1)} collective-permute-done((bf16[256,2048]{1,0:T(8,128)(2,1)S(1)}, bf16[256,2048]{1,0:T(8,128)(2,1)S(1)}, u32[]{:S(2)}, u32[]{:S(2)}) %collective-permute-start.61) | collective-permute-done | bytes 1048608 | tf_op jit(solution)/shard_map/ppermute | solution.py:412
  494.7 19.3 %collective-permute-done.52 = bf16[256,2048]{1,0:T(8,128)(2,1)S(1)} collective-permute-done((bf16[256,2048]{1,0:T(8,128)(2,1)S(1)}, bf16[256,2048]{1,0:T(8,128)(2,1)S(1)}, u32[]{:S(2)}, u32[]{:S(2)}) %collective-permute-start.52) | collective-permute-done | bytes 1048608 | tf_op jit(solution)/shard_map/ppermute | solution.py:412
  516.4 18.6 %collective-permute-done.43 = bf16[256,2048]{1,0:T(8,128)(2,1)S(1)} collective-permute-done((bf16[256,2048]{1,0:T(8,128)(2,1)S(1)}, bf16[256,2048]{1,0:T(8,128)(2,1)S(1)}, u32[]{:S(2)}, u32[]{:S(2)}) %collective-permute-start.43) | collective-permute-done | bytes 1048608 | tf_op jit(solution)/shard_map/ppermute | solution.py:412
  534.9 3.8 collective-permute-start.57
  539.6 3.8 collective-permute-start.48
  544.4 12.8 %collective-permute-done.46 = bf16[64,2048]{1,0:T(8,128)(2,1)S(1)} collective-permute-done((bf16[64,2048]{1,0:T(8,128)(2,1)S(1)}, bf16[64,2048]{1,0:T(8,128)(2,1)S(1)}, u32[]{:S(2)}, u32[]{:S(2)}) %collective-permute-start.46) | collective-permute-done | bytes 262176 | tf_op jit(solution)/shard_map/ppermute | solution.py:409
  557.2 12.3 %collective-permute-start.56 = (bf16[64,2048]{1,0:T(8,128)(2,1)S(1)}, bf16[64,2048]{1,0:T(8,128)(2,1)S(1)}, u32[]{:S(2)}, u32[]{:S(2)}) collective-permute-start(bf16[64,2048]{1,0:T(8,128)(2,1)S(1)} %get-tuple-element.160), channel_id=1, source_target_pairs={{16,0},{17,1},{18,2},{19,3},{20,4},{21,5},{22,6},{23,7},{24,8},{25... | collective-permute-start | bytes 786440 | tf_op jit(solution)/shard_map/ppermute | solution.py:409
  569.5 7.9 %collective-permute-done.47 = bf16[64,2048]{1,0:T(8,128)(2,1)S(1)} collective-permute-done((bf16[64,2048]{1,0:T(8,128)(2,1)S(1)}, bf16[64,2048]{1,0:T(8,128)(2,1)S(1)}, u32[]{:S(2)}, u32[]{:S(2)}) %collective-permute-start.47) | collective-permute-done | bytes 262176 | tf_op jit(solution)/shard_map/ppermute | solution.py:409
  (394 shorter events, 145.1 us)
Async XLA Ops:
  0.7 36.4 %collective-permute-start.22 = (bf16[64,2048]{1,0:T(8,128)(2,1)}, bf16[64,2048]{1,0:T(8,128)(2,1)S(1)}, u32[]{:S(2)}, u32[]{:S(2)}) collective-permute-start(bf16[64,2048]{1,0:T(8,128)(2,1)} %bitcast.86), channel_id=1, source_target_pairs={{24,0},{25,1},{26,2},{27,3},{28,4},{29,5},{30,6},{31,7},{0,8},{1,9... | collective-permute-start | bytes 786440 | tf_op jit(solution)/shard_map/ppermute | solution.py:409
  3.8 33.3 %collective-permute-start.21 = (bf16[64,2048]{1,0:T(8,128)(2,1)}, bf16[64,2048]{1,0:T(8,128)(2,1)S(1)}, u32[]{:S(2)}, u32[]{:S(2)}) collective-permute-start(bf16[64,2048]{1,0:T(8,128)(2,1)} %bitcast.87), channel_id=1, source_target_pairs={{16,0},{17,1},{18,2},{19,3},{20,4},{21,5},{22,6},{23,7},{24,8},{25... | collective-permute-start | bytes 786440 | tf_op jit(solution)/shard_map/ppermute | solution.py:409
  9.9 60.3 %collective-permute-start.15 = (bf16[64,2048]{1,0:T(8,128)(2,1)}, bf16[64,2048]{1,0:T(8,128)(2,1)}, u32[]{:S(2)}, u32[]{:S(2)}) collective-permute-start(bf16[64,2048]{1,0:T(8,128)(2,1)} %param.32), channel_id=1, source_target_pairs={{16,0},{17,1},{18,2},{19,3},{20,4},{21,5},{22,6},{23,7},{24,8},{25... | collective-permute-start | bytes 786440 | tf_op jit(solution)/shard_map/ppermute | solution.py:409
  19.9 23.5 %collective-permute-start.14 = (bf16[64,2048]{1,0:T(8,128)(2,1)S(1)}, bf16[64,2048]{1,0:T(8,128)(2,1)S(1)}, u32[]{:S(2)}, u32[]{:S(2)}) collective-permute-start(bf16[64,2048]{1,0:T(8,128)(2,1)S(1)} %copy-done.50), channel_id=1, source_target_pairs={{8,0},{9,1},{10,2},{11,3},{12,4},{13,5},{14,6},{15,7},{16,8},{17,9... | collective-permute-start | bytes 786440 | tf_op jit(solution)/shard_map/ppermute | solution.py:409
  22.6 51.0 %collective-permute-start.16 = (bf16[64,2048]{1,0:T(8,128)(2,1)S(1)}, bf16[64,2048]{1,0:T(8,128)(2,1)S(1)}, u32[]{:S(2)}, u32[]{:S(2)}) collective-permute-start(bf16[64,2048]{1,0:T(8,128)(2,1)S(1)} %copy-done.50), channel_id=1, source_target_pairs={{24,0},{25,1},{26,2},{27,3},{28,4},{29,5},{30,6},{31,7},{0,8},{1,9... | collective-permute-start | bytes 786440 | tf_op jit(solution)/shard_map/ppermute | solution.py:409
  37.1 31.6 %collective-permute-start.2 = (bf16[64,2048]{1,0:T(8,128)(2,1)}, bf16[64,2048]{1,0:T(8,128)(2,1)S(1)}, u32[]{:S(2)}, u32[]{:S(2)}) collective-permute-start(bf16[64,2048]{1,0:T(8,128)(2,1)} %get-tuple-element.192), channel_id=1, source_target_pairs={{16,0},{17,1},{18,2},{19,3},{20,4},{21,5},{22,6},{23,7},{24,8},{25... | collective-permute-start | bytes 786440 | tf_op jit(solution)/shard_map/ppermute | solution.py:409
  37.1 29.1 %collective-permute-start.1 = (bf16[64,2048]{1,0:T(8,128)(2,1)}, bf16[64,2048]{1,0:T(8,128)(2,1)S(1)}, u32[]{:S(2)}, u32[]{:S(2)}) collective-permute-start(bf16[64,2048]{1,0:T(8,128)(2,1)} %get-tuple-element.192), channel_id=1, source_target_pairs={{8,0},{9,1},{10,2},{11,3},{12,4},{13,5},{14,6},{15,7},{16,8},{17,9... | collective-permute-start | bytes 786440 | tf_op jit(solution)/shard_map/ppermute | solution.py:409
  43.4 28.6 %collective-permute-start.3 = (bf16[64,2048]{1,0:T(8,128)(2,1)}, bf16[64,2048]{1,0:T(8,128)(2,1)S(1)}, u32[]{:S(2)}, u32[]{:S(2)}) collective-permute-start(bf16[64,2048]{1,0:T(8,128)(2,1)} %get-tuple-element.192), channel_id=1, source_target_pairs={{24,0},{25,1},{26,2},{27,3},{28,4},{29,5},{30,6},{31,7},{0,8},{1,9... | collective-permute-start | bytes 786440 | tf_op jit(solution)/shard_map/ppermute | solution.py:409
  66.2 26.1 %collective-permute-start = (bf16[512,1024]{1,0:T(8,128)(2,1)S(1)}, bf16[512,1024]{1,0:T(8,128)(2,1)S(1)}, u32[]{:S(2)}, u32[]{:S(2)}) collective-permute-start(bf16[512,1024]{1,0:T(8,128)(2,1)S(1)} %pad_maximum_fusion.4), channel_id=1, source_target_pairs={{1,0},{0,1},{3,2},{2,3},{5,4},{4,5},{7,6},{6,7},{9,8},{8,9},{11,10... | collective-permute-start | bytes 3145736 | tf_op jit(solution)/shard_map/ppermute | solution.py:412
  68.6 46.1 %collective-permute-start.32 = (bf16[256,2048]{1,0:T(8,128)(2,1)S(1)}, bf16[256,2048]{1,0:T(8,128)(2,1)S(1)}, u32[]{:S(2)}, u32[]{:S(2)}) collective-permute-start(bf16[256,2048]{1,0:T(8,128)(2,1)S(1)} %pad_maximum_fusion.9), channel_id=1, source_target_pairs={{1,0},{0,1},{3,2},{2,3},{5,4},{4,5},{7,6},{6,7},{9,8},{8,9},{11,10... | collective-permute-start | bytes 3145736 | tf_op jit(solution)/shard_map/ppermute | solution.py:412
  70.2 91.0 %collective-permute-start.24 = (bf16[256,2048]{1,0:T(8,128)(2,1)S(1)}, bf16[256,2048]{1,0:T(8,128)(2,1)S(1)}, u32[]{:S(2)}, u32[]{:S(2)}) collective-permute-start(bf16[256,2048]{1,0:T(8,128)(2,1)S(1)} %pad_maximum_fusion.9), channel_id=1, source_target_pairs={{2,0},{3,1},{0,2},{1,3},{6,4},{7,5},{4,6},{5,7},{10,8},{11,9},{8,1... | collective-permute-start | bytes 3145736 | tf_op jit(solution)/shard_map/ppermute | solution.py:418
  72.0 87.9 %collective-permute-start.23 = (bf16[256,2048]{1,0:T(8,128)(2,1)S(1)}, bf16[256,2048]{1,0:T(8,128)(2,1)S(1)}, u32[]{:S(2)}, u32[]{:S(2)}) collective-permute-start(bf16[256,2048]{1,0:T(8,128)(2,1)S(1)} %pad_maximum_fusion.9), channel_id=1, source_target_pairs={{4,0},{5,1},{6,2},{7,3},{0,4},{1,5},{2,6},{3,7},{12,8},{13,9},{14,... | collective-permute-start | bytes 3145736 | tf_op jit(solution)/shard_map/ppermute | solution.py:415
  73.6 63.5 %collective-permute-start.7 = (bf16[256,2048]{1,0:T(8,128)(2,1)S(1)}, bf16[256,2048]{1,0:T(8,128)(2,1)S(1)}, u32[]{:S(2)}, u32[]{:S(2)}) collective-permute-start(bf16[256,2048]{1,0:T(8,128)(2,1)S(1)} %pad_maximum_fusion.5), channel_id=1, source_target_pairs={{1,0},{0,1},{3,2},{2,3},{5,4},{4,5},{7,6},{6,7},{9,8},{8,9},{11,10... | collective-permute-start | bytes 3145736 | tf_op jit(solution)/shard_map/ppermute | solution.py:412
  92.2 66.0 %collective-permute-start.26 = (bf16[256,2048]{1,0:T(8,128)(2,1)S(1)}, bf16[256,2048]{1,0:T(8,128)(2,1)S(1)}, u32[]{:S(2)}, u32[]{:S(2)}) collective-permute-start(bf16[256,2048]{1,0:T(8,128)(2,1)S(1)} %get-tuple-element.185), channel_id=1, source_target_pairs={{1,0},{0,1},{3,2},{2,3},{5,4},{4,5},{7,6},{6,7},{9,8},{8,9},{11,10... | collective-permute-start | bytes 3145736 | tf_op jit(solution)/shard_map/ppermute | solution.py:412
  114.7 48.2 %collective-permute-start.4 = (bf16[256,2048]{1,0:T(8,128)(2,1)S(1)}, bf16[256,2048]{1,0:T(8,128)(2,1)S(1)}, u32[]{:S(2)}, u32[]{:S(2)}) collective-permute-start(bf16[256,2048]{1,0:T(8,128)(2,1)S(1)} %pad_maximum_fusion.5), channel_id=1, source_target_pairs={{4,0},{5,1},{6,2},{7,3},{0,4},{1,5},{2,6},{3,7},{12,8},{13,9},{14,... | collective-permute-start | bytes 3145736 | tf_op jit(solution)/shard_map/ppermute | solution.py:415
  137.2 27.3 %collective-permute-start.5 = (bf16[256,2048]{1,0:T(8,128)(2,1)S(1)}, bf16[256,2048]{1,0:T(8,128)(2,1)S(1)}, u32[]{:S(2)}, u32[]{:S(2)}) collective-permute-start(bf16[256,2048]{1,0:T(8,128)(2,1)S(1)} %pad_maximum_fusion.5), channel_id=1, source_target_pairs={{2,0},{3,1},{0,2},{1,3},{6,4},{7,5},{4,6},{5,7},{10,8},{11,9},{8,1... | collective-permute-start | bytes 3145736 | tf_op jit(solution)/shard_map/ppermute | solution.py:418
  158.3 26.1 %collective-permute-start.17 = (bf16[256,2048]{1,0:T(8,128)(2,1)S(1)}, bf16[256,2048]{1,0:T(8,128)(2,1)S(1)}, u32[]{:S(2)}, u32[]{:S(2)}) collective-permute-start(bf16[256,2048]{1,0:T(8,128)(2,1)S(1)} %get-tuple-element.185), channel_id=1, source_target_pairs={{4,0},{5,1},{6,2},{7,3},{0,4},{1,5},{2,6},{3,7},{12,8},{13,9},{14,... | collective-permute-start | bytes 3145736 | tf_op jit(solution)/shard_map/ppermute | solution.py:415
  159.9 26.1 %collective-permute-start.18 = (bf16[256,2048]{1,0:T(8,128)(2,1)S(1)}, bf16[256,2048]{1,0:T(8,128)(2,1)S(1)}, u32[]{:S(2)}, u32[]{:S(2)}) collective-permute-start(bf16[256,2048]{1,0:T(8,128)(2,1)S(1)} %get-tuple-element.185), channel_id=1, source_target_pairs={{2,0},{3,1},{0,2},{1,3},{6,4},{7,5},{4,6},{5,7},{10,8},{11,9},{8,1... | collective-permute-start | bytes 3145736 | tf_op jit(solution)/shard_map/ppermute | solution.py:418
  161.2 34.5 %collective-permute-start.34 = (bf16[128,2048]{1,0:T(8,128)(2,1)S(1)}, bf16[128,2048]{1,0:T(8,128)(2,1)S(1)}, u32[]{:S(2)}, u32[]{:S(2)}) collective-permute-start(bf16[128,2048]{1,0:T(8,128)(2,1)S(1)} %slice.532), channel_id=1, source_target_pairs={{4,0},{5,1},{6,2},{7,3},{0,4},{1,5},{2,6},{3,7},{12,8},{13,9},{14,... | collective-permute-start | bytes 1572872 | tf_op jit(solution)/shard_map/ppermute | solution.py:415
  162.9 24.9 %collective-permute-start.33 = (bf16[128,2048]{1,0:T(8,128)(2,1)S(1)}, bf16[128,2048]{1,0:T(8,128)(2,1)S(1)}, u32[]{:S(2)}, u32[]{:S(2)}) collective-permute-start(bf16[128,2048]{1,0:T(8,128)(2,1)S(1)} %slice.531), channel_id=1, source_target_pairs={{1,0},{0,1},{3,2},{2,3},{5,4},{4,5},{7,6},{6,7},{9,8},{8,9},{11,10... | collective-permute-start | bytes 1572872 | tf_op jit(solution)/shard_map/ppermute | solution.py:412
  164.5 42.4 %collective-permute-start.9 = (bf16[128,2048]{1,0:T(8,128)(2,1)S(1)}, bf16[128,2048]{1,0:T(8,128)(2,1)S(1)}, u32[]{:S(2)}, u32[]{:S(2)}) collective-permute-start(bf16[128,2048]{1,0:T(8,128)(2,1)S(1)} %slice.514), channel_id=1, source_target_pairs={{4,0},{5,1},{6,2},{7,3},{0,4},{1,5},{2,6},{3,7},{12,8},{13,9},{14,... | collective-permute-start | bytes 1572872 | tf_op jit(solution)/shard_map/ppermute | solution.py:415
  186.0 29.8 %collective-permute-start.28 = (bf16[128,2048]{1,0:T(8,128)(2,1)S(1)}, bf16[128,2048]{1,0:T(8,128)(2,1)S(1)}, u32[]{:S(2)}, u32[]{:S(2)}) collective-permute-start(bf16[128,2048]{1,0:T(8,128)(2,1)S(1)} %slice.529), channel_id=1, source_target_pairs={{4,0},{5,1},{6,2},{7,3},{0,4},{1,5},{2,6},{3,7},{12,8},{13,9},{14,... | collective-permute-start | bytes 1572872 | tf_op jit(solution)/shard_map/ppermute | solution.py:415
  195.6 20.2 %collective-permute-start.35 = (bf16[256,2048]{1,0:T(8,128)(2,1)S(1)}, bf16[256,2048]{1,0:T(8,128)(2,1)S(1)}, u32[]{:S(2)}, u32[]{:S(2)}) collective-permute-start(bf16[256,2048]{1,0:T(8,128)(2,1)S(1)} %collective-permute-done.32), channel_id=1, source_target_pairs={{2,0},{3,1},{0,2},{1,3},{6,4},{7,5},{4,6},{5,7},{10,8},{11,9},{8,1... | collective-permute-start | bytes 3145736 | tf_op jit(solution)/shard_map/ppermute | solution.py:418
  216.5 30.9 %collective-permute-start.37 = (bf16[128,2048]{1,0:T(8,128)(2,1)S(1)}, bf16[128,2048]{1,0:T(8,128)(2,1)S(1)}, u32[]{:S(2)}, u32[]{:S(2)}) collective-permute-start(bf16[128,2048]{1,0:T(8,128)(2,1)S(1)} %collective-permute-done.34), channel_id=1, source_target_pairs={{2,0},{3,1},{0,2},{1,3},{6,4},{7,5},{4,6},{5,7},{10,8},{11,9},{8,1... | collective-permute-start | bytes 1572872 | tf_op jit(solution)/shard_map/ppermute | solution.py:418
  217.8 23.4 %collective-permute-start.36 = (bf16[128,2048]{1,0:T(8,128)(2,1)S(1)}, bf16[128,2048]{1,0:T(8,128)(2,1)S(1)}, u32[]{:S(2)}, u32[]{:S(2)}) collective-permute-start(bf16[128,2048]{1,0:T(8,128)(2,1)S(1)} %collective-permute-done.33), channel_id=1, source_target_pairs={{2,0},{3,1},{0,2},{1,3},{6,4},{7,5},{4,6},{5,7},{10,8},{11,9},{8,1... | collective-permute-start | bytes 1572872 | tf_op jit(solution)/shard_map/ppermute | solution.py:418
  221.9 21.2 %collective-permute-start.31 = (bf16[128,2048]{1,0:T(8,128)(2,1)S(1)}, bf16[128,2048]{1,0:T(8,128)(2,1)S(1)}, u32[]{:S(2)}, u32[]{:S(2)}) collective-permute-start(bf16[128,2048]{1,0:T(8,128)(2,1)S(1)} %collective-permute-done.28), channel_id=1, source_target_pairs={{2,0},{3,1},{0,2},{1,3},{6,4},{7,5},{4,6},{5,7},{10,8},{11,9},{8,1... | collective-permute-start | bytes 1572872 | tf_op jit(solution)/shard_map/ppermute | solution.py:418
  327.0 91.9 %collective-permute-start.59 = (bf16[512,2048]{1,0:T(8,128)(2,1)}, bf16[512,2048]{1,0:T(8,128)(2,1)}, u32[]{:S(2)}, u32[]{:S(2)}) collective-permute-start(bf16[512,2048]{1,0:T(8,128)(2,1)} %convolution_convert_fusion.2), channel_id=1, source_target_pairs={{2,0},{3,1},{0,2},{1,3},{6,4},{7,5},{4,6},{5,7},{10,8},{11,9},{8,1... | collective-permute-start | bytes 6291464 | tf_op jit(solution)/shard_map/ppermute | solution.py:418
  327.1 95.7 %collective-permute-start.50 = (bf16[512,2048]{1,0:T(8,128)(2,1)}, bf16[512,2048]{1,0:T(8,128)(2,1)}, u32[]{:S(2)}, u32[]{:S(2)}) collective-permute-start(bf16[512,2048]{1,0:T(8,128)(2,1)} %convolution_convert_fusion.4), channel_id=1, source_target_pairs={{2,0},{3,1},{0,2},{1,3},{6,4},{7,5},{4,6},{5,7},{10,8},{11,9},{8,1... | collective-permute-start | bytes 6291464 | tf_op jit(solution)/shard_map/ppermute | solution.py:418
  340.7 73.8 %collective-permute-start.38 = (bf16[256,1024]{1,0:T(8,128)(2,1)}, bf16[256,1024]{1,0:T(8,128)(2,1)}, u32[]{:S(2)}, u32[]{:S(2)}) collective-permute-start(bf16[256,1024]{1,0:T(8,128)(2,1)} %get-tuple-element.181), channel_id=1, source_target_pairs={{1,0},{0,1},{3,2},{2,3},{5,4},{4,5},{7,6},{6,7},{9,8},{8,9},{11,10... | collective-permute-start | bytes 1572872 | tf_op jit(solution)/shard_map/ppermute | solution.py:412
  403.5 31.4 %collective-permute-start.58 = (bf16[512,2048]{1,0:T(8,128)(2,1)}, bf16[512,2048]{1,0:T(8,128)(2,1)}, u32[]{:S(2)}, u32[]{:S(2)}) collective-permute-start(bf16[512,2048]{1,0:T(8,128)(2,1)} %convolution_convert_fusion.3), channel_id=1, source_target_pairs={{2,0},{3,1},{0,2},{1,3},{6,4},{7,5},{4,6},{5,7},{10,8},{11,9},{8,1... | collective-permute-start | bytes 6291464 | tf_op jit(solution)/shard_map/ppermute | solution.py:418
  414.5 24.1 %collective-permute-start.49 = (bf16[512,2048]{1,0:T(8,128)(2,1)}, bf16[512,2048]{1,0:T(8,128)(2,1)S(1)}, u32[]{:S(2)}, u32[]{:S(2)}) collective-permute-start(bf16[512,2048]{1,0:T(8,128)(2,1)} %convolution_convert_fusion.5), channel_id=1, source_target_pairs={{2,0},{3,1},{0,2},{1,3},{6,4},{7,5},{4,6},{5,7},{10,8},{11,9},{8,1... | collective-permute-start | bytes 6291464 | tf_op jit(solution)/shard_map/ppermute | solution.py:418
  435.0 22.9 %collective-permute-start.53 = (bf16[128,2048]{1,0:T(8,128)(2,1)S(1)}, bf16[128,2048]{1,0:T(8,128)(2,1)S(1)}, u32[]{:S(2)}, u32[]{:S(2)}) collective-permute-start(bf16[128,2048]{1,0:T(8,128)(2,1)S(1)} %copy-done.42), channel_id=1, source_target_pairs={{1,0},{0,1},{3,2},{2,3},{5,4},{4,5},{7,6},{6,7},{9,8},{8,9},{11,10... | collective-permute-start | bytes 1572872 | tf_op jit(solution)/shard_map/ppermute | solution.py:412
  438.6 21.2 %collective-permute-start.42 = (bf16[128,2048]{1,0:T(8,128)(2,1)S(1)}, bf16[128,2048]{1,0:T(8,128)(2,1)S(1)}, u32[]{:S(2)}, u32[]{:S(2)}) collective-permute-start(bf16[128,2048]{1,0:T(8,128)(2,1)S(1)} %get-tuple-element.166), channel_id=1, source_target_pairs={{4,0},{5,1},{6,2},{7,3},{0,4},{1,5},{2,6},{3,7},{12,8},{13,9},{14,... | collective-permute-start | bytes 1572872 | tf_op jit(solution)/shard_map/ppermute | solution.py:415
  440.5 28.6 %collective-permute-start.44 = (bf16[128,2048]{1,0:T(8,128)(2,1)S(1)}, bf16[128,2048]{1,0:T(8,128)(2,1)S(1)}, u32[]{:S(2)}, u32[]{:S(2)}) collective-permute-start(bf16[128,2048]{1,0:T(8,128)(2,1)S(1)} %get-tuple-element.167), channel_id=1, source_target_pairs={{1,0},{0,1},{3,2},{2,3},{5,4},{4,5},{7,6},{6,7},{9,8},{8,9},{11,10... | collective-permute-start | bytes 1572872 | tf_op jit(solution)/shard_map/ppermute | solution.py:412
  448.6 43.0 %collective-permute-start.61 = (bf16[256,2048]{1,0:T(8,128)(2,1)S(1)}, bf16[256,2048]{1,0:T(8,128)(2,1)S(1)}, u32[]{:S(2)}, u32[]{:S(2)}) collective-permute-start(bf16[256,2048]{1,0:T(8,128)(2,1)S(1)} %convert_element_type.339), channel_id=1, source_target_pairs={{1,0},{0,1},{3,2},{2,3},{5,4},{4,5},{7,6},{6,7},{9,8},{8,9},{11,10... | collective-permute-start | bytes 3145736 | tf_op jit(solution)/shard_map/ppermute | solution.py:412
  450.6 63.5 %collective-permute-start.52 = (bf16[256,2048]{1,0:T(8,128)(2,1)S(1)}, bf16[256,2048]{1,0:T(8,128)(2,1)S(1)}, u32[]{:S(2)}, u32[]{:S(2)}) collective-permute-start(bf16[256,2048]{1,0:T(8,128)(2,1)S(1)} %convert_element_type.316), channel_id=1, source_target_pairs={{1,0},{0,1},{3,2},{2,3},{5,4},{4,5},{7,6},{6,7},{9,8},{8,9},{11,10... | collective-permute-start | bytes 3145736 | tf_op jit(solution)/shard_map/ppermute | solution.py:412
  457.9 34.6 %collective-permute-start.63 = (bf16[256,2048]{1,0:T(8,128)(2,1)S(1)}, bf16[256,2048]{1,0:T(8,128)(2,1)S(1)}, u32[]{:S(2)}, u32[]{:S(2)}) collective-permute-start(bf16[256,2048]{1,0:T(8,128)(2,1)S(1)} %convert_element_type.345), channel_id=1, source_target_pairs={{4,0},{5,1},{6,2},{7,3},{0,4},{1,5},{2,6},{3,7},{12,8},{13,9},{14,... | collective-permute-start | bytes 3145736 | tf_op jit(solution)/shard_map/ppermute | solution.py:415
  459.8 55.8 %collective-permute-start.54 = (bf16[256,2048]{1,0:T(8,128)(2,1)S(1)}, bf16[256,2048]{1,0:T(8,128)(2,1)S(1)}, u32[]{:S(2)}, u32[]{:S(2)}) collective-permute-start(bf16[256,2048]{1,0:T(8,128)(2,1)S(1)} %convert_element_type.322), channel_id=1, source_target_pairs={{4,0},{5,1},{6,2},{7,3},{0,4},{1,5},{2,6},{3,7},{12,8},{13,9},{14,... | collective-permute-start | bytes 3145736 | tf_op jit(solution)/shard_map/ppermute | solution.py:415
  469.1 65.8 %collective-permute-start.43 = (bf16[256,2048]{1,0:T(8,128)(2,1)S(1)}, bf16[256,2048]{1,0:T(8,128)(2,1)S(1)}, u32[]{:S(2)}, u32[]{:S(2)}) collective-permute-start(bf16[256,2048]{1,0:T(8,128)(2,1)S(1)} %convert_element_type.293), channel_id=1, source_target_pairs={{1,0},{0,1},{3,2},{2,3},{5,4},{4,5},{7,6},{6,7},{9,8},{8,9},{11,10... | collective-permute-start | bytes 3145736 | tf_op jit(solution)/shard_map/ppermute | solution.py:412
  491.6 43.4 %collective-permute-start.45 = (bf16[256,2048]{1,0:T(8,128)(2,1)S(1)}, bf16[256,2048]{1,0:T(8,128)(2,1)S(1)}, u32[]{:S(2)}, u32[]{:S(2)}) collective-permute-start(bf16[256,2048]{1,0:T(8,128)(2,1)S(1)} %convert_element_type.299), channel_id=1, source_target_pairs={{4,0},{5,1},{6,2},{7,3},{0,4},{1,5},{2,6},{3,7},{12,8},{13,9},{14,... | collective-permute-start | bytes 3145736 | tf_op jit(solution)/shard_map/ppermute | solution.py:415
  494.7 44.9 %collective-permute-start.64 = (bf16[64,2048]{1,0:T(8,128)(2,1)S(1)}, bf16[64,2048]{1,0:T(8,128)(2,1)S(1)}, u32[]{:S(2)}, u32[]{:S(2)}) collective-permute-start(bf16[64,2048]{1,0:T(8,128)(2,1)S(1)} %get-tuple-element.153), channel_id=1, source_target_pairs={{24,0},{25,1},{26,2},{27,3},{28,4},{29,5},{30,6},{31,7},{0,8},{1,9... | collective-permute-start | bytes 786440 | tf_op jit(solution)/shard_map/ppermute | solution.py:409
  514.1 25.6 %collective-permute-start.66 = (bf16[64,2048]{1,0:T(8,128)(2,1)S(1)}, bf16[64,2048]{1,0:T(8,128)(2,1)S(1)}, u32[]{:S(2)}, u32[]{:S(2)}) collective-permute-start(bf16[64,2048]{1,0:T(8,128)(2,1)S(1)} %get-tuple-element.154), channel_id=1, source_target_pairs={{8,0},{9,1},{10,2},{11,3},{12,4},{13,5},{14,6},{15,7},{16,8},{17,9... | collective-permute-start | bytes 786440 | tf_op jit(solution)/shard_map/ppermute | solution.py:409
  515.6 27.8 %collective-permute-start.65 = (bf16[64,2048]{1,0:T(8,128)(2,1)S(1)}, bf16[64,2048]{1,0:T(8,128)(2,1)S(1)}, u32[]{:S(2)}, u32[]{:S(2)}) collective-permute-start(bf16[64,2048]{1,0:T(8,128)(2,1)S(1)} %get-tuple-element.155), channel_id=1, source_target_pairs={{16,0},{17,1},{18,2},{19,3},{20,4},{21,5},{22,6},{23,7},{24,8},{25... | collective-permute-start | bytes 786440 | tf_op jit(solution)/shard_map/ppermute | solution.py:409
  534.9 44.0 %collective-permute-start.55 = (bf16[64,2048]{1,0:T(8,128)(2,1)S(1)}, bf16[64,2048]{1,0:T(8,128)(2,1)S(1)}, u32[]{:S(2)}, u32[]{:S(2)}) collective-permute-start(bf16[64,2048]{1,0:T(8,128)(2,1)S(1)} %get-tuple-element.158), channel_id=1, source_target_pairs={{24,0},{25,1},{26,2},{27,3},{28,4},{29,5},{30,6},{31,7},{0,8},{1,9... | collective-permute-start | bytes 786440 | tf_op jit(solution)/shard_map/ppermute | solution.py:409
  534.9 44.0 %collective-permute-start.57 = (bf16[64,2048]{1,0:T(8,128)(2,1)S(1)}, bf16[64,2048]{1,0:T(8,128)(2,1)S(1)}, u32[]{:S(2)}, u32[]{:S(2)}) collective-permute-start(bf16[64,2048]{1,0:T(8,128)(2,1)S(1)} %get-tuple-element.159), channel_id=1, source_target_pairs={{8,0},{9,1},{10,2},{11,3},{12,4},{13,5},{14,6},{15,7},{16,8},{17,9... | collective-permute-start | bytes 786440 | tf_op jit(solution)/shard_map/ppermute | solution.py:409
  539.6 29.8 %collective-permute-start.48 = (bf16[64,2048]{1,0:T(8,128)(2,1)S(1)}, bf16[64,2048]{1,0:T(8,128)(2,1)S(1)}, u32[]{:S(2)}, u32[]{:S(2)}) collective-permute-start(bf16[64,2048]{1,0:T(8,128)(2,1)S(1)} %get-tuple-element.164), channel_id=1, source_target_pairs={{8,0},{9,1},{10,2},{11,3},{12,4},{13,5},{14,6},{15,7},{16,8},{17,9... | collective-permute-start | bytes 786440 | tf_op jit(solution)/shard_map/ppermute | solution.py:409
  543.4 33.9 %collective-permute-start.47 = (bf16[64,2048]{1,0:T(8,128)(2,1)S(1)}, bf16[64,2048]{1,0:T(8,128)(2,1)S(1)}, u32[]{:S(2)}, u32[]{:S(2)}) collective-permute-start(bf16[64,2048]{1,0:T(8,128)(2,1)S(1)} %get-tuple-element.165), channel_id=1, source_target_pairs={{16,0},{17,1},{18,2},{19,3},{20,4},{21,5},{22,6},{23,7},{24,8},{25... | collective-permute-start | bytes 786440 | tf_op jit(solution)/shard_map/ppermute | solution.py:409
  557.2 23.9 %collective-permute-start.56 = (bf16[64,2048]{1,0:T(8,128)(2,1)S(1)}, bf16[64,2048]{1,0:T(8,128)(2,1)S(1)}, u32[]{:S(2)}, u32[]{:S(2)}) collective-permute-start(bf16[64,2048]{1,0:T(8,128)(2,1)S(1)} %get-tuple-element.160), channel_id=1, source_target_pairs={{16,0},{17,1},{18,2},{19,3},{20,4},{21,5},{22,6},{23,7},{24,8},{25... | collective-permute-start | bytes 786440 | tf_op jit(solution)/shard_map/ppermute | solution.py:409
  (85 other events, 1315.8 us)

commit v2 on v1

--- a/solution.py
+++ b/solution.py
@@ -417,61 +417,61 @@
     def c(self, rows):
         return lax.ppermute(rows, AXES, self.twin)
 
-
-def gather_chunk(links, shard):
-    along = jnp.concatenate([shard] + [links.from_z(shard, k) for k in range(1, links.nz)], axis=0)
+    def flip(self, rows, bit):
+        swap = self.table(lambda z, y, c, x: (z ^ bit, y, c, x))
+        return lax.ppermute(rows, AXES, swap)
+
+
+def after(done, *values):
+    return lax.optimization_barrier((values, done))[0]
+
+
+def gather_along(links, shard):
+    steps = [links.from_z(shard, k) for k in range(1, links.nz)]
+    return jnp.concatenate([shard] + steps, axis=0)
+
+
+def gather_near(links, along):
+    return links.x(along), links.y(along)
+
+
+def gather_far(links, along, near):
+    by_x, by_y = near
     half = along.shape[0] // 2
-    by_x = links.x(along)
-    by_y = links.y(along)
     far_a = links.x(by_y[:half])
     far_b = links.y(by_x[half:])
-    mine = (along, by_x, by_y, far_a, far_b)
-    other = tuple(links.c(piece) for piece in mine)
+    other = [links.c(piece) for piece in (along, by_x, by_y, far_a, far_b)]
     own_half = jnp.concatenate([along, by_y, other[0], other[2]], axis=0)
-    far_half = jnp.concatenate(
-        [by_x, far_a, far_b, other[1], other[3], other[4]], axis=0
-    )
+    far_half = jnp.concatenate([by_x, far_a, far_b, other[1], other[3], other[4]], axis=0)
     return own_half, far_half
 
 
-def scatter_chunk(links, make_piece, rows_all):
-    half_rows = rows_all // 2
-    quarter = rows_all // 4
-    sent = [make_piece(half_rows, half_rows, kx, None) for kx in range(2)]
-    got = [links.c(piece) for piece in sent]
-    keep = {
-        (kx, ky): make_piece(ky * quarter, quarter, kx, got[kx][ky * quarter : (ky + 1) * quarter])
-        for kx, ky in ((1, 1), (1, 0), (0, 1), (0, 0))
-    }
+def scatter_keep(links, keep):
+    f32 = jnp.float32
+    quarter = keep[0, 0].shape[0]
     mid = quarter // 2
-    f32 = jnp.float32
     far_a = links.x(keep[1, 1][:mid])
     far_b = links.y(keep[1, 1][mid:])
-    out_y = (
-        keep[0, 1]
-        .astype(f32)
-        .at[:mid]
-        .add(far_a.astype(f32))
-        .astype(jnp.bfloat16)
-    )
-    out_x = (
-        keep[1, 0]
-        .astype(f32)
-        .at[mid:]
-        .add(far_b.astype(f32))
-        .astype(jnp.bfloat16)
-    )
-    total = (
-        keep[0, 0].astype(f32) + links.x(out_x).astype(f32) + links.y(out_y).astype(f32)
-    )
+    out_y = keep[0, 1].astype(f32).at[:mid].add(far_a.astype(f32)).astype(jnp.bfloat16)
+    out_x = keep[1, 0].astype(f32).at[mid:].add(far_b.astype(f32)).astype(jnp.bfloat16)
+    total = keep[0, 0].astype(f32) + links.x(out_x).astype(f32) + links.y(out_y).astype(f32)
     shard_rows = quarter // links.nz
     total_b = total.astype(jnp.bfloat16)
     final = total[:shard_rows]
     for k in range(1, links.nz):
         block = total_b[k * shard_rows : (k + 1) * shard_rows]
-        back = links.from_z(block, links.nz - k)
-        final = final + back.astype(f32)
+        final = final + links.from_z(block, links.nz - k).astype(f32)
     return final
+
+
+def total_over_all(links, rows):
+    for move in (links.c, links.x, links.y):
+        rows = rows + move(rows)
+    bit = 1
+    while bit < links.nz:
+        rows = rows + links.flip(rows, bit)
+        bit *= 2
+    return rows
 
 
 def own_slot(
@@ -514,28 +514,35 @@
     order_f = order.astype(f32)
 
     pick = lambda both, at: lax.dynamic_index_in_dim(both, at, 0, keepdims=False)
-    sent_rows = jnp.concatenate([pick(clips, 1 - t), pick(cotangent, 1 - t)], axis=0)
-    got_rows = links.x(sent_rows)
+    halves = lambda rows, size: (rows[:, :size], rows[:, size:])
     live = pick(clip_live, t).astype(f32)
-    x_b = jnp.concatenate([pick(clips, t), got_rows[:shard_rows]], axis=0)
-    cot_b = jnp.concatenate([pick(cotangent, t), got_rows[shard_rows:]], axis=0)
+    got_x = links.x(pick(clips, 1 - t))
+    qkv_cols = 3 * heads_cols
+    along_one = gather_along(links, qkv_weight.reshape(block, qkv_cols))
+    got_cot = links.x(after(got_x, pick(cotangent, 1 - t))[0])
+    far_small = jnp.concatenate([q_bias, v_bias, fc1_bias]).reshape(-1, 128)
+    far_small = links.x(far_small).reshape(-1)
+    chunk_two = jnp.concatenate([fc1_weight, proj_weight.T], axis=1)
+    along_two = gather_along(links, after(got_x, chunk_two)[0])
+    near_one = gather_near(links, after(got_cot, along_one)[0])
+    along_three = gather_along(links, after(along_two, fc2_weight.T)[0])
+    w_qkv = gather_far(links, along_one, near_one)
+    near_two = gather_near(links, after(near_one, along_two)[0])
+    w_two = gather_far(links, along_two, near_two)
+    w_fc1 = [w[:, :hidden_here] for w in w_two]
+    w_proj = [w[:, hidden_here:] for w in w_two]
+    near_three = gather_near(links, after(near_two, along_three)[0])
+    w_fc2 = gather_far(links, along_three, near_three)
+
+    x_b = jnp.concatenate([pick(clips, t), got_x], axis=0)
+    cot_b = jnp.concatenate([pick(cotangent, t), got_cot], axis=0)
     x_rows = nn_dot(x_b, order_b)
     cot_rows = nn_dot(cot_b, order_b)
     vectors = exact(jnp.concatenate([ln_gains, ln_biases, out_bias], axis=0), order_f)
     gains, shifts, outs = vectors[0:2], vectors[2:4], vectors[4:6]
-    far_small = jnp.concatenate([q_bias, v_bias, fc1_bias])[None]
-    far_small = links.x(far_small)[0]
     q_biases = (q_bias, far_small[:heads_cols])
     v_biases = (v_bias, far_small[heads_cols : 2 * heads_cols])
     fc1_biases = (fc1_bias, far_small[2 * heads_cols :])
-
-    chunk_one = jnp.concatenate([qkv_weight.reshape(block, 3 * heads_cols), proj_weight.T], axis=1)
-    w_one = gather_chunk(links, chunk_one)
-    w_fc1 = gather_chunk(links, fc1_weight)
-    w_fc2 = gather_chunk(links, fc2_weight.T)
-    qkv_cols = 3 * heads_cols
-    w_qkv = [w[:, :qkv_cols] for w in w_one]
-    w_proj = [w[:, qkv_cols:] for w in w_one]
 
     norm_one, unit_one, inv_one = layer_norm(x_rows, gains[0], shifts[0])
     h1 = norm_one.astype(bf16)
@@ -547,7 +554,6 @@
         values.append((projected[:, 2 * heads_cols :] + v_biases[kx]).astype(bf16))
     query, key_rows, value_rows = (jnp.concatenate(part, axis=1) for part in (queries, keys, values))
     attn_out, lse = attend_fwd(query, key_rows, value_rows)
-    halves = lambda rows, size: (rows[:, :size], rows[:, size:])
     attn_halves = halves(attn_out, heads_cols)
     mid_rows = (
         x_rows + nt_dot(attn_halves[0], w_proj[0]) + nt_dot(attn_halves[1], w_proj[1]) + outs[0]
@@ -562,51 +568,69 @@
         slope.append(cdf_part + pre_act * jnp.exp(-0.5 * pre_act * pre_act) * inv_root_two_pi)
     out_grad = live * cot_rows
     e_b = out_grad.astype(bf16)
-
-    def fc2_piece(first, count, kx, extra):
-        piece = contract_first(e_b[:, first : first + count], hidden[kx])
-        return (piece if extra is None else piece + extra.astype(f32)).astype(bf16)
-
-    g_fc2 = scatter_chunk(links, fc2_piece, width)
-    mlp_sum = nt_dot(hidden[0], w_fc2[0]) + nt_dot(hidden[1], w_fc2[1])
-    block_out = (live * (mid_rows + mlp_sum + outs[1])).astype(bf16)
-    pre_grad = [nn_dot(e_b, w_fc2[kx]) * slope[kx] for kx in range(2)]
+    half_rows, quarter = width // 2, width // 4
+
+    def pieces_sent(left, right):
+        return [contract_first(left[:, half_rows:], right[kx]).astype(bf16) for kx in range(2)]
+
+    def pieces_kept(left, right, got):
+        keep = {}
+        for kx, ky in ((1, 1), (1, 0), (0, 1), (0, 0)):
+            rows = slice(ky * quarter, (ky + 1) * quarter)
+            piece = contract_first(left[:, rows], right[kx]) + got[kx][rows].astype(f32)
+            keep[kx, ky] = piece.astype(bf16)
+        return keep
+
+    sent_fc2 = pieces_sent(e_b, hidden)
+    got_fc2 = [links.c(piece) for piece in sent_fc2]
+    (hold_e,) = after((sent_fc2, w_fc2), e_b)
+    pre_grad = [nn_dot(hold_e, w_fc2[kx]) * slope[kx] for kx in range(2)]
     pre_grad_b = [rows.astype(bf16) for rows in pre_grad]
     g_fc1b = [jnp.sum(rows, axis=0) for rows in pre_grad]
-
-    def fc1_piece(first, count, kx, extra):
-        piece = contract_first(h2[:, first : first + count], pre_grad_b[kx])
-        return (piece if extra is None else piece + extra.astype(f32)).astype(bf16)
-
-    g_fc1 = scatter_chunk(links, fc1_piece, width)
-    norm_two_grad = nt_dot(pre_grad_b[0], w_fc1[0]) + nt_dot(pre_grad_b[1], w_fc1[1])
+    keep_fc2 = pieces_kept(*after(pre_grad_b, e_b), hidden, got_fc2)
+    sent_fc1 = pieces_sent(*after(keep_fc2, h2), pre_grad_b)
+    got_fc1 = [links.c(piece) for piece in sent_fc1]
+    hold_du = after(sent_fc1, *pre_grad_b)
+    norm_two_grad = nt_dot(hold_du[0], w_fc1[0]) + nt_dot(hold_du[1], w_fc1[1])
     mid_grad = out_grad + norm_back(norm_two_grad, unit_two, inv_two, gains[1])
-    da_b = mid_grad.astype(bf16)
+    keep_fc1 = pieces_kept(*after(mid_grad, h2), pre_grad_b, got_fc1)
+    da_b = after(keep_fc1, mid_grad)[0].astype(bf16)
     mixed_grad = jnp.concatenate([nn_dot(da_b, w_proj[kx]) for kx in range(2)], axis=1).astype(bf16)
+    g_fc2 = scatter_keep(links, keep_fc2)
+    g_fc1 = scatter_keep(links, keep_fc1)
     dq, dk, dv, q_sums, v_sums = attend_bwd(query, key_rows, value_rows, mixed_grad, lse.T)
     parts = [halves(rows, heads_cols) for rows in (dq, dk, dv)]
     one_sides = [jnp.concatenate([p[kx] for p in parts], axis=1) for kx in range(2)]
 
-    def one_piece(first, count, kx, extra):
-        cols = slice(first, first + count)
-        piece = jnp.concatenate(
+    def one_piece(rows, kx):
+        return jnp.concatenate(
             [
-                contract_first(h1[:, cols], one_sides[kx]),
-                contract_first(da_b[:, cols], attn_halves[kx]),
+                contract_first(h1[:, rows], one_sides[kx]),
+                contract_first(da_b[:, rows], attn_halves[kx]),
             ],
             axis=1,
         )
-        return (piece if extra is None else piece + extra.astype(f32)).astype(bf16)
-
-    g_one = scatter_chunk(links, one_piece, width)
-    norm_one_grad = nt_dot(one_sides[0], w_qkv[0]) + nt_dot(one_sides[1], w_qkv[1])
-    in_grad = mid_grad + norm_back(norm_one_grad, unit_one, inv_one, gains[0])
-
+
+    sent_one = [one_piece(slice(half_rows, width), kx).astype(bf16) for kx in range(2)]
+    got_one = [links.c(piece) for piece in sent_one]
+    hold_dp = after(sent_one, *one_sides)
+    norm_one_grad = nt_dot(hold_dp[0], w_qkv[0]) + nt_dot(hold_dp[1], w_qkv[1])
+    keep_one = {}
+    for kx, ky in ((1, 1), (1, 0), (0, 1), (0, 0)):
+        rows = slice(ky * quarter, (ky + 1) * quarter)
+        keep_one[kx, ky] = (one_piece(rows, kx) + got_one[kx][rows].astype(f32)).astype(bf16)
+    (hold_grad,) = after(keep_one, norm_one_grad)
+    in_grad = mid_grad + norm_back(hold_grad, unit_one, inv_one, gains[0])
+    g_one = scatter_keep(links, keep_one)
+
+    (hold_mid,) = after(keep_one, mid_rows)
+    mlp_sum = nt_dot(hidden[0], w_fc2[0]) + nt_dot(hidden[1], w_fc2[1])
+    block_out = (live * (hold_mid + mlp_sum + outs[1])).astype(bf16)
     sums = jnp.stack(
         [
-            jnp.sum(norm_one_grad * unit_one, axis=0),
+            jnp.sum(hold_grad * unit_one, axis=0),
             jnp.sum(norm_two_grad * unit_two, axis=0),
-            jnp.sum(norm_one_grad, axis=0),
+            jnp.sum(hold_grad, axis=0),
             jnp.sum(norm_two_grad, axis=0),
             jnp.sum(mid_grad, axis=0),
             jnp.sum(out_grad, axis=0),
@@ -618,11 +642,15 @@
     placed = lambda near, far: jnp.where(
         t == 0, jnp.concatenate([near, far]), jnp.concatenate([far, near])
     )
-    q_all = placed(*(q_sums[0, :heads_cols], q_sums[0, heads_cols:]))
-    v_all = placed(*(v_sums[0, :heads_cols], v_sums[0, heads_cols:]))
-    fc1b_all = placed(*g_fc1b)
-    sums, q_all, v_all, fc1b_all = lax.psum((sums, q_all, v_all, fc1b_all), AXES)
-    own = lambda full, size: lax.dynamic_slice_in_dim(full, t * size, size, 0) * grad_scale
+    small = [
+        sums.reshape(-1),
+        placed(q_sums[0, :heads_cols], q_sums[0, heads_cols:]),
+        placed(v_sums[0, :heads_cols], v_sums[0, heads_cols:]),
+        placed(*g_fc1b),
+    ]
+    small = total_over_all(links, jnp.concatenate(small).reshape(-1, 128)).reshape(-1) * grad_scale
+    sums = small[: 6 * width].reshape(6, width)
+    own = lambda first, size: lax.dynamic_slice_in_dim(small, first + t * size, size, 0)
 
     def back_home(rows_rel):
         rows = lax.dot_general(
@@ -636,15 +664,15 @@
         back_home(block_out),
         back_home(in_grad).astype(f32),
         g_one[:, :qkv_cols].reshape(block, 3, heads_cols) * grad_scale,
-        own(q_all, heads_cols),
-        own(v_all, heads_cols),
+        own(6 * width, heads_cols),
+        own(6 * width + 2 * heads_cols, heads_cols),
         g_one[:, qkv_cols:].T * grad_scale,
         g_fc1 * grad_scale,
-        own(fc1b_all, hidden_here),
+        own(6 * width + 4 * heads_cols, hidden_here),
         g_fc2.T * grad_scale,
-        sums[0:2] * grad_scale,
-        sums[2:4] * grad_scale,
-        sums[4:6] * grad_scale,
+        sums[0:2],
+        sums[2:4],
+        sums[4:6],
     )
 
 

time: 586 us -> 458 us (0.78)
  waiting for transfers between devices: 224 us -> 174 us
  blocking collectives: 47.7 us -> 0 us
  starting transfers between devices: 112 us -> 86.7 us
  matrix products: 106 us -> 88.7 us
  local copies, waits for them, and re-layouts: 35.9 us -> 48.2 us
    ppermute x16 -> x18, waiting for transfers between devices: 152 us -> 81.3 us  [x(): return lax.ppermute(rows, AXES, self.across)]
    psum x1 -> x0, blocking collectives: 47.7 us -> none  [own_slot(): lax.psum((sums, q_all, v_all, fc1b_all), AXES)]
    ppermute x18, starting transfers between devices: 72.1 us -> 39.6 us  [from_z(): return lax.ppermute(rows, AXES, shift)]
    ppermute x18, waiting for transfers between devices: 23.8 us -> 52.5 us  [from_z(): return lax.ppermute(rows, AXES, shift)]
    dot_general x24, matrix products: 41.7 us -> 22.8 us  [contract_first(): lax.dot_general(left_op, right_op, (((0,), (0,)), ((), ())), preferred_el...]
    ppermute x12 -> x13, waiting for transfers between devices: 48.1 us -> 34.8 us  [y(): return lax.ppermute(rows, AXES, self.beside)]
    unnamed x164 -> x121, local copies, waits for them, and re-layouts: 23.9 us -> 26.8 us
    ppermute x12 -> x13, starting transfers between devices: 15.6 us -> 17.1 us  [y(): return lax.ppermute(rows, AXES, self.beside)]
  transfers between devices with their start and end apart: 67 -> 73, of which waited for: 20 -> 29; matrix products, arithmetic and copies ran while one was open for 16% -> 28% of each run, Pallas kernels for 2% -> 3%
where the time goes in v2:
time: 458 us; the launch traced here: 449 us
  waiting for transfers between devices  174 us (38%)
  matrix products  88.7 us (19%)
  starting transfers between devices  86.7 us (19%)
  local copies, waits for them, and re-layouts  48.2 us (11%)
  Pallas kernels  28.7 us (6%)
  other arithmetic  20.3 us (4%)
    ppermute x18, waiting for transfers between devices, x(): return lax.ppermute(rows, AXES, self.across)  81.3 us
    ppermute x18, waiting for transfers between devices, from_z(): return lax.ppermute(rows, AXES, shift)  52.5 us
    ppermute x18, starting transfers between devices, from_z(): return lax.ppermute(rows, AXES, shift)  39.6 us
    ppermute x13, waiting for transfers between devices, y(): return lax.ppermute(rows, AXES, self.beside)  34.8 us
    dot_general x10, matrix products, nn_dot(): lax.dot_general(left_op, right_op, (((1,), (0,)), ((), ())), preferred_el...  31.9 us
    unnamed x121, local copies, waits for them, and re-layouts  26.8 us
    dot_general x24, matrix products, contract_first(): lax.dot_general(left_op, right_op, (((0,), (0,)), ((), ())), preferred_el...  22.8 us
    ppermute x18, starting transfers between devices, x(): return lax.ppermute(rows, AXES, self.across)  19.6 us
  transfers between devices with their start and end apart: 73, of which 29 were waited for; matrix products, arithmetic and copies ran while one was open for 28% of the time, Pallas kernels for 3%

profile of v2, /device:TPU:0, one launch (start us, length us, event | category | flops | bytes accessed | tf_op | source)
XLA Modules:
  0.0 449.1 jit_solution(1613333281647046954)
XLA Ops:
  1.7 5.1 %collective-permute-start.1 = (bf16[64,1536]{1,0:T(8,128)(2,1)S(1)}, bf16[64,1536]{1,0:T(8,128)(2,1)}, u32[]{:S(2)}, u32[]{:S(2)}) collective-permute-start(bf16[64,1536]{1,0:T(8,128)(2,1)S(1)} %bitcast.96), channel_id=1, source_target_pairs={{8,0},{9,1},{10,2},{11,3},{12,4},{13,5},{14,6},{15,7},{16,8},{17,9... | collective-permute-start | bytes 589832 | tf_op jit(solution)/shard_map/ppermute | solution.py:409
  17.7 4.8 %collective-permute-done.14 = f32[24,128]{1,0:T(8,128)} collective-permute-done((f32[24,128]{1,0:T(8,128)}, f32[24,128]{1,0:T(8,128)}, u32[]{:S(2)}, u32[]{:S(2)}) %collective-permute-start.14) | collective-permute-done | bytes 12320 | tf_op jit(solution)/shard_map/ppermute | solution.py:412
  28.7 3.1 collective-permute-start.15
  34.4 2.4 fusion.199
  40.8 21.0 %collective-permute-done.16 = bf16[64,2560]{1,0:T(8,128)(2,1)S(1)} collective-permute-done((bf16[64,2560]{1,0:T(8,128)(2,1)S(1)}, bf16[64,2560]{1,0:T(8,128)(2,1)S(1)}, u32[]{:S(2)}, u32[]{:S(2)}) %collective-permute-start.16) | collective-permute-done | bytes 327712 | tf_op jit(solution)/shard_map/ppermute | solution.py:409
  68.1 3.0 multiply_convert_fusion.3
  72.7 10.5 %collective-permute-start.29 = (bf16[64,2048]{1,0:T(8,128)(2,1)S(1)}, bf16[64,2048]{1,0:T(8,128)(2,1)S(1)}, u32[]{:S(2)}, u32[]{:S(2)}) collective-permute-start(bf16[64,2048]{1,0:T(8,128)(2,1)S(1)} %bitcast.105), channel_id=1, source_target_pairs={{24,0},{25,1},{26,2},{27,3},{28,4},{29,5},{30,6},{31,7},{0,8},{1,9... | collective-permute-start | bytes 786440 | tf_op jit(solution)/shard_map/ppermute | solution.py:409
  84.0 2.9 collective-permute-done.28
  92.6 7.6 %collective-permute-done.9 = bf16[128,1536]{1,0:T(8,128)(2,1)S(1)} collective-permute-done((bf16[128,1536]{1,0:T(8,128)(2,1)S(1)}, bf16[128,1536]{1,0:T(8,128)(2,1)S(1)}, u32[]{:S(2)}, u32[]{:S(2)}) %collective-permute-start.9) | collective-permute-done | bytes 393248 | tf_op jit(solution)/shard_map/ppermute | solution.py:412
  110.4 11.9 %attend_fwd.1 = (bf16[512,1024]{1,0:T(8,128)(2,1)S(1)}, f32[512,128]{1,0:T(8,128)S(1)}) custom-call(bf16[512,1024]{1,0:T(8,128)(2,1)S(1)} %get-tuple-element.278.q_ref, bf16[512,1024]{1,0:T(8,128)(2,1)S(1)} %pad_maximum_fusion.5.k_ref, bf16[512,1024]{1,0:T(8,128)(2,1)S(1)} %get-tuple-element.279.v_ref), custom_call_target="tpu_custom_call" | custom-call | flops 2147483648 | bytes 4194304 | tf_op jit(solution)/shard_map/attend_fwd/pallas_call | solution.py:314
  124.1 7.9 %collective-permute-done.18 = bf16[256,2560]{1,0:T(8,128)(2,1)} collective-permute-done((bf16[256,2560]{1,0:T(8,128)(2,1)}, bf16[256,2560]{1,0:T(8,128)(2,1)}, u32[]{:S(2)}, u32[]{:S(2)}) %collective-permute-start.18) | collective-permute-done | bytes 1310752 | tf_op jit(solution)/shard_map/ppermute | solution.py:415
  139.6 2.5 constant_dynamic-update-slice_fusion.23
  143.6 2.5 constant_dynamic-update-slice_fusion.22
  146.1 25.3 %collective-permute-done.22 = bf16[128,2560]{1,0:T(8,128)(2,1)S(1)} collective-permute-done((bf16[128,2560]{1,0:T(8,128)(2,1)S(1)}, bf16[128,2560]{1,0:T(8,128)(2,1)S(1)}, u32[]{:S(2)}, u32[]{:S(2)}) %collective-permute-start.22) | collective-permute-done | bytes 655392 | tf_op jit(solution)/shard_map/ppermute | solution.py:412
  175.7 2.3 constant_dynamic-update-slice_fusion.39
  184.2 4.1 multiply_convert_fusion.1
  188.2 4.2 multiply_convert_fusion
  192.4 2.6 convolution_convert_fusion.4
  197.7 2.2 collective-permute-done.37
  201.8 5.4 %fusion.184 = (f32[2048]{0:T(1024)S(1)}, bf16[512,2048]{1,0:T(8,128)(2,1)S(1)}) fusion(f32[512,2048]{1,0:T(8,128)} %get-tuple-element.266, f32[2048]{0:T(1024)S(1)} %copy-done.37, bf16[512,1024]{1,0:T(8,128)(2,1)S(1)} %copy-done.17, bf16[1024,2048]{1,0:T(8,128)(2,1)S(1)} %constant_dynamic-update-slice_fusion.45), kind=kOutput, calls=%fused_computation.335 | convolution fusion | flops 2160064512 | bytes 11550720 | tf_op jit(solution)/shard_map/dot_general | solution.py:284
  207.1 6.6 %fusion.183 = (f32[2048]{0:T(1024)S(1)}, bf16[512,2048]{1,0:T(8,128)(2,1)S(1)}) fusion(f32[512,2048]{1,0:T(8,128)} %get-tuple-element.264, f32[2048]{0:T(1024)S(1)} %copy-done.36, bf16[512,1024]{1,0:T(8,128)(2,1)S(1)} %copy-done.17, bf16[1024,2048]{1,0:T(8,128)(2,1)} %constant_dynamic-update-slice_fusion.38), kind=kOutput, calls=%fused_computation.334 | convolution fusion | flops 2160064512 | bytes 11550720 | tf_op jit(solution)/shard_map/dot_general | solution.py:284
  213.8 3.7 fusion.207
  220.6 2.6 convolution_convert_fusion.2
  227.7 3.8 fusion.16
  231.5 7.5 %collective-permute-done.66 = bf16[128,2048]{1,0:T(8,128)(2,1)S(1)} collective-permute-done((bf16[128,2048]{1,0:T(8,128)(2,1)S(1)}, bf16[128,2048]{1,0:T(8,128)(2,1)S(1)}, u32[]{:S(2)}, u32[]{:S(2)}) %collective-permute-start.66) | collective-permute-done | bytes 524320 | tf_op jit(solution)/shard_map/ppermute | solution.py:415
  242.6 5.9 %multiply_reduce_fusion = (f32[1024]{0:T(1024)S(1)}, f32[512]{0:T(512)S(1)}, f32[512]{0:T(512)S(1)}, f32[1024]{0:T(1024)S(1)}, f32[512,1024]{1,0:T(8,128)S(1)}) fusion(f32[512,1024]{1,0:T(8,128)S(1)} %get-tuple-element.126, f32[512]{0:T(512)S(1)} %add_rsqrt_fusion, f32[512]{0:T(512)S(1)} %broadcast_multiply_fusion.4, f32[1024]{0:T(1024)S(1)} %bitcast.114, ...), kind=kOutput, calls=%fused_computation.49 | convolution fusion | flops 2152723456 | bytes 12603392 | tf_op jit(solution)/shard_map/dot_general | solution.py:278
  248.7 15.1 %collective-permute-done.67 = bf16[256,2048]{1,0:T(8,128)(2,1)S(1)} collective-permute-done((bf16[256,2048]{1,0:T(8,128)(2,1)S(1)}, bf16[256,2048]{1,0:T(8,128)(2,1)S(1)}, u32[]{:S(2)}, u32[]{:S(2)}) %collective-permute-start.67) | collective-permute-done | bytes 1048608 | tf_op jit(solution)/shard_map/ppermute | solution.py:412
  266.0 3.7 collective-permute-start.72
  270.6 6.3 %collective-permute-done.70 = bf16[64,2048]{1,0:T(8,128)(2,1)S(1)} collective-permute-done((bf16[64,2048]{1,0:T(8,128)(2,1)S(1)}, bf16[64,2048]{1,0:T(8,128)(2,1)S(1)}, u32[]{:S(2)}, u32[]{:S(2)}) %collective-permute-start.70) | collective-permute-done | bytes 262176 | tf_op jit(solution)/shard_map/ppermute | solution.py:409
  276.9 8.5 %collective-permute-done.71 = bf16[64,2048]{1,0:T(8,128)(2,1)S(1)} collective-permute-done((bf16[64,2048]{1,0:T(8,128)(2,1)S(1)}, bf16[64,2048]{1,0:T(8,128)(2,1)S(1)}, u32[]{:S(2)}, u32[]{:S(2)}) %collective-permute-start.71) | collective-permute-done | bytes 262176 | tf_op jit(solution)/shard_map/ppermute | solution.py:409
  293.6 16.8 %attend_bwd.1 = (bf16[512,1024]{1,0:T(8,128)(2,1)S(1)}, bf16[512,1024]{1,0:T(8,128)(2,1)S(1)}, bf16[512,1024]{1,0:T(8,128)(2,1)S(1)}, f32[1,1024]{1,0:T(1,128)S(1)}, f32[1,1024]{1,0:T(1,128)S(1)}) custom-call(bf16[512,1024]{1,0:T(8,128)(2,1)S(1)} %get-tuple-element.278.q_ref, bf16[512,1024]{1,0:T(8,128)(2,1)S(1)} %pad_maximum_fusion.5.k_ref, ...), custom_call_target="tpu_custom_call" | custom-call | flops 5368709120 | bytes 7340032 | tf_op jit(solution)/shard_map/attend_bwd/pallas_call | solution.py:372
  326.7 3.5 collective-permute-done.59
  331.6 7.3 %collective-permute-done.61 = bf16[128,2048]{1,0:T(8,128)(2,1)S(1)} collective-permute-done((bf16[128,2048]{1,0:T(8,128)(2,1)S(1)}, bf16[128,2048]{1,0:T(8,128)(2,1)S(1)}, u32[]{:S(2)}, u32[]{:S(2)}) %collective-permute-start.61) | collective-permute-done | bytes 524320 | tf_op jit(solution)/shard_map/ppermute | solution.py:412
  343.5 15.9 %collective-permute-done.60 = bf16[256,2048]{1,0:T(8,128)(2,1)S(1)} collective-permute-done((bf16[256,2048]{1,0:T(8,128)(2,1)S(1)}, bf16[256,2048]{1,0:T(8,128)(2,1)S(1)}, u32[]{:S(2)}, u32[]{:S(2)}) %collective-permute-start.60) | collective-permute-done | bytes 1048608 | tf_op jit(solution)/shard_map/ppermute | solution.py:412
  363.6 9.1 %collective-permute-done.47 = bf16[128,2048]{1,0:T(8,128)(2,1)S(1)} collective-permute-done((bf16[128,2048]{1,0:T(8,128)(2,1)S(1)}, bf16[128,2048]{1,0:T(8,128)(2,1)S(1)}, u32[]{:S(2)}, u32[]{:S(2)}) %collective-permute-start.47) | collective-permute-done | bytes 524320 | tf_op jit(solution)/shard_map/ppermute | solution.py:415
  374.5 2.5 collective-permute-start.50
  377.1 5.3 %collective-permute-start.63 = (bf16[64,2048]{1,0:T(8,128)(2,1)S(1)}, bf16[64,2048]{1,0:T(8,128)(2,1)S(1)}, u32[]{:S(2)}, u32[]{:S(2)}) collective-permute-start(bf16[64,2048]{1,0:T(8,128)(2,1)S(1)} %get-tuple-element.192), channel_id=1, source_target_pairs={{24,0},{25,1},{26,2},{27,3},{28,4},{29,5},{30,6},{31,7},{0,8},{1,9... | collective-permute-start | bytes 786440 | tf_op jit(solution)/shard_map/ppermute | solution.py:409
  382.4 2.6 collective-permute-start.65
  385.3 2.2 collective-permute-done.63
  387.5 8.2 %collective-permute-done.64 = bf16[64,2048]{1,0:T(8,128)(2,1)S(1)} collective-permute-done((bf16[64,2048]{1,0:T(8,128)(2,1)S(1)}, bf16[64,2048]{1,0:T(8,128)(2,1)S(1)}, u32[]{:S(2)}, u32[]{:S(2)}) %collective-permute-start.64) | collective-permute-done | bytes 262176 | tf_op jit(solution)/shard_map/ppermute | solution.py:409
  402.5 4.0 collective-permute-start.51
  406.5 2.4 collective-permute-start.52
  410.2 4.0 fusion.38
  418.4 2.1 collective-permute-start.57
  420.5 8.0 %fusion.37 = bf16[512,1024]{1,0:T(8,128)(2,1)} fusion(s32[1024]{0:T(1024)S(1)} %copy-done.41, f32[512,1024]{1,0:T(8,128)S(1)} %copy-done.7, f32[512,1024]{1,0:T(8,128)} %fusion.207, bf16[512,2048]{1,0:T(8,128)(2,1)} %copy-done.8, bf16[1024,2048]{1,0:T(8,128)(2,1)} %constant_dynamic-update-slice_fusion.38, f32[1024]{0:T(1024)S(1)} %bitcast.129, f32[]{:T(128)} %bitcast), kind=kOutput, calls=%fused_computation.86 | convolution fusion | flops 3225419776 | bytes 11542532 | tf_op jit(solution)/shard_map/dot_general | solution.py:656
  428.5 3.2 collective-permute-start.58
  441.1 2.7 fusion.57
  443.8 3.9 collective-permute-done.45
  (372 shorter events, 147.4 us)
Async XLA Ops:
  1.7 22.8 %collective-permute-start.1 = (bf16[64,1536]{1,0:T(8,128)(2,1)S(1)}, bf16[64,1536]{1,0:T(8,128)(2,1)}, u32[]{:S(2)}, u32[]{:S(2)}) collective-permute-start(bf16[64,1536]{1,0:T(8,128)(2,1)S(1)} %bitcast.96), channel_id=1, source_target_pairs={{8,0},{9,1},{10,2},{11,3},{12,4},{13,5},{14,6},{15,7},{16,8},{17,9... | collective-permute-start | bytes 589832 | tf_op jit(solution)/shard_map/ppermute | solution.py:409
  6.8 19.4 %collective-permute-start.2 = (bf16[64,1536]{1,0:T(8,128)(2,1)S(1)}, bf16[64,1536]{1,0:T(8,128)(2,1)S(1)}, u32[]{:S(2)}, u32[]{:S(2)}) collective-permute-start(bf16[64,1536]{1,0:T(8,128)(2,1)S(1)} %bitcast.97), channel_id=1, source_target_pairs={{16,0},{17,1},{18,2},{19,3},{20,4},{21,5},{22,6},{23,7},{24,8},{25... | collective-permute-start | bytes 589832 | tf_op jit(solution)/shard_map/ppermute | solution.py:409
  6.8 20.2 %collective-permute-start.3 = (bf16[64,1536]{1,0:T(8,128)(2,1)S(1)}, bf16[64,1536]{1,0:T(8,128)(2,1)S(1)}, u32[]{:S(2)}, u32[]{:S(2)}) collective-permute-start(bf16[64,1536]{1,0:T(8,128)(2,1)S(1)} %bitcast.98), channel_id=1, source_target_pairs={{24,0},{25,1},{26,2},{27,3},{28,4},{29,5},{30,6},{31,7},{0,8},{1,9... | collective-permute-start | bytes 589832 | tf_op jit(solution)/shard_map/ppermute | solution.py:409
  9.2 18.6 %collective-permute-start = (bf16[256,1024]{1,0:T(8,128)(2,1)S(1)}, bf16[256,1024]{1,0:T(8,128)(2,1)}, u32[]{:S(2)}, u32[]{:S(2)}) collective-permute-start(bf16[256,1024]{1,0:T(8,128)(2,1)S(1)} %get-tuple-element.215), channel_id=1, source_target_pairs={{1,0},{0,1},{3,2},{2,3},{5,4},{4,5},{7,6},{6,7},{9,8},{8,9},{11,10... | collective-permute-start | bytes 1572872 | tf_op jit(solution)/shard_map/ppermute | solution.py:412
  27.8 64.2 %collective-permute-start.6 = (bf16[256,1536]{1,0:T(8,128)(2,1)}, bf16[256,1536]{1,0:T(8,128)(2,1)S(1)}, u32[]{:S(2)}, u32[]{:S(2)}) collective-permute-start(bf16[256,1536]{1,0:T(8,128)(2,1)} %get-tuple-element.109), channel_id=1, source_target_pairs={{2,0},{3,1},{0,2},{1,3},{6,4},{7,5},{4,6},{5,7},{10,8},{11,9},{8,1... | collective-permute-start | bytes 2359304 | tf_op jit(solution)/shard_map/ppermute | solution.py:418
  31.8 30.0 %collective-permute-start.16 = (bf16[64,2560]{1,0:T(8,128)(2,1)S(1)}, bf16[64,2560]{1,0:T(8,128)(2,1)S(1)}, u32[]{:S(2)}, u32[]{:S(2)}) collective-permute-start(bf16[64,2560]{1,0:T(8,128)(2,1)S(1)} %pad_maximum_fusion.8), channel_id=1, source_target_pairs={{16,0},{17,1},{18,2},{19,3},{20,4},{21,5},{22,6},{23,7},{24,8},{25... | collective-permute-start | bytes 983048 | tf_op jit(solution)/shard_map/ppermute | solution.py:409
  32.6 30.1 %collective-permute-start.17 = (bf16[64,2560]{1,0:T(8,128)(2,1)S(1)}, bf16[64,2560]{1,0:T(8,128)(2,1)S(1)}, u32[]{:S(2)}, u32[]{:S(2)}) collective-permute-start(bf16[64,2560]{1,0:T(8,128)(2,1)S(1)} %pad_maximum_fusion.8), channel_id=1, source_target_pairs={{24,0},{25,1},{26,2},{27,3},{28,4},{29,5},{30,6},{31,7},{0,8},{1,9... | collective-permute-start | bytes 983048 | tf_op jit(solution)/shard_map/ppermute | solution.py:409
  32.9 32.2 %collective-permute-start.4 = (bf16[256,1024]{1,0:T(8,128)(2,1)S(1)}, bf16[256,1024]{1,0:T(8,128)(2,1)S(1)}, u32[]{:S(2)}, u32[]{:S(2)}) collective-permute-start(bf16[256,1024]{1,0:T(8,128)(2,1)S(1)} %copy-done.18), channel_id=1, source_target_pairs={{1,0},{0,1},{3,2},{2,3},{5,4},{4,5},{7,6},{6,7},{9,8},{8,9},{11,10... | collective-permute-start | bytes 1572872 | tf_op jit(solution)/shard_map/ppermute | solution.py:412
  63.6 23.4 %collective-permute-start.28 = (bf16[64,2048]{1,0:T(8,128)(2,1)S(1)}, bf16[64,2048]{1,0:T(8,128)(2,1)S(1)}, u32[]{:S(2)}, u32[]{:S(2)}) collective-permute-start(bf16[64,2048]{1,0:T(8,128)(2,1)S(1)} %bitcast.103), channel_id=1, source_target_pairs={{16,0},{17,1},{18,2},{19,3},{20,4},{21,5},{22,6},{23,7},{24,8},{25... | collective-permute-start | bytes 786440 | tf_op jit(solution)/shard_map/ppermute | solution.py:409
  65.1 23.6 %collective-permute-start.5 = (bf16[256,1536]{1,0:T(8,128)(2,1)S(1)}, bf16[256,1536]{1,0:T(8,128)(2,1)S(1)}, u32[]{:S(2)}, u32[]{:S(2)}) collective-permute-start(bf16[256,1536]{1,0:T(8,128)(2,1)S(1)} %copy-done.26), channel_id=1, source_target_pairs={{4,0},{5,1},{6,2},{7,3},{0,4},{1,5},{2,6},{3,7},{12,8},{13,9},{14,... | collective-permute-start | bytes 2359304 | tf_op jit(solution)/shard_map/ppermute | solution.py:415
  66.6 23.7 %collective-permute-start.8 = (bf16[256,1536]{1,0:T(8,128)(2,1)S(1)}, bf16[256,1536]{1,0:T(8,128)(2,1)S(1)}, u32[]{:S(2)}, u32[]{:S(2)}) collective-permute-start(bf16[256,1536]{1,0:T(8,128)(2,1)S(1)} %copy-done.26), channel_id=1, source_target_pairs={{1,0},{0,1},{3,2},{2,3},{5,4},{4,5},{7,6},{6,7},{9,8},{8,9},{11,10... | collective-permute-start | bytes 2359304 | tf_op jit(solution)/shard_map/ppermute | solution.py:412
  72.7 15.1 %collective-permute-start.29 = (bf16[64,2048]{1,0:T(8,128)(2,1)S(1)}, bf16[64,2048]{1,0:T(8,128)(2,1)S(1)}, u32[]{:S(2)}, u32[]{:S(2)}) collective-permute-start(bf16[64,2048]{1,0:T(8,128)(2,1)S(1)} %bitcast.105), channel_id=1, source_target_pairs={{24,0},{25,1},{26,2},{27,3},{28,4},{29,5},{30,6},{31,7},{0,8},{1,9... | collective-permute-start | bytes 786440 | tf_op jit(solution)/shard_map/ppermute | solution.py:409
  87.0 55.1 %collective-permute-start.19 = (bf16[256,2560]{1,0:T(8,128)(2,1)}, bf16[256,2560]{1,0:T(8,128)(2,1)}, u32[]{:S(2)}, u32[]{:S(2)}) collective-permute-start(bf16[256,2560]{1,0:T(8,128)(2,1)} %get-tuple-element.112), channel_id=1, source_target_pairs={{2,0},{3,1},{0,2},{1,3},{6,4},{7,5},{4,6},{5,7},{10,8},{11,9},{8,1... | collective-permute-start | bytes 3932168 | tf_op jit(solution)/shard_map/ppermute | solution.py:418
  100.3 74.6 %collective-permute-start.31 = (bf16[256,2048]{1,0:T(8,128)(2,1)}, bf16[256,2048]{1,0:T(8,128)(2,1)}, u32[]{:S(2)}, u32[]{:S(2)}) collective-permute-start(bf16[256,2048]{1,0:T(8,128)(2,1)} %get-tuple-element.114), channel_id=1, source_target_pairs={{2,0},{3,1},{0,2},{1,3},{6,4},{7,5},{4,6},{5,7},{10,8},{11,9},{8,1... | collective-permute-start | bytes 3145736 | tf_op jit(solution)/shard_map/ppermute | solution.py:418
  101.6 30.4 %collective-permute-start.18 = (bf16[256,2560]{1,0:T(8,128)(2,1)}, bf16[256,2560]{1,0:T(8,128)(2,1)}, u32[]{:S(2)}, u32[]{:S(2)}) collective-permute-start(bf16[256,2560]{1,0:T(8,128)(2,1)} %get-tuple-element.112), channel_id=1, source_target_pairs={{4,0},{5,1},{6,2},{7,3},{0,4},{1,5},{2,6},{3,7},{12,8},{13,9},{14,... | collective-permute-start | bytes 3932168 | tf_op jit(solution)/shard_map/ppermute | solution.py:415
  103.2 30.2 %collective-permute-start.21 = (bf16[256,2560]{1,0:T(8,128)(2,1)}, bf16[256,2560]{1,0:T(8,128)(2,1)}, u32[]{:S(2)}, u32[]{:S(2)}) collective-permute-start(bf16[256,2560]{1,0:T(8,128)(2,1)} %get-tuple-element.112), channel_id=1, source_target_pairs={{1,0},{0,1},{3,2},{2,3},{5,4},{4,5},{7,6},{6,7},{9,8},{8,9},{11,10... | collective-permute-start | bytes 3932168 | tf_op jit(solution)/shard_map/ppermute | solution.py:412
  133.3 40.2 %collective-permute-start.33 = (bf16[256,2048]{1,0:T(8,128)(2,1)}, bf16[256,2048]{1,0:T(8,128)(2,1)S(1)}, u32[]{:S(2)}, u32[]{:S(2)}) collective-permute-start(bf16[256,2048]{1,0:T(8,128)(2,1)} %get-tuple-element.114), channel_id=1, source_target_pairs={{1,0},{0,1},{3,2},{2,3},{5,4},{4,5},{7,6},{6,7},{9,8},{8,9},{11,10... | collective-permute-start | bytes 3145736 | tf_op jit(solution)/shard_map/ppermute | solution.py:412
  134.7 38.2 %collective-permute-start.30 = (bf16[256,2048]{1,0:T(8,128)(2,1)}, bf16[256,2048]{1,0:T(8,128)(2,1)S(1)}, u32[]{:S(2)}, u32[]{:S(2)}) collective-permute-start(bf16[256,2048]{1,0:T(8,128)(2,1)} %get-tuple-element.114), channel_id=1, source_target_pairs={{4,0},{5,1},{6,2},{7,3},{0,4},{1,5},{2,6},{3,7},{12,8},{13,9},{14,... | collective-permute-start | bytes 3145736 | tf_op jit(solution)/shard_map/ppermute | solution.py:415
  136.4 35.1 %collective-permute-start.22 = (bf16[128,2560]{1,0:T(8,128)(2,1)S(1)}, bf16[128,2560]{1,0:T(8,128)(2,1)S(1)}, u32[]{:S(2)}, u32[]{:S(2)}) collective-permute-start(bf16[128,2560]{1,0:T(8,128)(2,1)S(1)} %slice.547), channel_id=1, source_target_pairs={{1,0},{0,1},{3,2},{2,3},{5,4},{4,5},{7,6},{6,7},{9,8},{8,9},{11,10... | collective-permute-start | bytes 1966088 | tf_op jit(solution)/shard_map/ppermute | solution.py:412
  142.1 30.8 %collective-permute-start.23 = (bf16[128,2560]{1,0:T(8,128)(2,1)S(1)}, bf16[128,2560]{1,0:T(8,128)(2,1)S(1)}, u32[]{:S(2)}, u32[]{:S(2)}) collective-permute-start(bf16[128,2560]{1,0:T(8,128)(2,1)S(1)} %slice.548), channel_id=1, source_target_pairs={{4,0},{5,1},{6,2},{7,3},{0,4},{1,5},{2,6},{3,7},{12,8},{13,9},{14,... | collective-permute-start | bytes 1966088 | tf_op jit(solution)/shard_map/ppermute | solution.py:415
  174.8 21.5 %collective-permute-start.34 = (bf16[128,2048]{1,0:T(8,128)(2,1)S(1)}, bf16[128,2048]{1,0:T(8,128)(2,1)S(1)}, u32[]{:S(2)}, u32[]{:S(2)}) collective-permute-start(bf16[128,2048]{1,0:T(8,128)(2,1)S(1)} %slice.558), channel_id=1, source_target_pairs={{1,0},{0,1},{3,2},{2,3},{5,4},{4,5},{7,6},{6,7},{9,8},{8,9},{11,10... | collective-permute-start | bytes 1572872 | tf_op jit(solution)/shard_map/ppermute | solution.py:412
  178.1 18.9 %collective-permute-start.35 = (bf16[128,2048]{1,0:T(8,128)(2,1)S(1)}, bf16[128,2048]{1,0:T(8,128)(2,1)S(1)}, u32[]{:S(2)}, u32[]{:S(2)}) collective-permute-start(bf16[128,2048]{1,0:T(8,128)(2,1)S(1)} %slice.559), channel_id=1, source_target_pairs={{4,0},{5,1},{6,2},{7,3},{0,4},{1,5},{2,6},{3,7},{12,8},{13,9},{14,... | collective-permute-start | bytes 1572872 | tf_op jit(solution)/shard_map/ppermute | solution.py:415
  178.7 18.4 %collective-permute-start.36 = (bf16[256,2048]{1,0:T(8,128)(2,1)S(1)}, bf16[256,2048]{1,0:T(8,128)(2,1)S(1)}, u32[]{:S(2)}, u32[]{:S(2)}) collective-permute-start(bf16[256,2048]{1,0:T(8,128)(2,1)S(1)} %collective-permute-done.33), channel_id=1, source_target_pairs={{2,0},{3,1},{0,2},{1,3},{6,4},{7,5},{4,6},{5,7},{10,8},{11,9},{8,1... | collective-permute-start | bytes 3145736 | tf_op jit(solution)/shard_map/ppermute | solution.py:418
  179.7 21.0 %collective-permute-start.32 = (bf16[256,2048]{1,0:T(8,128)(2,1)S(1)}, bf16[256,2048]{1,0:T(8,128)(2,1)S(1)}, u32[]{:S(2)}, u32[]{:S(2)}) collective-permute-start(bf16[256,2048]{1,0:T(8,128)(2,1)S(1)} %collective-permute-done.30), channel_id=1, source_target_pairs={{2,0},{3,1},{0,2},{1,3},{6,4},{7,5},{4,6},{5,7},{10,8},{11,9},{8,1... | collective-permute-start | bytes 3145736 | tf_op jit(solution)/shard_map/ppermute | solution.py:418
  195.0 22.5 %collective-permute-start.40 = (bf16[512,2048]{1,0:T(8,128)(2,1)}, bf16[512,2048]{1,0:T(8,128)(2,1)S(1)}, u32[]{:S(2)}, u32[]{:S(2)}) collective-permute-start(bf16[512,2048]{1,0:T(8,128)(2,1)} %convolution_convert_fusion.4), channel_id=1, source_target_pairs={{2,0},{3,1},{0,2},{1,3},{6,4},{7,5},{4,6},{5,7},{10,8},{11,9},{8,1... | collective-permute-start | bytes 6291464 | tf_op jit(solution)/shard_map/ppermute | solution.py:418
  197.1 22.0 %collective-permute-start.39 = (bf16[512,2048]{1,0:T(8,128)(2,1)S(1)}, bf16[512,2048]{1,0:T(8,128)(2,1)S(1)}, u32[]{:S(2)}, u32[]{:S(2)}) collective-permute-start(bf16[512,2048]{1,0:T(8,128)(2,1)S(1)} %convolution_convert_fusion.5), channel_id=1, source_target_pairs={{2,0},{3,1},{0,2},{1,3},{6,4},{7,5},{4,6},{5,7},{10,8},{11,9},{8,1... | collective-permute-start | bytes 6291464 | tf_op jit(solution)/shard_map/ppermute | solution.py:418
  224.5 61.8 %collective-permute-start.42 = (bf16[512,2048]{1,0:T(8,128)(2,1)}, bf16[512,2048]{1,0:T(8,128)(2,1)S(1)}, u32[]{:S(2)}, u32[]{:S(2)}) collective-permute-start(bf16[512,2048]{1,0:T(8,128)(2,1)} %convolution_convert_fusion.2), channel_id=1, source_target_pairs={{2,0},{3,1},{0,2},{1,3},{6,4},{7,5},{4,6},{5,7},{10,8},{11,9},{8,1... | collective-permute-start | bytes 6291464 | tf_op jit(solution)/shard_map/ppermute | solution.py:418
  224.7 64.0 %collective-permute-start.41 = (bf16[512,2048]{1,0:T(8,128)(2,1)S(1)}, bf16[512,2048]{1,0:T(8,128)(2,1)S(1)}, u32[]{:S(2)}, u32[]{:S(2)}) collective-permute-start(bf16[512,2048]{1,0:T(8,128)(2,1)S(1)} %convolution_convert_fusion.3), channel_id=1, source_target_pairs={{2,0},{3,1},{0,2},{1,3},{6,4},{7,5},{4,6},{5,7},{10,8},{11,9},{8,1... | collective-permute-start | bytes 6291464 | tf_op jit(solution)/shard_map/ppermute | solution.py:418
  225.1 13.9 %collective-permute-start.66 = (bf16[128,2048]{1,0:T(8,128)(2,1)S(1)}, bf16[128,2048]{1,0:T(8,128)(2,1)S(1)}, u32[]{:S(2)}, u32[]{:S(2)}) collective-permute-start(bf16[128,2048]{1,0:T(8,128)(2,1)S(1)} %get-tuple-element.190), channel_id=1, source_target_pairs={{4,0},{5,1},{6,2},{7,3},{0,4},{1,5},{2,6},{3,7},{12,8},{13,9},{14,... | collective-permute-start | bytes 1572872 | tf_op jit(solution)/shard_map/ppermute | solution.py:415
  226.6 14.0 %collective-permute-start.68 = (bf16[128,2048]{1,0:T(8,128)(2,1)S(1)}, bf16[128,2048]{1,0:T(8,128)(2,1)S(1)}, u32[]{:S(2)}, u32[]{:S(2)}) collective-permute-start(bf16[128,2048]{1,0:T(8,128)(2,1)S(1)} %get-tuple-element.191), channel_id=1, source_target_pairs={{1,0},{0,1},{3,2},{2,3},{5,4},{4,5},{7,6},{6,7},{9,8},{8,9},{11,10... | collective-permute-start | bytes 1572872 | tf_op jit(solution)/shard_map/ppermute | solution.py:412
  239.4 24.4 %collective-permute-start.67 = (bf16[256,2048]{1,0:T(8,128)(2,1)S(1)}, bf16[256,2048]{1,0:T(8,128)(2,1)S(1)}, u32[]{:S(2)}, u32[]{:S(2)}) collective-permute-start(bf16[256,2048]{1,0:T(8,128)(2,1)S(1)} %convert_element_type.341), channel_id=1, source_target_pairs={{1,0},{0,1},{3,2},{2,3},{5,4},{4,5},{7,6},{6,7},{9,8},{8,9},{11,10... | collective-permute-start | bytes 3145736 | tf_op jit(solution)/shard_map/ppermute | solution.py:412
  241.0 24.2 %collective-permute-start.69 = (bf16[256,2048]{1,0:T(8,128)(2,1)S(1)}, bf16[256,2048]{1,0:T(8,128)(2,1)S(1)}, u32[]{:S(2)}, u32[]{:S(2)}) collective-permute-start(bf16[256,2048]{1,0:T(8,128)(2,1)S(1)} %convert_element_type.345), channel_id=1, source_target_pairs={{4,0},{5,1},{6,2},{7,3},{0,4},{1,5},{2,6},{3,7},{12,8},{13,9},{14,... | collective-permute-start | bytes 3145736 | tf_op jit(solution)/shard_map/ppermute | solution.py:415
  265.9 19.5 %collective-permute-start.71 = (bf16[64,2048]{1,0:T(8,128)(2,1)S(1)}, bf16[64,2048]{1,0:T(8,128)(2,1)S(1)}, u32[]{:S(2)}, u32[]{:S(2)}) collective-permute-start(bf16[64,2048]{1,0:T(8,128)(2,1)S(1)} %get-tuple-element.189), channel_id=1, source_target_pairs={{16,0},{17,1},{18,2},{19,3},{20,4},{21,5},{22,6},{23,7},{24,8},{25... | collective-permute-start | bytes 786440 | tf_op jit(solution)/shard_map/ppermute | solution.py:409
  266.0 19.5 %collective-permute-start.72 = (bf16[64,2048]{1,0:T(8,128)(2,1)S(1)}, bf16[64,2048]{1,0:T(8,128)(2,1)S(1)}, u32[]{:S(2)}, u32[]{:S(2)}) collective-permute-start(bf16[64,2048]{1,0:T(8,128)(2,1)S(1)} %get-tuple-element.188), channel_id=1, source_target_pairs={{8,0},{9,1},{10,2},{11,3},{12,4},{13,5},{14,6},{15,7},{16,8},{17,9... | collective-permute-start | bytes 786440 | tf_op jit(solution)/shard_map/ppermute | solution.py:409
  319.9 41.2 %collective-permute-start.44 = (bf16[512,2048]{1,0:T(8,128)(2,1)S(1)}, bf16[512,2048]{1,0:T(8,128)(2,1)S(1)}, u32[]{:S(2)}, u32[]{:S(2)}) collective-permute-start(bf16[512,2048]{1,0:T(8,128)(2,1)S(1)} %pad_maximum_fusion.1), channel_id=1, source_target_pairs={{2,0},{3,1},{0,2},{1,3},{6,4},{7,5},{4,6},{5,7},{10,8},{11,9},{8,1... | collective-permute-start | bytes 6291464 | tf_op jit(solution)/shard_map/ppermute | solution.py:418
  320.3 43.1 %collective-permute-start.43 = (bf16[512,2048]{1,0:T(8,128)(2,1)S(1)}, bf16[512,2048]{1,0:T(8,128)(2,1)S(1)}, u32[]{:S(2)}, u32[]{:S(2)}) collective-permute-start(bf16[512,2048]{1,0:T(8,128)(2,1)S(1)} %pad_maximum_fusion), channel_id=1, source_target_pairs={{2,0},{3,1},{0,2},{1,3},{6,4},{7,5},{4,6},{5,7},{10,8},{11,9},{8,1... | collective-permute-start | bytes 6291464 | tf_op jit(solution)/shard_map/ppermute | solution.py:418
  323.9 14.9 %collective-permute-start.61 = (bf16[128,2048]{1,0:T(8,128)(2,1)S(1)}, bf16[128,2048]{1,0:T(8,128)(2,1)S(1)}, u32[]{:S(2)}, u32[]{:S(2)}) collective-permute-start(bf16[128,2048]{1,0:T(8,128)(2,1)S(1)} %get-tuple-element.196), channel_id=1, source_target_pairs={{1,0},{0,1},{3,2},{2,3},{5,4},{4,5},{7,6},{6,7},{9,8},{8,9},{11,10... | collective-permute-start | bytes 1572872 | tf_op jit(solution)/shard_map/ppermute | solution.py:412
  330.6 28.7 %collective-permute-start.60 = (bf16[256,2048]{1,0:T(8,128)(2,1)S(1)}, bf16[256,2048]{1,0:T(8,128)(2,1)S(1)}, u32[]{:S(2)}, u32[]{:S(2)}) collective-permute-start(bf16[256,2048]{1,0:T(8,128)(2,1)S(1)} %convert_element_type.328), channel_id=1, source_target_pairs={{1,0},{0,1},{3,2},{2,3},{5,4},{4,5},{7,6},{6,7},{9,8},{8,9},{11,10... | collective-permute-start | bytes 3145736 | tf_op jit(solution)/shard_map/ppermute | solution.py:412
  339.2 21.3 %collective-permute-start.62 = (bf16[256,2048]{1,0:T(8,128)(2,1)S(1)}, bf16[256,2048]{1,0:T(8,128)(2,1)S(1)}, u32[]{:S(2)}, u32[]{:S(2)}) collective-permute-start(bf16[256,2048]{1,0:T(8,128)(2,1)S(1)} %convert_element_type.332), channel_id=1, source_target_pairs={{4,0},{5,1},{6,2},{7,3},{0,4},{1,5},{2,6},{3,7},{12,8},{13,9},{14,... | collective-permute-start | bytes 3145736 | tf_op jit(solution)/shard_map/ppermute | solution.py:415
  373.1 23.5 %collective-permute-start.48 = (bf16[256,2048]{1,0:T(8,128)(2,1)S(1)}, bf16[256,2048]{1,0:T(8,128)(2,1)S(1)}, u32[]{:S(2)}, u32[]{:S(2)}) collective-permute-start(bf16[256,2048]{1,0:T(8,128)(2,1)S(1)} %convert_element_type.315), channel_id=1, source_target_pairs={{1,0},{0,1},{3,2},{2,3},{5,4},{4,5},{7,6},{6,7},{9,8},{8,9},{11,10... | collective-permute-start | bytes 3145736 | tf_op jit(solution)/shard_map/ppermute | solution.py:412
  374.5 22.1 %collective-permute-start.50 = (bf16[256,2048]{1,0:T(8,128)(2,1)S(1)}, bf16[256,2048]{1,0:T(8,128)(2,1)S(1)}, u32[]{:S(2)}, u32[]{:S(2)}) collective-permute-start(bf16[256,2048]{1,0:T(8,128)(2,1)S(1)} %convert_element_type.319), channel_id=1, source_target_pairs={{4,0},{5,1},{6,2},{7,3},{0,4},{1,5},{2,6},{3,7},{12,8},{13,9},{14,... | collective-permute-start | bytes 3145736 | tf_op jit(solution)/shard_map/ppermute | solution.py:415
  382.4 13.3 %collective-permute-start.64 = (bf16[64,2048]{1,0:T(8,128)(2,1)S(1)}, bf16[64,2048]{1,0:T(8,128)(2,1)S(1)}, u32[]{:S(2)}, u32[]{:S(2)}) collective-permute-start(bf16[64,2048]{1,0:T(8,128)(2,1)S(1)} %get-tuple-element.194), channel_id=1, source_target_pairs={{16,0},{17,1},{18,2},{19,3},{20,4},{21,5},{22,6},{23,7},{24,8},{25... | collective-permute-start | bytes 786440 | tf_op jit(solution)/shard_map/ppermute | solution.py:409
  382.4 13.3 %collective-permute-start.65 = (bf16[64,2048]{1,0:T(8,128)(2,1)S(1)}, bf16[64,2048]{1,0:T(8,128)(2,1)S(1)}, u32[]{:S(2)}, u32[]{:S(2)}) collective-permute-start(bf16[64,2048]{1,0:T(8,128)(2,1)S(1)} %get-tuple-element.193), channel_id=1, source_target_pairs={{8,0},{9,1},{10,2},{11,3},{12,4},{13,5},{14,6},{15,7},{16,8},{17,9... | collective-permute-start | bytes 786440 | tf_op jit(solution)/shard_map/ppermute | solution.py:409
  402.5 35.8 %collective-permute-start.51 = (bf16[64,2048]{1,0:T(8,128)(2,1)}, bf16[64,2048]{1,0:T(8,128)(2,1)S(1)}, u32[]{:S(2)}, u32[]{:S(2)}) collective-permute-start(bf16[64,2048]{1,0:T(8,128)(2,1)} %get-tuple-element.197), channel_id=1, source_target_pairs={{24,0},{25,1},{26,2},{27,3},{28,4},{29,5},{30,6},{31,7},{0,8},{1,9... | collective-permute-start | bytes 786440 | tf_op jit(solution)/shard_map/ppermute | solution.py:409
  406.5 31.8 %collective-permute-start.52 = (bf16[64,2048]{1,0:T(8,128)(2,1)}, bf16[64,2048]{1,0:T(8,128)(2,1)}, u32[]{:S(2)}, u32[]{:S(2)}) collective-permute-start(bf16[64,2048]{1,0:T(8,128)(2,1)} %get-tuple-element.199), channel_id=1, source_target_pairs={{16,0},{17,1},{18,2},{19,3},{20,4},{21,5},{22,6},{23,7},{24,8},{25... | collective-permute-start | bytes 786440 | tf_op jit(solution)/shard_map/ppermute | solution.py:409
  408.9 29.4 %collective-permute-start.53 = (bf16[64,2048]{1,0:T(8,128)(2,1)}, bf16[64,2048]{1,0:T(8,128)(2,1)}, u32[]{:S(2)}, u32[]{:S(2)}) collective-permute-start(bf16[64,2048]{1,0:T(8,128)(2,1)} %get-tuple-element.198), channel_id=1, source_target_pairs={{8,0},{9,1},{10,2},{11,3},{12,4},{13,5},{14,6},{15,7},{16,8},{17,9... | collective-permute-start | bytes 786440 | tf_op jit(solution)/shard_map/ppermute | solution.py:409
  415.8 25.3 %collective-permute-start.46 = (bf16[256,1024]{1,0:T(8,128)(2,1)S(1)}, bf16[256,1024]{1,0:T(8,128)(2,1)}, u32[]{:S(2)}, u32[]{:S(2)}) collective-permute-start(bf16[256,1024]{1,0:T(8,128)(2,1)S(1)} %get-tuple-element.201), channel_id=1, source_target_pairs={{1,0},{0,1},{3,2},{2,3},{5,4},{4,5},{7,6},{6,7},{9,8},{8,9},{11,10... | collective-permute-start | bytes 1572872 | tf_op jit(solution)/shard_map/ppermute | solution.py:412
  434.1 13.7 %collective-permute-start.45 = (bf16[256,1024]{1,0:T(8,128)(2,1)S(1)}, bf16[256,1024]{1,0:T(8,128)(2,1)S(1)}, u32[]{:S(2)}, u32[]{:S(2)}) collective-permute-start(bf16[256,1024]{1,0:T(8,128)(2,1)S(1)} %get-tuple-element.203), channel_id=1, source_target_pairs={{1,0},{0,1},{3,2},{2,3},{5,4},{4,5},{7,6},{6,7},{9,8},{8,9},{11,10... | collective-permute-start | bytes 1572872 | tf_op jit(solution)/shard_map/ppermute | solution.py:412
  (70 other events, 777.6 us)

commit v3 on v0

--- a/solution.py
+++ b/solution.py
@@ -4,6 +4,8 @@
 import jax
 import jax.numpy as jnp
 from jax import lax
+from jax.experimental import pallas as pl
+from jax.experimental.pallas import tpu as pltpu
 from jax.sharding import PartitionSpec as P
 
 HEAD_DIM = 64
@@ -71,7 +73,7 @@
     return (dquery, d_keys, dvalues)
 
 
-def per_device(
+def shared_slots(
     clips,
     cotangent,
     clip_live,
@@ -264,9 +266,963 @@
     )
 
 
+AXES = ("wide", "tp")
+PAIR = 128
+TILE = 512
+VMEM_MIB = 60
+WIDE = 1024
+bf16 = jnp.bfloat16
+f32 = jnp.float32
+
+
+def fits_own_slot(mesh):
+    return mesh.shape["tp"] == 2 and mesh.shape["wide"] % 4 == 0
+
+
+def nt_dot(left_op, right_op):
+    return lax.dot_general(
+        left_op, right_op, (((1,), (1,)), ((), ())), preferred_element_type=f32
+    )
+
+
+def nn_dot(left_op, right_op):
+    return lax.dot_general(
+        left_op, right_op, (((1,), (0,)), ((), ())), preferred_element_type=f32
+    )
+
+
+def kernel_call(body, name, grid, in_specs, out_specs, out_shape, scratch=(), scalars=0, vmem=VMEM_MIB):
+    return pl.pallas_call(
+        body,
+        grid_spec=pltpu.PrefetchScalarGridSpec(
+            num_scalar_prefetch=scalars,
+            grid=grid,
+            in_specs=in_specs,
+            out_specs=out_specs,
+            scratch_shapes=list(scratch),
+        ),
+        out_shape=out_shape,
+        compiler_params=pltpu.CompilerParams(vmem_limit_bytes=vmem * 1024 * 1024),
+        cost_estimate=pl.CostEstimate(flops=1, bytes_accessed=1, transcendentals=0),
+        name=name,
+    )
+
+
+def whole(shape):
+    return pl.BlockSpec(shape, lambda *at: (0,) * len(shape))
+
+
+def array(*shape, dtype=bf16):
+    return jax.ShapeDtypeStruct(shape, dtype)
+
+
+def norm_stats(rows):
+    row_mean = jnp.mean(rows, axis=-1, keepdims=True)
+    centred = rows - row_mean
+    spread = jnp.mean(centred * centred, axis=-1, keepdims=True)
+    inverse = lax.rsqrt(spread + norm_eps)
+    return centred * inverse, inverse
+
+
+NEAR = (0, 2, 5, 7)
+FAR = (1, 3, 4, 6, 8, 9)
+
+
+class Pieces:
+    def __init__(self, pieces, columns, first=0):
+        self.pieces, self.columns, self.first = pieces, columns, first
+        self.args = list(pieces)
+        self.specs = [pl.BlockSpec(memory_space=pl.ANY)] * len(pieces)
+        rows = sum(pieces[i].shape[0] for i in NEAR)
+        self.scratch = [
+            pltpu.VMEM((2, rows, columns), bf16),
+            pltpu.SemaphoreType.DMA((len(pieces),)),
+        ]
+
+    def copies(self, refs, side, w_ref, sems):
+        at, found = 0, []
+        for index in FAR if side else NEAR:
+            rows = self.pieces[index].shape[0]
+            found.append(
+                pltpu.make_async_copy(
+                    refs[index].at[:, pl.ds(self.first, self.columns)],
+                    w_ref.at[side, pl.ds(at, rows)],
+                    sems.at[index],
+                )
+            )
+            at += rows
+        return found
+
+    def start(self, refs, w_ref, sems):
+        for side in range(2):
+            for copy in self.copies(refs, side, w_ref, sems):
+                copy.start()
+
+    def wait(self, refs, side, w_ref, sems):
+        for copy in self.copies(refs, side, w_ref, sems):
+            copy.wait()
+
+
+class Gathered:
+    def __init__(self, weights):
+        self.wide, _, self.rows, self.columns = weights.shape
+        self.args = [weights]
+        self.specs = [pl.BlockSpec(memory_space=pl.ANY)]
+        self.scratch = [
+            pltpu.VMEM((2, self.wide * self.rows, self.columns), bf16),
+            pltpu.SemaphoreType.DMA((2, self.wide)),
+        ]
+
+    def copies(self, refs, side, w_ref, sems):
+        place_ref, all_ref = refs
+        return [
+            pltpu.make_async_copy(
+                all_ref.at[place_ref[1 + j], place_ref[0] ^ side],
+                w_ref.at[side, pl.ds(j * self.rows, self.rows)],
+                sems.at[side, j],
+            )
+            for j in range(self.wide)
+        ]
+
+    start = Pieces.start
+    wait = Pieces.wait
+
+
+def enter_kernel(own_ref, got_ref, order_ref, gain_ref, shift_ref, x_ref, h_ref, ht_ref):
+    half = own_ref.shape[0]
+    for part, ref in enumerate((own_ref, got_ref)):
+        rows = nn_dot(ref[...], order_ref[...])
+        here = pl.ds(part * half, half)
+        x_ref[here, :] = rows.astype(bf16)
+        unit, _ = norm_stats(rows)
+        normed = (unit * gain_ref[...] + shift_ref[...]).astype(bf16)
+        h_ref[here, :] = normed
+        ht_ref[:, here] = normed.T
+
+
+def enter(own, got, order_b, gain, shift):
+    half, width = own.shape
+    length = 2 * half
+    return kernel_call(
+        enter_kernel,
+        "enter",
+        (1,),
+        [whole((half, width))] * 2 + [whole((width, width))] + [whole((1, width))] * 2,
+        [whole((length, width))] * 2 + [whole((width, length))],
+        [array(length, width)] * 2 + [array(width, length)],
+    )(own, got, order_b, gain, shift)
+
+
+def cot_kernel(own_ref, got_ref, order_ref, live_ref, e_ref, et_ref):
+    half = own_ref.shape[0]
+    for part, ref in enumerate((own_ref, got_ref)):
+        rows = (live_ref[...] * nn_dot(ref[...], order_ref[...])).astype(bf16)
+        here = pl.ds(part * half, half)
+        e_ref[here, :] = rows
+        et_ref[:, here] = rows.T
+
+
+def enter_cot(own, got, order_b, live):
+    half, width = own.shape
+    length = 2 * half
+    return kernel_call(
+        cot_kernel,
+        "enter_cot",
+        (1,),
+        [whole((half, width))] * 2 + [whole((width, width)), whole((1, width))],
+        [whole((length, width)), whole((width, length))],
+        [array(length, width), array(width, length)],
+    )(own, got, order_b, live)
+
+
+def project(h, pieces, biases):
+    length, width = h.shape
+    cols = pieces[0].shape[1]
+    each = cols // 3
+    q_scale = 1.0 / math.sqrt(HEAD_DIM)
+    load = Pieces(pieces, cols)
+
+    def body(h_ref, bias_ref, *refs):
+        refs, out_ref, w_ref, sems = refs[:-3], *refs[-3:]
+        pl.when(pl.program_id(0) == 0)(lambda: load.start(refs, w_ref, sems))
+        for side in range(2):
+
+            @pl.when(pl.program_id(0) == side)
+            def _():
+                load.wait(refs, side, w_ref, sems)
+                acc = nn_dot(h_ref[...], w_ref[side]) + bias_ref[0]
+                out_ref[0] = (acc[:, :each] * q_scale).astype(bf16)
+                out_ref[1] = acc[:, each : 2 * each].astype(bf16)
+                out_ref[2] = acc[:, 2 * each :].astype(bf16)
+
+    return kernel_call(
+        body,
+        "project",
+        (2,),
+        [whole((length, width)), pl.BlockSpec((1, 1, cols), lambda s: (s, 0, 0))] + load.specs,
+        pl.BlockSpec((3, length, each), lambda s: (0, 0, s)),
+        array(3, length, width),
+        load.scratch,
+        vmem=VMEM_MIB,
+    )(h, biases, *load.args)
+
+
+def attend_kernel(q_ref, k_ref, v_ref, o_ref, lse_ref):
+    pair = pl.program_id(0)
+    rows = q_ref.shape[1]
+    lanes = lax.broadcasted_iota(jnp.int32, (rows, PAIR), 1)
+    keys = k_ref[0]
+    values = v_ref[0]
+    total = jnp.zeros((rows, PAIR), f32)
+    for half in range(2):
+        mask = (lanes // HEAD_DIM) == half
+        query = jnp.where(mask, q_ref[0], jnp.zeros_like(keys))
+        scores = nt_dot(query, keys)
+        row_max = jnp.max(scores, axis=-1, keepdims=True)
+        weights = jnp.exp(scores - row_max)
+        row_sum = jnp.sum(weights, axis=-1, keepdims=True)
+        probs = (weights * (1.0 / row_sum)).astype(bf16)
+        mixed = nn_dot(probs, values)
+        total = jnp.where(mask, mixed, total)
+        lse = row_max + jnp.log(row_sum)
+        lse_ref[...] = jnp.where(lanes == 2 * pair + half, lse, lse_ref[...])
+    o_ref[...] = total.astype(bf16)
+
+
+def head_spec(length, index):
+    return pl.BlockSpec((1, length, PAIR), lambda i: (index, 0, i))
+
+
+def attend_fwd(qkv):
+    _, length, width = qkv.shape
+    return kernel_call(
+        attend_kernel,
+        "attend_fwd",
+        (width // PAIR,),
+        [head_spec(length, j) for j in range(3)],
+        [pl.BlockSpec((length, PAIR), lambda i: (0, i)), whole((length, PAIR))],
+        [array(length, width), array(length, PAIR, dtype=f32)],
+    )(qkv, qkv, qkv)
+
+
+def join_heads(attn, x, pieces, first, bias, gain, shift):
+    length, width = x.shape
+    load = Pieces(pieces, TILE, first)
+
+    def body(attn_ref, x_ref, bias_ref, gain_ref, shift_ref, *refs):
+        refs, (y_ref, h_ref, ht_ref, w_ref, sems) = refs[:-5], refs[-5:]
+        load.start(refs, w_ref, sems)
+        load.wait(refs, 0, w_ref, sems)
+        load.wait(refs, 1, w_ref, sems)
+        half = length // 2
+        for part in range(2):
+            here = pl.ds(part * half, half)
+            rows = nt_dot(attn_ref[here, :TILE], w_ref[0]) + nt_dot(attn_ref[here, TILE:], w_ref[1])
+            rows = x_ref[here, :].astype(f32) + rows + bias_ref[...]
+            y_ref[here, :] = rows
+            unit, _ = norm_stats(rows)
+            normed = (unit * gain_ref[...] + shift_ref[...]).astype(bf16)
+            h_ref[here, :] = normed
+            ht_ref[:, here] = normed.T
+
+    return kernel_call(
+        body,
+        "join_heads",
+        (1,),
+        [whole((length, width))] * 2 + [whole((1, width))] * 3 + load.specs,
+        [whole((length, width))] * 2 + [whole((width, length))],
+        [array(length, width, dtype=f32), array(length, width), array(width, length)],
+        load.scratch,
+    )(attn, x, bias, gain, shift, *load.args)
+
+
+def expand(h, pieces, bias, hidden):
+    length, width = h.shape
+    per = hidden // WIDE
+    load = Pieces(pieces, hidden)
+
+    def body(h_ref, bias_ref, *refs):
+        refs, (g_ref, slope_ref, w_ref, sems) = refs[:-4], refs[-4:]
+        step = pl.program_id(0)
+        pl.when(step == 0)(lambda: load.start(refs, w_ref, sems))
+        for side in range(2):
+            pl.when(step == side * per)(partial(load.wait, refs, side, w_ref, sems))
+        at = pl.ds(pl.multiple_of(step % per * WIDE, WIDE), WIDE)
+        pre = nn_dot(h_ref[...], w_ref[step // per, :, at]) + bias_ref[...]
+        cdf = 0.5 * (1.0 + lax.erf(pre * root_half))
+        g_ref[...] = (pre * cdf).astype(bf16)
+        density = jnp.exp(-0.5 * pre * pre) * inv_root_two_pi
+        slope_ref[...] = (cdf + pre * density).astype(bf16)
+
+    block = pl.BlockSpec((length, WIDE), lambda s: (0, s))
+    return kernel_call(
+        body,
+        "expand",
+        (2 * per,),
+        [whole((length, width)), pl.BlockSpec((1, WIDE), lambda s: (0, s))] + load.specs,
+        [block] * 2,
+        [array(length, 2 * hidden)] * 2,
+        load.scratch,
+        vmem=VMEM_MIB,
+    )(h, bias, *load.args)
+
+
+def hidden_back(e, slope, weights, place):
+    length, width = e.shape
+    hidden = weights.shape[3]
+    per = hidden // WIDE
+    load = Gathered(weights)
+
+    def body(place_ref, e_ref, slope_ref, all_ref, du_ref, sum_ref, w_ref, sems):
+        refs = (place_ref, all_ref)
+        step = pl.program_id(0)
+        pl.when(step == 0)(lambda: load.start(refs, w_ref, sems))
+        for side in range(2):
+            pl.when(step == side * per)(partial(load.wait, refs, side, w_ref, sems))
+        at = pl.ds(pl.multiple_of(step % per * WIDE, WIDE), WIDE)
+        du = nn_dot(e_ref[...], w_ref[step // per, :, at]) * slope_ref[...].astype(f32)
+        du_ref[...] = du.astype(bf16)
+        sum_ref[...] = jnp.sum(du, axis=0, keepdims=True)
+
+    block = pl.BlockSpec((length, WIDE), lambda s, *_: (0, s))
+    row = pl.BlockSpec((1, WIDE), lambda s, *_: (0, s))
+    return kernel_call(
+        body,
+        "hidden_back",
+        (2 * per,),
+        [whole((length, width)), block] + load.specs,
+        [block, row],
+        [array(length, 2 * hidden), array(1, 2 * hidden, dtype=f32)],
+        load.scratch,
+        scalars=1,
+        vmem=VMEM_MIB,
+    )(place, e, slope, weights)
+
+
+def heads_back(da, pieces, first):
+    length, width = da.shape
+    load = Pieces(pieces, TILE, first)
+
+    def body(da_ref, *refs):
+        refs, (out_ref, w_ref, sems) = refs[:-3], refs[-3:]
+        load.start(refs, w_ref, sems)
+        for side in range(2):
+            load.wait(refs, side, w_ref, sems)
+            out_ref[:, pl.ds(side * TILE, TILE)] = nn_dot(da_ref[...], w_ref[side]).astype(bf16)
+
+    return kernel_call(
+        body,
+        "heads_back",
+        (1,),
+        [whole((length, width))] + load.specs,
+        whole((length, 2 * TILE)),
+        array(length, 2 * TILE),
+        load.scratch,
+        vmem=VMEM_MIB,
+    )(da, *load.args)
+
+
+def contract_back(rows, rows_specs, left_of, load, extras, extra_specs, finish, name, outs, place=()):
+    count = len(extras)
+    length, width = extras[0].shape
+
+    def body(*refs):
+        place_refs, refs = refs[: len(place)], refs[len(place) :]
+        rows_refs, refs = refs[: len(rows)], refs[len(rows) :]
+        extra_refs, refs = refs[:count], refs[count:]
+        w_refs, refs = place_refs + refs[: len(load.args)], refs[len(load.args) :]
+        out_refs, (w_ref, sems, acc_ref) = refs[:-3], refs[-3:]
+
+        @pl.when(pl.program_id(0) == 0)
+        def _():
+            load.start(w_refs, w_ref, sems)
+            load.wait(w_refs, 0, w_ref, sems)
+            acc_ref[...] = nt_dot(left_of(rows_refs, 0), w_ref[0])
+
+        @pl.when(pl.program_id(0) == 1)
+        def _():
+            load.wait(w_refs, 1, w_ref, sems)
+            acc_ref[...] += nt_dot(left_of(rows_refs, 1), w_ref[1])
+            finish(acc_ref, extra_refs, out_refs)
+
+    return kernel_call(
+        body,
+        name,
+        (2,),
+        rows_specs + extra_specs + load.specs,
+        [whole(o.shape) for o in outs],
+        outs,
+        load.scratch + [pltpu.VMEM((length, width), f32)],
+        scalars=len(place),
+        vmem=VMEM_MIB,
+    )(*place, *rows, *extras, *load.args)
+
+
+def to_home(rows, order_ref):
+    return nt_dot(rows.astype(bf16), order_ref[...]).astype(bf16)
+
+
+def layer_out(hidden, weights, place, y, bias, live, order_b):
+    length, width = y.shape
+    half = length // 2
+    columns = weights.shape[3]
+
+    def finish(acc_ref, ins, outs):
+        y_ref, bias_ref, live_ref, order_ref = ins
+        for part in range(2):
+            here = pl.ds(part * half, half)
+            rows = live_ref[...] * (y_ref[here, :] + acc_ref[here, :] + bias_ref[...])
+            outs[part][...] = to_home(rows, order_ref)
+
+    return contract_back(
+        [hidden],
+        [pl.BlockSpec((length, columns), lambda s, *_: (0, s))],
+        lambda refs, side: refs[0][...],
+        Gathered(weights),
+        (y, bias, live, order_b),
+        [whole((length, width)), whole((1, width)), whole((1, width)), whole((width, width))],
+        finish,
+        "layer_out",
+        [array(half, width)] * 2,
+        (place,),
+    )
+
+
+def second_back(du, pieces, hidden, y, e, gain):
+    length, width = y.shape
+    half = length // 2
+
+    def finish(acc_ref, ins, outs):
+        y_ref, e_ref, gain_ref = ins
+        mid_ref, da_ref, dat_ref, sum_ref = outs
+        sums = [jnp.zeros((1, width), f32)] * 4
+        for part in range(2):
+            here = pl.ds(part * half, half)
+            unit, inverse = norm_stats(y_ref[here, :])
+            grad = acc_ref[here, :]
+            e_rows = e_ref[here, :].astype(f32)
+            mid = e_rows + norm_back(grad, unit, inverse, gain_ref[...])
+            mid_ref[here, :] = mid
+            mid_b = mid.astype(bf16)
+            da_ref[here, :] = mid_b
+            dat_ref[:, here] = mid_b.T
+            terms = (grad * unit, grad, mid, e_rows)
+            sums = [s + jnp.sum(term, axis=0, keepdims=True) for s, term in zip(sums, terms)]
+        sum_ref[...] = jnp.concatenate(sums, axis=0)
+
+    return contract_back(
+        [du],
+        [pl.BlockSpec((length, hidden), lambda s: (0, s))],
+        lambda refs, side: refs[0][...],
+        Pieces(pieces, hidden),
+        (y, e, gain),
+        [whole((length, width)), whole((length, width)), whole((1, width))],
+        finish,
+        "second_back",
+        [
+            array(length, width, dtype=f32),
+            array(length, width),
+            array(width, length),
+            array(4, width, dtype=f32),
+        ],
+    )
+
+
+def first_back(dps, pieces, x, mid, gain, order_b):
+    length, width = x.shape
+    half = length // 2
+
+    def finish(acc_ref, ins, outs):
+        x_ref, mid_ref, gain_ref, order_ref = ins
+        sum_ref = outs[2]
+        sums = [jnp.zeros((1, width), f32)] * 2
+        for part in range(2):
+            here = pl.ds(part * half, half)
+            unit, inverse = norm_stats(x_ref[here, :].astype(f32))
+            grad = acc_ref[here, :]
+            rows = mid_ref[here, :] + norm_back(grad, unit, inverse, gain_ref[...])
+            outs[part][...] = to_home(rows, order_ref)
+            terms = (grad * unit, grad)
+            sums = [s + jnp.sum(term, axis=0, keepdims=True) for s, term in zip(sums, terms)]
+        sum_ref[...] = jnp.concatenate(sums, axis=0)
+
+    return contract_back(
+        dps,
+        [whole(dps[0].shape)] * 2,
+        lambda refs, side: jnp.concatenate([refs[side][j] for j in range(3)], axis=1),
+        Pieces(pieces, pieces[0].shape[1]),
+        (x, mid, gain, order_b),
+        [whole((length, width)), whole((length, width)), whole((1, width)), whole((width, width))],
+        finish,
+        "first_back",
+        [array(half, width)] * 2 + [array(2, width, dtype=f32)],
+    )
+
+
+def attend_back_kernel(first, q_ref, k_ref, v_ref, g_ref, lse_ref, dp_ref, qs_ref, vs_ref):
+    pair = first + pl.program_id(0)
+    rows = q_ref.shape[1]
+    lanes = lax.broadcasted_iota(jnp.int32, (rows, PAIR), 1)
+    sub = lax.broadcasted_iota(jnp.int32, (PAIR, rows), 0)
+    query = q_ref[0]
+    keys = k_ref[0]
+    values = v_ref[0]
+    grads = g_ref[...]
+    blank = jnp.zeros_like(keys)
+    keys_t = keys.T
+    dq_t = jnp.zeros((PAIR, rows), f32)
+    dk = jnp.zeros((rows, PAIR), f32)
+    dv = jnp.zeros((rows, PAIR), f32)
+    for half in range(2):
+        mask = (lanes // HEAD_DIM) == half
+        scores_t = nt_dot(jnp.where(mask, keys, blank), query)
+        lse = lse_ref[pl.ds(2 * pair + half, 1), :]
+        probs_t = jnp.exp(scores_t - lse)
+        dprobs_t = nt_dot(jnp.where(mask, values, blank), grads)
+        delta = jnp.sum(probs_t * dprobs_t, axis=0, keepdims=True)
+        ds_t = (probs_t * (dprobs_t - delta)).astype(bf16)
+        dv = jnp.where(mask, nn_dot(probs_t.astype(bf16), grads), dv)
+        dk = jnp.where(mask, nn_dot(ds_t, query), dk)
+        dq_t = jnp.where((sub // HEAD_DIM) == half, nn_dot(keys_t, ds_t), dq_t)
+    dq = dq_t.T * (1.0 / math.sqrt(HEAD_DIM))
+    dp_ref[0] = dq.astype(bf16)
+    dp_ref[1] = dk.astype(bf16)
+    dp_ref[2] = dv.astype(bf16)
+    qs_ref[...] = jnp.sum(dq, axis=0, keepdims=True)
+    vs_ref[...] = jnp.sum(dv, axis=0, keepdims=True)
+
+
+def attend_bwd(qkv, grads, lse_rows, side):
+    _, length, width = qkv.shape
+    count = width // PAIR // 2
+    first = side * count
+    head = lambda j: pl.BlockSpec((1, length, PAIR), lambda i: (j, 0, first + i))
+    row = pl.BlockSpec((1, PAIR), lambda i: (0, i))
+    sums = array(1, width // 2, dtype=f32)
+    return kernel_call(
+        partial(attend_back_kernel, first),
+        "attend_bwd",
+        (count,),
+        [head(j) for j in range(3)]
+        + [pl.BlockSpec((length, PAIR), lambda i: (0, first + i)), whole((PAIR, length))],
+        [pl.BlockSpec((3, length, PAIR), lambda i: (0, 0, i)), row, row],
+        [array(3, length, width // 2), sums, sums],
+    )(qkv, qkv, qkv, grads, lse_rows)
+
+
+def grad_call(args, specs, terms, cuts, name, steps):
+    count = len(args)
+    kinds, choose, terms = terms
+
+    def body(*refs):
+        def run(kind):
+            left, right = terms(refs[:count], kind)
+            acc = nn_dot(left, right).astype(bf16)
+            for ref, ranges in zip(refs[count:], cuts):
+                at = 0
+                for start, stop in ranges:
+                    ref[pl.ds(at, stop - start), :] = acc[start:stop]
+                    at += stop - start
+
+        for kind in range(kinds):
+            if kinds == 1:
+                run(kind)
+            else:
+                pl.when(choose(pl.program_id(0)) == kind)(partial(run, kind))
+
+    sizes = [sum(b - a for a, b in ranges) for ranges in cuts]
+    return kernel_call(
+        body,
+        name,
+        (steps,),
+        specs,
+        [pl.BlockSpec((size, TILE), lambda s: (0, s)) for size in sizes],
+        [array(size, steps * TILE) for size in sizes],
+    )(*args)
+
+
+def add_mid_kernel(k01_ref, rx_ref, k10_ref, ry_ref, y_ref, x_ref):
+    half = k01_ref.shape[0]
+    y_ref[...] = (k01_ref[...].astype(f32) + rx_ref[pl.ds(half, half), :].astype(f32)).astype(bf16)
+    x_ref[...] = (k10_ref[...].astype(f32) + ry_ref[pl.ds(0, half), :].astype(f32)).astype(bf16)
+
+
+def add_last_kernel(k00_ref, rx_ref, ry_ref, y2_ref, x2_ref, out_ref):
+    half = y2_ref.shape[0]
+    top, low = pl.ds(0, half), pl.ds(half, half)
+    near = (rx_ref[top, :], y2_ref[...]), (ry_ref[low, :], x2_ref[...])
+    for here, (one, two) in zip((top, low), near):
+        total = k00_ref[here, :].astype(f32) + one.astype(f32) + two.astype(f32)
+        out_ref[here, :] = total.astype(bf16)
+
+
+def small_call(body, name, args, shapes):
+    out_specs = [whole(s.shape) for s in shapes]
+    return kernel_call(body, name, (1,), [whole(a.shape) for a in args], out_specs, shapes)(*args)
+
+
+class Links:
+    def __init__(self):
+        self.nz = lax.axis_size("wide") // 4
+        self.across = self.table(lambda z, y, c, x: (z, y, c, 1 - x))
+        self.beside = self.table(lambda z, y, c, x: (z, 1 - y, c, x))
+        self.twin = self.table(lambda z, y, c, x: (z, y, 1 - c, x))
+
+    def table(self, source):
+        pairs = []
+        for z in range(self.nz):
+            for y in range(2):
+                for c in range(2):
+                    for x in range(2):
+                        zs, ys, cs, xs = source(z, y, c, x)
+                        pairs.append(
+                            (((zs * 2 + ys) * 2 + cs) * 2 + xs, ((z * 2 + y) * 2 + c) * 2 + x)
+                        )
+        return pairs
+
+    def from_z(self, rows, step):
+        shift = self.table(lambda z, y, c, x: ((z + step) % self.nz, y, c, x))
+        return lax.ppermute(rows, AXES, shift)
+
+    def z_groups(self):
+        rest = [(y, c, x) for y in range(2) for c in range(2) for x in range(2)]
+        return [
+            [((z * 2 + y) * 2 + c) * 2 + x for z in range(self.nz)] for y, c, x in rest
+        ]
+
+    def z_sum_apart(self, rows):
+        return lax.psum_scatter(
+            rows, AXES, scatter_dimension=0, tiled=True, axis_index_groups=self.z_groups()
+        )
+
+    def z_sum(self, rows):
+        got = lax.all_to_all(rows, AXES, 0, 0, tiled=True, axis_index_groups=self.z_groups())
+        return got.reshape(self.nz, -1, rows.shape[1])
+
+    def z_all(self, rows):
+        return lax.all_gather(
+            rows, AXES, axis=0, tiled=True, axis_index_groups=self.z_groups()
+        )
+
+    def x(self, rows):
+        return lax.ppermute(rows, AXES, self.across)
+
+    def y(self, rows):
+        return lax.ppermute(rows, AXES, self.beside)
+
+    def c(self, rows):
+        return lax.ppermute(rows, AXES, self.twin)
+
+    def flip(self, rows, bit):
+        swap = self.table(lambda z, y, c, x: (z ^ bit, y, c, x))
+        return lax.ppermute(rows, AXES, swap)
+
+
+def after(done, *values):
+    out = lax.optimization_barrier((values, done))[0]
+    return out if len(values) > 1 else out[0]
+
+
+def total_over_all(links, rows):
+    for move in (links.c, links.x, links.y):
+        rows = rows + move(rows)
+    bit = 1
+    while bit < links.nz:
+        rows = rows + links.flip(rows, bit)
+        bit *= 2
+    return rows
+
+
+def start_far(links, near):
+    by_x, by_y = near
+    half = by_x.shape[0] // 2
+    return links.x(by_y[:half]), links.y(by_x[half:])
+
+
+class Home:
+    def __init__(self, links):
+        self.links = links
+
+    def first(self, far, near):
+        x_first, y_low_far, self.k10_low = far
+        self.k00, self.k01_top, y_low_near = near
+        self.x_got = self.links.x(x_first)
+        self.y_got = self.links.y(jnp.concatenate([y_low_far, y_low_near], axis=0))
+
+    def middle(self):
+        half = self.k01_top.shape[0]
+        args = (self.k01_top, self.x_got, self.k10_low, self.y_got)
+        shape = array(*self.k01_top.shape)
+        out_y, out_x = small_call(add_mid_kernel, "add_mid", args, [shape, shape])
+        return out_y, out_x
+
+    def second(self, out_y, out_x):
+        self.y_last, self.x_last = self.links.y(out_y), self.links.x(out_x)
+
+    def last(self, done, apart):
+        y_last, x_last = after(done, self.y_last, self.x_last)
+        args = (self.k00, self.x_got, self.y_got, y_last, x_last)
+        (total,) = small_call(add_last_kernel, "add_last", args, [array(*self.k00.shape)])
+        self.home = self.links.z_sum_apart(total)[None] if apart else self.links.z_sum(total)
+        return total
+
+    def value(self, done, scale):
+        return jnp.sum(after(done, self.home).astype(f32), axis=0) * scale
+
+
+def own_slot(
+    clips,
+    cotangent,
+    clip_live,
+    qkv_weight,
+    q_bias,
+    v_bias,
+    proj_weight,
+    fc1_weight,
+    fc1_bias,
+    fc2_weight,
+    ln_gains,
+    ln_biases,
+    out_bias,
+):
+    links = Links()
+    slot_count, shard_rows, width = clips.shape
+    wide_count = lax.axis_size("wide")
+    length = 2 * shard_rows
+    block = qkv_weight.shape[0]
+    heads_cols = qkv_weight.shape[2]
+    hidden_here = fc1_weight.shape[1]
+    grad_scale = 1.0 / math.sqrt(wide_count * slot_count * length)
+    wide_at = lax.axis_index("wide")
+    t = lax.axis_index("tp")
+    z_at, y_at, c_at = wide_at // 4, (wide_at // 2) % 2, wide_at % 2
+    qkv_cols = 3 * heads_cols
+    pick = lambda both, at: lax.dynamic_index_in_dim(both, at, 0, keepdims=False)
+    row = lambda vector: vector.reshape(1, -1)
+
+    two_shard = jnp.concatenate([fc1_weight, proj_weight.T], axis=1)
+    along_two = links.z_all(two_shard)
+    q_shard = qkv_weight.reshape(block, qkv_cols)
+    steps_one = [links.from_z(q_shard, k) for k in range(1, links.nz)]
+    got_rows = links.x(jnp.concatenate([pick(clips, 1 - t), pick(cotangent, 1 - t)], axis=0))
+    far_small = jnp.concatenate([q_bias, v_bias, fc1_bias]).reshape(-1, 128)
+    far_small = links.x(far_small).reshape(-1)
+
+    spot = jnp.arange(width)
+    rel = spot // block
+    kc, ky, kz = rel // (2 * links.nz), (rel // links.nz) % 2, rel % links.nz
+    home = (kz * 2 + (y_at ^ ky)) * 2 + (c_at ^ kc)
+    order = spot[:, None] == (home * block + spot % block)[None, :]
+    place = jnp.concatenate([t.reshape(1), home[::block]]).astype(jnp.int32)
+    order_b = order.astype(bf16)
+    order_f = order.astype(f32)
+    vectors = jnp.dot(
+        jnp.concatenate([ln_gains, ln_biases, out_bias], axis=0),
+        order_f,
+        precision=lax.Precision.HIGHEST,
+    )
+    gains, shifts, outs = (
+        (vectors[2 * i : 2 * i + 1], vectors[2 * i + 1 : 2 * i + 2]) for i in range(3)
+    )
+    live = jnp.full((1, width), pick(clip_live, t).astype(f32))
+    along_one = jnp.zeros((links.nz * block, qkv_cols), bf16)
+    for step, piece in enumerate([q_shard] + steps_one):
+        at = (z_at + step) % links.nz * block
+        along_one = lax.dynamic_update_slice(along_one, piece, (at, 0))
+    got_rows, far_small = after(along_one, got_rows, far_small)
+    near_one = links.x(along_one), links.y(along_one)
+    x, h1, h1_t = enter(pick(clips, t), got_rows[:shard_rows], order_b, gains[0], shifts[0])
+    e, e_t = enter_cot(pick(cotangent, t), got_rows[shard_rows:], order_b, live)
+    half = width // 2
+    twin_rows = jnp.concatenate([e_t[half:], h1_t[half:]], axis=0)
+    near_one, along_two, twin_rows, fc2_turned = after(
+        (twin_rows, h1, e), near_one, along_two, twin_rows, fc2_weight.T
+    )
+    w_fc2 = lax.all_gather(after(along_two, fc2_turned), AXES, axis=0, tiled=True)
+    w_fc2 = w_fc2.reshape(wide_count, 2, block, hidden_here)
+    far_one = start_far(links, near_one)
+    other_one = [links.c(piece) for piece in (after(near_one, along_one), *near_one)]
+    far_one, other_one, along_two, twin_rows = after((), far_one, other_one, along_two, twin_rows)
+    near_two = links.x(along_two), links.y(along_two)
+    other_one += [links.c(piece) for piece in far_one]
+    twin_rows = links.c(twin_rows)
+    twin_rows, other_one = after((), twin_rows, other_one)
+    twin_e, twin_h1 = twin_rows[:half], twin_rows[half:]
+    w_one = [along_one, *near_one, *far_one, *other_one]
+    zero_row = jnp.zeros((heads_cols,), f32)
+    biases = jnp.stack(
+        [
+            jnp.concatenate([q_bias, zero_row, v_bias]),
+            jnp.concatenate(
+                [far_small[:heads_cols], zero_row, far_small[heads_cols : 2 * heads_cols]]
+            ),
+        ]
+    )[:, None]
+    fc1_biases = row(jnp.concatenate([fc1_bias, far_small[2 * heads_cols :]]))
+    qkv = project(h1, w_one, biases)
+    attn, lse = attend_fwd(qkv)
+    lse_rows = lse.T
+
+    near_two = after(attn, near_two)
+    far_two = start_far(links, near_two)
+    other_two = [links.c(piece) for piece in (after(near_two, along_two), *near_two)]
+    far_two, other_two = after((), far_two, other_two)
+    other_two += [links.c(piece) for piece in far_two]
+    twin_attn = links.c(after(far_two, attn))
+    other_two, twin_attn = after((), other_two, twin_attn)
+    w_two = [along_two, *near_two, *far_two, *other_two]
+    y, h2, h2_t = join_heads(attn, x, w_two, hidden_here, outs[0], gains[1], shifts[1])
+    twin_h2 = links.c(h2_t[half:])
+    hidden, slope = expand(h2, w_two, fc1_biases, hidden_here)
+    twin_hidden = links.c(hidden)
+
+    quarter, mid_row = width // 4, width // 8
+    top, low = (0, mid_row), (mid_row, quarter)
+    top_y, low_y = (quarter, quarter + mid_row), (quarter + mid_row, half)
+    far_cuts = [[top, top_y], [low_y], [low]]
+    near_cuts = [[(0, quarter)], [top_y], [low_y]]
+
+    cuts = (near_cuts, far_cuts)
+    stack = lambda one, two: jnp.concatenate([one[...], two[...]], axis=0)
+    join = lambda one, two: jnp.concatenate([one[...], two[...]], axis=1)
+    left_spec = pl.BlockSpec((half, length), lambda *_: (0, 0))
+
+    def grad_of(lefts, rights, side, name, done):
+        steps = hidden_here // TILE
+        cols = pl.BlockSpec((length, TILE), lambda s: (0, side * steps + s))
+        terms = lambda refs, kind: (join(*refs[:2]), stack(*refs[2:4]))
+        args = [*lefts, *after(done, *rights)]
+        specs = [left_spec] * 2 + [cols] * 2
+        return grad_call(args, specs, (1, None, terms), cuts[side], name, steps)
+
+    def grad_one(lefts, dps, attns, side, name, done):
+        cols = pl.BlockSpec((length, heads_cols), lambda *_: (0, side))
+        one_dp = pl.BlockSpec((1, length, heads_cols), lambda s: (jnp.minimum(s, 2), 0, 0))
+
+        def terms(refs, kind):
+            if kind == 0:
+                return join(*refs[:2]), jnp.concatenate([refs[4][0], refs[5][0]], axis=0)
+            return join(*refs[2:4]), stack(*refs[6:8])
+
+        args = [*lefts, *after(done, *dps), *attns]
+        specs = [left_spec] * 4 + [one_dp] * 2 + [cols] * 2
+        return grad_call(args, specs, (2, lambda s: s // 3, terms), cuts[side], name, 4)
+
+    w_fc2 = after(hidden, w_fc2)
+    home_fc2, home_fc1, home_one = Home(links), Home(links), Home(links)
+
+    du, fc1b_sum = hidden_back(e, slope, w_fc2, place)
+    du, twin_hidden, twin_h2 = after((), du, twin_hidden, twin_h2)
+
+    twin_du = links.c(du)
+    fc2_args = (e_t, twin_e), (hidden, twin_hidden)
+    far = grad_of(*fc2_args, 1, "fc2_far", ())
+    near = grad_of(*fc2_args, 0, "fc2_near", far)
+    far, near, twin_du = after((), far, near, twin_du)
+
+    home_fc2.first(far, near)
+    mid, da, da_t, second_sums = second_back(
+        after(near, du), w_two, hidden_here, y, e, gains[1]
+    )
+    fc1_args = (h2_t, twin_h2), (du, twin_du)
+    far = grad_of(*fc1_args, 1, "fc1_far", da)
+    near = grad_of(*fc1_args, 0, "fc1_near", far)
+    far, near, home_fc2.x_got, home_fc2.y_got = after(
+        (), far, near, home_fc2.x_got, home_fc2.y_got
+    )
+
+    home_fc1.first(far, near)
+    moved_fc2 = home_fc2.middle()
+    d_heads = heads_back(after((near, moved_fc2), da), w_two, hidden_here)
+    dp_far, q_far, v_far = attend_bwd(qkv, d_heads, lse_rows, 1)
+    dp_near, q_near, v_near = attend_bwd(after(dp_far, qkv), d_heads, lse_rows, 0)
+    dp_far, dp_near, home_fc1.x_got, home_fc1.y_got = after(
+        (), dp_far, dp_near, home_fc1.x_got, home_fc1.y_got
+    )
+
+    moved_fc1 = home_fc1.middle()
+    dp_far, dp_near, moved_fc2, moved_fc1, da_t_far = after(
+        (), dp_far, dp_near, moved_fc2, moved_fc1, da_t[half:]
+    )
+    twin_dp = links.c(jnp.concatenate([dp_far, dp_near], axis=0))
+    twin_da = links.c(da_t_far)
+    home_fc2.second(*moved_fc2)
+    home_fc1.second(*moved_fc1)
+    grad_near, grad_sent_rows, first_sums = first_back(
+        [dp_near, dp_far], w_one, x, mid, gains[0], order_b
+    )
+    twin_dp, twin_da, grad_sent_rows = after(
+        grad_near, twin_dp, twin_da, grad_sent_rows
+    )
+    twin_far, twin_near = twin_dp[:3], twin_dp[3:]
+    lefts, attns = (h1_t, twin_h1, da_t, twin_da), (attn, twin_attn)
+    far = grad_one(lefts, (dp_far, twin_far), attns, 1, "one_far", ())
+    near = grad_one(lefts, (dp_near, twin_near), attns, 0, "one_near", far)
+    lasts = [home_fc2.y_last, home_fc2.x_last, home_fc1.y_last, home_fc1.x_last]
+    far, near, lasts = after((), far, near, lasts)
+    home_fc2.y_last, home_fc2.x_last, home_fc1.y_last, home_fc1.x_last = lasts
+
+    home_one.first(far, near)
+    moved = home_fc2.last(near, True)
+    moved = home_fc1.last(moved, True)
+    out_near, out_sent = layer_out(
+        after(moved, hidden), w_fc2, place, y, outs[1], live, order_b
+    )
+    home_one.x_got, home_one.y_got = after(out_near, home_one.x_got, home_one.y_got)
+    moved_one = home_one.middle()
+    moved_one, grad_sent_rows = after((), moved_one, grad_sent_rows)
+    home_one.second(*moved_one)
+    grad_got = links.x(grad_sent_rows)
+    moved = home_one.last((), False)
+    out_got = links.x(after(moved, out_sent))
+
+    sums = jnp.concatenate(
+        [first_sums[:1], second_sums[:1], first_sums[1:], second_sums[1:]], axis=0
+    )
+    sums = lax.dot_general(
+        sums, order_f, (((1,), (1,)), ((), ())), precision=lax.Precision.HIGHEST
+    )
+
+    def placed(near, far):
+        return jnp.where(t == 0, jnp.concatenate([near, far]), jnp.concatenate([far, near]))
+
+    small = [
+        sums.reshape(-1),
+        placed(q_near[0], q_far[0]),
+        placed(v_near[0], v_far[0]),
+        placed(fc1b_sum[0, :hidden_here], fc1b_sum[0, hidden_here:]),
+    ]
+    small = total_over_all(links, jnp.concatenate(small).reshape(-1, 128)).reshape(-1) * grad_scale
+    sums = small[: 6 * width].reshape(6, width)
+    own = lambda first, size: lax.dynamic_slice_in_dim(small, first + t * size, size, 0)
+
+    g_one = home_one.value((), grad_scale)
+    g_fc2 = home_fc2.value(moved, grad_scale)
+    g_fc1 = home_fc1.value(moved, grad_scale)
+
+    def both_slots(near, got):
+        return jnp.where(t == 0, jnp.stack([near, got]), jnp.stack([got, near]))
+
+    return (
+        both_slots(out_near, out_got),
+        both_slots(grad_near, grad_got).astype(f32),
+        g_one[:, :qkv_cols].reshape(block, 3, heads_cols),
+        own(6 * width, heads_cols),
+        own(6 * width + 2 * heads_cols, heads_cols),
+        g_one[:, qkv_cols:].T,
+        g_fc1,
+        own(6 * width + 4 * heads_cols, hidden_here),
+        g_fc2.T,
+        sums[0:2],
+        sums[2:4],
+        sums[4:6],
+    )
+
+
 def solution(mesh):
+    body = own_slot if fits_own_slot(mesh) else shared_slots
     return jax.shard_map(
-        per_device,
+        body,
         mesh=mesh,
         in_specs=(
             P("wide", "tp", None),

time: 1460 us -> 411 us (0.28)
  waiting for transfers between devices: 1100 us -> 109 us
  Pallas kernels: 0 us -> 180 us
  matrix products: 161 us -> 3.32 us
  other arithmetic: 94 us -> 18.6 us
  starting transfers between devices: 1.32 us -> 49.4 us
  blocking collectives: 40.5 us -> 0 us
  local copies, waits for them, and re-layouts: 45.6 us -> 27.4 us
    reduce_scatter x16 -> x2, waiting for transfers between devices: 647 us -> 0.01 us  [z_sum_apart(): lax.psum_scatter(rows, AXES, scatter_dimension=0, tiled=True, axis_index_...]
    all_gather x16 -> x2, waiting for transfers between devices: 447 us -> 0.02 us  [the longest x1 0.02 us: z_all(): lax.all_gather(rows, AXES, axis=0, tiled=True, axis_index_groups=self.z_g...]
    pallas_call x0 -> x25, Pallas kernels: none -> 180 us  [the longest x3 38.9 us: contract_back(): kernel_call(body, name, (2,), rows_specs + extra_specs + load.specs, [who...]
    dot_general x36 -> x2, matrix products: 161 us -> 3.32 us  [the longest x1 1.94 us: own_slot(): lax.dot_general(sums, order_f, (((1,), (1,)), ((), ())), precision=lax.Pr...]
    ppermute x0 -> x49, waiting for transfers between devices: none -> 101 us  [the longest x15 73.9 us: x(): return lax.ppermute(rows, AXES, self.across)]
    ppermute x0 -> x49, starting transfers between devices: none -> 44.9 us  [the longest x15 16.3 us: x(): return lax.ppermute(rows, AXES, self.across)]
    psum x1 -> x0, blocking collectives: 40.5 us -> none  [per_device(): lax.psum((gain_acc, shift_acc, bias_acc, qvb_pad, fc1b_pad), ('wide', 'tp'))]
    reduce_sum x18 -> x1, other arithmetic: 29 us -> 0.16 us  [value(): return jnp.sum(after(done, self.home).astype(f32), axis=0) * scale]
  transfers between devices with their start and end apart: 32 -> 54, of which waited for: 30 -> 21; matrix products, arithmetic and copies ran while one was open for 16% -> 8% of each run, Pallas kernels for 0% -> 43%
where the time goes in v3:
time: 411 us; the launch traced here: 404 us
  Pallas kernels  180 us (44%)
  waiting for transfers between devices  109 us (27%)
  starting transfers between devices  49.4 us (12%)
  local copies, waits for them, and re-layouts  27.4 us (7%)
  other arithmetic  18.6 us (5%)
  between operations  15.6 us (4%)
    ppermute x15, waiting for transfers between devices, x(): return lax.ppermute(rows, AXES, self.across)  73.9 us
    pallas_call x3, Pallas kernels, contract_back(): kernel_call(body, name, (2,), rows_specs + extra_specs + load.specs, [who...  38.9 us
    pallas_call x6, Pallas kernels, grad_call(): kernel_call(body, name, (steps,), specs, [pl.BlockSpec((size, TILE), lamb...  37 us
    pallas_call x6, Pallas kernels, small_call(): kernel_call(body, name, (1,), [whole(a.shape) for a in args], out_specs,...  19.7 us
    pallas_call x2, Pallas kernels, attend_bwd(): kernel_call(partial(attend_back_kernel, first), 'attend_bwd', (count,), [...  18.9 us
    ppermute x15, starting transfers between devices, x(): return lax.ppermute(rows, AXES, self.across)  16.3 us
    ppermute x11, starting transfers between devices, y(): return lax.ppermute(rows, AXES, self.beside)  14.7 us
    pallas_call x1, Pallas kernels, expand(): kernel_call(body, 'expand', (2 * per,), [whole((length, width)), pl.Block...  13.1 us
  transfers between devices with their start and end apart: 54, of which 21 were waited for; matrix products, arithmetic and copies ran while one was open for 8% of the time, Pallas kernels for 43%

profile of v3, /device:TPU:0, one launch (start us, length us, event | category | flops | bytes accessed | tf_op | source)
XLA Modules:
  0.0 404.0 jit_solution(9173856877646883518)
XLA Ops:
  8.2 5.1 %collective-permute-start.2 = (bf16[64,1536]{1,0:T(8,128)(2,1)S(1)}, bf16[64,1536]{1,0:T(8,128)(2,1)S(1)}, u32[]{:S(2)}, u32[]{:S(2)}) collective-permute-start(bf16[64,1536]{1,0:T(8,128)(2,1)S(1)} %bitcast.58), channel_id=1, source_target_pairs={{8,0},{9,1},{10,2},{11,3},{12,4},{13,5},{14,6},{15,7},{16,8},{17,9... | collective-permute-start | bytes 589832 | tf_op jit(solution)/shard_map/ppermute | solution.py:885
  14.3 2.7 dynamic-slice_bitcast_fusion
  21.2 2.2 fusion.2.order_ref.refs_5_
  23.5 6.5 %collective-permute-done.3 = bf16[64,1536]{1,0:T(8,128)(2,1)S(1)} collective-permute-done((bf16[64,1536]{1,0:T(8,128)(2,1)S(1)}, bf16[64,1536]{1,0:T(8,128)(2,1)S(1)}, u32[]{:S(2)}, u32[]{:S(2)}) %collective-permute-start.3) | collective-permute-done | bytes 196640 | tf_op jit(solution)/shard_map/ppermute | solution.py:885
  36.4 8.3 %collective-permute-done.1 = f32[24,128]{1,0:T(8,128)S(1)} collective-permute-done((f32[24,128]{1,0:T(8,128)S(1)}, f32[24,128]{1,0:T(8,128)S(1)}, u32[]{:S(2)}, u32[]{:S(2)}) %collective-permute-start.1) | collective-permute-done | bytes 12320 | tf_op jit(solution)/shard_map/ppermute | solution.py:908
  46.3 4.5 %enter_cot.1 = (bf16[512,1024]{1,0:T(8,128)(2,1)}, bf16[1024,512]{1,0:T(8,128)(2,1)}) custom-call(bf16[256,1024]{1,0:T(8,128)(2,1)} %get-tuple-element.356.own_ref, bf16[256,1024]{1,0:T(8,128)(2,1)} %get-tuple-element.354.got_ref, bf16[1024,1024]{1,0:T(8,128)(2,1)} %fusion.2.order_ref.refs_5_, f32[1,1024]{1,0:T(1,128)} %broadcast_in_dim.23.live_ref.refs_4_), custom_call_target="tpu_custom_call" | custom-call | flops 1 | bytes 1 | tf_op jit(solution)/shard_map/enter_cot/pallas_call | solution.py:428
  50.8 5.0 %enter.1 = (bf16[512,1024]{1,0:T(8,128)(2,1)}, bf16[512,1024]{1,0:T(8,128)(2,1)}, bf16[1024,512]{1,0:T(8,128)(2,1)}) custom-call(bf16[256,1024]{1,0:T(8,128)(2,1)} %get-tuple-element.379.own_ref, bf16[256,1024]{1,0:T(8,128)(2,1)} %get-tuple-element.355.got_ref, bf16[1024,1024]{1,0:T(8,128)(2,1)} %fusion.2.order_ref.refs_5_, ...), custom_call_target="tpu_custom_call" | custom-call | flops 1 | bytes 1 | tf_op jit(solution)/shard_map/enter/pallas_call | solution.py:406
  63.5 9.4 %collective-permute-done.7.refs_3_.refs_9_ = bf16[128,1536]{1,0:T(8,128)(2,1)S(1)} collective-permute-done((bf16[128,1536]{1,0:T(8,128)(2,1)S(1)}, bf16[128,1536]{1,0:T(8,128)(2,1)S(1)}, u32[]{:S(2)}, u32[]{:S(2)}) %collective-permute-start.7) | collective-permute-done | bytes 393248 | tf_op jit(solution)/shard_map/ppermute | solution.py:908
  72.9 2.2 collective-permute-done.8.refs_4_.refs_10_
  81.9 8.0 %project.1.q_ref.k_ref.v_ref = bf16[3,512,1024]{2,1,0:T(8,128)(2,1)} custom-call(bf16[512,1024]{1,0:T(8,128)(2,1)} %get-tuple-element.176.h_ref, f32[2,1,1536]{2,1,0:T(1,128)} %broadcast_in_dim.22.bias_ref, bf16[256,1536]{1,0:T(8,128)(2,1)} %copy-done.13, bf16[256,1536]{1,0:T(8,128)(2,1)} %copy-done.17, bf16[256,1536]{1,0:T(8,128)(2,1)} %copy-done.18, ...), custom_call_target="tpu_custom_call" | custom-call | flops 1 | bytes 1 | tf_op jit(solution)/shard_map/project/pallas_call | solution.py:458
  89.9 12.4 %attend_fwd.1 = (bf16[512,1024]{1,0:T(8,128)(2,1)}, f32[512,128]{1,0:T(8,128)}) custom-call(bf16[3,512,1024]{2,1,0:T(8,128)(2,1)} %project.1.q_ref.k_ref.v_ref, bf16[3,512,1024]{2,1,0:T(8,128)(2,1)} %project.1.q_ref.k_ref.v_ref, bf16[3,512,1024]{2,1,0:T(8,128)(2,1)} %project.1.q_ref.k_ref.v_ref), custom_call_target="tpu_custom_call" | custom-call | flops 1 | bytes 1 | tf_op jit(solution)/shard_map/attend_fwd/pallas_call | solution.py:498
  102.3 9.5 %collective-permute-done.15.refs_1_.refs_5_ = bf16[256,2560]{1,0:T(8,128)(2,1)S(1)} collective-permute-done((bf16[256,2560]{1,0:T(8,128)(2,1)}, bf16[256,2560]{1,0:T(8,128)(2,1)S(1)}, u32[]{:S(2)}, u32[]{:S(2)}) %collective-permute-start.15) | collective-permute-done | bytes 1310752 | tf_op jit(solution)/shard_map/ppermute | solution.py:908
  115.5 25.8 %collective-permute-done.17.refs_3_.refs_7_ = bf16[128,2560]{1,0:T(8,128)(2,1)S(1)} collective-permute-done((bf16[128,2560]{1,0:T(8,128)(2,1)S(1)}, bf16[128,2560]{1,0:T(8,128)(2,1)S(1)}, u32[]{:S(2)}, u32[]{:S(2)}) %collective-permute-start.17) | collective-permute-done | bytes 655392 | tf_op jit(solution)/shard_map/ppermute | solution.py:908
  141.4 2.6 collective-permute-done.18.refs_4_.refs_8_
  146.9 2.4 collective-permute-done.22.refs_8_.refs_12_
  151.4 6.6 %join_heads.1 = (f32[512,1024]{1,0:T(8,128)}, bf16[512,1024]{1,0:T(8,128)(2,1)}, bf16[1024,512]{1,0:T(8,128)(2,1)}) custom-call(bf16[512,1024]{1,0:T(8,128)(2,1)} %get-tuple-element.208.attn_ref.refs_6_, bf16[512,1024]{1,0:T(8,128)(2,1)} %get-tuple-element.198.x_ref.refs_2_, f32[1,1024]{1,0:T(1,128)} %get-tuple-element.368.bias_ref, ...), custom_call_target="tpu_custom_call" | custom-call | flops 1 | bytes 1 | tf_op jit(solution)/shard_map/join_heads/pallas_call | solution.py:528
  158.0 13.1 %expand.1 = (bf16[512,4096]{1,0:T(8,128)(2,1)}, bf16[512,4096]{1,0:T(8,128)(2,1)}) custom-call(bf16[512,1024]{1,0:T(8,128)(2,1)} %get-tuple-element.214.h_ref, f32[1,4096]{1,0:T(1,128)} %bitcast.73, bf16[256,2560]{1,0:T(8,128)(2,1)} %all-gather.3.cloned.1.call-done.refs_0_.refs_4_, bf16[256,2560]{1,0:T(8,128)(2,1)} %copy-done, bf16[256,2560]{1,0:T(8,128)(2,1)} %copy-done.1, ...), custom_call_target="tpu_custom_call" | custom-call | flops 1 | bytes 1 | tf_op jit(solution)/shard_map/expand/pallas_call | solution.py:558
  172.6 11.3 %hidden_back.1 = (bf16[512,4096]{1,0:T(8,128)(2,1)}, f32[1,4096]{1,0:T(1,128)}) custom-call(s32[17]{0:T(128)} %pad_add_fusion.place_ref.refs_0_, bf16[512,1024]{1,0:T(8,128)(2,1)} %get-tuple-element.180.e_ref.refs_2_, bf16[512,4096]{1,0:T(8,128)(2,1)} %get-tuple-element.217.slope_ref, bf16[16,2,64,2048]{3,2,1,0:T(8,128)(2,1)} %bitcast.52), custom_call_target="tpu_custom_call" | custom-call | flops 1 | bytes 1 | tf_op jit(solution)/shard_map/hidden_back/pallas_call | solution.py:589
  184.1 2.2 fusion.47
  186.4 5.9 %fc2_far.1 = (bf16[256,2048]{1,0:T(8,128)(2,1)}, bf16[128,2048]{1,0:T(8,128)(2,1)}, bf16[128,2048]{1,0:T(8,128)(2,1)}) custom-call(bf16[1024,512]{1,0:T(8,128)(2,1)} %get-tuple-element.178.refs_0_, bf16[512,512]{1,0:T(8,128)(2,1)} %get-tuple-element.353.refs_1_, bf16[512,4096]{1,0:T(8,128)(2,1)} %get-tuple-element.312.refs_2_.refs_1_, ...), custom_call_target="tpu_custom_call" | custom-call | flops 1 | bytes 1 | tf_op jit(solution)/shard_map/fc2_far/pallas_call | solution.py:834
  192.3 5.9 %fc2_near.1 = (bf16[256,2048]{1,0:T(8,128)(2,1)}, bf16[128,2048]{1,0:T(8,128)(2,1)}, bf16[128,2048]{1,0:T(8,128)(2,1)}) custom-call(bf16[1024,512]{1,0:T(8,128)(2,1)} %get-tuple-element.178.refs_0_, bf16[512,512]{1,0:T(8,128)(2,1)} %get-tuple-element.353.refs_1_, bf16[512,4096]{1,0:T(8,128)(2,1)} %get-tuple-element.312.refs_2_.refs_1_, ...), custom_call_target="tpu_custom_call" | custom-call | flops 1 | bytes 1 | tf_op jit(solution)/shard_map/fc2_near/pallas_call | solution.py:834
  198.3 2.1 pad_maximum_fusion.3
  200.4 2.4 collective-permute-start.29
  204.4 13.3 %second_back.1 = (f32[512,1024]{1,0:T(8,128)}, bf16[512,1024]{1,0:T(8,128)(2,1)}, bf16[1024,512]{1,0:T(8,128)(2,1)}, f32[4,1024]{1,0:T(4,128)}) custom-call(bf16[512,4096]{1,0:T(8,128)(2,1)} %get-tuple-element.248.refs_0_.refs_2_, f32[512,1024]{1,0:T(8,128)} %get-tuple-element.241.refs_1_.refs_2_, bf16[512,1024]{1,0:T(8,128)(2,1)} %get-tuple-element.180.e_ref.refs_2_, ...), custom_call_target="tpu_custom_call" | custom-call | flops 1 | bytes 1 | tf_op jit(solution)/shard_map/second_back/pallas_call | solution.py:648
  217.7 6.0 %fc1_far.1 = (bf16[256,2048]{1,0:T(8,128)(2,1)}, bf16[128,2048]{1,0:T(8,128)(2,1)}, bf16[128,2048]{1,0:T(8,128)(2,1)}) custom-call(bf16[1024,512]{1,0:T(8,128)(2,1)} %get-tuple-element.216.refs_0_, bf16[512,512]{1,0:T(8,128)(2,1)} %copy-done.27, bf16[512,4096]{1,0:T(8,128)(2,1)} %get-tuple-element.248.refs_0_.refs_2_, ...), custom_call_target="tpu_custom_call" | custom-call | flops 1 | bytes 1 | tf_op jit(solution)/shard_map/fc1_far/pallas_call | solution.py:834
  223.7 5.9 %fc1_near.1 = (bf16[256,2048]{1,0:T(8,128)(2,1)}, bf16[128,2048]{1,0:T(8,128)(2,1)}, bf16[128,2048]{1,0:T(8,128)(2,1)}) custom-call(bf16[1024,512]{1,0:T(8,128)(2,1)} %get-tuple-element.216.refs_0_, bf16[512,512]{1,0:T(8,128)(2,1)} %copy-done.27, bf16[512,4096]{1,0:T(8,128)(2,1)} %get-tuple-element.248.refs_0_.refs_2_, ...), custom_call_target="tpu_custom_call" | custom-call | flops 1 | bytes 1 | tf_op jit(solution)/shard_map/fc1_near/pallas_call | solution.py:834
  229.7 2.7 pad_maximum_fusion.4
  234.6 3.0 add_mid.3
  237.5 4.9 %heads_back.1.g_ref = bf16[512,1024]{1,0:T(8,128)(2,1)} custom-call(bf16[512,1024]{1,0:T(8,128)(2,1)} %get-tuple-element.263.da_ref, bf16[256,2560]{1,0:T(8,128)(2,1)} %all-gather.3.cloned.1.call-done.refs_0_.refs_4_, bf16[256,2560]{1,0:T(8,128)(2,1)} %copy-done, bf16[256,2560]{1,0:T(8,128)(2,1)} %copy-done.1, bf16[128,2560]{1,0:T(8,128)(2,1)} %copy-done.8, ...), custom_call_target="tpu_custom_call" | custom-call | flops 1 | bytes 1 | tf_op jit(solution)/shard_map/heads_back/pallas_call | solution.py:613
  242.4 9.5 %attend_bwd.2 = (bf16[3,512,512]{2,1,0:T(8,128)(2,1)}, f32[1,512]{1,0:T(1,128)}, f32[1,512]{1,0:T(1,128)}) custom-call(bf16[3,512,1024]{2,1,0:T(8,128)(2,1)} %project.1.q_ref.k_ref.v_ref, bf16[3,512,1024]{2,1,0:T(8,128)(2,1)} %project.1.q_ref.k_ref.v_ref, bf16[3,512,1024]{2,1,0:T(8,128)(2,1)} %project.1.q_ref.k_ref.v_ref, ...), custom_call_target="tpu_custom_call" | custom-call | flops 1 | bytes 1 | tf_op jit(solution)/shard_map/attend_bwd/pallas_call | solution.py:802
  251.9 9.4 %attend_bwd.3 = (bf16[3,512,512]{2,1,0:T(8,128)(2,1)}, f32[1,512]{1,0:T(1,128)}, f32[1,512]{1,0:T(1,128)}) custom-call(bf16[3,512,1024]{2,1,0:T(8,128)(2,1)} %project.1.q_ref.k_ref.v_ref, bf16[3,512,1024]{2,1,0:T(8,128)(2,1)} %project.1.q_ref.k_ref.v_ref, bf16[3,512,1024]{2,1,0:T(8,128)(2,1)} %project.1.q_ref.k_ref.v_ref, ...), custom_call_target="tpu_custom_call" | custom-call | flops 1 | bytes 1 | tf_op jit(solution)/shard_map/attend_bwd/pallas_call | solution.py:802
  261.4 3.2 add_mid.4
  274.1 12.4 %first_back.1 = (bf16[256,1024]{1,0:T(8,128)(2,1)}, bf16[256,1024]{1,0:T(8,128)(2,1)}, f32[2,1024]{1,0:T(2,128)}) custom-call(bf16[3,512,512]{2,1,0:T(8,128)(2,1)} %get-tuple-element.292.refs_0_.refs_4_, bf16[3,512,512]{2,1,0:T(8,128)(2,1)} %get-tuple-element.286.refs_1_.refs_4_, bf16[512,1024]{1,0:T(8,128)(2,1)} %get-tuple-element.198.x_ref.refs_2_, ...), custom_call_target="tpu_custom_call" | custom-call | flops 1 | bytes 1 | tf_op jit(solution)/shard_map/first_back/pallas_call | solution.py:648
  288.5 6.6 %one_far.1 = (bf16[256,2048]{1,0:T(8,128)(2,1)}, bf16[128,2048]{1,0:T(8,128)(2,1)}, bf16[128,2048]{1,0:T(8,128)(2,1)}) custom-call(bf16[1024,512]{1,0:T(8,128)(2,1)} %get-tuple-element.179.refs_0_, bf16[512,512]{1,0:T(8,128)(2,1)} %get-tuple-element.352.refs_1_, bf16[1024,512]{1,0:T(8,128)(2,1)} %get-tuple-element.272.refs_2_, bf16[512,512]{1,0:T(8,128)(2,1)} %copy-done.28, ...), custom_call_target="tpu_custom_call" | custom-call | flops 1 | bytes 1 | tf_op jit(solution)/shard_map/one_far/pallas_call | solution.py:834
  295.1 6.6 %one_near.1 = (bf16[256,2048]{1,0:T(8,128)(2,1)}, bf16[128,2048]{1,0:T(8,128)(2,1)}, bf16[128,2048]{1,0:T(8,128)(2,1)}) custom-call(bf16[1024,512]{1,0:T(8,128)(2,1)} %get-tuple-element.179.refs_0_, bf16[512,512]{1,0:T(8,128)(2,1)} %get-tuple-element.352.refs_1_, bf16[1024,512]{1,0:T(8,128)(2,1)} %get-tuple-element.272.refs_2_, bf16[512,512]{1,0:T(8,128)(2,1)} %copy-done.28, ...), custom_call_target="tpu_custom_call" | custom-call | flops 1 | bytes 1 | tf_op jit(solution)/shard_map/one_near/pallas_call | solution.py:834
  301.8 3.6 add_last.3
  308.2 3.5 add_last.4
  313.9 13.2 %layer_out.1 = (bf16[256,1024]{1,0:T(8,128)(2,1)}, bf16[256,1024]{1,0:T(8,128)(2,1)}) custom-call(s32[17]{0:T(128)} %pad_add_fusion.place_ref.refs_0_, bf16[512,4096]{1,0:T(8,128)(2,1)} %get-tuple-element.312.refs_2_.refs_1_, f32[512,1024]{1,0:T(8,128)} %get-tuple-element.241.refs_1_.refs_2_, f32[1,1024]{1,0:T(1,128)} %get-tuple-element.365.refs_3_, ...), custom_call_target="tpu_custom_call" | custom-call | flops 1 | bytes 1 | tf_op jit(solution)/shard_map/layer_out/pallas_call | solution.py:648
  327.1 4.0 collective-permute-done.39.ry_ref
  333.7 3.0 add_mid.5
  339.2 12.1 %collective-permute-done.45 = f32[96,128]{1,0:T(8,128)S(1)} collective-permute-done((f32[96,128]{1,0:T(8,128)S(1)}, f32[96,128]{1,0:T(8,128)S(1)}, u32[]{:S(2)}, u32[]{:S(2)}) %collective-permute-start.45) | collective-permute-done | bytes 49184 | tf_op jit(solution)/shard_map/ppermute | solution.py:908
  352.6 2.8 collective-permute-done.46
  355.4 3.0 collective-permute-start.47
  358.5 2.6 collective-permute-done.47
  364.7 3.5 add_last.5
  369.5 4.2 %all-to-all-start = ((bf16[4,64,2048]{2,1,0:T(8,128)(2,1)}), bf16[4,64,2048]{2,1,0:T(8,128)(2,1)S(1)}, u32[]{:S(2)}, u32[]{:S(2)}) async-start(bf16[4,64,2048]{2,1,0:T(8,128)(2,1)} %bitcast.54), calls=%async_computation | async-start | bytes 2097152 | tf_op jit(solution)/shard_map/all_to_all | solution.py:899
  378.9 5.2 %collective-permute-done.42 = bf16[256,1024]{1,0:T(8,128)(2,1)S(1)} collective-permute-done((bf16[256,1024]{1,0:T(8,128)(2,1)}, bf16[256,1024]{1,0:T(8,128)(2,1)S(1)}, u32[]{:S(2)}, u32[]{:S(2)}) %collective-permute-start.42) | collective-permute-done | bytes 524320 | tf_op jit(solution)/shard_map/ppermute | solution.py:908
  386.9 8.7 %all-to-all-done = bf16[4,64,2048]{2,1,0:T(8,128)(2,1)S(1)} async-done(((bf16[4,64,2048]{2,1,0:T(8,128)(2,1)}), bf16[4,64,2048]{2,1,0:T(8,128)(2,1)S(1)}, u32[]{:S(2)}, u32[]{:S(2)}) %all-to-all-start) | async-done | bytes 1048608 | tf_op jit(solution)/shard_map/all_to_all | solution.py:899
  (290 shorter events, 79.5 us)
Async XLA Ops:
  7.2 52.3 %all-gather.3.cloned.1.call-start = ((), (), s32[]{:S(2)}) async-start(), calls=%async_computation.3 | async-start | bytes 1638400 | tf_op jit(solution)/shard_map/all_gather | solution.py:903
  8.2 15.3 %collective-permute-start.2 = (bf16[64,1536]{1,0:T(8,128)(2,1)S(1)}, bf16[64,1536]{1,0:T(8,128)(2,1)S(1)}, u32[]{:S(2)}, u32[]{:S(2)}) collective-permute-start(bf16[64,1536]{1,0:T(8,128)(2,1)S(1)} %bitcast.58), channel_id=1, source_target_pairs={{8,0},{9,1},{10,2},{11,3},{12,4},{13,5},{14,6},{15,7},{16,8},{17,9... | collective-permute-start | bytes 589832 | tf_op jit(solution)/shard_map/ppermute | solution.py:885
  13.3 16.7 %collective-permute-start.3 = (bf16[64,1536]{1,0:T(8,128)(2,1)S(1)}, bf16[64,1536]{1,0:T(8,128)(2,1)S(1)}, u32[]{:S(2)}, u32[]{:S(2)}) collective-permute-start(bf16[64,1536]{1,0:T(8,128)(2,1)S(1)} %bitcast.59), channel_id=1, source_target_pairs={{16,0},{17,1},{18,2},{19,3},{20,4},{21,5},{22,6},{23,7},{24,8},{25... | collective-permute-start | bytes 589832 | tf_op jit(solution)/shard_map/ppermute | solution.py:885
  13.3 16.7 %collective-permute-start.4 = (bf16[64,1536]{1,0:T(8,128)(2,1)S(1)}, bf16[64,1536]{1,0:T(8,128)(2,1)S(1)}, u32[]{:S(2)}, u32[]{:S(2)}) collective-permute-start(bf16[64,1536]{1,0:T(8,128)(2,1)S(1)} %bitcast.60), channel_id=1, source_target_pairs={{24,0},{25,1},{26,2},{27,3},{28,4},{29,5},{30,6},{31,7},{0,8},{1,9... | collective-permute-start | bytes 589832 | tf_op jit(solution)/shard_map/ppermute | solution.py:885
  18.0 26.6 %collective-permute-start = (bf16[512,1024]{1,0:T(8,128)(2,1)}, bf16[512,1024]{1,0:T(8,128)(2,1)S(1)}, u32[]{:S(2)}, u32[]{:S(2)}) collective-permute-start(bf16[512,1024]{1,0:T(8,128)(2,1)} %pad_maximum_fusion.1), channel_id=1, source_target_pairs={{1,0},{0,1},{3,2},{2,3},{5,4},{4,5},{7,6},{6,7},{9,8},{8,9},{11,10... | collective-permute-start | bytes 3145736 | tf_op jit(solution)/shard_map/ppermute | solution.py:908
  19.6 25.1 %collective-permute-start.1 = (f32[24,128]{1,0:T(8,128)S(1)}, f32[24,128]{1,0:T(8,128)S(1)}, u32[]{:S(2)}, u32[]{:S(2)}) collective-permute-start(f32[24,128]{1,0:T(8,128)S(1)} %maximum_bitcast_fusion.1), channel_id=1, source_target_pairs={{1,0},{0,1},{3,2},{2,3},{5,4},{4,5},{7,6},{6,7},{9,8},{8,9},{11,10... | collective-permute-start | bytes 36872 | tf_op jit(solution)/shard_map/ppermute | solution.py:908
  20.9 151.6 %all-gather.5.cloned.1.call-start = ((), (), s32[]{:S(2)}) async-start(), calls=%async_computation.4 | async-start | bytes 8650752 | tf_op jit(solution)/shard_map/all_gather | solution.py:1041
  30.0 29.4 %collective-permute-start.5 = (bf16[256,1536]{1,0:T(8,128)(2,1)S(1)}, bf16[256,1536]{1,0:T(8,128)(2,1)S(1)}, u32[]{:S(2)}, u32[]{:S(2)}) collective-permute-start(bf16[256,1536]{1,0:T(8,128)(2,1)S(1)} %constant_dynamic-update-slice_fusion.refs_0_.refs_6_), channel_id=1, source_target_pairs={{1,0},{0,1},{3,2},{2,3},{5,4},{4,5},{7,6},{6,7},{9,8},{8,9},{11,10... | collective-permute-start | bytes 2359304 | tf_op jit(solution)/shard_map/ppermute | solution.py:908
  31.6 27.9 %collective-permute-start.6 = (bf16[256,1536]{1,0:T(8,128)(2,1)S(1)}, bf16[256,1536]{1,0:T(8,128)(2,1)S(1)}, u32[]{:S(2)}, u32[]{:S(2)}) collective-permute-start(bf16[256,1536]{1,0:T(8,128)(2,1)S(1)} %constant_dynamic-update-slice_fusion.refs_0_.refs_6_), channel_id=1, source_target_pairs={{4,0},{5,1},{6,2},{7,3},{0,4},{1,5},{2,6},{3,7},{12,8},{13,9},{14,... | collective-permute-start | bytes 2359304 | tf_op jit(solution)/shard_map/ppermute | solution.py:911
  59.5 319.4 %reduce-scatter.5.cloned.1.call-start = ((), (), s32[]{:S(2)}) async-start(), calls=%async_computation.6 | async-start | bytes 1310720 | tf_op jit(solution)/shard_map/reduce_scatter | solution.py:894
  59.7 15.3 %collective-permute-start.9 = (bf16[256,1536]{1,0:T(8,128)(2,1)S(1)}, bf16[256,1536]{1,0:T(8,128)(2,1)S(1)}, u32[]{:S(2)}, u32[]{:S(2)}) collective-permute-start(bf16[256,1536]{1,0:T(8,128)(2,1)S(1)} %constant_dynamic-update-slice_fusion.refs_0_.refs_6_), channel_id=1, source_target_pairs={{2,0},{3,1},{0,2},{1,3},{6,4},{7,5},{4,6},{5,7},{10,8},{11,9},{8,1... | collective-permute-start | bytes 2359304 | tf_op jit(solution)/shard_map/ppermute | solution.py:914
  59.8 15.3 %collective-permute-start.10 = (bf16[256,1536]{1,0:T(8,128)(2,1)S(1)}, bf16[256,1536]{1,0:T(8,128)(2,1)S(1)}, u32[]{:S(2)}, u32[]{:S(2)}) collective-permute-start(bf16[256,1536]{1,0:T(8,128)(2,1)S(1)} %collective-permute-done.5.refs_1_.refs_7_), channel_id=1, source_target_pairs={{2,0},{3,1},{0,2},{1,3},{6,4},{7,5},{4,6},{5,7},{10,8},{11,9},{8,1... | collective-permute-start | bytes 2359304 | tf_op jit(solution)/shard_map/ppermute | solution.py:914
  60.3 14.8 %collective-permute-start.11 = (bf16[256,1536]{1,0:T(8,128)(2,1)S(1)}, bf16[256,1536]{1,0:T(8,128)(2,1)S(1)}, u32[]{:S(2)}, u32[]{:S(2)}) collective-permute-start(bf16[256,1536]{1,0:T(8,128)(2,1)S(1)} %collective-permute-done.6.refs_2_.refs_8_), channel_id=1, source_target_pairs={{2,0},{3,1},{0,2},{1,3},{6,4},{7,5},{4,6},{5,7},{10,8},{11,9},{8,1... | collective-permute-start | bytes 2359304 | tf_op jit(solution)/shard_map/ppermute | solution.py:914
  60.4 12.4 %collective-permute-start.7 = (bf16[128,1536]{1,0:T(8,128)(2,1)S(1)}, bf16[128,1536]{1,0:T(8,128)(2,1)S(1)}, u32[]{:S(2)}, u32[]{:S(2)}) collective-permute-start(bf16[128,1536]{1,0:T(8,128)(2,1)S(1)} %slice.145), channel_id=1, source_target_pairs={{1,0},{0,1},{3,2},{2,3},{5,4},{4,5},{7,6},{6,7},{9,8},{8,9},{11,10... | collective-permute-start | bytes 1179656 | tf_op jit(solution)/shard_map/ppermute | solution.py:908
  62.0 13.1 %collective-permute-start.8 = (bf16[128,1536]{1,0:T(8,128)(2,1)S(1)}, bf16[128,1536]{1,0:T(8,128)(2,1)S(1)}, u32[]{:S(2)}, u32[]{:S(2)}) collective-permute-start(bf16[128,1536]{1,0:T(8,128)(2,1)S(1)} %slice.146), channel_id=1, source_target_pairs={{4,0},{5,1},{6,2},{7,3},{0,4},{1,5},{2,6},{3,7},{12,8},{13,9},{14,... | collective-permute-start | bytes 1179656 | tf_op jit(solution)/shard_map/ppermute | solution.py:911
  75.1 36.7 %collective-permute-start.15 = (bf16[256,2560]{1,0:T(8,128)(2,1)}, bf16[256,2560]{1,0:T(8,128)(2,1)S(1)}, u32[]{:S(2)}, u32[]{:S(2)}) collective-permute-start(bf16[256,2560]{1,0:T(8,128)(2,1)} %all-gather.3.cloned.1.call-done.refs_0_.refs_4_), channel_id=1, source_target_pairs={{1,0},{0,1},{3,2},{2,3},{5,4},{4,5},{7,6},{6,7},{9,8},{8,9},{11,10... | collective-permute-start | bytes 3932168 | tf_op jit(solution)/shard_map/ppermute | solution.py:908
  76.0 35.9 %collective-permute-start.16 = (bf16[256,2560]{1,0:T(8,128)(2,1)}, bf16[256,2560]{1,0:T(8,128)(2,1)S(1)}, u32[]{:S(2)}, u32[]{:S(2)}) collective-permute-start(bf16[256,2560]{1,0:T(8,128)(2,1)} %all-gather.3.cloned.1.call-done.refs_0_.refs_4_), channel_id=1, source_target_pairs={{4,0},{5,1},{6,2},{7,3},{0,4},{1,5},{2,6},{3,7},{12,8},{13,9},{14,... | collective-permute-start | bytes 3932168 | tf_op jit(solution)/shard_map/ppermute | solution.py:911
  111.9 32.1 %collective-permute-start.19 = (bf16[256,2560]{1,0:T(8,128)(2,1)S(1)}, bf16[256,2560]{1,0:T(8,128)(2,1)S(1)}, u32[]{:S(2)}, u32[]{:S(2)}) collective-permute-start(bf16[256,2560]{1,0:T(8,128)(2,1)S(1)} %copy-done.2), channel_id=1, source_target_pairs={{2,0},{3,1},{0,2},{1,3},{6,4},{7,5},{4,6},{5,7},{10,8},{11,9},{8,1... | collective-permute-start | bytes 3932168 | tf_op jit(solution)/shard_map/ppermute | solution.py:914
  111.9 32.0 %collective-permute-start.20 = (bf16[256,2560]{1,0:T(8,128)(2,1)S(1)}, bf16[256,2560]{1,0:T(8,128)(2,1)S(1)}, u32[]{:S(2)}, u32[]{:S(2)}) collective-permute-start(bf16[256,2560]{1,0:T(8,128)(2,1)S(1)} %collective-permute-done.15.refs_1_.refs_5_), channel_id=1, source_target_pairs={{2,0},{3,1},{0,2},{1,3},{6,4},{7,5},{4,6},{5,7},{10,8},{11,9},{8,1... | collective-permute-start | bytes 3932168 | tf_op jit(solution)/shard_map/ppermute | solution.py:914
  112.4 31.6 %collective-permute-start.21 = (bf16[256,2560]{1,0:T(8,128)(2,1)S(1)}, bf16[256,2560]{1,0:T(8,128)(2,1)S(1)}, u32[]{:S(2)}, u32[]{:S(2)}) collective-permute-start(bf16[256,2560]{1,0:T(8,128)(2,1)S(1)} %collective-permute-done.16.refs_2_.refs_6_), channel_id=1, source_target_pairs={{2,0},{3,1},{0,2},{1,3},{6,4},{7,5},{4,6},{5,7},{10,8},{11,9},{8,1... | collective-permute-start | bytes 3932168 | tf_op jit(solution)/shard_map/ppermute | solution.py:914
  112.6 28.7 %collective-permute-start.17 = (bf16[128,2560]{1,0:T(8,128)(2,1)S(1)}, bf16[128,2560]{1,0:T(8,128)(2,1)S(1)}, u32[]{:S(2)}, u32[]{:S(2)}) collective-permute-start(bf16[128,2560]{1,0:T(8,128)(2,1)S(1)} %slice.150), channel_id=1, source_target_pairs={{1,0},{0,1},{3,2},{2,3},{5,4},{4,5},{7,6},{6,7},{9,8},{8,9},{11,10... | collective-permute-start | bytes 1966088 | tf_op jit(solution)/shard_map/ppermute | solution.py:908
  113.5 30.4 %collective-permute-start.18 = (bf16[128,2560]{1,0:T(8,128)(2,1)S(1)}, bf16[128,2560]{1,0:T(8,128)(2,1)S(1)}, u32[]{:S(2)}, u32[]{:S(2)}) collective-permute-start(bf16[128,2560]{1,0:T(8,128)(2,1)S(1)} %slice.151), channel_id=1, source_target_pairs={{4,0},{5,1},{6,2},{7,3},{0,4},{1,5},{2,6},{3,7},{12,8},{13,9},{14,... | collective-permute-start | bytes 1966088 | tf_op jit(solution)/shard_map/ppermute | solution.py:911
  145.1 5.0 %collective-permute-start.24 = (bf16[512,1024]{1,0:T(8,128)(2,1)S(1)}, bf16[512,1024]{1,0:T(8,128)(2,1)S(1)}, u32[]{:S(2)}, u32[]{:S(2)}) collective-permute-start(bf16[512,1024]{1,0:T(8,128)(2,1)S(1)} %copy-done.12), channel_id=1, source_target_pairs={{2,0},{3,1},{0,2},{1,3},{6,4},{7,5},{4,6},{5,7},{10,8},{11,9},{8,1... | collective-permute-start | bytes 3145736 | tf_op jit(solution)/shard_map/ppermute | solution.py:914
  171.1 12.8 %collective-permute-start.25 = (bf16[512,4096]{1,0:T(8,128)(2,1)}, bf16[512,4096]{1,0:T(8,128)(2,1)}, u32[]{:S(2)}, u32[]{:S(2)}) collective-permute-start(bf16[512,4096]{1,0:T(8,128)(2,1)} %get-tuple-element.312.refs_2_.refs_1_), channel_id=1, source_target_pairs={{2,0},{3,1},{0,2},{1,3},{6,4},{7,5},{4,6},{5,7},{10,8},{11,9},{8,1... | collective-permute-start | bytes 12582920 | tf_op jit(solution)/shard_map/ppermute | solution.py:914
  171.4 12.4 %collective-permute-start.26 = (bf16[512,512]{1,0:T(8,128)(2,1)S(1)}, bf16[512,512]{1,0:T(8,128)(2,1)S(1)}, u32[]{:S(2)}, u32[]{:S(2)}) collective-permute-start(bf16[512,512]{1,0:T(8,128)(2,1)S(1)} %slice.153), channel_id=1, source_target_pairs={{2,0},{3,1},{0,2},{1,3},{6,4},{7,5},{4,6},{5,7},{10,8},{11,9},{8,1... | collective-permute-start | bytes 1572872 | tf_op jit(solution)/shard_map/ppermute | solution.py:914
  183.9 14.4 %collective-permute-start.27 = (bf16[512,4096]{1,0:T(8,128)(2,1)}, bf16[512,4096]{1,0:T(8,128)(2,1)}, u32[]{:S(2)}, u32[]{:S(2)}) collective-permute-start(bf16[512,4096]{1,0:T(8,128)(2,1)} %get-tuple-element.248.refs_0_.refs_2_), channel_id=1, source_target_pairs={{2,0},{3,1},{0,2},{1,3},{6,4},{7,5},{4,6},{5,7},{10,8},{11,9},{8,1... | collective-permute-start | bytes 12582920 | tf_op jit(solution)/shard_map/ppermute | solution.py:914
  200.4 29.2 %collective-permute-start.29 = (bf16[256,2048]{1,0:T(8,128)(2,1)}, bf16[256,2048]{1,0:T(8,128)(2,1)S(1)}, u32[]{:S(2)}, u32[]{:S(2)}) collective-permute-start(bf16[256,2048]{1,0:T(8,128)(2,1)} %pad_maximum_fusion.3), channel_id=1, source_target_pairs={{4,0},{5,1},{6,2},{7,3},{0,4},{1,5},{2,6},{3,7},{12,8},{13,9},{14,... | collective-permute-start | bytes 3145736 | tf_op jit(solution)/shard_map/ppermute | solution.py:911
  202.8 26.8 %collective-permute-start.28 = (bf16[256,2048]{1,0:T(8,128)(2,1)}, bf16[256,2048]{1,0:T(8,128)(2,1)S(1)}, u32[]{:S(2)}, u32[]{:S(2)}) collective-permute-start(bf16[256,2048]{1,0:T(8,128)(2,1)} %get-tuple-element.253), channel_id=1, source_target_pairs={{1,0},{0,1},{3,2},{2,3},{5,4},{4,5},{7,6},{6,7},{9,8},{8,9},{11,10... | collective-permute-start | bytes 3145736 | tf_op jit(solution)/shard_map/ppermute | solution.py:908
  232.4 29.0 %collective-permute-start.31 = (bf16[256,2048]{1,0:T(8,128)(2,1)}, bf16[256,2048]{1,0:T(8,128)(2,1)}, u32[]{:S(2)}, u32[]{:S(2)}) collective-permute-start(bf16[256,2048]{1,0:T(8,128)(2,1)} %pad_maximum_fusion.4), channel_id=1, source_target_pairs={{4,0},{5,1},{6,2},{7,3},{0,4},{1,5},{2,6},{3,7},{12,8},{13,9},{14,... | collective-permute-start | bytes 3145736 | tf_op jit(solution)/shard_map/ppermute | solution.py:911
  232.4 29.0 %collective-permute-start.30 = (bf16[256,2048]{1,0:T(8,128)(2,1)}, bf16[256,2048]{1,0:T(8,128)(2,1)}, u32[]{:S(2)}, u32[]{:S(2)}) collective-permute-start(bf16[256,2048]{1,0:T(8,128)(2,1)} %get-tuple-element.268), channel_id=1, source_target_pairs={{1,0},{0,1},{3,2},{2,3},{5,4},{4,5},{7,6},{6,7},{9,8},{8,9},{11,10... | collective-permute-start | bytes 3145736 | tf_op jit(solution)/shard_map/ppermute | solution.py:908
  266.5 20.0 %collective-permute-start.32 = (bf16[6,512,512]{2,1,0:T(8,128)(2,1)}, bf16[6,512,512]{2,1,0:T(8,128)(2,1)S(1)}, u32[]{:S(2)}, u32[]{:S(2)}) collective-permute-start(bf16[6,512,512]{2,1,0:T(8,128)(2,1)} %pad_maximum_fusion), channel_id=1, source_target_pairs={{2,0},{3,1},{0,2},{1,3},{6,4},{7,5},{4,6},{5,7},{10,8},{11,9},{8,1... | collective-permute-start | bytes 9437192 | tf_op jit(solution)/shard_map/ppermute | solution.py:914
  266.5 6.0 %collective-permute-start.33 = (bf16[512,512]{1,0:T(8,128)(2,1)S(1)}, bf16[512,512]{1,0:T(8,128)(2,1)S(1)}, u32[]{:S(2)}, u32[]{:S(2)}) collective-permute-start(bf16[512,512]{1,0:T(8,128)(2,1)S(1)} %copy-done.36), channel_id=1, source_target_pairs={{2,0},{3,1},{0,2},{1,3},{6,4},{7,5},{4,6},{5,7},{10,8},{11,9},{8,1... | collective-permute-start | bytes 1572872 | tf_op jit(solution)/shard_map/ppermute | solution.py:914
  267.0 34.7 %collective-permute-start.34 = (bf16[128,2048]{1,0:T(8,128)(2,1)}, bf16[128,2048]{1,0:T(8,128)(2,1)}, u32[]{:S(2)}, u32[]{:S(2)}) collective-permute-start(bf16[128,2048]{1,0:T(8,128)(2,1)} %get-tuple-element.297), channel_id=1, source_target_pairs={{4,0},{5,1},{6,2},{7,3},{0,4},{1,5},{2,6},{3,7},{12,8},{13,9},{14,... | collective-permute-start | bytes 1572872 | tf_op jit(solution)/shard_map/ppermute | solution.py:911
  268.9 32.8 %collective-permute-start.35 = (bf16[128,2048]{1,0:T(8,128)(2,1)}, bf16[128,2048]{1,0:T(8,128)(2,1)}, u32[]{:S(2)}, u32[]{:S(2)}) collective-permute-start(bf16[128,2048]{1,0:T(8,128)(2,1)} %get-tuple-element.298), channel_id=1, source_target_pairs={{1,0},{0,1},{3,2},{2,3},{5,4},{4,5},{7,6},{6,7},{9,8},{8,9},{11,10... | collective-permute-start | bytes 1572872 | tf_op jit(solution)/shard_map/ppermute | solution.py:908
  270.5 31.2 %collective-permute-start.36 = (bf16[128,2048]{1,0:T(8,128)(2,1)}, bf16[128,2048]{1,0:T(8,128)(2,1)}, u32[]{:S(2)}, u32[]{:S(2)}) collective-permute-start(bf16[128,2048]{1,0:T(8,128)(2,1)} %get-tuple-element.299), channel_id=1, source_target_pairs={{4,0},{5,1},{6,2},{7,3},{0,4},{1,5},{2,6},{3,7},{12,8},{13,9},{14,... | collective-permute-start | bytes 1572872 | tf_op jit(solution)/shard_map/ppermute | solution.py:911
  272.5 29.2 %collective-permute-start.37 = (bf16[128,2048]{1,0:T(8,128)(2,1)}, bf16[128,2048]{1,0:T(8,128)(2,1)}, u32[]{:S(2)}, u32[]{:S(2)}) collective-permute-start(bf16[128,2048]{1,0:T(8,128)(2,1)} %get-tuple-element.300), channel_id=1, source_target_pairs={{1,0},{0,1},{3,2},{2,3},{5,4},{4,5},{7,6},{6,7},{9,8},{8,9},{11,10... | collective-permute-start | bytes 1572872 | tf_op jit(solution)/shard_map/ppermute | solution.py:908
  305.4 73.5 %reduce-scatter.3.cloned.1.call-start = ((), (), s32[]{:S(2)}) async-start(), calls=%async_computation.5 | async-start | bytes 1310720 | tf_op jit(solution)/shard_map/reduce_scatter | solution.py:894
  305.6 25.5 %collective-permute-start.39 = (bf16[256,2048]{1,0:T(8,128)(2,1)S(1)}, bf16[256,2048]{1,0:T(8,128)(2,1)S(1)}, u32[]{:S(2)}, u32[]{:S(2)}) collective-permute-start(bf16[256,2048]{1,0:T(8,128)(2,1)S(1)} %pad_maximum_fusion.5), channel_id=1, source_target_pairs={{4,0},{5,1},{6,2},{7,3},{0,4},{1,5},{2,6},{3,7},{12,8},{13,9},{14,... | collective-permute-start | bytes 3145736 | tf_op jit(solution)/shard_map/ppermute | solution.py:911
  307.7 25.1 %collective-permute-start.38 = (bf16[256,2048]{1,0:T(8,128)(2,1)}, bf16[256,2048]{1,0:T(8,128)(2,1)S(1)}, u32[]{:S(2)}, u32[]{:S(2)}) collective-permute-start(bf16[256,2048]{1,0:T(8,128)(2,1)} %get-tuple-element.315), channel_id=1, source_target_pairs={{1,0},{0,1},{3,2},{2,3},{5,4},{4,5},{7,6},{6,7},{9,8},{8,9},{11,10... | collective-permute-start | bytes 3145736 | tf_op jit(solution)/shard_map/ppermute | solution.py:908
  313.8 23.7 %collective-permute-start.44 = (f32[96,128]{1,0:T(8,128)S(1)}, f32[96,128]{1,0:T(8,128)S(1)}, u32[]{:S(2)}, u32[]{:S(2)}) collective-permute-start(f32[96,128]{1,0:T(8,128)S(1)} %maximum_bitcast_fusion), channel_id=1, source_target_pairs={{2,0},{3,1},{0,2},{1,3},{6,4},{7,5},{4,6},{5,7},{10,8},{11,9},{8,1... | collective-permute-start | bytes 147464 | tf_op jit(solution)/shard_map/ppermute | solution.py:914
  336.7 26.5 %collective-permute-start.40 = (bf16[128,2048]{1,0:T(8,128)(2,1)}, bf16[128,2048]{1,0:T(8,128)(2,1)S(1)}, u32[]{:S(2)}, u32[]{:S(2)}) collective-permute-start(bf16[128,2048]{1,0:T(8,128)(2,1)} %get-tuple-element.323), channel_id=1, source_target_pairs={{4,0},{5,1},{6,2},{7,3},{0,4},{1,5},{2,6},{3,7},{12,8},{13,9},{14,... | collective-permute-start | bytes 1572872 | tf_op jit(solution)/shard_map/ppermute | solution.py:911
  337.1 26.0 %collective-permute-start.41 = (bf16[128,2048]{1,0:T(8,128)(2,1)}, bf16[128,2048]{1,0:T(8,128)(2,1)S(1)}, u32[]{:S(2)}, u32[]{:S(2)}) collective-permute-start(bf16[128,2048]{1,0:T(8,128)(2,1)} %get-tuple-element.324), channel_id=1, source_target_pairs={{1,0},{0,1},{3,2},{2,3},{5,4},{4,5},{7,6},{6,7},{9,8},{8,9},{11,10... | collective-permute-start | bytes 1572872 | tf_op jit(solution)/shard_map/ppermute | solution.py:908
  337.5 13.7 %collective-permute-start.45 = (f32[96,128]{1,0:T(8,128)S(1)}, f32[96,128]{1,0:T(8,128)S(1)}, u32[]{:S(2)}, u32[]{:S(2)}) collective-permute-start(f32[96,128]{1,0:T(8,128)S(1)} %fusion.45), channel_id=1, source_target_pairs={{1,0},{0,1},{3,2},{2,3},{5,4},{4,5},{7,6},{6,7},{9,8},{8,9},{11,10... | collective-permute-start | bytes 147464 | tf_op jit(solution)/shard_map/ppermute | solution.py:908
  355.4 5.6 %collective-permute-start.47 = (f32[96,128]{1,0:T(8,128)S(1)}, f32[96,128]{1,0:T(8,128)S(1)}, u32[]{:S(2)}, u32[]{:S(2)}) collective-permute-start(f32[96,128]{1,0:T(8,128)S(1)} %add.173), channel_id=1, source_target_pairs={{8,0},{9,1},{10,2},{11,3},{12,4},{13,5},{14,6},{15,7},{0,8},{1,9},... | collective-permute-start | bytes 147464 | tf_op jit(solution)/shard_map/ppermute | solution.py:918
  361.1 8.4 %collective-permute-start.48 = (f32[96,128]{1,0:T(8,128)S(1)}, f32[96,128]{1,0:T(8,128)S(1)}, u32[]{:S(2)}, u32[]{:S(2)}) collective-permute-start(f32[96,128]{1,0:T(8,128)S(1)} %add.174), channel_id=1, source_target_pairs={{16,0},{17,1},{18,2},{19,3},{20,4},{21,5},{22,6},{23,7},{24,8},{25... | collective-permute-start | bytes 147464 | tf_op jit(solution)/shard_map/ppermute | solution.py:918
  362.3 15.1 %collective-permute-start.43 = (bf16[256,1024]{1,0:T(8,128)(2,1)}, bf16[256,1024]{1,0:T(8,128)(2,1)S(1)}, u32[]{:S(2)}, u32[]{:S(2)}) collective-permute-start(bf16[256,1024]{1,0:T(8,128)(2,1)} %get-tuple-element.328), channel_id=1, source_target_pairs={{1,0},{0,1},{3,2},{2,3},{5,4},{4,5},{7,6},{6,7},{9,8},{8,9},{11,10... | collective-permute-start | bytes 1572872 | tf_op jit(solution)/shard_map/ppermute | solution.py:908
  368.3 15.9 %collective-permute-start.42 = (bf16[256,1024]{1,0:T(8,128)(2,1)}, bf16[256,1024]{1,0:T(8,128)(2,1)S(1)}, u32[]{:S(2)}, u32[]{:S(2)}) collective-permute-start(bf16[256,1024]{1,0:T(8,128)(2,1)} %get-tuple-element.327), channel_id=1, source_target_pairs={{1,0},{0,1},{3,2},{2,3},{5,4},{4,5},{7,6},{6,7},{9,8},{8,9},{11,10... | collective-permute-start | bytes 1572872 | tf_op jit(solution)/shard_map/ppermute | solution.py:908
  369.5 26.1 %all-to-all-start = ((bf16[4,64,2048]{2,1,0:T(8,128)(2,1)}), bf16[4,64,2048]{2,1,0:T(8,128)(2,1)S(1)}, u32[]{:S(2)}, u32[]{:S(2)}) async-start(bf16[4,64,2048]{2,1,0:T(8,128)(2,1)} %bitcast.54), calls=%async_computation | async-start | bytes 2097152 | tf_op jit(solution)/shard_map/all_to_all | solution.py:899
  (69 other events, 527.4 us)
Sparse Core Ops, SparseCore 0:
  21.1 33.1 all-gather.2
  59.6 98.9 all-gather.4
  305.5 27.4 reduce-scatter.4
  335.3 26.6 reduce-scatter.2

commit v4 on v3

--- a/solution.py
+++ b/solution.py
@@ -269,7 +269,8 @@
 AXES = ("wide", "tp")
 PAIR = 128
 TILE = 512
-VMEM_MIB = 60
+MIB = 1024 * 1024
+GRANT = {"project": 60, "hidden_back": 60, "heads_back": 60, "layer_out": 60}
 WIDE = 1024
 bf16 = jnp.bfloat16
 f32 = jnp.float32
@@ -291,7 +292,7 @@
     )
 
 
-def kernel_call(body, name, grid, in_specs, out_specs, out_shape, scratch=(), scalars=0, vmem=VMEM_MIB):
+def kernel_call(body, name, grid, in_specs, out_specs, out_shape, scratch=(), scalars=0):
     return pl.pallas_call(
         body,
         grid_spec=pltpu.PrefetchScalarGridSpec(
@@ -302,7 +303,7 @@
             scratch_shapes=list(scratch),
         ),
         out_shape=out_shape,
-        compiler_params=pltpu.CompilerParams(vmem_limit_bytes=vmem * 1024 * 1024),
+        compiler_params=pltpu.CompilerParams(vmem_limit_bytes=GRANT.get(name, 60) * MIB),
         cost_estimate=pl.CostEstimate(flops=1, bytes_accessed=1, transcendentals=0),
         name=name,
     )
@@ -329,25 +330,27 @@
 
 
 class Pieces:
-    def __init__(self, pieces, columns, first=0):
+    def __init__(self, pieces, columns, first=0, tile=WIDE):
         self.pieces, self.columns, self.first = pieces, columns, first
+        self.tile = min(tile, columns)
+        self.tiles = columns // self.tile
         self.args = list(pieces)
         self.specs = [pl.BlockSpec(memory_space=pl.ANY)] * len(pieces)
         rows = sum(pieces[i].shape[0] for i in NEAR)
         self.scratch = [
             pltpu.VMEM((2, rows, columns), bf16),
-            pltpu.SemaphoreType.DMA((len(pieces),)),
+            pltpu.SemaphoreType.DMA((self.tiles, len(pieces))),
         ]
 
-    def copies(self, refs, side, w_ref, sems):
+    def copies(self, refs, side, tile, w_ref, sems):
         at, found = 0, []
         for index in FAR if side else NEAR:
             rows = self.pieces[index].shape[0]
             found.append(
                 pltpu.make_async_copy(
-                    refs[index].at[:, pl.ds(self.first, self.columns)],
-                    w_ref.at[side, pl.ds(at, rows)],
-                    sems.at[index],
+                    refs[index].at[:, pl.ds(self.first + tile * self.tile, self.tile)],
+                    w_ref.at[side, pl.ds(at, rows), pl.ds(tile * self.tile, self.tile)],
+                    sems.at[tile, index],
                 )
             )
             at += rows
@@ -355,37 +358,26 @@
 
     def start(self, refs, w_ref, sems):
         for side in range(2):
-            for copy in self.copies(refs, side, w_ref, sems):
-                copy.start()
-
-    def wait(self, refs, side, w_ref, sems):
-        for copy in self.copies(refs, side, w_ref, sems):
+            for tile in range(self.tiles):
+                for copy in self.copies(refs, side, tile, w_ref, sems):
+                    copy.start()
+
+    def wait(self, refs, side, tile, w_ref, sems):
+        for copy in self.copies(refs, side, tile, w_ref, sems):
             copy.wait()
 
-
-class Gathered:
-    def __init__(self, weights):
-        self.wide, _, self.rows, self.columns = weights.shape
-        self.args = [weights]
-        self.specs = [pl.BlockSpec(memory_space=pl.ANY)]
-        self.scratch = [
-            pltpu.VMEM((2, self.wide * self.rows, self.columns), bf16),
-            pltpu.SemaphoreType.DMA((2, self.wide)),
-        ]
-
-    def copies(self, refs, side, w_ref, sems):
-        place_ref, all_ref = refs
-        return [
-            pltpu.make_async_copy(
-                all_ref.at[place_ref[1 + j], place_ref[0] ^ side],
-                w_ref.at[side, pl.ds(j * self.rows, self.rows)],
-                sems.at[side, j],
-            )
-            for j in range(self.wide)
-        ]
-
-    start = Pieces.start
-    wait = Pieces.wait
+    def get(self, refs, side, tile, w_ref, sems):
+        self.wait(refs, side, tile, w_ref, sems)
+        return w_ref[side, :, pl.ds(tile * self.tile, self.tile)]
+
+    def each_step(self, step, refs, w_ref, sems, work):
+        pl.when(step == 0)(lambda: self.start(refs, w_ref, sems))
+        for side in range(2):
+            for tile in range(self.tiles):
+
+                @pl.when(step == side * self.tiles + tile)
+                def _():
+                    work(side, tile, self.get(refs, side, tile, w_ref, sems))
 
 
 def enter_kernel(own_ref, got_ref, order_ref, gain_ref, shift_ref, x_ref, h_ref, ht_ref):
@@ -437,33 +429,28 @@
 
 def project(h, pieces, biases):
     length, width = h.shape
-    cols = pieces[0].shape[1]
-    each = cols // 3
-    q_scale = 1.0 / math.sqrt(HEAD_DIM)
-    load = Pieces(pieces, cols)
+    each = pieces[0].shape[1] // 3
+    load = Pieces(pieces, 3 * each, 0, each)
+    scales = (1.0 / math.sqrt(HEAD_DIM), None, None)
 
     def body(h_ref, bias_ref, *refs):
-        refs, out_ref, w_ref, sems = refs[:-3], *refs[-3:]
-        pl.when(pl.program_id(0) == 0)(lambda: load.start(refs, w_ref, sems))
-        for side in range(2):
-
-            @pl.when(pl.program_id(0) == side)
-            def _():
-                load.wait(refs, side, w_ref, sems)
-                acc = nn_dot(h_ref[...], w_ref[side]) + bias_ref[0]
-                out_ref[0] = (acc[:, :each] * q_scale).astype(bf16)
-                out_ref[1] = acc[:, each : 2 * each].astype(bf16)
-                out_ref[2] = acc[:, 2 * each :].astype(bf16)
+        refs, (out_ref, w_ref, sems) = refs[:-3], refs[-3:]
+
+        def work(side, tile, weight):
+            acc = nn_dot(h_ref[...], weight) + bias_ref[0]
+            out_ref[0] = (acc if scales[tile] is None else acc * scales[tile]).astype(bf16)
+
+        load.each_step(pl.program_id(0), refs, w_ref, sems, work)
 
     return kernel_call(
         body,
         "project",
-        (2,),
-        [whole((length, width)), pl.BlockSpec((1, 1, cols), lambda s: (s, 0, 0))] + load.specs,
-        pl.BlockSpec((3, length, each), lambda s: (0, 0, s)),
+        (6,),
+        [whole((length, width)), pl.BlockSpec((1, 1, each), lambda s: (s // 3, 0, s % 3))]
+        + load.specs,
+        pl.BlockSpec((1, length, each), lambda s: (s % 3, 0, s // 3)),
         array(3, length, width),
         load.scratch,
-        vmem=VMEM_MIB,
     )(h, biases, *load.args)
 
 
@@ -512,8 +499,8 @@
     def body(attn_ref, x_ref, bias_ref, gain_ref, shift_ref, *refs):
         refs, (y_ref, h_ref, ht_ref, w_ref, sems) = refs[:-5], refs[-5:]
         load.start(refs, w_ref, sems)
-        load.wait(refs, 0, w_ref, sems)
-        load.wait(refs, 1, w_ref, sems)
+        load.wait(refs, 0, 0, w_ref, sems)
+        load.wait(refs, 1, 0, w_ref, sems)
         half = length // 2
         for part in range(2):
             here = pl.ds(part * half, half)
@@ -538,65 +525,58 @@
 
 def expand(h, pieces, bias, hidden):
     length, width = h.shape
-    per = hidden // WIDE
     load = Pieces(pieces, hidden)
 
     def body(h_ref, bias_ref, *refs):
         refs, (g_ref, slope_ref, w_ref, sems) = refs[:-4], refs[-4:]
-        step = pl.program_id(0)
-        pl.when(step == 0)(lambda: load.start(refs, w_ref, sems))
-        for side in range(2):
-            pl.when(step == side * per)(partial(load.wait, refs, side, w_ref, sems))
-        at = pl.ds(pl.multiple_of(step % per * WIDE, WIDE), WIDE)
-        pre = nn_dot(h_ref[...], w_ref[step // per, :, at]) + bias_ref[...]
-        cdf = 0.5 * (1.0 + lax.erf(pre * root_half))
-        g_ref[...] = (pre * cdf).astype(bf16)
-        density = jnp.exp(-0.5 * pre * pre) * inv_root_two_pi
-        slope_ref[...] = (cdf + pre * density).astype(bf16)
+
+        def work(side, tile, weight):
+            pre = nn_dot(h_ref[...], weight) + bias_ref[...]
+            cdf = 0.5 * (1.0 + lax.erf(pre * root_half))
+            g_ref[...] = (pre * cdf).astype(bf16)
+            density = jnp.exp(-0.5 * pre * pre) * inv_root_two_pi
+            slope_ref[...] = (cdf + pre * density).astype(bf16)
+
+        load.each_step(pl.program_id(0), refs, w_ref, sems, work)
 
     block = pl.BlockSpec((length, WIDE), lambda s: (0, s))
     return kernel_call(
         body,
         "expand",
-        (2 * per,),
+        (2 * load.tiles,),
         [whole((length, width)), pl.BlockSpec((1, WIDE), lambda s: (0, s))] + load.specs,
         [block] * 2,
         [array(length, 2 * hidden)] * 2,
         load.scratch,
-        vmem=VMEM_MIB,
     )(h, bias, *load.args)
 
 
-def hidden_back(e, slope, weights, place):
+def hidden_back(e, slope, pieces):
     length, width = e.shape
-    hidden = weights.shape[3]
-    per = hidden // WIDE
-    load = Gathered(weights)
-
-    def body(place_ref, e_ref, slope_ref, all_ref, du_ref, sum_ref, w_ref, sems):
-        refs = (place_ref, all_ref)
-        step = pl.program_id(0)
-        pl.when(step == 0)(lambda: load.start(refs, w_ref, sems))
-        for side in range(2):
-            pl.when(step == side * per)(partial(load.wait, refs, side, w_ref, sems))
-        at = pl.ds(pl.multiple_of(step % per * WIDE, WIDE), WIDE)
-        du = nn_dot(e_ref[...], w_ref[step // per, :, at]) * slope_ref[...].astype(f32)
-        du_ref[...] = du.astype(bf16)
-        sum_ref[...] = jnp.sum(du, axis=0, keepdims=True)
-
-    block = pl.BlockSpec((length, WIDE), lambda s, *_: (0, s))
-    row = pl.BlockSpec((1, WIDE), lambda s, *_: (0, s))
+    hidden = pieces[0].shape[1]
+    load = Pieces(pieces, hidden)
+
+    def body(e_ref, slope_ref, *refs):
+        refs, (du_ref, sum_ref, w_ref, sems) = refs[:-4], refs[-4:]
+
+        def work(side, tile, weight):
+            du = nn_dot(e_ref[...], weight) * slope_ref[...].astype(f32)
+            du_ref[...] = du.astype(bf16)
+            sum_ref[...] = jnp.sum(du, axis=0, keepdims=True)
+
+        load.each_step(pl.program_id(0), refs, w_ref, sems, work)
+
+    block = pl.BlockSpec((length, WIDE), lambda s: (0, s))
+    row = pl.BlockSpec((1, WIDE), lambda s: (0, s))
     return kernel_call(
         body,
         "hidden_back",
-        (2 * per,),
+        (2 * load.tiles,),
         [whole((length, width)), block] + load.specs,
         [block, row],
         [array(length, 2 * hidden), array(1, 2 * hidden, dtype=f32)],
         load.scratch,
-        scalars=1,
-        vmem=VMEM_MIB,
-    )(place, e, slope, weights)
+    )(e, slope, *load.args)
 
 
 def heads_back(da, pieces, first):
@@ -607,7 +587,7 @@
         refs, (out_ref, w_ref, sems) = refs[:-3], refs[-3:]
         load.start(refs, w_ref, sems)
         for side in range(2):
-            load.wait(refs, side, w_ref, sems)
+            load.wait(refs, side, 0, w_ref, sems)
             out_ref[:, pl.ds(side * TILE, TILE)] = nn_dot(da_ref[...], w_ref[side]).astype(bf16)
 
     return kernel_call(
@@ -618,54 +598,60 @@
         whole((length, 2 * TILE)),
         array(length, 2 * TILE),
         load.scratch,
-        vmem=VMEM_MIB,
     )(da, *load.args)
 
 
-def contract_back(rows, rows_specs, left_of, load, extras, extra_specs, finish, name, outs, place=()):
+def contract_back(rows, rows_specs, left_of, load, extras, finish, name, outs):
     count = len(extras)
     length, width = extras[0].shape
 
     def body(*refs):
-        place_refs, refs = refs[: len(place)], refs[len(place) :]
         rows_refs, refs = refs[: len(rows)], refs[len(rows) :]
         extra_refs, refs = refs[:count], refs[count:]
-        w_refs, refs = place_refs + refs[: len(load.args)], refs[len(load.args) :]
-        out_refs, (w_ref, sems, acc_ref) = refs[:-3], refs[-3:]
-
-        @pl.when(pl.program_id(0) == 0)
-        def _():
-            load.start(w_refs, w_ref, sems)
-            load.wait(w_refs, 0, w_ref, sems)
-            acc_ref[...] = nt_dot(left_of(rows_refs, 0), w_ref[0])
-
-        @pl.when(pl.program_id(0) == 1)
-        def _():
-            load.wait(w_refs, 1, w_ref, sems)
-            acc_ref[...] += nt_dot(left_of(rows_refs, 1), w_ref[1])
-            finish(acc_ref, extra_refs, out_refs)
+        w_refs, refs = refs[: len(load.args)], refs[len(load.args) :]
+        out_refs, refs = refs[: len(outs)], refs[len(outs) :]
+        w_ref, sems, acc_ref, extra_sems = refs[:4]
+        held = refs[4:]
+        copies = [
+            pltpu.make_async_copy(source, target, extra_sems.at[i])
+            for i, (source, target) in enumerate(zip(extra_refs, held))
+        ]
+
+        def work(side, tile, weight):
+            term = nt_dot(left_of(rows_refs), weight)
+            if side == 0 and tile == 0:
+                for copy in copies:
+                    copy.start()
+                acc_ref[...] = term
+            else:
+                acc_ref[...] += term
+            if side == 1 and tile == load.tiles - 1:
+                for copy in copies:
+                    copy.wait()
+                finish(acc_ref, held, out_refs)
+
+        load.each_step(pl.program_id(0), w_refs, w_ref, sems, work)
 
     return kernel_call(
         body,
         name,
-        (2,),
-        rows_specs + extra_specs + load.specs,
+        (2 * load.tiles,),
+        rows_specs + [pl.BlockSpec(memory_space=pl.ANY)] * count + load.specs,
         [whole(o.shape) for o in outs],
         outs,
-        load.scratch + [pltpu.VMEM((length, width), f32)],
-        scalars=len(place),
-        vmem=VMEM_MIB,
-    )(*place, *rows, *extras, *load.args)
+        load.scratch
+        + [pltpu.VMEM((length, width), f32), pltpu.SemaphoreType.DMA((count,))]
+        + [pltpu.VMEM(extra.shape, extra.dtype) for extra in extras],
+    )(*rows, *extras, *load.args)
 
 
 def to_home(rows, order_ref):
     return nt_dot(rows.astype(bf16), order_ref[...]).astype(bf16)
 
 
-def layer_out(hidden, weights, place, y, bias, live, order_b):
+def layer_out(hidden, pieces, y, bias, live, order_b):
     length, width = y.shape
     half = length // 2
-    columns = weights.shape[3]
 
     def finish(acc_ref, ins, outs):
         y_ref, bias_ref, live_ref, order_ref = ins
@@ -676,15 +662,13 @@
 
     return contract_back(
         [hidden],
-        [pl.BlockSpec((length, columns), lambda s, *_: (0, s))],
-        lambda refs, side: refs[0][...],
-        Gathered(weights),
+        [pl.BlockSpec((length, WIDE), lambda s, *_: (0, s))],
+        lambda refs: refs[0][...],
+        Pieces(pieces, pieces[0].shape[1]),
         (y, bias, live, order_b),
-        [whole((length, width)), whole((1, width)), whole((1, width)), whole((width, width))],
         finish,
         "layer_out",
         [array(half, width)] * 2,
-        (place,),
     )
 
 
@@ -712,11 +696,10 @@
 
     return contract_back(
         [du],
-        [pl.BlockSpec((length, hidden), lambda s: (0, s))],
-        lambda refs, side: refs[0][...],
+        [pl.BlockSpec((length, WIDE), lambda s: (0, s))],
+        lambda refs: refs[0][...],
         Pieces(pieces, hidden),
         (y, e, gain),
-        [whole((length, width)), whole((length, width)), whole((1, width))],
         finish,
         "second_back",
         [
@@ -728,7 +711,7 @@
     )
 
 
-def first_back(dps, pieces, x, mid, gain, order_b):
+def first_back(dp, pieces, x, mid, gain, order_b):
     length, width = x.shape
     half = length // 2
 
@@ -747,20 +730,19 @@
         sum_ref[...] = jnp.concatenate(sums, axis=0)
 
     return contract_back(
-        dps,
-        [whole(dps[0].shape)] * 2,
-        lambda refs, side: jnp.concatenate([refs[side][j] for j in range(3)], axis=1),
-        Pieces(pieces, pieces[0].shape[1]),
+        [dp],
+        [pl.BlockSpec((3, length, width // 2), lambda s: (0, 0, s))],
+        lambda refs: jnp.concatenate([refs[0][j] for j in range(3)], axis=1),
+        Pieces(pieces, pieces[0].shape[1], 0, pieces[0].shape[1]),
         (x, mid, gain, order_b),
-        [whole((length, width)), whole((length, width)), whole((1, width)), whole((width, width))],
         finish,
         "first_back",
         [array(half, width)] * 2 + [array(2, width, dtype=f32)],
     )
 
 
-def attend_back_kernel(first, q_ref, k_ref, v_ref, g_ref, lse_ref, dp_ref, qs_ref, vs_ref):
-    pair = first + pl.program_id(0)
+def attend_back_kernel(q_ref, k_ref, v_ref, g_ref, lse_ref, dp_ref, qs_ref, vs_ref):
+    pair = pl.program_id(0)
     rows = q_ref.shape[1]
     lanes = lax.broadcasted_iota(jnp.int32, (rows, PAIR), 1)
     sub = lax.broadcasted_iota(jnp.int32, (PAIR, rows), 0)
@@ -792,52 +774,60 @@
     vs_ref[...] = jnp.sum(dv, axis=0, keepdims=True)
 
 
-def attend_bwd(qkv, grads, lse_rows, side):
+def attend_bwd(qkv, grads, lse_rows):
     _, length, width = qkv.shape
-    count = width // PAIR // 2
-    first = side * count
-    head = lambda j: pl.BlockSpec((1, length, PAIR), lambda i: (j, 0, first + i))
     row = pl.BlockSpec((1, PAIR), lambda i: (0, i))
-    sums = array(1, width // 2, dtype=f32)
+    sums = array(1, width, dtype=f32)
     return kernel_call(
-        partial(attend_back_kernel, first),
+        attend_back_kernel,
         "attend_bwd",
-        (count,),
-        [head(j) for j in range(3)]
-        + [pl.BlockSpec((length, PAIR), lambda i: (0, first + i)), whole((PAIR, length))],
+        (width // PAIR,),
+        [head_spec(length, j) for j in range(3)]
+        + [pl.BlockSpec((length, PAIR), lambda i: (0, i)), whole((PAIR, length))],
         [pl.BlockSpec((3, length, PAIR), lambda i: (0, 0, i)), row, row],
-        [array(3, length, width // 2), sums, sums],
+        [array(3, length, width), sums, sums],
     )(qkv, qkv, qkv, grads, lse_rows)
 
 
-def grad_call(args, specs, terms, cuts, name, steps):
+def both_sides(args, specs, kinds, terms, name, tiles):
     count = len(args)
-    kinds, choose, terms = terms
+    half = args[0].shape[0] // 2
+    mid = half // 4
 
     def body(*refs):
-        def run(kind):
+        x_ref, y_ref, k10_ref, k00_ref, k01_ref = refs[count:]
+        step = pl.program_id(0)
+
+        def run(kind, side):
             left, right = terms(refs[:count], kind)
             acc = nn_dot(left, right).astype(bf16)
-            for ref, ranges in zip(refs[count:], cuts):
-                at = 0
-                for start, stop in ranges:
-                    ref[pl.ds(at, stop - start), :] = acc[start:stop]
-                    at += stop - start
-
-        for kind in range(kinds):
-            if kinds == 1:
-                run(kind)
+            y_ref[...] = acc[3 * mid :]
+            if side:
+                x_ref[pl.ds(0, mid), :] = acc[:mid]
+                x_ref[pl.ds(mid, mid), :] = acc[2 * mid : 3 * mid]
+                k10_ref[...] = acc[mid : 2 * mid]
             else:
-                pl.when(choose(pl.program_id(0)) == kind)(partial(run, kind))
-
-    sizes = [sum(b - a for a, b in ranges) for ranges in cuts]
+                k00_ref[...] = acc[: 2 * mid]
+                k01_ref[...] = acc[2 * mid : 3 * mid]
+
+        for side in range(2):
+            for kind, first in enumerate(kinds):
+                last = kinds[kind + 1] if kind + 1 < len(kinds) else tiles
+                base = 0 if side else tiles
+                here = (step >= base + first) & (step < base + last)
+                pl.when(here)(partial(run, kind, side))
+
+    far = lambda size: pl.BlockSpec((size, TILE), lambda s: (0, jnp.minimum(s, tiles - 1)))
+    near = lambda size: pl.BlockSpec((size, TILE), lambda s: (0, jnp.maximum(s - tiles, 0)))
+    both = pl.BlockSpec((mid, TILE), lambda s: (s // tiles, s % tiles))
+    sizes = (2 * mid, 2 * mid, mid, 2 * mid, mid)
     return kernel_call(
         body,
         name,
-        (steps,),
+        (2 * tiles,),
         specs,
-        [pl.BlockSpec((size, TILE), lambda s: (0, s)) for size in sizes],
-        [array(size, steps * TILE) for size in sizes],
+        [far(2 * mid), both, far(mid), near(2 * mid), near(mid)],
+        [array(size, tiles * TILE) for size in sizes],
     )(*args)
 
 
@@ -943,11 +933,9 @@
     def __init__(self, links):
         self.links = links
 
-    def first(self, far, near):
-        x_first, y_low_far, self.k10_low = far
-        self.k00, self.k01_top, y_low_near = near
-        self.x_got = self.links.x(x_first)
-        self.y_got = self.links.y(jnp.concatenate([y_low_far, y_low_near], axis=0))
+    def first(self, pieces):
+        x_first, y_first, self.k10_low, self.k00, self.k01_top = pieces
+        self.x_got, self.y_got = self.links.x(x_first), self.links.y(y_first)
 
     def middle(self):
         half = self.k01_top.shape[0]
@@ -1013,7 +1001,6 @@
     kc, ky, kz = rel // (2 * links.nz), (rel // links.nz) % 2, rel % links.nz
     home = (kz * 2 + (y_at ^ ky)) * 2 + (c_at ^ kc)
     order = spot[:, None] == (home * block + spot % block)[None, :]
-    place = jnp.concatenate([t.reshape(1), home[::block]]).astype(jnp.int32)
     order_b = order.astype(bf16)
     order_f = order.astype(f32)
     vectors = jnp.dot(
@@ -1038,8 +1025,7 @@
     near_one, along_two, twin_rows, fc2_turned = after(
         (twin_rows, h1, e), near_one, along_two, twin_rows, fc2_weight.T
     )
-    w_fc2 = lax.all_gather(after(along_two, fc2_turned), AXES, axis=0, tiled=True)
-    w_fc2 = w_fc2.reshape(wide_count, 2, block, hidden_here)
+    along_three = links.z_all(after(along_two, fc2_turned))
     far_one = start_far(links, near_one)
     other_one = [links.c(piece) for piece in (after(near_one, along_one), *near_one)]
     far_one, other_one, along_two, twin_rows = after((), far_one, other_one, along_two, twin_rows)
@@ -1047,7 +1033,6 @@
     other_one += [links.c(piece) for piece in far_one]
     twin_rows = links.c(twin_rows)
     twin_rows, other_one = after((), twin_rows, other_one)
-    twin_e, twin_h1 = twin_rows[:half], twin_rows[half:]
     w_one = [along_one, *near_one, *far_one, *other_one]
     zero_row = jnp.zeros((heads_cols,), f32)
     biases = jnp.stack(
@@ -1061,119 +1046,123 @@
     fc1_biases = row(jnp.concatenate([fc1_bias, far_small[2 * heads_cols :]]))
     qkv = project(h1, w_one, biases)
     attn, lse = attend_fwd(qkv)
-    lse_rows = lse.T
-
-    near_two = after(attn, near_two)
+
+    near_two, lse_rows = after(attn, near_two, lse.T)
     far_two = start_far(links, near_two)
     other_two = [links.c(piece) for piece in (after(near_two, along_two), *near_two)]
-    far_two, other_two = after((), far_two, other_two)
+    far_two, other_two, along_three, attn_sent = after((), far_two, other_two, along_three, attn)
+
+    near_three = links.x(along_three), links.y(along_three)
     other_two += [links.c(piece) for piece in far_two]
-    twin_attn = links.c(after(far_two, attn))
+    twin_attn = links.c(attn_sent)
     other_two, twin_attn = after((), other_two, twin_attn)
     w_two = [along_two, *near_two, *far_two, *other_two]
     y, h2, h2_t = join_heads(attn, x, w_two, hidden_here, outs[0], gains[1], shifts[1])
-    twin_h2 = links.c(h2_t[half:])
     hidden, slope = expand(h2, w_two, fc1_biases, hidden_here)
+    near_three, hidden, slope, h2_t, along_three = after(
+        (), near_three, hidden, slope, h2_t, along_three
+    )
+
+    far_three = start_far(links, near_three)
     twin_hidden = links.c(hidden)
-
-    quarter, mid_row = width // 4, width // 8
-    top, low = (0, mid_row), (mid_row, quarter)
-    top_y, low_y = (quarter, quarter + mid_row), (quarter + mid_row, half)
-    far_cuts = [[top, top_y], [low_y], [low]]
-    near_cuts = [[(0, quarter)], [top_y], [low_y]]
-
-    cuts = (near_cuts, far_cuts)
+    other_three = [links.c(piece) for piece in (along_three, near_three[0])]
+    far_three, twin_hidden, other_three, near_three, h2_sent = after(
+        (), far_three, twin_hidden, other_three, near_three, h2_t[half:]
+    )
+
     stack = lambda one, two: jnp.concatenate([one[...], two[...]], axis=0)
     join = lambda one, two: jnp.concatenate([one[...], two[...]], axis=1)
-    left_spec = pl.BlockSpec((half, length), lambda *_: (0, 0))
-
-    def grad_of(lefts, rights, side, name, done):
-        steps = hidden_here // TILE
-        cols = pl.BlockSpec((length, TILE), lambda s: (0, side * steps + s))
-        terms = lambda refs, kind: (join(*refs[:2]), stack(*refs[2:4]))
-        args = [*lefts, *after(done, *rights)]
-        specs = [left_spec] * 2 + [cols] * 2
-        return grad_call(args, specs, (1, None, terms), cuts[side], name, steps)
-
-    def grad_one(lefts, dps, attns, side, name, done):
-        cols = pl.BlockSpec((length, heads_cols), lambda *_: (0, side))
-        one_dp = pl.BlockSpec((1, length, heads_cols), lambda s: (jnp.minimum(s, 2), 0, 0))
+    tiles = hidden_here // TILE
+    left_at = lambda at: pl.BlockSpec((half, length), lambda s: (at, 0))
+
+    def tile_spec(count):
+        def at(s):
+            tile = jnp.minimum(s % count, tiles - 1)
+            return (0, jnp.where(s < count, tiles, 0) + tile)
+
+        return pl.BlockSpec((length, TILE), at)
+
+    attn_spec = lambda count: pl.BlockSpec((length, TILE), lambda s: (0, 1 - s // count))
+
+    def grad_fc2():
+        terms = lambda refs, kind: (join(*refs[:2]), stack(*refs[2:]))
+        args = [e_t, twin_rows, hidden, twin_hidden]
+        specs = [left_at(0), left_at(0)] + [tile_spec(tiles)] * 2
+        return both_sides(args, specs, (0,), terms, "grad_fc2", tiles)
+
+    def grad_two():
+        count = tiles + 1
 
         def terms(refs, kind):
-            if kind == 0:
-                return join(*refs[:2]), jnp.concatenate([refs[4][0], refs[5][0]], axis=0)
-            return join(*refs[2:4]), stack(*refs[6:8])
-
-        args = [*lefts, *after(done, *dps), *attns]
-        specs = [left_spec] * 4 + [one_dp] * 2 + [cols] * 2
-        return grad_call(args, specs, (2, lambda s: s // 3, terms), cuts[side], name, 4)
-
-    w_fc2 = after(hidden, w_fc2)
-    home_fc2, home_fc1, home_one = Home(links), Home(links), Home(links)
-
-    du, fc1b_sum = hidden_back(e, slope, w_fc2, place)
-    du, twin_hidden, twin_h2 = after((), du, twin_hidden, twin_h2)
+            return join(*refs[4 * kind :][:2]), stack(*refs[4 * kind + 2 :][:2])
+
+        args = [h2_t, twin_h2, du, twin_du, da_t, twin_da, attn, twin_attn]
+        specs = [left_at(0)] * 2 + [tile_spec(count)] * 2
+        specs += [left_at(0)] * 2 + [attn_spec(count)] * 2
+        return both_sides(args, specs, (0, tiles), terms, "grad_two", count)
+
+    def grad_qkv():
+        def terms(refs, kind):
+            return join(*refs[:2]), jnp.concatenate([refs[2][0], refs[3][0]], axis=0)
+
+        args = [h1_t, twin_rows, dp, twin_dp]
+        dp_spec = pl.BlockSpec((1, length, TILE), lambda s: (s % 3, 0, 1 - s // 3))
+        specs = [left_at(0), left_at(1)] + [dp_spec] * 2
+        return both_sides(args, specs, (0,), terms, "grad_qkv", 3)
+
+    def enter_window(done, *homes):
+        for home in homes:
+            home.x_got, home.y_got = after(done, home.x_got, home.y_got)
+
+    home_fc2, home_two, home_qkv = Home(links), Home(links), Home(links)
+
+    other_three += [links.c(piece) for piece in (near_three[1], *far_three)]
+    twin_h2 = links.c(h2_sent)
+    pieces = grad_fc2()
+    pieces, other_three, twin_h2 = after((), pieces, other_three, twin_h2)
+    w_fc2 = [along_three, *near_three, *far_three, *other_three]
+
+    home_fc2.first(pieces)
+    du, fc1b_sum = hidden_back(e, slope, w_fc2)
+    mid, da, da_t, second_sums = second_back(du, w_two, hidden_here, y, e, gains[1])
+    enter_window(da, home_fc2)
+    du, da, da_t, da_t_far = after(home_fc2.x_got, du, da, da_t, da_t[half:])
 
     twin_du = links.c(du)
-    fc2_args = (e_t, twin_e), (hidden, twin_hidden)
-    far = grad_of(*fc2_args, 1, "fc2_far", ())
-    near = grad_of(*fc2_args, 0, "fc2_near", far)
-    far, near, twin_du = after((), far, near, twin_du)
-
-    home_fc2.first(far, near)
-    mid, da, da_t, second_sums = second_back(
-        after(near, du), w_two, hidden_here, y, e, gains[1]
-    )
-    fc1_args = (h2_t, twin_h2), (du, twin_du)
-    far = grad_of(*fc1_args, 1, "fc1_far", da)
-    near = grad_of(*fc1_args, 0, "fc1_near", far)
-    far, near, home_fc2.x_got, home_fc2.y_got = after(
-        (), far, near, home_fc2.x_got, home_fc2.y_got
-    )
-
-    home_fc1.first(far, near)
-    moved_fc2 = home_fc2.middle()
-    d_heads = heads_back(after((near, moved_fc2), da), w_two, hidden_here)
-    dp_far, q_far, v_far = attend_bwd(qkv, d_heads, lse_rows, 1)
-    dp_near, q_near, v_near = attend_bwd(after(dp_far, qkv), d_heads, lse_rows, 0)
-    dp_far, dp_near, home_fc1.x_got, home_fc1.y_got = after(
-        (), dp_far, dp_near, home_fc1.x_got, home_fc1.y_got
-    )
-
-    moved_fc1 = home_fc1.middle()
-    dp_far, dp_near, moved_fc2, moved_fc1, da_t_far = after(
-        (), dp_far, dp_near, moved_fc2, moved_fc1, da_t[half:]
-    )
-    twin_dp = links.c(jnp.concatenate([dp_far, dp_near], axis=0))
     twin_da = links.c(da_t_far)
-    home_fc2.second(*moved_fc2)
-    home_fc1.second(*moved_fc1)
+    home_fc2.second(*home_fc2.middle())
+    d_heads = heads_back(da, w_two, hidden_here)
+    twin_du, twin_da = after(d_heads, twin_du, twin_da)
+    pieces = grad_two()
+    pieces, d_heads, home_fc2.y_last, home_fc2.x_last = after(
+        (), pieces, d_heads, home_fc2.y_last, home_fc2.x_last
+    )
+
+    home_two.first(pieces)
+    moved = home_fc2.last(pieces, True)
+    dp, q_sums, v_sums = attend_bwd(qkv, after(moved, d_heads), lse_rows)
     grad_near, grad_sent_rows, first_sums = first_back(
-        [dp_near, dp_far], w_one, x, mid, gains[0], order_b
-    )
-    twin_dp, twin_da, grad_sent_rows = after(
-        grad_near, twin_dp, twin_da, grad_sent_rows
-    )
-    twin_far, twin_near = twin_dp[:3], twin_dp[3:]
-    lefts, attns = (h1_t, twin_h1, da_t, twin_da), (attn, twin_attn)
-    far = grad_one(lefts, (dp_far, twin_far), attns, 1, "one_far", ())
-    near = grad_one(lefts, (dp_near, twin_near), attns, 0, "one_near", far)
-    lasts = [home_fc2.y_last, home_fc2.x_last, home_fc1.y_last, home_fc1.x_last]
-    far, near, lasts = after((), far, near, lasts)
-    home_fc2.y_last, home_fc2.x_last, home_fc1.y_last, home_fc1.x_last = lasts
-
-    home_one.first(far, near)
-    moved = home_fc2.last(near, True)
-    moved = home_fc1.last(moved, True)
-    out_near, out_sent = layer_out(
-        after(moved, hidden), w_fc2, place, y, outs[1], live, order_b
-    )
-    home_one.x_got, home_one.y_got = after(out_near, home_one.x_got, home_one.y_got)
-    moved_one = home_one.middle()
-    moved_one, grad_sent_rows = after((), moved_one, grad_sent_rows)
-    home_one.second(*moved_one)
+        dp, w_one, x, mid, gains[0], order_b
+    )
+    enter_window(grad_near, home_two)
+    dp = after(home_two.x_got, dp)
+
+    twin_dp = links.c(dp)
+    home_two.second(*home_two.middle())
+    out_near, out_sent = layer_out(after(dp, hidden), w_fc2, y, outs[1], live, order_b)
+    twin_dp = after(out_near, twin_dp)
+    pieces = grad_qkv()
+    pieces, home_two.y_last, home_two.x_last = after(
+        (), pieces, home_two.y_last, home_two.x_last
+    )
+
+    home_qkv.first(pieces)
+    moved = home_two.last(pieces, True)
+    enter_window(moved, home_qkv)
+    moved, grad_sent_rows = after((), home_qkv.middle(), grad_sent_rows)
+    home_qkv.second(*moved)
     grad_got = links.x(grad_sent_rows)
-    moved = home_one.last((), False)
+    moved = home_qkv.last((), False)
     out_got = links.x(after(moved, out_sent))
 
     sums = jnp.concatenate(
@@ -1183,22 +1172,18 @@
         sums, order_f, (((1,), (1,)), ((), ())), precision=lax.Precision.HIGHEST
     )
 
-    def placed(near, far):
-        return jnp.where(t == 0, jnp.concatenate([near, far]), jnp.concatenate([far, near]))
-
-    small = [
-        sums.reshape(-1),
-        placed(q_near[0], q_far[0]),
-        placed(v_near[0], v_far[0]),
-        placed(fc1b_sum[0, :hidden_here], fc1b_sum[0, hidden_here:]),
-    ]
+    def placed(both):
+        size = both.shape[1] // 2
+        return jnp.where(t == 0, both[0], jnp.concatenate([both[0, size:], both[0, :size]]))
+
+    small = [sums.reshape(-1), placed(q_sums), placed(v_sums), placed(fc1b_sum)]
     small = total_over_all(links, jnp.concatenate(small).reshape(-1, 128)).reshape(-1) * grad_scale
     sums = small[: 6 * width].reshape(6, width)
     own = lambda first, size: lax.dynamic_slice_in_dim(small, first + t * size, size, 0)
 
-    g_one = home_one.value((), grad_scale)
+    g_qkv = home_qkv.value((), grad_scale)
     g_fc2 = home_fc2.value(moved, grad_scale)
-    g_fc1 = home_fc1.value(moved, grad_scale)
+    g_two = home_two.value(moved, grad_scale)
 
     def both_slots(near, got):
         return jnp.where(t == 0, jnp.stack([near, got]), jnp.stack([got, near]))
@@ -1206,11 +1191,11 @@
     return (
         both_slots(out_near, out_got),
         both_slots(grad_near, grad_got).astype(f32),
-        g_one[:, :qkv_cols].reshape(block, 3, heads_cols),
+        g_qkv.reshape(block, 3, heads_cols),
         own(6 * width, heads_cols),
         own(6 * width + 2 * heads_cols, heads_cols),
-        g_one[:, qkv_cols:].T,
-        g_fc1,
+        g_two[:, hidden_here:].T,
+        g_two[:, :hidden_here],
         own(6 * width + 4 * heads_cols, hidden_here),
         g_fc2.T,
         sums[0:2],

time: 411 us -> 390 us (0.949)
  waiting for transfers between devices: 109 us -> 97.6 us
  Pallas kernels: 180 us -> 170 us
  other arithmetic: 18.6 us -> 11.4 us
  local copies, waits for them, and re-layouts: 27.4 us -> 32.6 us
    pallas_call x14 -> x10, Pallas kernels: 127 us -> 117 us  [the longest x3 35.5 us: contract_back(): kernel_call(body, name, (2 * load.tiles,), rows_specs + [pl.BlockSpec(mem...]
    all_to_all x1, waiting for transfers between devices: 8.66 us -> 0.01 us  [z_sum(): lax.all_to_all(rows, AXES, 0, 0, tiled=True, axis_index_groups=self.z_gro...]
    concatenate x5 -> x0, other arithmetic: 7.56 us -> none  [the longest x3 4.98 us: first(): self.y_got = self.links.y(jnp.concatenate([y_low_far, y_low_near], axis=0))]
    unnamed x126 -> x98, local copies, waits for them, and re-layouts: 7.43 us -> 11.2 us
    ppermute x15 -> x17, starting transfers between devices: 16.3 us -> 18.4 us  [x(): return lax.ppermute(rows, AXES, self.across)]
    ppermute x15 -> x17, waiting for transfers between devices: 73.9 us -> 72.5 us  [x(): return lax.ppermute(rows, AXES, self.across)]
    ppermute x11 -> x13, waiting for transfers between devices: 11.6 us -> 11.9 us  [y(): return lax.ppermute(rows, AXES, self.beside)]
    ppermute x11 -> x13, starting transfers between devices: 14.7 us -> 14.8 us  [y(): return lax.ppermute(rows, AXES, self.beside)]
  transfers between devices with their start and end apart: 54 -> 63, of which waited for: 21 -> 21; matrix products, arithmetic and copies ran while one was open for 8% -> 9% of each run, Pallas kernels for 43% -> 44%
where the time goes in v4:
time: 390 us; the launch traced here: 383 us
  Pallas kernels  170 us (44%)
  waiting for transfers between devices  97.6 us (25%)
  starting transfers between devices  52.8 us (14%)
  local copies, waits for them, and re-layouts  32.6 us (8%)
  between operations  15.8 us (4%)
  other arithmetic  11.4 us (3%)
    ppermute x17, waiting for transfers between devices, x(): return lax.ppermute(rows, AXES, self.across)  72.5 us
    pallas_call x3, Pallas kernels, contract_back(): kernel_call(body, name, (2 * load.tiles,), rows_specs + [pl.BlockSpec(mem...  35.5 us
    pallas_call x3, Pallas kernels, both_sides(): kernel_call(body, name, (2 * tiles,), specs, [far(2 * mid), both, far(mid...  32.7 us
    pallas_call x6, Pallas kernels, small_call(): kernel_call(body, name, (1,), [whole(a.shape) for a in args], out_specs,...  19.4 us
    ppermute x17, starting transfers between devices, x(): return lax.ppermute(rows, AXES, self.across)  18.4 us
    pallas_call x1, Pallas kernels, attend_bwd(): kernel_call(attend_back_kernel, 'attend_bwd', (width // PAIR,), [head_spe...  16.8 us
    ppermute x13, starting transfers between devices, y(): return lax.ppermute(rows, AXES, self.beside)  14.8 us
    pallas_call x1, Pallas kernels, expand(): kernel_call(body, 'expand', (2 * load.tiles,), [whole((length, width)), p...  12.9 us
  transfers between devices with their start and end apart: 63, of which 21 were waited for; matrix products, arithmetic and copies ran while one was open for 9% of the time, Pallas kernels for 44%

profile of v4, /device:TPU:0, one launch (start us, length us, event | category | flops | bytes accessed | tf_op | source)
XLA Modules:
  0.0 383.3 jit_solution(17033671911341606174)
XLA Ops:
  8.2 5.1 %collective-permute-start = (bf16[64,1536]{1,0:T(8,128)(2,1)S(1)}, bf16[64,1536]{1,0:T(8,128)(2,1)S(1)}, u32[]{:S(2)}, u32[]{:S(2)}) collective-permute-start(bf16[64,1536]{1,0:T(8,128)(2,1)S(1)} %bitcast.56), channel_id=1, source_target_pairs={{8,0},{9,1},{10,2},{11,3},{12,4},{13,5},{14,6},{15,7},{16,8},{17,9... | collective-permute-start | bytes 589832 | tf_op jit(solution)/shard_map/ppermute | solution.py:875
  14.3 2.7 dynamic-slice_bitcast_fusion.2
  21.1 2.2 fusion.2.order_ref.refs_4_
  23.5 6.5 %collective-permute-done.1 = bf16[64,1536]{1,0:T(8,128)(2,1)S(1)} collective-permute-done((bf16[64,1536]{1,0:T(8,128)(2,1)S(1)}, bf16[64,1536]{1,0:T(8,128)(2,1)S(1)}, u32[]{:S(2)}, u32[]{:S(2)}) %collective-permute-start.1) | collective-permute-done | bytes 196640 | tf_op jit(solution)/shard_map/ppermute | solution.py:875
  30.0 1.6 collective-permute-start.3
  31.6 1.5 collective-permute-start.4
  36.4 8.2 %collective-permute-done.6 = f32[24,128]{1,0:T(8,128)S(1)} collective-permute-done((f32[24,128]{1,0:T(8,128)S(1)}, f32[24,128]{1,0:T(8,128)S(1)}, u32[]{:S(2)}, u32[]{:S(2)}) %collective-permute-start.6) | collective-permute-done | bytes 12320 | tf_op jit(solution)/shard_map/ppermute | solution.py:898
  46.3 4.7 %enter_cot.1 = (bf16[512,1024]{1,0:T(8,128)(2,1)}, bf16[1024,512]{1,0:T(8,128)(2,1)}) custom-call(bf16[256,1024]{1,0:T(8,128)(2,1)} %get-tuple-element.362.own_ref, bf16[256,1024]{1,0:T(8,128)(2,1)} %get-tuple-element.332.got_ref, bf16[1024,1024]{1,0:T(8,128)(2,1)} %fusion.2.order_ref.refs_4_, f32[1,1024]{1,0:T(1,128)} %broadcast_in_dim.21.live_ref.refs_3_), custom_call_target="tpu_custom_call" | custom-call | flops 1 | bytes 1 | tf_op jit(solution)/shard_map/enter_cot/pallas_call | solution.py:420
  50.9 5.1 %enter.1 = (bf16[512,1024]{1,0:T(8,128)(2,1)}, bf16[512,1024]{1,0:T(8,128)(2,1)}, bf16[1024,512]{1,0:T(8,128)(2,1)}) custom-call(bf16[256,1024]{1,0:T(8,128)(2,1)} %get-tuple-element.337.own_ref, bf16[256,1024]{1,0:T(8,128)(2,1)} %get-tuple-element.333.got_ref, bf16[1024,1024]{1,0:T(8,128)(2,1)} %fusion.2.order_ref.refs_4_, ...), custom_call_target="tpu_custom_call" | custom-call | flops 1 | bytes 1 | tf_op jit(solution)/shard_map/enter/pallas_call | solution.py:398
  60.2 1.6 collective-permute-start.7
  61.7 1.5 collective-permute-start.8
  63.3 8.6 %collective-permute-done.7.refs_3_.refs_8_ = bf16[128,1536]{1,0:T(8,128)(2,1)} collective-permute-done((bf16[128,1536]{1,0:T(8,128)(2,1)S(1)}, bf16[128,1536]{1,0:T(8,128)(2,1)}, u32[]{:S(2)}, u32[]{:S(2)}) %collective-permute-start.7) | collective-permute-done | bytes 393248 | tf_op jit(solution)/shard_map/ppermute | solution.py:898
  75.0 1.5 collective-permute-start.13
  78.0 2.0 collective-permute-done.15.refs_8_.refs_13_
  80.6 8.6 %project.1.q_ref.k_ref.v_ref = bf16[3,512,1024]{2,1,0:T(8,128)(2,1)} custom-call(bf16[512,1024]{1,0:T(8,128)(2,1)} %get-tuple-element.169.h_ref, f32[2,1,1536]{2,1,0:T(1,128)} %broadcast_in_dim.23.bias_ref, bf16[256,1536]{1,0:T(8,128)(2,1)} %copy-done.6, bf16[256,1536]{1,0:T(8,128)(2,1)} %copy-done.7, bf16[256,1536]{1,0:T(8,128)(2,1)} %copy-done.8, ...), custom_call_target="tpu_custom_call" | custom-call | flops 1 | bytes 1 | tf_op jit(solution)/shard_map/project/pallas_call | solution.py:445
  89.2 12.3 %attend_fwd.1 = (bf16[512,1024]{1,0:T(8,128)(2,1)}, f32[512,128]{1,0:T(8,128)}) custom-call(bf16[3,512,1024]{2,1,0:T(8,128)(2,1)} %project.1.q_ref.k_ref.v_ref, bf16[3,512,1024]{2,1,0:T(8,128)(2,1)} %project.1.q_ref.k_ref.v_ref, bf16[3,512,1024]{2,1,0:T(8,128)(2,1)} %project.1.q_ref.k_ref.v_ref), custom_call_target="tpu_custom_call" | custom-call | flops 1 | bytes 1 | tf_op jit(solution)/shard_map/attend_fwd/pallas_call | solution.py:485
  101.5 1.8 copy.28
  108.3 1.5 collective-permute-start.18
  109.8 15.0 %collective-permute-done.17.refs_3_.refs_7_ = bf16[128,2560]{1,0:T(8,128)(2,1)S(1)} collective-permute-done((bf16[128,2560]{1,0:T(8,128)(2,1)}, bf16[128,2560]{1,0:T(8,128)(2,1)S(1)}, u32[]{:S(2)}, u32[]{:S(2)}) %collective-permute-start.17) | collective-permute-done | bytes 655392 | tf_op jit(solution)/shard_map/ppermute | solution.py:898
  129.5 1.9 collective-permute-done.24.refs_8_.refs_12_
  134.1 6.5 %join_heads.1 = (f32[512,1024]{1,0:T(8,128)}, bf16[512,1024]{1,0:T(8,128)(2,1)}, bf16[1024,512]{1,0:T(8,128)(2,1)}) custom-call(bf16[512,1024]{1,0:T(8,128)(2,1)} %get-tuple-element.203.attn_ref.refs_6_, bf16[512,1024]{1,0:T(8,128)(2,1)} %get-tuple-element.197.x_ref.refs_1_, f32[1,1024]{1,0:T(1,128)} %get-tuple-element.346.bias_ref, ...), custom_call_target="tpu_custom_call" | custom-call | flops 1 | bytes 1 | tf_op jit(solution)/shard_map/join_heads/pallas_call | solution.py:515
  140.6 12.9 %expand.1 = (bf16[512,4096]{1,0:T(8,128)(2,1)}, bf16[512,4096]{1,0:T(8,128)(2,1)}) custom-call(bf16[512,1024]{1,0:T(8,128)(2,1)} %get-tuple-element.209.h_ref, f32[1,4096]{1,0:T(1,128)} %bitcast.71, bf16[256,2560]{1,0:T(8,128)(2,1)} %all-gather.3.cloned.1.call-done.refs_0_.refs_4_, bf16[256,2560]{1,0:T(8,128)(2,1)} %copy-done, bf16[256,2560]{1,0:T(8,128)(2,1)} %copy-done.1, ...), custom_call_target="tpu_custom_call" | custom-call | flops 1 | bytes 1 | tf_op jit(solution)/shard_map/expand/pallas_call | solution.py:543
  158.1 12.7 %collective-permute-done.27.refs_3_.refs_8_ = bf16[128,2048]{1,0:T(8,128)(2,1)S(1)} collective-permute-done((bf16[128,2048]{1,0:T(8,128)(2,1)S(1)}, bf16[128,2048]{1,0:T(8,128)(2,1)S(1)}, u32[]{:S(2)}, u32[]{:S(2)}) %collective-permute-start.27) | collective-permute-done | bytes 524320 | tf_op jit(solution)/shard_map/ppermute | solution.py:898
  174.3 10.5 %grad_fc2.1 = (bf16[256,2048]{1,0:T(8,128)(2,1)}, bf16[256,2048]{1,0:T(8,128)(2,1)}, bf16[128,2048]{1,0:T(8,128)(2,1)}, bf16[256,2048]{1,0:T(8,128)(2,1)}, bf16[128,2048]{1,0:T(8,128)(2,1)}) custom-call(bf16[1024,512]{1,0:T(8,128)(2,1)} %get-tuple-element.167.refs_0_, bf16[1024,512]{1,0:T(8,128)(2,1)} %collective-permute-done.14.refs_1_, ...), custom_call_target="tpu_custom_call" | custom-call | flops 1 | bytes 1 | tf_op jit(solution)/shard_map/grad_fc2/pallas_call | solution.py:824
  187.5 10.2 %hidden_back.1 = (bf16[512,4096]{1,0:T(8,128)(2,1)}, f32[1,4096]{1,0:T(1,128)}) custom-call(bf16[512,1024]{1,0:T(8,128)(2,1)} %get-tuple-element.170.e_ref.refs_2_, bf16[512,4096]{1,0:T(8,128)(2,1)} %get-tuple-element.232.slope_ref, bf16[256,2048]{1,0:T(8,128)(2,1)} %all-gather.5.cloned.1.call-done.refs_0_.refs_5_, ...), custom_call_target="tpu_custom_call" | custom-call | flops 1 | bytes 1 | tf_op jit(solution)/shard_map/hidden_back/pallas_call | solution.py:571
  197.7 12.7 %second_back.1 = (f32[512,1024]{1,0:T(8,128)}, bf16[512,1024]{1,0:T(8,128)(2,1)}, bf16[1024,512]{1,0:T(8,128)(2,1)}, f32[4,1024]{1,0:T(4,128)}) custom-call(bf16[512,4096]{1,0:T(8,128)(2,1)} %get-tuple-element.246.refs_0_.refs_2_, f32[512,1024]{1,0:T(8,128)} %get-tuple-element.240.refs_1_, bf16[512,1024]{1,0:T(8,128)(2,1)} %get-tuple-element.170.e_ref.refs_2_, ...), custom_call_target="tpu_custom_call" | custom-call | flops 1 | bytes 1 | tf_op jit(solution)/shard_map/second_back/pallas_call | solution.py:635
  213.0 3.0 add_mid.3
  218.1 4.9 %heads_back.1.g_ref = bf16[512,1024]{1,0:T(8,128)(2,1)} custom-call(bf16[512,1024]{1,0:T(8,128)(2,1)} %get-tuple-element.248.da_ref, bf16[256,2560]{1,0:T(8,128)(2,1)} %all-gather.3.cloned.1.call-done.refs_0_.refs_4_, bf16[256,2560]{1,0:T(8,128)(2,1)} %copy-done, bf16[256,2560]{1,0:T(8,128)(2,1)} %copy-done.1, bf16[128,2560]{1,0:T(8,128)(2,1)} %copy-done.3, ...), custom_call_target="tpu_custom_call" | custom-call | flops 1 | bytes 1 | tf_op jit(solution)/shard_map/heads_back/pallas_call | solution.py:593
  223.9 13.8 %grad_two.1 = (bf16[256,2560]{1,0:T(8,128)(2,1)}, bf16[256,2560]{1,0:T(8,128)(2,1)}, bf16[128,2560]{1,0:T(8,128)(2,1)}, bf16[256,2560]{1,0:T(8,128)(2,1)}, bf16[128,2560]{1,0:T(8,128)(2,1)}) custom-call(bf16[1024,512]{1,0:T(8,128)(2,1)} %get-tuple-element.214.refs_0_, bf16[512,512]{1,0:T(8,128)(2,1)} %collective-permute-done.35.refs_1_, ...), custom_call_target="tpu_custom_call" | custom-call | flops 1 | bytes 1 | tf_op jit(solution)/shard_map/grad_two/pallas_call | solution.py:824
  239.8 3.5 add_last.3
  243.3 16.8 %attend_bwd.1 = (bf16[3,512,1024]{2,1,0:T(8,128)(2,1)}, f32[1,1024]{1,0:T(1,128)}, f32[1,1024]{1,0:T(1,128)}) custom-call(bf16[3,512,1024]{2,1,0:T(8,128)(2,1)} %project.1.q_ref.k_ref.v_ref, bf16[3,512,1024]{2,1,0:T(8,128)(2,1)} %project.1.q_ref.k_ref.v_ref, bf16[3,512,1024]{2,1,0:T(8,128)(2,1)} %project.1.q_ref.k_ref.v_ref, ...), custom_call_target="tpu_custom_call" | custom-call | flops 1 | bytes 1 | tf_op jit(solution)/shard_map/attend_bwd/pallas_call | solution.py:781
  260.2 11.1 %first_back.1 = (bf16[256,1024]{1,0:T(8,128)(2,1)}, bf16[256,1024]{1,0:T(8,128)(2,1)}, f32[2,1024]{1,0:T(2,128)}) custom-call(bf16[3,512,1024]{2,1,0:T(8,128)(2,1)} %get-tuple-element.280.refs_0_.refs_2_, bf16[512,1024]{1,0:T(8,128)(2,1)} %get-tuple-element.197.x_ref.refs_1_, f32[512,1024]{1,0:T(8,128)} %get-tuple-element.277.refs_2_, ...), custom_call_target="tpu_custom_call" | custom-call | flops 1 | bytes 1 | tf_op jit(solution)/shard_map/first_back/pallas_call | solution.py:635
  272.3 3.3 add_mid.4
  277.8 1.9 fusion
  279.8 11.7 %layer_out.1 = (bf16[256,1024]{1,0:T(8,128)(2,1)}, bf16[256,1024]{1,0:T(8,128)(2,1)}) custom-call(bf16[512,4096]{1,0:T(8,128)(2,1)} %get-tuple-element.281.refs_2_.refs_0_, f32[512,1024]{1,0:T(8,128)} %get-tuple-element.240.refs_1_, f32[1,1024]{1,0:T(1,128)} %get-tuple-element.343.refs_2_, f32[1,1024]{1,0:T(1,128)} %broadcast_in_dim.21.live_ref.refs_3_, ...), custom_call_target="tpu_custom_call" | custom-call | flops 1 | bytes 1 | tf_op jit(solution)/shard_map/layer_out/pallas_call | solution.py:635
  291.6 8.4 %grad_qkv.1 = (bf16[256,1536]{1,0:T(8,128)(2,1)}, bf16[256,1536]{1,0:T(8,128)(2,1)}, bf16[128,1536]{1,0:T(8,128)(2,1)}, bf16[256,1536]{1,0:T(8,128)(2,1)}, bf16[128,1536]{1,0:T(8,128)(2,1)}) custom-call(bf16[1024,512]{1,0:T(8,128)(2,1)} %get-tuple-element.168.refs_0_, bf16[1024,512]{1,0:T(8,128)(2,1)} %collective-permute-done.14.refs_1_, ...), custom_call_target="tpu_custom_call" | custom-call | flops 1 | bytes 1 | tf_op jit(solution)/shard_map/grad_qkv/pallas_call | solution.py:824
  302.1 4.0 %add_last.4 = bf16[256,2560]{1,0:T(8,128)(2,1)} custom-call(bf16[256,2560]{1,0:T(8,128)(2,1)} %get-tuple-element.270.k00_ref, bf16[256,2560]{1,0:T(8,128)(2,1)} %collective-permute-done.42.rx_ref, bf16[256,2560]{1,0:T(8,128)(2,1)} %collective-permute-done.43.ry_ref, bf16[128,2560]{1,0:T(8,128)(2,1)} %collective-permute-done.45.y2_ref, ...), custom_call_target="tpu_custom_call" | custom-call | flops 1 | bytes 1 | tf_op jit(solution)/shard_map/add_last/pallas_call | solution.py:851
  307.1 13.1 %collective-permute-done.47.rx_ref = bf16[256,1536]{1,0:T(8,128)(2,1)S(1)} collective-permute-done((bf16[256,1536]{1,0:T(8,128)(2,1)}, bf16[256,1536]{1,0:T(8,128)(2,1)S(1)}, u32[]{:S(2)}, u32[]{:S(2)}) %collective-permute-start.47) | collective-permute-done | bytes 786464 | tf_op jit(solution)/shard_map/ppermute | solution.py:898
  322.0 2.6 add_mid.5
  327.8 7.7 %collective-permute-done.55 = f32[96,128]{1,0:T(8,128)S(1)} collective-permute-done((f32[96,128]{1,0:T(8,128)S(1)}, f32[96,128]{1,0:T(8,128)S(1)}, u32[]{:S(2)}, u32[]{:S(2)}) %collective-permute-start.55) | collective-permute-done | bytes 49184 | tf_op jit(solution)/shard_map/ppermute | solution.py:901
  335.5 2.5 collective-permute-start.56
  338.1 2.1 collective-permute-done.56
  340.1 1.8 collective-permute-start.57
  343.4 3.0 add_last.5
  346.4 4.1 %all-to-all-start = ((bf16[4,64,1536]{2,1,0:T(8,128)(2,1)}), bf16[4,64,1536]{2,1,0:T(8,128)(2,1)S(1)}, u32[]{:S(2)}, u32[]{:S(2)}) async-start(bf16[4,64,1536]{2,1,0:T(8,128)(2,1)} %bitcast.53), calls=%async_computation | async-start | bytes 1572864 | tf_op jit(solution)/shard_map/all_to_all | solution.py:889
  355.8 1.8 multiply_bitcast_fusion.1
  357.6 8.0 %collective-permute-done.52 = bf16[256,1024]{1,0:T(8,128)(2,1)S(1)} collective-permute-done((bf16[256,1024]{1,0:T(8,128)(2,1)S(1)}, bf16[256,1024]{1,0:T(8,128)(2,1)S(1)}, u32[]{:S(2)}, u32[]{:S(2)}) %collective-permute-start.52) | collective-permute-done | bytes 524320 | tf_op jit(solution)/shard_map/ppermute | solution.py:898
  367.1 4.7 %collective-permute-done.51 = bf16[256,1024]{1,0:T(8,128)(2,1)S(1)} collective-permute-done((bf16[256,1024]{1,0:T(8,128)(2,1)S(1)}, bf16[256,1024]{1,0:T(8,128)(2,1)S(1)}, u32[]{:S(2)}, u32[]{:S(2)}) %collective-permute-start.51) | collective-permute-done | bytes 524320 | tf_op jit(solution)/shard_map/ppermute | solution.py:898
  (271 shorter events, 74.2 us)
Async XLA Ops:
  7.2 52.3 %all-gather.3.cloned.1.call-start = ((), (), s32[]{:S(2)}) async-start(), calls=%async_computation.3 | async-start | bytes 1638400 | tf_op jit(solution)/shard_map/all_gather | solution.py:893
  8.2 15.3 %collective-permute-start = (bf16[64,1536]{1,0:T(8,128)(2,1)S(1)}, bf16[64,1536]{1,0:T(8,128)(2,1)S(1)}, u32[]{:S(2)}, u32[]{:S(2)}) collective-permute-start(bf16[64,1536]{1,0:T(8,128)(2,1)S(1)} %bitcast.56), channel_id=1, source_target_pairs={{8,0},{9,1},{10,2},{11,3},{12,4},{13,5},{14,6},{15,7},{16,8},{17,9... | collective-permute-start | bytes 589832 | tf_op jit(solution)/shard_map/ppermute | solution.py:875
  13.3 16.7 %collective-permute-start.1 = (bf16[64,1536]{1,0:T(8,128)(2,1)S(1)}, bf16[64,1536]{1,0:T(8,128)(2,1)S(1)}, u32[]{:S(2)}, u32[]{:S(2)}) collective-permute-start(bf16[64,1536]{1,0:T(8,128)(2,1)S(1)} %bitcast.57), channel_id=1, source_target_pairs={{16,0},{17,1},{18,2},{19,3},{20,4},{21,5},{22,6},{23,7},{24,8},{25... | collective-permute-start | bytes 589832 | tf_op jit(solution)/shard_map/ppermute | solution.py:875
  13.3 16.7 %collective-permute-start.2 = (bf16[64,1536]{1,0:T(8,128)(2,1)S(1)}, bf16[64,1536]{1,0:T(8,128)(2,1)S(1)}, u32[]{:S(2)}, u32[]{:S(2)}) collective-permute-start(bf16[64,1536]{1,0:T(8,128)(2,1)S(1)} %bitcast.58), channel_id=1, source_target_pairs={{24,0},{25,1},{26,2},{27,3},{28,4},{29,5},{30,6},{31,7},{0,8},{1,9... | collective-permute-start | bytes 589832 | tf_op jit(solution)/shard_map/ppermute | solution.py:875
  18.0 26.6 %collective-permute-start.5 = (bf16[512,1024]{1,0:T(8,128)(2,1)}, bf16[512,1024]{1,0:T(8,128)(2,1)S(1)}, u32[]{:S(2)}, u32[]{:S(2)}) collective-permute-start(bf16[512,1024]{1,0:T(8,128)(2,1)} %pad_maximum_fusion), channel_id=1, source_target_pairs={{1,0},{0,1},{3,2},{2,3},{5,4},{4,5},{7,6},{6,7},{9,8},{8,9},{11,10... | collective-permute-start | bytes 3145736 | tf_op jit(solution)/shard_map/ppermute | solution.py:898
  19.5 25.1 %collective-permute-start.6 = (f32[24,128]{1,0:T(8,128)S(1)}, f32[24,128]{1,0:T(8,128)S(1)}, u32[]{:S(2)}, u32[]{:S(2)}) collective-permute-start(f32[24,128]{1,0:T(8,128)S(1)} %maximum_bitcast_fusion.1), channel_id=1, source_target_pairs={{1,0},{0,1},{3,2},{2,3},{5,4},{4,5},{7,6},{6,7},{9,8},{8,9},{11,10... | collective-permute-start | bytes 36872 | tf_op jit(solution)/shard_map/ppermute | solution.py:898
  20.9 88.9 %all-gather.5.cloned.1.call-start = ((), (), s32[]{:S(2)}) async-start(), calls=%async_computation.4 | async-start | bytes 1310720 | tf_op jit(solution)/shard_map/all_gather | solution.py:893
  30.0 29.4 %collective-permute-start.3 = (bf16[256,1536]{1,0:T(8,128)(2,1)S(1)}, bf16[256,1536]{1,0:T(8,128)(2,1)S(1)}, u32[]{:S(2)}, u32[]{:S(2)}) collective-permute-start(bf16[256,1536]{1,0:T(8,128)(2,1)S(1)} %constant_dynamic-update-slice_fusion.refs_0_.refs_5_), channel_id=1, source_target_pairs={{1,0},{0,1},{3,2},{2,3},{5,4},{4,5},{7,6},{6,7},{9,8},{8,9},{11,10... | collective-permute-start | bytes 2359304 | tf_op jit(solution)/shard_map/ppermute | solution.py:898
  31.6 27.8 %collective-permute-start.4 = (bf16[256,1536]{1,0:T(8,128)(2,1)S(1)}, bf16[256,1536]{1,0:T(8,128)(2,1)S(1)}, u32[]{:S(2)}, u32[]{:S(2)}) collective-permute-start(bf16[256,1536]{1,0:T(8,128)(2,1)S(1)} %constant_dynamic-update-slice_fusion.refs_0_.refs_5_), channel_id=1, source_target_pairs={{4,0},{5,1},{6,2},{7,3},{0,4},{1,5},{2,6},{3,7},{12,8},{13,9},{14,... | collective-permute-start | bytes 2359304 | tf_op jit(solution)/shard_map/ppermute | solution.py:901
  59.5 13.6 %collective-permute-start.9 = (bf16[256,1536]{1,0:T(8,128)(2,1)S(1)}, bf16[256,1536]{1,0:T(8,128)(2,1)S(1)}, u32[]{:S(2)}, u32[]{:S(2)}) collective-permute-start(bf16[256,1536]{1,0:T(8,128)(2,1)S(1)} %constant_dynamic-update-slice_fusion.refs_0_.refs_5_), channel_id=1, source_target_pairs={{2,0},{3,1},{0,2},{1,3},{6,4},{7,5},{4,6},{5,7},{10,8},{11,9},{8,1... | collective-permute-start | bytes 2359304 | tf_op jit(solution)/shard_map/ppermute | solution.py:904
  59.5 13.5 %collective-permute-start.10 = (bf16[256,1536]{1,0:T(8,128)(2,1)S(1)}, bf16[256,1536]{1,0:T(8,128)(2,1)S(1)}, u32[]{:S(2)}, u32[]{:S(2)}) collective-permute-start(bf16[256,1536]{1,0:T(8,128)(2,1)S(1)} %collective-permute-done.3.refs_1_.refs_6_), channel_id=1, source_target_pairs={{2,0},{3,1},{0,2},{1,3},{6,4},{7,5},{4,6},{5,7},{10,8},{11,9},{8,1... | collective-permute-start | bytes 2359304 | tf_op jit(solution)/shard_map/ppermute | solution.py:904
  60.0 13.0 %collective-permute-start.11 = (bf16[256,1536]{1,0:T(8,128)(2,1)S(1)}, bf16[256,1536]{1,0:T(8,128)(2,1)S(1)}, u32[]{:S(2)}, u32[]{:S(2)}) collective-permute-start(bf16[256,1536]{1,0:T(8,128)(2,1)S(1)} %collective-permute-done.4.refs_2_.refs_7_), channel_id=1, source_target_pairs={{2,0},{3,1},{0,2},{1,3},{6,4},{7,5},{4,6},{5,7},{10,8},{11,9},{8,1... | collective-permute-start | bytes 2359304 | tf_op jit(solution)/shard_map/ppermute | solution.py:904
  60.2 11.6 %collective-permute-start.7 = (bf16[128,1536]{1,0:T(8,128)(2,1)S(1)}, bf16[128,1536]{1,0:T(8,128)(2,1)}, u32[]{:S(2)}, u32[]{:S(2)}) collective-permute-start(bf16[128,1536]{1,0:T(8,128)(2,1)S(1)} %slice.145), channel_id=1, source_target_pairs={{1,0},{0,1},{3,2},{2,3},{5,4},{4,5},{7,6},{6,7},{9,8},{8,9},{11,10... | collective-permute-start | bytes 1179656 | tf_op jit(solution)/shard_map/ppermute | solution.py:898
  74.1 30.2 %collective-permute-start.12 = (bf16[256,2560]{1,0:T(8,128)(2,1)}, bf16[256,2560]{1,0:T(8,128)(2,1)S(1)}, u32[]{:S(2)}, u32[]{:S(2)}) collective-permute-start(bf16[256,2560]{1,0:T(8,128)(2,1)} %all-gather.3.cloned.1.call-done.refs_0_.refs_4_), channel_id=1, source_target_pairs={{1,0},{0,1},{3,2},{2,3},{5,4},{4,5},{7,6},{6,7},{9,8},{8,9},{11,10... | collective-permute-start | bytes 3932168 | tf_op jit(solution)/shard_map/ppermute | solution.py:898
  75.0 30.2 %collective-permute-start.13 = (bf16[256,2560]{1,0:T(8,128)(2,1)}, bf16[256,2560]{1,0:T(8,128)(2,1)S(1)}, u32[]{:S(2)}, u32[]{:S(2)}) collective-permute-start(bf16[256,2560]{1,0:T(8,128)(2,1)} %all-gather.3.cloned.1.call-done.refs_0_.refs_4_), channel_id=1, source_target_pairs={{4,0},{5,1},{6,2},{7,3},{0,4},{1,5},{2,6},{3,7},{12,8},{13,9},{14,... | collective-permute-start | bytes 3932168 | tf_op jit(solution)/shard_map/ppermute | solution.py:901
  77.0 277.9 %reduce-scatter.5.cloned.1.call-start = ((), (), s32[]{:S(2)}) async-start(), calls=%async_computation.6 | async-start | bytes 1310720 | tf_op jit(solution)/shard_map/reduce_scatter | solution.py:884
  105.2 20.3 %collective-permute-start.19 = (bf16[256,2560]{1,0:T(8,128)(2,1)}, bf16[256,2560]{1,0:T(8,128)(2,1)}, u32[]{:S(2)}, u32[]{:S(2)}) collective-permute-start(bf16[256,2560]{1,0:T(8,128)(2,1)} %all-gather.3.cloned.1.call-done.refs_0_.refs_4_), channel_id=1, source_target_pairs={{2,0},{3,1},{0,2},{1,3},{6,4},{7,5},{4,6},{5,7},{10,8},{11,9},{8,1... | collective-permute-start | bytes 3932168 | tf_op jit(solution)/shard_map/ppermute | solution.py:904
  105.2 20.3 %collective-permute-start.20 = (bf16[256,2560]{1,0:T(8,128)(2,1)S(1)}, bf16[256,2560]{1,0:T(8,128)(2,1)}, u32[]{:S(2)}, u32[]{:S(2)}) collective-permute-start(bf16[256,2560]{1,0:T(8,128)(2,1)S(1)} %collective-permute-done.12.refs_1_.refs_5_), channel_id=1, source_target_pairs={{2,0},{3,1},{0,2},{1,3},{6,4},{7,5},{4,6},{5,7},{10,8},{11,9},{8,1... | collective-permute-start | bytes 3932168 | tf_op jit(solution)/shard_map/ppermute | solution.py:904
  105.7 19.8 %collective-permute-start.21 = (bf16[256,2560]{1,0:T(8,128)(2,1)S(1)}, bf16[256,2560]{1,0:T(8,128)(2,1)}, u32[]{:S(2)}, u32[]{:S(2)}) collective-permute-start(bf16[256,2560]{1,0:T(8,128)(2,1)S(1)} %collective-permute-done.13.refs_2_.refs_6_), channel_id=1, source_target_pairs={{2,0},{3,1},{0,2},{1,3},{6,4},{7,5},{4,6},{5,7},{10,8},{11,9},{8,1... | collective-permute-start | bytes 3932168 | tf_op jit(solution)/shard_map/ppermute | solution.py:904
  107.5 17.4 %collective-permute-start.17 = (bf16[128,2560]{1,0:T(8,128)(2,1)}, bf16[128,2560]{1,0:T(8,128)(2,1)S(1)}, u32[]{:S(2)}, u32[]{:S(2)}) collective-permute-start(bf16[128,2560]{1,0:T(8,128)(2,1)} %slice.149), channel_id=1, source_target_pairs={{1,0},{0,1},{3,2},{2,3},{5,4},{4,5},{7,6},{6,7},{9,8},{8,9},{11,10... | collective-permute-start | bytes 1966088 | tf_op jit(solution)/shard_map/ppermute | solution.py:898
  108.3 17.2 %collective-permute-start.18 = (bf16[128,2560]{1,0:T(8,128)(2,1)}, bf16[128,2560]{1,0:T(8,128)(2,1)}, u32[]{:S(2)}, u32[]{:S(2)}) collective-permute-start(bf16[128,2560]{1,0:T(8,128)(2,1)} %slice.150), channel_id=1, source_target_pairs={{4,0},{5,1},{6,2},{7,3},{0,4},{1,5},{2,6},{3,7},{12,8},{13,9},{14,... | collective-permute-start | bytes 1966088 | tf_op jit(solution)/shard_map/ppermute | solution.py:901
  125.6 28.0 %collective-permute-start.22 = (bf16[256,2048]{1,0:T(8,128)(2,1)}, bf16[256,2048]{1,0:T(8,128)(2,1)}, u32[]{:S(2)}, u32[]{:S(2)}) collective-permute-start(bf16[256,2048]{1,0:T(8,128)(2,1)} %all-gather.5.cloned.1.call-done.refs_0_.refs_5_), channel_id=1, source_target_pairs={{1,0},{0,1},{3,2},{2,3},{5,4},{4,5},{7,6},{6,7},{9,8},{8,9},{11,10... | collective-permute-start | bytes 3145736 | tf_op jit(solution)/shard_map/ppermute | solution.py:898
  126.8 26.8 %collective-permute-start.23 = (bf16[256,2048]{1,0:T(8,128)(2,1)}, bf16[256,2048]{1,0:T(8,128)(2,1)}, u32[]{:S(2)}, u32[]{:S(2)}) collective-permute-start(bf16[256,2048]{1,0:T(8,128)(2,1)} %all-gather.5.cloned.1.call-done.refs_0_.refs_5_), channel_id=1, source_target_pairs={{4,0},{5,1},{6,2},{7,3},{0,4},{1,5},{2,6},{3,7},{12,8},{13,9},{14,... | collective-permute-start | bytes 3145736 | tf_op jit(solution)/shard_map/ppermute | solution.py:901
  153.6 19.7 %collective-permute-start.29 = (bf16[512,4096]{1,0:T(8,128)(2,1)}, bf16[512,4096]{1,0:T(8,128)(2,1)}, u32[]{:S(2)}, u32[]{:S(2)}) collective-permute-start(bf16[512,4096]{1,0:T(8,128)(2,1)} %get-tuple-element.281.refs_2_.refs_0_), channel_id=1, source_target_pairs={{2,0},{3,1},{0,2},{1,3},{6,4},{7,5},{4,6},{5,7},{10,8},{11,9},{8,1... | collective-permute-start | bytes 12582920 | tf_op jit(solution)/shard_map/ppermute | solution.py:904
  153.8 17.5 %collective-permute-start.30 = (bf16[256,2048]{1,0:T(8,128)(2,1)S(1)}, bf16[256,2048]{1,0:T(8,128)(2,1)S(1)}, u32[]{:S(2)}, u32[]{:S(2)}) collective-permute-start(bf16[256,2048]{1,0:T(8,128)(2,1)S(1)} %copy-done.11), channel_id=1, source_target_pairs={{2,0},{3,1},{0,2},{1,3},{6,4},{7,5},{4,6},{5,7},{10,8},{11,9},{8,1... | collective-permute-start | bytes 3145736 | tf_op jit(solution)/shard_map/ppermute | solution.py:904
  154.2 18.2 %collective-permute-start.31 = (bf16[256,2048]{1,0:T(8,128)(2,1)}, bf16[256,2048]{1,0:T(8,128)(2,1)S(1)}, u32[]{:S(2)}, u32[]{:S(2)}) collective-permute-start(bf16[256,2048]{1,0:T(8,128)(2,1)} %collective-permute-done.22.refs_1_.refs_6_), channel_id=1, source_target_pairs={{2,0},{3,1},{0,2},{1,3},{6,4},{7,5},{4,6},{5,7},{10,8},{11,9},{8,1... | collective-permute-start | bytes 3145736 | tf_op jit(solution)/shard_map/ppermute | solution.py:904
  156.5 14.3 %collective-permute-start.27 = (bf16[128,2048]{1,0:T(8,128)(2,1)S(1)}, bf16[128,2048]{1,0:T(8,128)(2,1)S(1)}, u32[]{:S(2)}, u32[]{:S(2)}) collective-permute-start(bf16[128,2048]{1,0:T(8,128)(2,1)S(1)} %slice.155), channel_id=1, source_target_pairs={{1,0},{0,1},{3,2},{2,3},{5,4},{4,5},{7,6},{6,7},{9,8},{8,9},{11,10... | collective-permute-start | bytes 1572872 | tf_op jit(solution)/shard_map/ppermute | solution.py:898
  157.4 13.9 %collective-permute-start.28 = (bf16[128,2048]{1,0:T(8,128)(2,1)S(1)}, bf16[128,2048]{1,0:T(8,128)(2,1)S(1)}, u32[]{:S(2)}, u32[]{:S(2)}) collective-permute-start(bf16[128,2048]{1,0:T(8,128)(2,1)S(1)} %slice.156), channel_id=1, source_target_pairs={{4,0},{5,1},{6,2},{7,3},{0,4},{1,5},{2,6},{3,7},{12,8},{13,9},{14,... | collective-permute-start | bytes 1572872 | tf_op jit(solution)/shard_map/ppermute | solution.py:901
  173.3 11.6 %collective-permute-start.32 = (bf16[256,2048]{1,0:T(8,128)(2,1)}, bf16[256,2048]{1,0:T(8,128)(2,1)S(1)}, u32[]{:S(2)}, u32[]{:S(2)}) collective-permute-start(bf16[256,2048]{1,0:T(8,128)(2,1)} %collective-permute-done.23.refs_2_.refs_7_), channel_id=1, source_target_pairs={{2,0},{3,1},{0,2},{1,3},{6,4},{7,5},{4,6},{5,7},{10,8},{11,9},{8,1... | collective-permute-start | bytes 3145736 | tf_op jit(solution)/shard_map/ppermute | solution.py:904
  173.3 11.5 %collective-permute-start.33 = (bf16[128,2048]{1,0:T(8,128)(2,1)S(1)}, bf16[128,2048]{1,0:T(8,128)(2,1)S(1)}, u32[]{:S(2)}, u32[]{:S(2)}) collective-permute-start(bf16[128,2048]{1,0:T(8,128)(2,1)S(1)} %collective-permute-done.27.refs_3_.refs_8_), channel_id=1, source_target_pairs={{2,0},{3,1},{0,2},{1,3},{6,4},{7,5},{4,6},{5,7},{10,8},{11,9},{8,1... | collective-permute-start | bytes 1572872 | tf_op jit(solution)/shard_map/ppermute | solution.py:904
  185.8 25.7 %collective-permute-start.36 = (bf16[256,2048]{1,0:T(8,128)(2,1)}, bf16[256,2048]{1,0:T(8,128)(2,1)S(1)}, u32[]{:S(2)}, u32[]{:S(2)}) collective-permute-start(bf16[256,2048]{1,0:T(8,128)(2,1)} %get-tuple-element.243), channel_id=1, source_target_pairs={{1,0},{0,1},{3,2},{2,3},{5,4},{4,5},{7,6},{6,7},{9,8},{8,9},{11,10... | collective-permute-start | bytes 3145736 | tf_op jit(solution)/shard_map/ppermute | solution.py:898
  187.0 25.1 %collective-permute-start.37 = (bf16[256,2048]{1,0:T(8,128)(2,1)}, bf16[256,2048]{1,0:T(8,128)(2,1)S(1)}, u32[]{:S(2)}, u32[]{:S(2)}) collective-permute-start(bf16[256,2048]{1,0:T(8,128)(2,1)} %get-tuple-element.244), channel_id=1, source_target_pairs={{4,0},{5,1},{6,2},{7,3},{0,4},{1,5},{2,6},{3,7},{12,8},{13,9},{14,... | collective-permute-start | bytes 3145736 | tf_op jit(solution)/shard_map/ppermute | solution.py:901
  216.0 21.7 %collective-permute-start.40 = (bf16[128,2048]{1,0:T(8,128)(2,1)}, bf16[128,2048]{1,0:T(8,128)(2,1)S(1)}, u32[]{:S(2)}, u32[]{:S(2)}) collective-permute-start(bf16[128,2048]{1,0:T(8,128)(2,1)} %get-tuple-element.261), channel_id=1, source_target_pairs={{4,0},{5,1},{6,2},{7,3},{0,4},{1,5},{2,6},{3,7},{12,8},{13,9},{14,... | collective-permute-start | bytes 1572872 | tf_op jit(solution)/shard_map/ppermute | solution.py:901
  217.3 20.5 %collective-permute-start.41 = (bf16[128,2048]{1,0:T(8,128)(2,1)}, bf16[128,2048]{1,0:T(8,128)(2,1)S(1)}, u32[]{:S(2)}, u32[]{:S(2)}) collective-permute-start(bf16[128,2048]{1,0:T(8,128)(2,1)} %get-tuple-element.262), channel_id=1, source_target_pairs={{1,0},{0,1},{3,2},{2,3},{5,4},{4,5},{7,6},{6,7},{9,8},{8,9},{11,10... | collective-permute-start | bytes 1572872 | tf_op jit(solution)/shard_map/ppermute | solution.py:898
  237.7 33.5 %collective-permute-start.42 = (bf16[256,2560]{1,0:T(8,128)(2,1)}, bf16[256,2560]{1,0:T(8,128)(2,1)}, u32[]{:S(2)}, u32[]{:S(2)}) collective-permute-start(bf16[256,2560]{1,0:T(8,128)(2,1)} %get-tuple-element.267), channel_id=1, source_target_pairs={{1,0},{0,1},{3,2},{2,3},{5,4},{4,5},{7,6},{6,7},{9,8},{8,9},{11,10... | collective-permute-start | bytes 3932168 | tf_op jit(solution)/shard_map/ppermute | solution.py:898
  239.0 32.3 %collective-permute-start.43 = (bf16[256,2560]{1,0:T(8,128)(2,1)}, bf16[256,2560]{1,0:T(8,128)(2,1)}, u32[]{:S(2)}, u32[]{:S(2)}) collective-permute-start(bf16[256,2560]{1,0:T(8,128)(2,1)} %get-tuple-element.268), channel_id=1, source_target_pairs={{4,0},{5,1},{6,2},{7,3},{0,4},{1,5},{2,6},{3,7},{12,8},{13,9},{14,... | collective-permute-start | bytes 3932168 | tf_op jit(solution)/shard_map/ppermute | solution.py:901
  271.3 20.2 %collective-permute-start.44 = (bf16[3,512,1024]{2,1,0:T(8,128)(2,1)S(1)}, bf16[3,512,1024]{2,1,0:T(8,128)(2,1)}, u32[]{:S(2)}, u32[]{:S(2)}) collective-permute-start(bf16[3,512,1024]{2,1,0:T(8,128)(2,1)S(1)} %copy-done.2), channel_id=1, source_target_pairs={{2,0},{3,1},{0,2},{1,3},{6,4},{7,5},{4,6},{5,7},{10,8},{11,9},{8,1... | collective-permute-start | bytes 9437192 | tf_op jit(solution)/shard_map/ppermute | solution.py:904
  271.5 102.4 %reduce-scatter.3.cloned.1.call-start = ((), (), s32[]{:S(2)}) async-start(), calls=%async_computation.5 | async-start | bytes 1638400 | tf_op jit(solution)/shard_map/reduce_scatter | solution.py:884
  275.7 24.3 %collective-permute-start.45 = (bf16[128,2560]{1,0:T(8,128)(2,1)}, bf16[128,2560]{1,0:T(8,128)(2,1)}, u32[]{:S(2)}, u32[]{:S(2)}) collective-permute-start(bf16[128,2560]{1,0:T(8,128)(2,1)} %get-tuple-element.291), channel_id=1, source_target_pairs={{4,0},{5,1},{6,2},{7,3},{0,4},{1,5},{2,6},{3,7},{12,8},{13,9},{14,... | collective-permute-start | bytes 1966088 | tf_op jit(solution)/shard_map/ppermute | solution.py:901
  276.9 23.1 %collective-permute-start.46 = (bf16[128,2560]{1,0:T(8,128)(2,1)}, bf16[128,2560]{1,0:T(8,128)(2,1)}, u32[]{:S(2)}, u32[]{:S(2)}) collective-permute-start(bf16[128,2560]{1,0:T(8,128)(2,1)} %get-tuple-element.292), channel_id=1, source_target_pairs={{1,0},{0,1},{3,2},{2,3},{5,4},{4,5},{7,6},{6,7},{9,8},{8,9},{11,10... | collective-permute-start | bytes 1966088 | tf_op jit(solution)/shard_map/ppermute | solution.py:898
  300.0 20.2 %collective-permute-start.47 = (bf16[256,1536]{1,0:T(8,128)(2,1)}, bf16[256,1536]{1,0:T(8,128)(2,1)S(1)}, u32[]{:S(2)}, u32[]{:S(2)}) collective-permute-start(bf16[256,1536]{1,0:T(8,128)(2,1)} %get-tuple-element.294), channel_id=1, source_target_pairs={{1,0},{0,1},{3,2},{2,3},{5,4},{4,5},{7,6},{6,7},{9,8},{8,9},{11,10... | collective-permute-start | bytes 2359304 | tf_op jit(solution)/shard_map/ppermute | solution.py:898
  301.3 19.3 %collective-permute-start.48 = (bf16[256,1536]{1,0:T(8,128)(2,1)}, bf16[256,1536]{1,0:T(8,128)(2,1)S(1)}, u32[]{:S(2)}, u32[]{:S(2)}) collective-permute-start(bf16[256,1536]{1,0:T(8,128)(2,1)} %get-tuple-element.295), channel_id=1, source_target_pairs={{4,0},{5,1},{6,2},{7,3},{0,4},{1,5},{2,6},{3,7},{12,8},{13,9},{14,... | collective-permute-start | bytes 2359304 | tf_op jit(solution)/shard_map/ppermute | solution.py:901
  306.2 20.3 %collective-permute-start.54 = (f32[96,128]{1,0:T(8,128)S(1)}, f32[96,128]{1,0:T(8,128)S(1)}, u32[]{:S(2)}, u32[]{:S(2)}) collective-permute-start(f32[96,128]{1,0:T(8,128)S(1)} %fusion.46), channel_id=1, source_target_pairs={{1,0},{0,1},{3,2},{2,3},{5,4},{4,5},{7,6},{6,7},{9,8},{8,9},{11,10... | collective-permute-start | bytes 147464 | tf_op jit(solution)/shard_map/ppermute | solution.py:898
  324.6 17.4 %collective-permute-start.49 = (bf16[128,1536]{1,0:T(8,128)(2,1)}, bf16[128,1536]{1,0:T(8,128)(2,1)S(1)}, u32[]{:S(2)}, u32[]{:S(2)}) collective-permute-start(bf16[128,1536]{1,0:T(8,128)(2,1)} %get-tuple-element.307), channel_id=1, source_target_pairs={{4,0},{5,1},{6,2},{7,3},{0,4},{1,5},{2,6},{3,7},{12,8},{13,9},{14,... | collective-permute-start | bytes 1179656 | tf_op jit(solution)/shard_map/ppermute | solution.py:901
  325.3 16.6 %collective-permute-start.50 = (bf16[128,1536]{1,0:T(8,128)(2,1)}, bf16[128,1536]{1,0:T(8,128)(2,1)S(1)}, u32[]{:S(2)}, u32[]{:S(2)}) collective-permute-start(bf16[128,1536]{1,0:T(8,128)(2,1)} %get-tuple-element.308), channel_id=1, source_target_pairs={{1,0},{0,1},{3,2},{2,3},{5,4},{4,5},{7,6},{6,7},{9,8},{8,9},{11,10... | collective-permute-start | bytes 1179656 | tf_op jit(solution)/shard_map/ppermute | solution.py:898
  346.4 26.5 %all-to-all-start = ((bf16[4,64,1536]{2,1,0:T(8,128)(2,1)}), bf16[4,64,1536]{2,1,0:T(8,128)(2,1)S(1)}, u32[]{:S(2)}, u32[]{:S(2)}) async-start(bf16[4,64,1536]{2,1,0:T(8,128)(2,1)} %bitcast.53), calls=%async_computation | async-start | bytes 1572864 | tf_op jit(solution)/shard_map/all_to_all | solution.py:889
  350.6 14.9 %collective-permute-start.52 = (bf16[256,1024]{1,0:T(8,128)(2,1)S(1)}, bf16[256,1024]{1,0:T(8,128)(2,1)S(1)}, u32[]{:S(2)}, u32[]{:S(2)}) collective-permute-start(bf16[256,1024]{1,0:T(8,128)(2,1)S(1)} %copy-done.43), channel_id=1, source_target_pairs={{1,0},{0,1},{3,2},{2,3},{5,4},{4,5},{7,6},{6,7},{9,8},{8,9},{11,10... | collective-permute-start | bytes 1572872 | tf_op jit(solution)/shard_map/ppermute | solution.py:898
  354.9 16.8 %collective-permute-start.51 = (bf16[256,1024]{1,0:T(8,128)(2,1)S(1)}, bf16[256,1024]{1,0:T(8,128)(2,1)S(1)}, u32[]{:S(2)}, u32[]{:S(2)}) collective-permute-start(bf16[256,1024]{1,0:T(8,128)(2,1)S(1)} %copy-done.44), channel_id=1, source_target_pairs={{1,0},{0,1},{3,2},{2,3},{5,4},{4,5},{7,6},{6,7},{9,8},{8,9},{11,10... | collective-permute-start | bytes 1572872 | tf_op jit(solution)/shard_map/ppermute | solution.py:898
  (64 other events, 490.9 us)
Sparse Core Ops, SparseCore 0:
  21.0 33.1 all-gather.2
  77.1 27.5 all-gather.4
  271.6 27.1 reduce-scatter.4
  306.3 31.2 reduce-scatter.2

commit v5 on v4

--- a/solution.py
+++ b/solution.py
@@ -678,7 +678,7 @@
 
     def finish(acc_ref, ins, outs):
         y_ref, e_ref, gain_ref = ins
-        mid_ref, da_ref, dat_ref, sum_ref = outs
+        mid_ref, da_ref, dat_ref, dat_far_ref, sum_ref = outs
         sums = [jnp.zeros((1, width), f32)] * 4
         for part in range(2):
             here = pl.ds(part * half, half)
@@ -689,7 +689,8 @@
             mid_ref[here, :] = mid
             mid_b = mid.astype(bf16)
             da_ref[here, :] = mid_b
-            dat_ref[:, here] = mid_b.T
+            dat_ref[:, here] = mid_b[:, : width // 2].T
+            dat_far_ref[:, here] = mid_b[:, width // 2 :].T
             terms = (grad * unit, grad, mid, e_rows)
             sums = [s + jnp.sum(term, axis=0, keepdims=True) for s, term in zip(sums, terms)]
         sum_ref[...] = jnp.concatenate(sums, axis=0)
@@ -705,7 +706,8 @@
         [
             array(length, width, dtype=f32),
             array(length, width),
-            array(width, length),
+            array(width // 2, length),
+            array(width // 2, length),
             array(4, width, dtype=f32),
         ],
     )
@@ -789,14 +791,24 @@
     )(qkv, qkv, qkv, grads, lse_rows)
 
 
-def both_sides(args, specs, kinds, terms, name, tiles):
+def both_sides(args, specs, kinds, terms, name, tiles, z_first=0):
     count = len(args)
     half = args[0].shape[0] // 2
     mid = half // 4
+    kept = tiles - 1 if z_first else tiles
 
     def body(*refs):
-        x_ref, y_ref, k10_ref, k00_ref, k01_ref = refs[count:]
+        x_ref, y_ref, k10_ref, k00_ref, k01_ref = refs[count : count + 5]
         step = pl.program_id(0)
+
+        def apart(kind):
+            left, right = terms(refs[:count], kind)
+            acc = nn_dot(left, right).astype(bf16)
+            size = acc.shape[0] // 2 // z_first
+            for z in range(z_first):
+                for ky in range(2):
+                    first = (ky * z_first + z) * size
+                    refs[-1][z, 0, pl.ds(ky * size, size), :] = acc[first : first + size]
 
         def run(kind, side):
             left, right = terms(refs[:count], kind)
@@ -814,21 +826,27 @@
             for kind, first in enumerate(kinds):
                 last = kinds[kind + 1] if kind + 1 < len(kinds) else tiles
                 base = 0 if side else tiles
-                here = (step >= base + first) & (step < base + last)
+                here = (step >= base + first) & (step < base + min(last, kept))
                 pl.when(here)(partial(run, kind, side))
-
-    far = lambda size: pl.BlockSpec((size, TILE), lambda s: (0, jnp.minimum(s, tiles - 1)))
-    near = lambda size: pl.BlockSpec((size, TILE), lambda s: (0, jnp.maximum(s - tiles, 0)))
-    both = pl.BlockSpec((mid, TILE), lambda s: (s // tiles, s % tiles))
+        if z_first:
+            pl.when(step % tiles == tiles - 1)(partial(apart, len(kinds) - 1))
+
+    most = kept - 1
+    far = lambda size: pl.BlockSpec((size, TILE), lambda s: (0, jnp.minimum(s, most)))
+    near = lambda size: pl.BlockSpec(
+        (size, TILE), lambda s: (0, jnp.minimum(jnp.maximum(s - tiles, 0), most))
+    )
+    both = pl.BlockSpec((mid, TILE), lambda s: (s // tiles, jnp.minimum(s % tiles, most)))
     sizes = (2 * mid, 2 * mid, mid, 2 * mid, mid)
-    return kernel_call(
-        body,
-        name,
-        (2 * tiles,),
-        specs,
-        [far(2 * mid), both, far(mid), near(2 * mid), near(mid)],
-        [array(size, tiles * TILE) for size in sizes],
-    )(*args)
+    out_specs = [far(2 * mid), both, far(mid), near(2 * mid), near(mid)]
+    shapes = [array(size, kept * TILE) for size in sizes]
+    if z_first:
+        each = half // z_first
+        out_specs.append(
+            pl.BlockSpec((z_first, 1, each, TILE), lambda s: (0, 1 - s // tiles, 0, 0))
+        )
+        shapes.append(array(z_first, 2, each, TILE))
+    return kernel_call(body, name, (2 * tiles,), specs, out_specs, shapes)(*args)
 
 
 def add_mid_kernel(k01_ref, rx_ref, k10_ref, ry_ref, y_ref, x_ref):
@@ -913,20 +931,10 @@
     return out if len(values) > 1 else out[0]
 
 
-def total_over_all(links, rows):
-    for move in (links.c, links.x, links.y):
-        rows = rows + move(rows)
-    bit = 1
-    while bit < links.nz:
-        rows = rows + links.flip(rows, bit)
-        bit *= 2
-    return rows
-
-
 def start_far(links, near):
     by_x, by_y = near
-    half = by_x.shape[0] // 2
-    return links.x(by_y[:half]), links.y(by_x[half:])
+    cut = by_x.shape[0] // 2
+    return links.x(by_y[:cut]), links.y(by_x[cut:])
 
 
 class Home:
@@ -988,11 +996,12 @@
     pick = lambda both, at: lax.dynamic_index_in_dim(both, at, 0, keepdims=False)
     row = lambda vector: vector.reshape(1, -1)
 
+    sent_rows = jnp.concatenate([pick(clips, 1 - t), pick(cotangent, 1 - t)], axis=0)
+    q_shard, sent_rows = after((), qkv_weight.reshape(block, qkv_cols), sent_rows)
     two_shard = jnp.concatenate([fc1_weight, proj_weight.T], axis=1)
     along_two = links.z_all(two_shard)
-    q_shard = qkv_weight.reshape(block, qkv_cols)
     steps_one = [links.from_z(q_shard, k) for k in range(1, links.nz)]
-    got_rows = links.x(jnp.concatenate([pick(clips, 1 - t), pick(cotangent, 1 - t)], axis=0))
+    got_rows = links.x(sent_rows)
     far_small = jnp.concatenate([q_bias, v_bias, fc1_bias]).reshape(-1, 128)
     far_small = links.x(far_small).reshape(-1)
 
@@ -1028,8 +1037,9 @@
     along_three = links.z_all(after(along_two, fc2_turned))
     far_one = start_far(links, near_one)
     other_one = [links.c(piece) for piece in (after(near_one, along_one), *near_one)]
-    far_one, other_one, along_two, twin_rows = after((), far_one, other_one, along_two, twin_rows)
+    other_one, along_two = after((), other_one, along_two)
     near_two = links.x(along_two), links.y(along_two)
+    far_one, twin_rows = after(other_one, far_one, twin_rows)
     other_one += [links.c(piece) for piece in far_one]
     twin_rows = links.c(twin_rows)
     twin_rows, other_one = after((), twin_rows, other_one)
@@ -1050,12 +1060,11 @@
     near_two, lse_rows = after(attn, near_two, lse.T)
     far_two = start_far(links, near_two)
     other_two = [links.c(piece) for piece in (after(near_two, along_two), *near_two)]
-    far_two, other_two, along_three, attn_sent = after((), far_two, other_two, along_three, attn)
+    other_two, along_three = after((), other_two, along_three)
 
     near_three = links.x(along_three), links.y(along_three)
+    far_two = after(other_two, far_two)
     other_two += [links.c(piece) for piece in far_two]
-    twin_attn = links.c(attn_sent)
-    other_two, twin_attn = after((), other_two, twin_attn)
     w_two = [along_two, *near_two, *far_two, *other_two]
     y, h2, h2_t = join_heads(attn, x, w_two, hidden_here, outs[0], gains[1], shifts[1])
     hidden, slope = expand(h2, w_two, fc1_biases, hidden_here)
@@ -1066,10 +1075,11 @@
     far_three = start_far(links, near_three)
     twin_hidden = links.c(hidden)
     other_three = [links.c(piece) for piece in (along_three, near_three[0])]
-    far_three, twin_hidden, other_three, near_three, h2_sent = after(
-        (), far_three, twin_hidden, other_three, near_three, h2_t[half:]
-    )
-
+    far_three, twin_hidden, other_three, near_three, h2_sent, attn_sent = after(
+        (), far_three, twin_hidden, other_three, near_three, h2_t[half:], attn
+    )
+
+    quarter = width // 8
     stack = lambda one, two: jnp.concatenate([one[...], two[...]], axis=0)
     join = lambda one, two: jnp.concatenate([one[...], two[...]], axis=1)
     tiles = hidden_here // TILE
@@ -1108,7 +1118,7 @@
         args = [h1_t, twin_rows, dp, twin_dp]
         dp_spec = pl.BlockSpec((1, length, TILE), lambda s: (s % 3, 0, 1 - s // 3))
         specs = [left_at(0), left_at(1)] + [dp_spec] * 2
-        return both_sides(args, specs, (0,), terms, "grad_qkv", 3)
+        return both_sides(args, specs, (0,), terms, "grad_qkv", 3, links.nz)
 
     def enter_window(done, *homes):
         for home in homes:
@@ -1119,14 +1129,19 @@
     other_three += [links.c(piece) for piece in (near_three[1], *far_three)]
     twin_h2 = links.c(h2_sent)
     pieces = grad_fc2()
-    pieces, other_three, twin_h2 = after((), pieces, other_three, twin_h2)
+    pieces, other_three, twin_h2, attn_sent = after(
+        (), pieces, other_three, twin_h2, attn_sent
+    )
     w_fc2 = [along_three, *near_three, *far_three, *other_three]
 
     home_fc2.first(pieces)
+    twin_attn = links.c(attn_sent)
     du, fc1b_sum = hidden_back(e, slope, w_fc2)
-    mid, da, da_t, second_sums = second_back(du, w_two, hidden_here, y, e, gains[1])
+    mid, da, da_t, da_t_far, second_sums = second_back(du, w_two, hidden_here, y, e, gains[1])
     enter_window(da, home_fc2)
-    du, da, da_t, da_t_far = after(home_fc2.x_got, du, da, da_t, da_t[half:])
+    du, da, da_t, da_t_far, twin_attn = after(
+        home_fc2.x_got, du, da, da_t, da_t_far, twin_attn
+    )
 
     twin_du = links.c(du)
     twin_da = links.c(da_t_far)
@@ -1145,31 +1160,16 @@
         dp, w_one, x, mid, gains[0], order_b
     )
     enter_window(grad_near, home_two)
-    dp = after(home_two.x_got, dp)
+    dp, first_sums = after(home_two.x_got, dp, first_sums)
 
     twin_dp = links.c(dp)
-    home_two.second(*home_two.middle())
-    out_near, out_sent = layer_out(after(dp, hidden), w_fc2, y, outs[1], live, order_b)
-    twin_dp = after(out_near, twin_dp)
-    pieces = grad_qkv()
-    pieces, home_two.y_last, home_two.x_last = after(
-        (), pieces, home_two.y_last, home_two.x_last
-    )
-
-    home_qkv.first(pieces)
-    moved = home_two.last(pieces, True)
-    enter_window(moved, home_qkv)
-    moved, grad_sent_rows = after((), home_qkv.middle(), grad_sent_rows)
-    home_qkv.second(*moved)
-    grad_got = links.x(grad_sent_rows)
-    moved = home_qkv.last((), False)
-    out_got = links.x(after(moved, out_sent))
-
+    moved = home_two.middle()
+    home_two.second(*moved)
     sums = jnp.concatenate(
         [first_sums[:1], second_sums[:1], first_sums[1:], second_sums[1:]], axis=0
     )
     sums = lax.dot_general(
-        sums, order_f, (((1,), (1,)), ((), ())), precision=lax.Precision.HIGHEST
+        after(moved, sums), order_f, (((1,), (1,)), ((), ())), precision=lax.Precision.HIGHEST
     )
 
     def placed(both):
@@ -1177,11 +1177,52 @@
         return jnp.where(t == 0, both[0], jnp.concatenate([both[0, size:], both[0, :size]]))
 
     small = [sums.reshape(-1), placed(q_sums), placed(v_sums), placed(fc1b_sum)]
-    small = total_over_all(links, jnp.concatenate(small).reshape(-1, 128)).reshape(-1) * grad_scale
+    small = jnp.concatenate(small).reshape(-1, 128)
+    small_got = links.c(after(moved, small))
+    twin_dp, small_got = after(moved, twin_dp, small_got)
+    small = small + small_got
+    small_got = links.flip(small, 1)
+    *pieces, by_z = grad_qkv()
+    pieces, by_z, home_two.y_last, home_two.x_last, small, small_got = after(
+        (), pieces, by_z, home_two.y_last, home_two.x_last, small, small_got
+    )
+
+    home_qkv.first(pieces)
+    by_z = links.z_sum(by_z.reshape(-1, heads_cols))
+    small = small + small_got
+    small_got = links.x(small)
+    moved = home_two.last(pieces, True)
+    enter_window(moved, home_qkv)
+    moved, small, small_got, hidden_out, grad_sent_rows = after(
+        (), home_qkv.middle(), small, small_got, hidden, grad_sent_rows
+    )
+
+    home_qkv.second(*moved)
+    grad_got = links.x(grad_sent_rows)
+    small = small + small_got
+    small_got = links.y(small)
+    out_near, out_sent = layer_out(hidden_out, w_fc2, y, outs[1], live, order_b)
+    moved = home_qkv.last(out_near, False)
+    moved, out_sent, small, small_got = after((), moved, out_sent, small, small_got)
+
+    by_z = jnp.sum(after(moved, by_z).astype(f32), axis=0)
+    v_got = links.x(by_z[quarter:].astype(bf16))
+    out_got = links.x(out_sent)
+    small = small + small_got
+    bit = 2
+    while bit < links.nz:
+        small = small + links.flip(small, bit)
+        bit *= 2
+    by_x = by_z[:quarter] + v_got.astype(f32)
+    by_x, small, out_got, grad_got, home_two.home, home_fc2.home = after(
+        (), by_x, small, out_got, grad_got, home_two.home, home_fc2.home
+    )
+    v_got = links.y(by_x[block:].astype(bf16))
+    g_v = (by_x[:block] + v_got.astype(f32)) * grad_scale
+    small = small.reshape(-1) * grad_scale
     sums = small[: 6 * width].reshape(6, width)
     own = lambda first, size: lax.dynamic_slice_in_dim(small, first + t * size, size, 0)
-
-    g_qkv = home_qkv.value((), grad_scale)
+    g_qkv = home_qkv.value(g_v, grad_scale)
     g_fc2 = home_fc2.value(moved, grad_scale)
     g_two = home_two.value(moved, grad_scale)
 
@@ -1191,7 +1232,7 @@
     return (
         both_slots(out_near, out_got),
         both_slots(grad_near, grad_got).astype(f32),
-        g_qkv.reshape(block, 3, heads_cols),
+        jnp.concatenate([g_qkv, g_v], axis=1).reshape(block, 3, heads_cols),
         own(6 * width, heads_cols),
         own(6 * width + 2 * heads_cols, heads_cols),
         g_two[:, hidden_here:].T,

time: 390 us -> 379 us (0.972)
  waiting for transfers between devices: 97.6 us -> 74.5 us
  starting transfers between devices: 52.8 us -> 69.2 us
    ppermute x17 -> x18, waiting for transfers between devices: 72.5 us -> 35.6 us  [x(): return lax.ppermute(rows, AXES, self.across)]
    all_to_all x1 -> x2, waiting for transfers between devices: 0.01 us -> 10.2 us  [z_sum(): lax.all_to_all(rows, AXES, 0, 0, tiled=True, axis_index_groups=self.z_gro...]
    all_to_all x1 -> x2, starting transfers between devices: 4.14 us -> 13 us  [z_sum(): lax.all_to_all(rows, AXES, 0, 0, tiled=True, axis_index_groups=self.z_gro...]
    ppermute x13 -> x14, waiting for transfers between devices: 11.9 us -> 4.48 us  [y(): return lax.ppermute(rows, AXES, self.beside)]
    ppermute x3, waiting for transfers between devices: 6.48 us -> 13.6 us  [from_z(): return lax.ppermute(rows, AXES, shift)]
    ppermute x13 -> x14, starting transfers between devices: 14.8 us -> 19.9 us  [y(): return lax.ppermute(rows, AXES, self.beside)]
    unnamed x98 -> x100, local copies, waits for them, and re-layouts: 11.2 us -> 8.79 us
    ppermute x17 -> x18, starting transfers between devices: 18.4 us -> 19.8 us  [x(): return lax.ppermute(rows, AXES, self.across)]
  transfers between devices with their start and end apart: 63 -> 66, of which waited for: 21 -> 22; matrix products, arithmetic and copies ran while one was open for 9% -> 8% of each run, Pallas kernels for 44% -> 45%
where the time goes in v5:
time: 379 us; the launch traced here: 372 us
  Pallas kernels  169 us (45%)
  waiting for transfers between devices  74.5 us (20%)
  starting transfers between devices  69.2 us (18%)
  local copies, waits for them, and re-layouts  30.4 us (8%)
  between operations  15.9 us (4%)
  other arithmetic  9.67 us (3%)
    ppermute x18, waiting for transfers between devices, x(): return lax.ppermute(rows, AXES, self.across)  35.6 us
    pallas_call x3, Pallas kernels, contract_back(): kernel_call(body, name, (2 * load.tiles,), rows_specs + [pl.BlockSpec(mem...  35.3 us
    pallas_call x3, Pallas kernels, both_sides(): kernel_call(body, name, (2 * tiles,), specs, out_specs, shapes)(*args)  33.2 us
    ppermute x14, starting transfers between devices, y(): return lax.ppermute(rows, AXES, self.beside)  19.9 us
    ppermute x18, starting transfers between devices, x(): return lax.ppermute(rows, AXES, self.across)  19.8 us
    pallas_call x6, Pallas kernels, small_call(): kernel_call(body, name, (1,), [whole(a.shape) for a in args], out_specs,...  18.6 us
    pallas_call x1, Pallas kernels, attend_bwd(): kernel_call(attend_back_kernel, 'attend_bwd', (width // PAIR,), [head_spe...  16.9 us
    ppermute x3, waiting for transfers between devices, from_z(): return lax.ppermute(rows, AXES, shift)  13.6 us
  transfers between devices with their start and end apart: 66, of which 22 were waited for; matrix products, arithmetic and copies ran while one was open for 8% of the time, Pallas kernels for 45%

profile of v5, /device:TPU:0, one launch (start us, length us, event | category | flops | bytes accessed | tf_op | source)
XLA Modules:
  0.0 371.9 jit_solution(852635926569073207)
XLA Ops:
  8.2 2.7 dynamic-slice_bitcast_fusion
  11.0 5.1 %collective-permute-start.2 = (bf16[64,1536]{1,0:T(8,128)(2,1)S(1)}, bf16[64,1536]{1,0:T(8,128)(2,1)S(1)}, u32[]{:S(2)}, u32[]{:S(2)}) collective-permute-start(bf16[64,1536]{1,0:T(8,128)(2,1)S(1)} %bitcast.57), channel_id=1, source_target_pairs={{8,0},{9,1},{10,2},{11,3},{12,4},{13,5},{14,6},{15,7},{16,8},{17,9... | collective-permute-start | bytes 589832 | tf_op jit(solution)/shard_map/ppermute | solution.py:893
  20.2 2.2 fusion.2.order_ref.refs_4_
  22.6 13.6 %collective-permute-done.3 = bf16[64,1536]{1,0:T(8,128)(2,1)S(1)} collective-permute-done((bf16[64,1536]{1,0:T(8,128)(2,1)S(1)}, bf16[64,1536]{1,0:T(8,128)(2,1)S(1)}, u32[]{:S(2)}, u32[]{:S(2)}) %collective-permute-start.3) | collective-permute-done | bytes 196640 | tf_op jit(solution)/shard_map/ppermute | solution.py:893
  36.2 1.7 collective-permute-start.5
  37.9 2.2 collective-permute-start.6
  43.5 2.2 fusion.40
  46.3 4.6 %enter_cot.1 = (bf16[512,1024]{1,0:T(8,128)(2,1)}, bf16[1024,512]{1,0:T(8,128)(2,1)}) custom-call(bf16[256,1024]{1,0:T(8,128)(2,1)} %get-tuple-element.374.own_ref, bf16[256,1024]{1,0:T(8,128)(2,1)} %get-tuple-element.372.got_ref, bf16[1024,1024]{1,0:T(8,128)(2,1)} %fusion.2.order_ref.refs_4_, f32[1,1024]{1,0:T(1,128)} %broadcast_in_dim.21.live_ref.refs_3_), custom_call_target="tpu_custom_call" | custom-call | flops 1 | bytes 1 | tf_op jit(solution)/shard_map/enter_cot/pallas_call | solution.py:420
  50.9 5.0 %enter.1 = (bf16[512,1024]{1,0:T(8,128)(2,1)}, bf16[512,1024]{1,0:T(8,128)(2,1)}, bf16[1024,512]{1,0:T(8,128)(2,1)}) custom-call(bf16[256,1024]{1,0:T(8,128)(2,1)} %get-tuple-element.403.own_ref, bf16[256,1024]{1,0:T(8,128)(2,1)} %get-tuple-element.373.got_ref, bf16[1024,1024]{1,0:T(8,128)(2,1)} %fusion.2.order_ref.refs_4_, ...), custom_call_target="tpu_custom_call" | custom-call | flops 1 | bytes 1 | tf_op jit(solution)/shard_map/enter/pallas_call | solution.py:398
  59.0 1.6 collective-permute-start.7
  60.6 1.5 collective-permute-start.8
  64.4 1.5 collective-permute-start.16
  65.9 5.2 %collective-permute-done.7.refs_3_.refs_8_ = bf16[128,1536]{1,0:T(8,128)(2,1)} collective-permute-done((bf16[128,1536]{1,0:T(8,128)(2,1)S(1)}, bf16[128,1536]{1,0:T(8,128)(2,1)}, u32[]{:S(2)}, u32[]{:S(2)}) %collective-permute-start.7) | collective-permute-done | bytes 393248 | tf_op jit(solution)/shard_map/ppermute | solution.py:916
  71.1 1.5 collective-permute-done.8.refs_4_.refs_9_
  74.2 2.0 collective-permute-done.13.refs_8_.refs_13_
  76.8 8.3 %project.1.q_ref.k_ref.v_ref = bf16[3,512,1024]{2,1,0:T(8,128)(2,1)} custom-call(bf16[512,1024]{1,0:T(8,128)(2,1)} %get-tuple-element.191.h_ref, f32[2,1,1536]{2,1,0:T(1,128)} %broadcast_in_dim.23.bias_ref, bf16[256,1536]{1,0:T(8,128)(2,1)} %copy-done.6, bf16[256,1536]{1,0:T(8,128)(2,1)} %copy-done.7, bf16[256,1536]{1,0:T(8,128)(2,1)} %copy-done.8, ...), custom_call_target="tpu_custom_call" | custom-call | flops 1 | bytes 1 | tf_op jit(solution)/shard_map/project/pallas_call | solution.py:445
  85.1 12.3 %attend_fwd.1 = (bf16[512,1024]{1,0:T(8,128)(2,1)}, f32[512,128]{1,0:T(8,128)}) custom-call(bf16[3,512,1024]{2,1,0:T(8,128)(2,1)} %project.1.q_ref.k_ref.v_ref, bf16[3,512,1024]{2,1,0:T(8,128)(2,1)} %project.1.q_ref.k_ref.v_ref, bf16[3,512,1024]{2,1,0:T(8,128)(2,1)} %project.1.q_ref.k_ref.v_ref), custom_call_target="tpu_custom_call" | custom-call | flops 1 | bytes 1 | tf_op jit(solution)/shard_map/attend_fwd/pallas_call | solution.py:485
  97.4 1.8 copy.28
  104.4 3.1 all-gather.5.cloned.1.call-done.refs_0_.refs_5_
  107.4 1.5 collective-permute-start.20
  110.5 9.4 %collective-permute-done.22.refs_3_.refs_7_ = bf16[128,2560]{1,0:T(8,128)(2,1)S(1)} collective-permute-done((bf16[128,2560]{1,0:T(8,128)(2,1)}, bf16[128,2560]{1,0:T(8,128)(2,1)S(1)}, u32[]{:S(2)}, u32[]{:S(2)}) %collective-permute-start.22) | collective-permute-done | bytes 655392 | tf_op jit(solution)/shard_map/ppermute | solution.py:916
  121.9 1.9 collective-permute-done.24.refs_8_.refs_12_
  125.5 6.6 %join_heads.1 = (f32[512,1024]{1,0:T(8,128)}, bf16[512,1024]{1,0:T(8,128)(2,1)}, bf16[1024,512]{1,0:T(8,128)(2,1)}) custom-call(bf16[512,1024]{1,0:T(8,128)(2,1)} %get-tuple-element.261.attn_ref.refs_6_, bf16[512,1024]{1,0:T(8,128)(2,1)} %get-tuple-element.220.x_ref.refs_1_, f32[1,1024]{1,0:T(1,128)} %get-tuple-element.388.bias_ref, ...), custom_call_target="tpu_custom_call" | custom-call | flops 1 | bytes 1 | tf_op jit(solution)/shard_map/join_heads/pallas_call | solution.py:515
  132.1 12.9 %expand.1 = (bf16[512,4096]{1,0:T(8,128)(2,1)}, bf16[512,4096]{1,0:T(8,128)(2,1)}) custom-call(bf16[512,1024]{1,0:T(8,128)(2,1)} %get-tuple-element.226.h_ref, f32[1,4096]{1,0:T(1,128)} %bitcast.70, bf16[256,2560]{1,0:T(8,128)(2,1)} %all-gather.3.cloned.1.call-done.refs_0_.refs_4_, bf16[256,2560]{1,0:T(8,128)(2,1)} %copy-done, bf16[256,2560]{1,0:T(8,128)(2,1)} %copy-done.1, ...), custom_call_target="tpu_custom_call" | custom-call | flops 1 | bytes 1 | tf_op jit(solution)/shard_map/expand/pallas_call | solution.py:543
  151.7 10.5 %collective-permute-done.26.refs_3_.refs_8_ = bf16[128,2048]{1,0:T(8,128)(2,1)S(1)} collective-permute-done((bf16[128,2048]{1,0:T(8,128)(2,1)S(1)}, bf16[128,2048]{1,0:T(8,128)(2,1)S(1)}, u32[]{:S(2)}, u32[]{:S(2)}) %collective-permute-start.26) | collective-permute-done | bytes 524320 | tf_op jit(solution)/shard_map/ppermute | solution.py:916
  166.3 10.5 %grad_fc2.1 = (bf16[256,2048]{1,0:T(8,128)(2,1)}, bf16[256,2048]{1,0:T(8,128)(2,1)}, bf16[128,2048]{1,0:T(8,128)(2,1)}, bf16[256,2048]{1,0:T(8,128)(2,1)}, bf16[128,2048]{1,0:T(8,128)(2,1)}) custom-call(bf16[1024,512]{1,0:T(8,128)(2,1)} %get-tuple-element.190.refs_0_, bf16[1024,512]{1,0:T(8,128)(2,1)} %collective-permute-done.12.refs_1_, ...), custom_call_target="tpu_custom_call" | custom-call | flops 1 | bytes 1 | tf_op jit(solution)/shard_map/grad_fc2/pallas_call | solution.py:849
  180.2 10.2 %hidden_back.1 = (bf16[512,4096]{1,0:T(8,128)(2,1)}, f32[1,4096]{1,0:T(1,128)}) custom-call(bf16[512,1024]{1,0:T(8,128)(2,1)} %get-tuple-element.192.e_ref.refs_2_, bf16[512,4096]{1,0:T(8,128)(2,1)} %get-tuple-element.249.slope_ref, bf16[256,2048]{1,0:T(8,128)(2,1)} %all-gather.5.cloned.1.call-done.refs_0_.refs_5_, ...), custom_call_target="tpu_custom_call" | custom-call | flops 1 | bytes 1 | tf_op jit(solution)/shard_map/hidden_back/pallas_call | solution.py:571
  190.4 12.8 %second_back.1 = (f32[512,1024]{1,0:T(8,128)}, bf16[512,1024]{1,0:T(8,128)(2,1)}, bf16[512,512]{1,0:T(8,128)(2,1)}, bf16[512,512]{1,0:T(8,128)(2,1)}, f32[4,1024]{1,0:T(4,128)}) custom-call(bf16[512,4096]{1,0:T(8,128)(2,1)} %get-tuple-element.265.refs_0_.refs_2_, f32[512,1024]{1,0:T(8,128)} %get-tuple-element.257.refs_1_, ...), custom_call_target="tpu_custom_call" | custom-call | flops 1 | bytes 1 | tf_op jit(solution)/shard_map/second_back/pallas_call | solution.py:635
  204.7 2.9 add_mid.3
  210.4 4.9 %heads_back.1.g_ref = bf16[512,1024]{1,0:T(8,128)(2,1)} custom-call(bf16[512,1024]{1,0:T(8,128)(2,1)} %get-tuple-element.267.da_ref, bf16[256,2560]{1,0:T(8,128)(2,1)} %all-gather.3.cloned.1.call-done.refs_0_.refs_4_, bf16[256,2560]{1,0:T(8,128)(2,1)} %copy-done, bf16[256,2560]{1,0:T(8,128)(2,1)} %copy-done.1, bf16[128,2560]{1,0:T(8,128)(2,1)} %copy-done.3, ...), custom_call_target="tpu_custom_call" | custom-call | flops 1 | bytes 1 | tf_op jit(solution)/shard_map/heads_back/pallas_call | solution.py:593
  216.2 13.9 %grad_two.1 = (bf16[256,2560]{1,0:T(8,128)(2,1)}, bf16[256,2560]{1,0:T(8,128)(2,1)}, bf16[128,2560]{1,0:T(8,128)(2,1)}, bf16[256,2560]{1,0:T(8,128)(2,1)}, bf16[128,2560]{1,0:T(8,128)(2,1)}) custom-call(bf16[1024,512]{1,0:T(8,128)(2,1)} %get-tuple-element.230.refs_0_, bf16[512,512]{1,0:T(8,128)(2,1)} %collective-permute-done.34.refs_1_, ...), custom_call_target="tpu_custom_call" | custom-call | flops 1 | bytes 1 | tf_op jit(solution)/shard_map/grad_two/pallas_call | solution.py:849
  231.4 3.5 add_last.3
  235.0 16.9 %attend_bwd.1 = (bf16[3,512,1024]{2,1,0:T(8,128)(2,1)}, f32[1,1024]{1,0:T(1,128)}, f32[1,1024]{1,0:T(1,128)}) custom-call(bf16[3,512,1024]{2,1,0:T(8,128)(2,1)} %project.1.q_ref.k_ref.v_ref, bf16[3,512,1024]{2,1,0:T(8,128)(2,1)} %project.1.q_ref.k_ref.v_ref, bf16[3,512,1024]{2,1,0:T(8,128)(2,1)} %project.1.q_ref.k_ref.v_ref, ...), custom_call_target="tpu_custom_call" | custom-call | flops 1 | bytes 1 | tf_op jit(solution)/shard_map/attend_bwd/pallas_call | solution.py:783
  251.9 11.1 %first_back.1 = (bf16[256,1024]{1,0:T(8,128)(2,1)}, bf16[256,1024]{1,0:T(8,128)(2,1)}, f32[2,1024]{1,0:T(2,128)}) custom-call(bf16[3,512,1024]{2,1,0:T(8,128)(2,1)} %get-tuple-element.300.refs_0_.refs_2_, bf16[512,1024]{1,0:T(8,128)(2,1)} %get-tuple-element.220.x_ref.refs_1_, f32[512,1024]{1,0:T(8,128)} %get-tuple-element.296.refs_2_, ...), custom_call_target="tpu_custom_call" | custom-call | flops 1 | bytes 1 | tf_op jit(solution)/shard_map/first_back/pallas_call | solution.py:635
  263.4 3.4 add_mid.4
  269.6 1.9 fusion
  272.9 5.4 %collective-permute-start.48 = (f32[96,128]{1,0:T(8,128)S(1)}, f32[96,128]{1,0:T(8,128)S(1)}, u32[]{:S(2)}, u32[]{:S(2)}) collective-permute-start(f32[96,128]{1,0:T(8,128)S(1)} %fusion.39), channel_id=1, source_target_pairs={{8,0},{9,1},{10,2},{11,3},{12,4},{13,5},{14,6},{15,7},{0,8},{1,9},... | collective-permute-start | bytes 147464 | tf_op jit(solution)/shard_map/ppermute | solution.py:926
  278.3 8.8 %grad_qkv.1 = (bf16[256,1024]{1,0:T(8,128)(2,1)}, bf16[256,1024]{1,0:T(8,128)(2,1)}, bf16[128,1024]{1,0:T(8,128)(2,1)}, bf16[256,1024]{1,0:T(8,128)(2,1)}, bf16[...) custom-call(bf16[1024,512]{1,0:T(8,128)(2,1)} %get-tuple-element.189.refs_0_, ...), custom_call_target="tpu_custom_call" | custom-call | flops 1 | bytes 1 | tf_op jit(solution)/shard_map/grad_qkv/pallas_call | solution.py:849
  287.1 4.0 %add_last.4 = bf16[256,2560]{1,0:T(8,128)(2,1)} custom-call(bf16[256,2560]{1,0:T(8,128)(2,1)} %get-tuple-element.289.k00_ref, bf16[256,2560]{1,0:T(8,128)(2,1)} %collective-permute-done.42.rx_ref, bf16[256,2560]{1,0:T(8,128)(2,1)} %collective-permute-done.43.ry_ref, bf16[128,2560]{1,0:T(8,128)(2,1)} %collective-permute-done.46.y2_ref, ...), custom_call_target="tpu_custom_call" | custom-call | flops 1 | bytes 1 | tf_op jit(solution)/shard_map/add_last/pallas_call | solution.py:869
  291.2 8.7 %all-to-all-start = ((bf16[4,256,512]{2,1,0:T(8,128)(2,1)}), bf16[4,256,512]{2,1,0:T(8,128)(2,1)S(1)}, u32[]{:S(2)}, u32[]{:S(2)}) async-start(bf16[4,256,512]{2,1,0:T(8,128)(2,1)} %bitcast.22), calls=%async_computation | async-start | bytes 2097152 | tf_op jit(solution)/shard_map/all_to_all | solution.py:907
  300.6 1.6 collective-permute-start.50
  303.6 10.0 %collective-permute-done.49.rx_ref = bf16[256,1024]{1,0:T(8,128)(2,1)S(1)} collective-permute-done((bf16[256,1024]{1,0:T(8,128)(2,1)S(1)}, bf16[256,1024]{1,0:T(8,128)(2,1)S(1)}, u32[]{:S(2)}, u32[]{:S(2)}) %collective-permute-start.49) | collective-permute-done | bytes 524320 | tf_op jit(solution)/shard_map/ppermute | solution.py:916
  315.2 2.2 add_mid.5
  321.5 11.4 %layer_out.1 = (bf16[256,1024]{1,0:T(8,128)(2,1)}, bf16[256,1024]{1,0:T(8,128)(2,1)}) custom-call(bf16[512,4096]{1,0:T(8,128)(2,1)} %get-tuple-element.335.refs_2_.refs_0_, f32[512,1024]{1,0:T(8,128)} %get-tuple-element.257.refs_1_, f32[1,1024]{1,0:T(1,128)} %get-tuple-element.385.refs_2_, f32[1,1024]{1,0:T(1,128)} %broadcast_in_dim.21.live_ref.refs_3_, ...), custom_call_target="tpu_custom_call" | custom-call | flops 1 | bytes 1 | tf_op jit(solution)/shard_map/layer_out/pallas_call | solution.py:635
  333.7 2.5 add_last.5
  336.9 10.1 %all-to-all-done = bf16[4,256,512]{2,1,0:T(8,128)(2,1)S(1)} async-done(((bf16[4,256,512]{2,1,0:T(8,128)(2,1)}), bf16[4,256,512]{2,1,0:T(8,128)(2,1)S(1)}, u32[]{:S(2)}, u32[]{:S(2)}) %all-to-all-start) | async-done | bytes 1048608 | tf_op jit(solution)/shard_map/all_to_all | solution.py:907
  347.8 4.3 %all-to-all-start.1 = ((bf16[4,64,1024]{2,1,0:T(8,128)(2,1)}), bf16[4,64,1024]{2,1,0:T(8,128)(2,1)S(1)}, u32[]{:S(2)}, u32[]{:S(2)}) async-start(bf16[4,64,1024]{2,1,0:T(8,128)(2,1)} %bitcast.54), calls=%async_computation.3 | async-start | bytes 1048576 | tf_op jit(solution)/shard_map/all_to_all | solution.py:907
  355.8 1.6 collective-permute-start.59
  (286 shorter events, 72.2 us)
Async XLA Ops:
  7.2 51.1 %all-gather.3.cloned.1.call-start = ((), (), s32[]{:S(2)}) async-start(), calls=%async_computation.4 | async-start | bytes 1638400 | tf_op jit(solution)/shard_map/all_gather | solution.py:911
  11.0 11.5 %collective-permute-start.2 = (bf16[64,1536]{1,0:T(8,128)(2,1)S(1)}, bf16[64,1536]{1,0:T(8,128)(2,1)S(1)}, u32[]{:S(2)}, u32[]{:S(2)}) collective-permute-start(bf16[64,1536]{1,0:T(8,128)(2,1)S(1)} %bitcast.57), channel_id=1, source_target_pairs={{8,0},{9,1},{10,2},{11,3},{12,4},{13,5},{14,6},{15,7},{16,8},{17,9... | collective-permute-start | bytes 589832 | tf_op jit(solution)/shard_map/ppermute | solution.py:893
  16.1 20.1 %collective-permute-start.3 = (bf16[64,1536]{1,0:T(8,128)(2,1)S(1)}, bf16[64,1536]{1,0:T(8,128)(2,1)S(1)}, u32[]{:S(2)}, u32[]{:S(2)}) collective-permute-start(bf16[64,1536]{1,0:T(8,128)(2,1)S(1)} %bitcast.58), channel_id=1, source_target_pairs={{16,0},{17,1},{18,2},{19,3},{20,4},{21,5},{22,6},{23,7},{24,8},{25... | collective-permute-start | bytes 589832 | tf_op jit(solution)/shard_map/ppermute | solution.py:893
  16.1 20.1 %collective-permute-start.4 = (bf16[64,1536]{1,0:T(8,128)(2,1)S(1)}, bf16[64,1536]{1,0:T(8,128)(2,1)S(1)}, u32[]{:S(2)}, u32[]{:S(2)}) collective-permute-start(bf16[64,1536]{1,0:T(8,128)(2,1)S(1)} %bitcast.59), channel_id=1, source_target_pairs={{24,0},{25,1},{26,2},{27,3},{28,4},{29,5},{30,6},{31,7},{0,8},{1,9... | collective-permute-start | bytes 589832 | tf_op jit(solution)/shard_map/ppermute | solution.py:893
  17.1 26.4 %collective-permute-start = (bf16[512,1024]{1,0:T(8,128)(2,1)S(1)}, bf16[512,1024]{1,0:T(8,128)(2,1)}, u32[]{:S(2)}, u32[]{:S(2)}) collective-permute-start(bf16[512,1024]{1,0:T(8,128)(2,1)S(1)} %pad_maximum_fusion), channel_id=1, source_target_pairs={{1,0},{0,1},{3,2},{2,3},{5,4},{4,5},{7,6},{6,7},{9,8},{8,9},{11,10... | collective-permute-start | bytes 3145736 | tf_op jit(solution)/shard_map/ppermute | solution.py:916
  18.6 24.9 %collective-permute-start.1 = (f32[24,128]{1,0:T(8,128)S(1)}, f32[24,128]{1,0:T(8,128)S(1)}, u32[]{:S(2)}, u32[]{:S(2)}) collective-permute-start(f32[24,128]{1,0:T(8,128)S(1)} %maximum_bitcast_fusion.1), channel_id=1, source_target_pairs={{1,0},{0,1},{3,2},{2,3},{5,4},{4,5},{7,6},{6,7},{9,8},{8,9},{11,10... | collective-permute-start | bytes 36872 | tf_op jit(solution)/shard_map/ppermute | solution.py:916
  20.0 87.4 %all-gather.5.cloned.1.call-start = ((), (), s32[]{:S(2)}) async-start(), calls=%async_computation.5 | async-start | bytes 1310720 | tf_op jit(solution)/shard_map/all_gather | solution.py:911
  36.2 22.0 %collective-permute-start.5 = (bf16[256,1536]{1,0:T(8,128)(2,1)S(1)}, bf16[256,1536]{1,0:T(8,128)(2,1)S(1)}, u32[]{:S(2)}, u32[]{:S(2)}) collective-permute-start(bf16[256,1536]{1,0:T(8,128)(2,1)S(1)} %constant_dynamic-update-slice_fusion.refs_0_.refs_5_), channel_id=1, source_target_pairs={{1,0},{0,1},{3,2},{2,3},{5,4},{4,5},{7,6},{6,7},{9,8},{8,9},{11,10... | collective-permute-start | bytes 2359304 | tf_op jit(solution)/shard_map/ppermute | solution.py:916
  37.9 20.4 %collective-permute-start.6 = (bf16[256,1536]{1,0:T(8,128)(2,1)S(1)}, bf16[256,1536]{1,0:T(8,128)(2,1)S(1)}, u32[]{:S(2)}, u32[]{:S(2)}) collective-permute-start(bf16[256,1536]{1,0:T(8,128)(2,1)S(1)} %constant_dynamic-update-slice_fusion.refs_0_.refs_5_), channel_id=1, source_target_pairs={{4,0},{5,1},{6,2},{7,3},{0,4},{1,5},{2,6},{3,7},{12,8},{13,9},{14,... | collective-permute-start | bytes 2359304 | tf_op jit(solution)/shard_map/ppermute | solution.py:919
  59.0 12.1 %collective-permute-start.7 = (bf16[128,1536]{1,0:T(8,128)(2,1)S(1)}, bf16[128,1536]{1,0:T(8,128)(2,1)}, u32[]{:S(2)}, u32[]{:S(2)}) collective-permute-start(bf16[128,1536]{1,0:T(8,128)(2,1)S(1)} %slice.156), channel_id=1, source_target_pairs={{1,0},{0,1},{3,2},{2,3},{5,4},{4,5},{7,6},{6,7},{9,8},{8,9},{11,10... | collective-permute-start | bytes 1179656 | tf_op jit(solution)/shard_map/ppermute | solution.py:916
  60.6 12.1 %collective-permute-start.8 = (bf16[128,1536]{1,0:T(8,128)(2,1)S(1)}, bf16[128,1536]{1,0:T(8,128)(2,1)}, u32[]{:S(2)}, u32[]{:S(2)}) collective-permute-start(bf16[128,1536]{1,0:T(8,128)(2,1)S(1)} %slice.157), channel_id=1, source_target_pairs={{4,0},{5,1},{6,2},{7,3},{0,4},{1,5},{2,6},{3,7},{12,8},{13,9},{14,... | collective-permute-start | bytes 1179656 | tf_op jit(solution)/shard_map/ppermute | solution.py:919
  63.1 36.2 %collective-permute-start.15 = (bf16[256,2560]{1,0:T(8,128)(2,1)}, bf16[256,2560]{1,0:T(8,128)(2,1)S(1)}, u32[]{:S(2)}, u32[]{:S(2)}) collective-permute-start(bf16[256,2560]{1,0:T(8,128)(2,1)} %all-gather.3.cloned.1.call-done.refs_0_.refs_4_), channel_id=1, source_target_pairs={{1,0},{0,1},{3,2},{2,3},{5,4},{4,5},{7,6},{6,7},{9,8},{8,9},{11,10... | collective-permute-start | bytes 3932168 | tf_op jit(solution)/shard_map/ppermute | solution.py:916
  64.4 35.5 %collective-permute-start.16 = (bf16[256,2560]{1,0:T(8,128)(2,1)}, bf16[256,2560]{1,0:T(8,128)(2,1)S(1)}, u32[]{:S(2)}, u32[]{:S(2)}) collective-permute-start(bf16[256,2560]{1,0:T(8,128)(2,1)} %all-gather.3.cloned.1.call-done.refs_0_.refs_4_), channel_id=1, source_target_pairs={{4,0},{5,1},{6,2},{7,3},{0,4},{1,5},{2,6},{3,7},{12,8},{13,9},{14,... | collective-permute-start | bytes 3932168 | tf_op jit(solution)/shard_map/ppermute | solution.py:919
  73.2 280.0 %reduce-scatter.5.cloned.1.call-start = ((), (), s32[]{:S(2)}) async-start(), calls=%async_computation.7 | async-start | bytes 1310720 | tf_op jit(solution)/shard_map/reduce_scatter | solution.py:902
  102.2 17.7 %collective-permute-start.22 = (bf16[128,2560]{1,0:T(8,128)(2,1)}, bf16[128,2560]{1,0:T(8,128)(2,1)S(1)}, u32[]{:S(2)}, u32[]{:S(2)}) collective-permute-start(bf16[128,2560]{1,0:T(8,128)(2,1)} %slice.163), channel_id=1, source_target_pairs={{1,0},{0,1},{3,2},{2,3},{5,4},{4,5},{7,6},{6,7},{9,8},{8,9},{11,10... | collective-permute-start | bytes 1966088 | tf_op jit(solution)/shard_map/ppermute | solution.py:916
  102.9 17.9 %collective-permute-start.23 = (bf16[128,2560]{1,0:T(8,128)(2,1)}, bf16[128,2560]{1,0:T(8,128)(2,1)}, u32[]{:S(2)}, u32[]{:S(2)}) collective-permute-start(bf16[128,2560]{1,0:T(8,128)(2,1)} %slice.164), channel_id=1, source_target_pairs={{4,0},{5,1},{6,2},{7,3},{0,4},{1,5},{2,6},{3,7},{12,8},{13,9},{14,... | collective-permute-start | bytes 1966088 | tf_op jit(solution)/shard_map/ppermute | solution.py:919
  107.4 37.6 %collective-permute-start.20 = (bf16[256,2048]{1,0:T(8,128)(2,1)}, bf16[256,2048]{1,0:T(8,128)(2,1)}, u32[]{:S(2)}, u32[]{:S(2)}) collective-permute-start(bf16[256,2048]{1,0:T(8,128)(2,1)} %all-gather.5.cloned.1.call-done.refs_0_.refs_5_), channel_id=1, source_target_pairs={{1,0},{0,1},{3,2},{2,3},{5,4},{4,5},{7,6},{6,7},{9,8},{8,9},{11,10... | collective-permute-start | bytes 3145736 | tf_op jit(solution)/shard_map/ppermute | solution.py:916
  109.0 36.0 %collective-permute-start.21 = (bf16[256,2048]{1,0:T(8,128)(2,1)}, bf16[256,2048]{1,0:T(8,128)(2,1)}, u32[]{:S(2)}, u32[]{:S(2)}) collective-permute-start(bf16[256,2048]{1,0:T(8,128)(2,1)} %all-gather.5.cloned.1.call-done.refs_0_.refs_5_), channel_id=1, source_target_pairs={{4,0},{5,1},{6,2},{7,3},{0,4},{1,5},{2,6},{3,7},{12,8},{13,9},{14,... | collective-permute-start | bytes 3145736 | tf_op jit(solution)/shard_map/ppermute | solution.py:919
  145.0 20.2 %collective-permute-start.28 = (bf16[512,4096]{1,0:T(8,128)(2,1)}, bf16[512,4096]{1,0:T(8,128)(2,1)}, u32[]{:S(2)}, u32[]{:S(2)}) collective-permute-start(bf16[512,4096]{1,0:T(8,128)(2,1)} %get-tuple-element.335.refs_2_.refs_0_), channel_id=1, source_target_pairs={{2,0},{3,1},{0,2},{1,3},{6,4},{7,5},{4,6},{5,7},{10,8},{11,9},{8,1... | collective-permute-start | bytes 12582920 | tf_op jit(solution)/shard_map/ppermute | solution.py:922
  145.2 18.0 %collective-permute-start.29 = (bf16[256,2048]{1,0:T(8,128)(2,1)S(1)}, bf16[256,2048]{1,0:T(8,128)(2,1)S(1)}, u32[]{:S(2)}, u32[]{:S(2)}) collective-permute-start(bf16[256,2048]{1,0:T(8,128)(2,1)S(1)} %copy-done.12), channel_id=1, source_target_pairs={{2,0},{3,1},{0,2},{1,3},{6,4},{7,5},{4,6},{5,7},{10,8},{11,9},{8,1... | collective-permute-start | bytes 3145736 | tf_op jit(solution)/shard_map/ppermute | solution.py:922
  145.6 18.6 %collective-permute-start.30 = (bf16[256,2048]{1,0:T(8,128)(2,1)}, bf16[256,2048]{1,0:T(8,128)(2,1)S(1)}, u32[]{:S(2)}, u32[]{:S(2)}) collective-permute-start(bf16[256,2048]{1,0:T(8,128)(2,1)} %collective-permute-done.20.refs_1_.refs_6_), channel_id=1, source_target_pairs={{2,0},{3,1},{0,2},{1,3},{6,4},{7,5},{4,6},{5,7},{10,8},{11,9},{8,1... | collective-permute-start | bytes 3145736 | tf_op jit(solution)/shard_map/ppermute | solution.py:922
  147.9 14.3 %collective-permute-start.26 = (bf16[128,2048]{1,0:T(8,128)(2,1)S(1)}, bf16[128,2048]{1,0:T(8,128)(2,1)S(1)}, u32[]{:S(2)}, u32[]{:S(2)}) collective-permute-start(bf16[128,2048]{1,0:T(8,128)(2,1)S(1)} %slice.166), channel_id=1, source_target_pairs={{1,0},{0,1},{3,2},{2,3},{5,4},{4,5},{7,6},{6,7},{9,8},{8,9},{11,10... | collective-permute-start | bytes 1572872 | tf_op jit(solution)/shard_map/ppermute | solution.py:916
  149.3 13.9 %collective-permute-start.27 = (bf16[128,2048]{1,0:T(8,128)(2,1)S(1)}, bf16[128,2048]{1,0:T(8,128)(2,1)S(1)}, u32[]{:S(2)}, u32[]{:S(2)}) collective-permute-start(bf16[128,2048]{1,0:T(8,128)(2,1)S(1)} %slice.167), channel_id=1, source_target_pairs={{4,0},{5,1},{6,2},{7,3},{0,4},{1,5},{2,6},{3,7},{12,8},{13,9},{14,... | collective-permute-start | bytes 1572872 | tf_op jit(solution)/shard_map/ppermute | solution.py:919
  165.2 11.6 %collective-permute-start.31 = (bf16[256,2048]{1,0:T(8,128)(2,1)}, bf16[256,2048]{1,0:T(8,128)(2,1)S(1)}, u32[]{:S(2)}, u32[]{:S(2)}) collective-permute-start(bf16[256,2048]{1,0:T(8,128)(2,1)} %collective-permute-done.21.refs_2_.refs_7_), channel_id=1, source_target_pairs={{2,0},{3,1},{0,2},{1,3},{6,4},{7,5},{4,6},{5,7},{10,8},{11,9},{8,1... | collective-permute-start | bytes 3145736 | tf_op jit(solution)/shard_map/ppermute | solution.py:922
  165.2 11.5 %collective-permute-start.32 = (bf16[128,2048]{1,0:T(8,128)(2,1)S(1)}, bf16[128,2048]{1,0:T(8,128)(2,1)S(1)}, u32[]{:S(2)}, u32[]{:S(2)}) collective-permute-start(bf16[128,2048]{1,0:T(8,128)(2,1)S(1)} %collective-permute-done.26.refs_3_.refs_8_), channel_id=1, source_target_pairs={{2,0},{3,1},{0,2},{1,3},{6,4},{7,5},{4,6},{5,7},{10,8},{11,9},{8,1... | collective-permute-start | bytes 1572872 | tf_op jit(solution)/shard_map/ppermute | solution.py:922
  178.0 25.3 %collective-permute-start.36 = (bf16[256,2048]{1,0:T(8,128)(2,1)}, bf16[256,2048]{1,0:T(8,128)(2,1)S(1)}, u32[]{:S(2)}, u32[]{:S(2)}) collective-permute-start(bf16[256,2048]{1,0:T(8,128)(2,1)} %get-tuple-element.262), channel_id=1, source_target_pairs={{1,0},{0,1},{3,2},{2,3},{5,4},{4,5},{7,6},{6,7},{9,8},{8,9},{11,10... | collective-permute-start | bytes 3145736 | tf_op jit(solution)/shard_map/ppermute | solution.py:916
  178.7 25.1 %collective-permute-start.37 = (bf16[256,2048]{1,0:T(8,128)(2,1)}, bf16[256,2048]{1,0:T(8,128)(2,1)S(1)}, u32[]{:S(2)}, u32[]{:S(2)}) collective-permute-start(bf16[256,2048]{1,0:T(8,128)(2,1)} %get-tuple-element.263), channel_id=1, source_target_pairs={{4,0},{5,1},{6,2},{7,3},{0,4},{1,5},{2,6},{3,7},{12,8},{13,9},{14,... | collective-permute-start | bytes 3145736 | tf_op jit(solution)/shard_map/ppermute | solution.py:919
  180.2 23.5 %collective-permute-start.35 = (bf16[512,1024]{1,0:T(8,128)(2,1)S(1)}, bf16[512,1024]{1,0:T(8,128)(2,1)}, u32[]{:S(2)}, u32[]{:S(2)}) collective-permute-start(bf16[512,1024]{1,0:T(8,128)(2,1)S(1)} %copy-done.9), channel_id=1, source_target_pairs={{2,0},{3,1},{0,2},{1,3},{6,4},{7,5},{4,6},{5,7},{10,8},{11,9},{8,1... | collective-permute-start | bytes 3145736 | tf_op jit(solution)/shard_map/ppermute | solution.py:922
  203.7 11.7 %collective-permute-start.38 = (bf16[512,4096]{1,0:T(8,128)(2,1)}, bf16[512,4096]{1,0:T(8,128)(2,1)}, u32[]{:S(2)}, u32[]{:S(2)}) collective-permute-start(bf16[512,4096]{1,0:T(8,128)(2,1)} %get-tuple-element.265.refs_0_.refs_2_), channel_id=1, source_target_pairs={{2,0},{3,1},{0,2},{1,3},{6,4},{7,5},{4,6},{5,7},{10,8},{11,9},{8,1... | collective-permute-start | bytes 12582920 | tf_op jit(solution)/shard_map/ppermute | solution.py:922
  203.8 11.6 %collective-permute-start.39 = (bf16[512,512]{1,0:T(8,128)(2,1)}, bf16[512,512]{1,0:T(8,128)(2,1)S(1)}, u32[]{:S(2)}, u32[]{:S(2)}) collective-permute-start(bf16[512,512]{1,0:T(8,128)(2,1)} %get-tuple-element.266), channel_id=1, source_target_pairs={{2,0},{3,1},{0,2},{1,3},{6,4},{7,5},{4,6},{5,7},{10,8},{11,9},{8,1... | collective-permute-start | bytes 1572872 | tf_op jit(solution)/shard_map/ppermute | solution.py:922
  207.6 22.5 %collective-permute-start.40 = (bf16[128,2048]{1,0:T(8,128)(2,1)}, bf16[128,2048]{1,0:T(8,128)(2,1)S(1)}, u32[]{:S(2)}, u32[]{:S(2)}) collective-permute-start(bf16[128,2048]{1,0:T(8,128)(2,1)} %get-tuple-element.280), channel_id=1, source_target_pairs={{4,0},{5,1},{6,2},{7,3},{0,4},{1,5},{2,6},{3,7},{12,8},{13,9},{14,... | collective-permute-start | bytes 1572872 | tf_op jit(solution)/shard_map/ppermute | solution.py:919
  209.1 21.0 %collective-permute-start.41 = (bf16[128,2048]{1,0:T(8,128)(2,1)}, bf16[128,2048]{1,0:T(8,128)(2,1)S(1)}, u32[]{:S(2)}, u32[]{:S(2)}) collective-permute-start(bf16[128,2048]{1,0:T(8,128)(2,1)} %get-tuple-element.281), channel_id=1, source_target_pairs={{1,0},{0,1},{3,2},{2,3},{5,4},{4,5},{7,6},{6,7},{9,8},{8,9},{11,10... | collective-permute-start | bytes 1572872 | tf_op jit(solution)/shard_map/ppermute | solution.py:916
  230.1 32.9 %collective-permute-start.42 = (bf16[256,2560]{1,0:T(8,128)(2,1)}, bf16[256,2560]{1,0:T(8,128)(2,1)}, u32[]{:S(2)}, u32[]{:S(2)}) collective-permute-start(bf16[256,2560]{1,0:T(8,128)(2,1)} %get-tuple-element.286), channel_id=1, source_target_pairs={{1,0},{0,1},{3,2},{2,3},{5,4},{4,5},{7,6},{6,7},{9,8},{8,9},{11,10... | collective-permute-start | bytes 3932168 | tf_op jit(solution)/shard_map/ppermute | solution.py:916
  230.9 32.1 %collective-permute-start.43 = (bf16[256,2560]{1,0:T(8,128)(2,1)}, bf16[256,2560]{1,0:T(8,128)(2,1)}, u32[]{:S(2)}, u32[]{:S(2)}) collective-permute-start(bf16[256,2560]{1,0:T(8,128)(2,1)} %get-tuple-element.287), channel_id=1, source_target_pairs={{4,0},{5,1},{6,2},{7,3},{0,4},{1,5},{2,6},{3,7},{12,8},{13,9},{14,... | collective-permute-start | bytes 3932168 | tf_op jit(solution)/shard_map/ppermute | solution.py:919
  263.3 90.0 %reduce-scatter.3.cloned.1.call-start = ((), (), s32[]{:S(2)}) async-start(), calls=%async_computation.6 | async-start | bytes 1638400 | tf_op jit(solution)/shard_map/reduce_scatter | solution.py:902
  266.8 20.3 %collective-permute-start.46 = (bf16[128,2560]{1,0:T(8,128)(2,1)}, bf16[128,2560]{1,0:T(8,128)(2,1)}, u32[]{:S(2)}, u32[]{:S(2)}) collective-permute-start(bf16[128,2560]{1,0:T(8,128)(2,1)} %get-tuple-element.304), channel_id=1, source_target_pairs={{4,0},{5,1},{6,2},{7,3},{0,4},{1,5},{2,6},{3,7},{12,8},{13,9},{14,... | collective-permute-start | bytes 1966088 | tf_op jit(solution)/shard_map/ppermute | solution.py:919
  268.3 18.8 %collective-permute-start.47 = (bf16[128,2560]{1,0:T(8,128)(2,1)}, bf16[128,2560]{1,0:T(8,128)(2,1)}, u32[]{:S(2)}, u32[]{:S(2)}) collective-permute-start(bf16[128,2560]{1,0:T(8,128)(2,1)} %get-tuple-element.305), channel_id=1, source_target_pairs={{1,0},{0,1},{3,2},{2,3},{5,4},{4,5},{7,6},{6,7},{9,8},{8,9},{11,10... | collective-permute-start | bytes 1966088 | tf_op jit(solution)/shard_map/ppermute | solution.py:916
  272.9 14.2 %collective-permute-start.48 = (f32[96,128]{1,0:T(8,128)S(1)}, f32[96,128]{1,0:T(8,128)S(1)}, u32[]{:S(2)}, u32[]{:S(2)}) collective-permute-start(f32[96,128]{1,0:T(8,128)S(1)} %fusion.39), channel_id=1, source_target_pairs={{8,0},{9,1},{10,2},{11,3},{12,4},{13,5},{14,6},{15,7},{0,8},{1,9},... | collective-permute-start | bytes 147464 | tf_op jit(solution)/shard_map/ppermute | solution.py:926
  291.2 55.8 %all-to-all-start = ((bf16[4,256,512]{2,1,0:T(8,128)(2,1)}), bf16[4,256,512]{2,1,0:T(8,128)(2,1)S(1)}, u32[]{:S(2)}, u32[]{:S(2)}) async-start(bf16[4,256,512]{2,1,0:T(8,128)(2,1)} %bitcast.22), calls=%async_computation | async-start | bytes 2097152 | tf_op jit(solution)/shard_map/all_to_all | solution.py:907
  299.9 13.6 %collective-permute-start.49 = (bf16[256,1024]{1,0:T(8,128)(2,1)S(1)}, bf16[256,1024]{1,0:T(8,128)(2,1)S(1)}, u32[]{:S(2)}, u32[]{:S(2)}) collective-permute-start(bf16[256,1024]{1,0:T(8,128)(2,1)S(1)} %copy-done.45), channel_id=1, source_target_pairs={{1,0},{0,1},{3,2},{2,3},{5,4},{4,5},{7,6},{6,7},{9,8},{8,9},{11,10... | collective-permute-start | bytes 1572872 | tf_op jit(solution)/shard_map/ppermute | solution.py:916
  300.6 13.0 %collective-permute-start.50 = (bf16[256,1024]{1,0:T(8,128)(2,1)S(1)}, bf16[256,1024]{1,0:T(8,128)(2,1)S(1)}, u32[]{:S(2)}, u32[]{:S(2)}) collective-permute-start(bf16[256,1024]{1,0:T(8,128)(2,1)S(1)} %copy-done.44), channel_id=1, source_target_pairs={{4,0},{5,1},{6,2},{7,3},{0,4},{1,5},{2,6},{3,7},{12,8},{13,9},{14,... | collective-permute-start | bytes 1572872 | tf_op jit(solution)/shard_map/ppermute | solution.py:919
  302.2 15.3 %collective-permute-start.51 = (f32[96,128]{1,0:T(8,128)S(1)}, f32[96,128]{1,0:T(8,128)S(1)}, u32[]{:S(2)}, u32[]{:S(2)}) collective-permute-start(f32[96,128]{1,0:T(8,128)S(1)} %add.178), channel_id=1, source_target_pairs={{1,0},{0,1},{3,2},{2,3},{5,4},{4,5},{7,6},{6,7},{9,8},{8,9},{11,10... | collective-permute-start | bytes 147464 | tf_op jit(solution)/shard_map/ppermute | solution.py:916
  317.4 15.5 %collective-permute-start.52 = (bf16[128,1024]{1,0:T(8,128)(2,1)}, bf16[128,1024]{1,0:T(8,128)(2,1)S(1)}, u32[]{:S(2)}, u32[]{:S(2)}) collective-permute-start(bf16[128,1024]{1,0:T(8,128)(2,1)} %get-tuple-element.338), channel_id=1, source_target_pairs={{4,0},{5,1},{6,2},{7,3},{0,4},{1,5},{2,6},{3,7},{12,8},{13,9},{14,... | collective-permute-start | bytes 786440 | tf_op jit(solution)/shard_map/ppermute | solution.py:919
  318.8 14.1 %collective-permute-start.53 = (bf16[128,1024]{1,0:T(8,128)(2,1)}, bf16[128,1024]{1,0:T(8,128)(2,1)S(1)}, u32[]{:S(2)}, u32[]{:S(2)}) collective-permute-start(bf16[128,1024]{1,0:T(8,128)(2,1)} %get-tuple-element.339), channel_id=1, source_target_pairs={{1,0},{0,1},{3,2},{2,3},{5,4},{4,5},{7,6},{6,7},{9,8},{8,9},{11,10... | collective-permute-start | bytes 786440 | tf_op jit(solution)/shard_map/ppermute | solution.py:916
  319.5 16.8 %collective-permute-start.54 = (f32[96,128]{1,0:T(8,128)S(1)}, f32[96,128]{1,0:T(8,128)S(1)}, u32[]{:S(2)}, u32[]{:S(2)}) collective-permute-start(f32[96,128]{1,0:T(8,128)S(1)} %add.179), channel_id=1, source_target_pairs={{4,0},{5,1},{6,2},{7,3},{0,4},{1,5},{2,6},{3,7},{12,8},{13,9},{14,... | collective-permute-start | bytes 147464 | tf_op jit(solution)/shard_map/ppermute | solution.py:919
  320.1 33.2 %collective-permute-start.58 = (bf16[256,1024]{1,0:T(8,128)(2,1)}, bf16[256,1024]{1,0:T(8,128)(2,1)S(1)}, u32[]{:S(2)}, u32[]{:S(2)}) collective-permute-start(bf16[256,1024]{1,0:T(8,128)(2,1)} %get-tuple-element.350), channel_id=1, source_target_pairs={{1,0},{0,1},{3,2},{2,3},{5,4},{4,5},{7,6},{6,7},{9,8},{8,9},{11,10... | collective-permute-start | bytes 1572872 | tf_op jit(solution)/shard_map/ppermute | solution.py:916
  336.2 17.0 %collective-permute-start.57 = (bf16[256,1024]{1,0:T(8,128)(2,1)}, bf16[256,1024]{1,0:T(8,128)(2,1)S(1)}, u32[]{:S(2)}, u32[]{:S(2)}) collective-permute-start(bf16[256,1024]{1,0:T(8,128)(2,1)} %get-tuple-element.349), channel_id=1, source_target_pairs={{1,0},{0,1},{3,2},{2,3},{5,4},{4,5},{7,6},{6,7},{9,8},{8,9},{11,10... | collective-permute-start | bytes 1572872 | tf_op jit(solution)/shard_map/ppermute | solution.py:916
  347.8 16.2 %all-to-all-start.1 = ((bf16[4,64,1024]{2,1,0:T(8,128)(2,1)}), bf16[4,64,1024]{2,1,0:T(8,128)(2,1)S(1)}, u32[]{:S(2)}, u32[]{:S(2)}) async-start(bf16[4,64,1024]{2,1,0:T(8,128)(2,1)} %bitcast.54), calls=%async_computation.3 | async-start | bytes 1048576 | tf_op jit(solution)/shard_map/all_to_all | solution.py:907
  (68 other events, 529.0 us)
Sparse Core Ops, SparseCore 0:
  20.1 34.0 all-gather.2
  73.3 34.0 all-gather.4
  263.4 34.2 reduce-scatter.4
  299.9 45.0 reduce-scatter.2

commit v6 on v5

--- a/solution.py
+++ b/solution.py
@@ -270,7 +270,7 @@
 PAIR = 128
 TILE = 512
 MIB = 1024 * 1024
-GRANT = {"project": 60, "hidden_back": 60, "heads_back": 60, "layer_out": 60}
+GRANT = {"project": 60, "hidden_back": 60, "heads_back": 60, "layer_out": 60, "join_heads": 30, "expand": 36, "enter": 30, "enter_cot": 30, "grad_fc2": 36}
 WIDE = 1024
 bf16 = jnp.bfloat16
 f32 = jnp.float32
@@ -791,7 +791,7 @@
     )(qkv, qkv, qkv, grads, lse_rows)
 
 
-def both_sides(args, specs, kinds, terms, name, tiles, z_first=0):
+def both_sides(args, specs, kinds, terms, name, tiles, width=TILE, z_first=0):
     count = len(args)
     half = args[0].shape[0] // 2
     mid = half // 4
@@ -832,20 +832,20 @@
             pl.when(step % tiles == tiles - 1)(partial(apart, len(kinds) - 1))
 
     most = kept - 1
-    far = lambda size: pl.BlockSpec((size, TILE), lambda s: (0, jnp.minimum(s, most)))
+    far = lambda size: pl.BlockSpec((size, width), lambda s: (0, jnp.minimum(s, most)))
     near = lambda size: pl.BlockSpec(
-        (size, TILE), lambda s: (0, jnp.minimum(jnp.maximum(s - tiles, 0), most))
-    )
-    both = pl.BlockSpec((mid, TILE), lambda s: (s // tiles, jnp.minimum(s % tiles, most)))
+        (size, width), lambda s: (0, jnp.minimum(jnp.maximum(s - tiles, 0), most))
+    )
+    both = pl.BlockSpec((mid, width), lambda s: (s // tiles, jnp.minimum(s % tiles, most)))
     sizes = (2 * mid, 2 * mid, mid, 2 * mid, mid)
     out_specs = [far(2 * mid), both, far(mid), near(2 * mid), near(mid)]
-    shapes = [array(size, kept * TILE) for size in sizes]
+    shapes = [array(size, kept * width) for size in sizes]
     if z_first:
         each = half // z_first
         out_specs.append(
-            pl.BlockSpec((z_first, 1, each, TILE), lambda s: (0, 1 - s // tiles, 0, 0))
-        )
-        shapes.append(array(z_first, 2, each, TILE))
+            pl.BlockSpec((z_first, 1, each, width), lambda s: (0, 1 - s // tiles, 0, 0))
+        )
+        shapes.append(array(z_first, 2, each, width))
     return kernel_call(body, name, (2 * tiles,), specs, out_specs, shapes)(*args)
 
 
@@ -1112,13 +1112,19 @@
         return both_sides(args, specs, (0, tiles), terms, "grad_two", count)
 
     def grad_qkv():
+        narrow = TILE // 2
+        count = qkv_cols // narrow
+
         def terms(refs, kind):
             return join(*refs[:2]), jnp.concatenate([refs[2][0], refs[3][0]], axis=0)
 
+        def at(s):
+            tile, side = s % count, 1 - s // count
+            return (tile // 2, 0, 2 * side + tile % 2)
+
         args = [h1_t, twin_rows, dp, twin_dp]
-        dp_spec = pl.BlockSpec((1, length, TILE), lambda s: (s % 3, 0, 1 - s // 3))
-        specs = [left_at(0), left_at(1)] + [dp_spec] * 2
-        return both_sides(args, specs, (0,), terms, "grad_qkv", 3, links.nz)
+        specs = [left_at(0), left_at(1)] + [pl.BlockSpec((1, length, narrow), at)] * 2
+        return both_sides(args, specs, (0,), terms, "grad_qkv", count, narrow, links.nz)
 
     def enter_window(done, *homes):
         for home in homes:
@@ -1188,7 +1194,7 @@
     )
 
     home_qkv.first(pieces)
-    by_z = links.z_sum(by_z.reshape(-1, heads_cols))
+    by_z = links.z_sum(by_z.reshape(-1, by_z.shape[-1]))
     small = small + small_got
     small_got = links.x(small)
     moved = home_two.last(pieces, True)

time: 379 us -> 366 us (0.966)
  Pallas kernels: 169 us -> 160 us
  starting transfers between devices: 69.2 us -> 62 us
  waiting for transfers between devices: 74.5 us -> 80.3 us
    ppermute x18, waiting for transfers between devices: 35.6 us -> 51.6 us  [x(): return lax.ppermute(rows, AXES, self.across)]
    all_to_all x2, waiting for transfers between devices: 10.2 us -> 0.01 us  [z_sum(): lax.all_to_all(rows, AXES, 0, 0, tiled=True, axis_index_groups=self.z_gro...]
    all_to_all x2, starting transfers between devices: 13 us -> 8.42 us  [z_sum(): lax.all_to_all(rows, AXES, 0, 0, tiled=True, axis_index_groups=self.z_gro...]
    unnamed x100 -> x138, local copies, waits for them, and re-layouts: 8.79 us -> 12.8 us
  transfers between devices with their start and end apart: 66 -> 66, of which waited for: 22 -> 21; matrix products, arithmetic and copies ran while one was open for 8% -> 7% of each run, Pallas kernels for 45% -> 44%
where the time goes in v6:
time: 366 us; the launch traced here: 359 us
  Pallas kernels  160 us (44%)
  waiting for transfers between devices  80.3 us (22%)
  starting transfers between devices  62 us (17%)
  local copies, waits for them, and re-layouts  28.9 us (8%)
  between operations  16.2 us (4%)
  other arithmetic  8.79 us (2%)
    ppermute x18, waiting for transfers between devices, x(): return lax.ppermute(rows, AXES, self.across)  51.6 us
    pallas_call x3, Pallas kernels, contract_back(): kernel_call(body, name, (2 * load.tiles,), rows_specs + [pl.BlockSpec(mem...  35.4 us
    pallas_call x3, Pallas kernels, both_sides(): kernel_call(body, name, (2 * tiles,), specs, out_specs, shapes)(*args)  33.8 us
    pallas_call x6, Pallas kernels, small_call(): kernel_call(body, name, (1,), [whole(a.shape) for a in args], out_specs,...  19.2 us
    ppermute x14, starting transfers between devices, y(): return lax.ppermute(rows, AXES, self.beside)  18.9 us
    ppermute x18, starting transfers between devices, x(): return lax.ppermute(rows, AXES, self.across)  18.8 us
    pallas_call x1, Pallas kernels, attend_bwd(): kernel_call(attend_back_kernel, 'attend_bwd', (width // PAIR,), [head_spe...  16.9 us
    ppermute x3, waiting for transfers between devices, from_z(): return lax.ppermute(rows, AXES, shift)  14.9 us
  transfers between devices with their start and end apart: 66, of which 21 were waited for; matrix products, arithmetic and copies ran while one was open for 7% of the time, Pallas kernels for 44%

profile of v6, /device:TPU:0, one launch (start us, length us, event | category | flops | bytes accessed | tf_op | source)
XLA Modules:
  0.0 359.3 jit_solution(5833987417111772738)
XLA Ops:
  8.2 1.7 dynamic-slice_bitcast_fusion
  11.0 5.0 %collective-permute-start.2 = (bf16[64,1536]{1,0:T(8,128)(2,1)S(1)}, bf16[64,1536]{1,0:T(8,128)(2,1)S(1)}, u32[]{:S(2)}, u32[]{:S(2)}) collective-permute-start(bf16[64,1536]{1,0:T(8,128)(2,1)S(1)} %bitcast.58), channel_id=1, source_target_pairs={{8,0},{9,1},{10,2},{11,3},{12,4},{13,5},{14,6},{15,7},{16,8},{17,9... | collective-permute-start | bytes 589832 | tf_op jit(solution)/shard_map/ppermute | solution.py:893
  21.4 14.7 %collective-permute-done.3 = bf16[64,1536]{1,0:T(8,128)(2,1)S(1)} collective-permute-done((bf16[64,1536]{1,0:T(8,128)(2,1)S(1)}, bf16[64,1536]{1,0:T(8,128)(2,1)S(1)}, u32[]{:S(2)}, u32[]{:S(2)}) %collective-permute-start.3) | collective-permute-done | bytes 196640 | tf_op jit(solution)/shard_map/ppermute | solution.py:893
  36.2 1.7 collective-permute-start.5
  37.9 2.2 collective-permute-start.6
  47.3 1.7 enter.1
  51.1 7.4 %collective-permute-done.5.refs_1_.refs_6_ = bf16[256,1536]{1,0:T(8,128)(2,1)S(1)} collective-permute-done((bf16[256,1536]{1,0:T(8,128)(2,1)S(1)}, bf16[256,1536]{1,0:T(8,128)(2,1)S(1)}, u32[]{:S(2)}, u32[]{:S(2)}) %collective-permute-start.5) | collective-permute-done | bytes 786464 | tf_op jit(solution)/shard_map/ppermute | solution.py:916
  60.2 1.6 collective-permute-start.7
  61.7 1.5 collective-permute-start.8
  64.8 1.5 collective-permute-start.16
  66.3 5.9 %collective-permute-done.7.refs_3_.refs_8_ = bf16[128,1536]{1,0:T(8,128)(2,1)S(1)} collective-permute-done((bf16[128,1536]{1,0:T(8,128)(2,1)S(1)}, bf16[128,1536]{1,0:T(8,128)(2,1)S(1)}, u32[]{:S(2)}, u32[]{:S(2)}) %collective-permute-start.7) | collective-permute-done | bytes 393248 | tf_op jit(solution)/shard_map/ppermute | solution.py:916
  72.2 1.6 collective-permute-done.8.refs_4_.refs_9_
  75.4 2.0 collective-permute-done.13.refs_8_.refs_13_
  77.9 8.3 %project.1.q_ref.k_ref.v_ref = bf16[3,512,1024]{2,1,0:T(8,128)(2,1)} custom-call(bf16[512,1024]{1,0:T(8,128)(2,1)} %copy-done.18, f32[2,1,1536]{2,1,0:T(1,128)} %broadcast_in_dim.23.bias_ref, bf16[256,1536]{1,0:T(8,128)(2,1)} %copy-done.25, bf16[256,1536]{1,0:T(8,128)(2,1)} %copy-done.28, bf16[256,1536]{1,0:T(8,128)(2,1)} %collective-permute-done.6.refs_2_.refs_7_, ...), custom_call_target="tpu_custom_call" | custom-call | flops 1 | bytes 1 | tf_op jit(solution)/shard_map/project/pallas_call | solution.py:445
  86.3 12.3 %attend_fwd.1 = (bf16[512,1024]{1,0:T(8,128)(2,1)}, f32[512,128]{1,0:T(8,128)}) custom-call(bf16[3,512,1024]{2,1,0:T(8,128)(2,1)} %project.1.q_ref.k_ref.v_ref, bf16[3,512,1024]{2,1,0:T(8,128)(2,1)} %project.1.q_ref.k_ref.v_ref, bf16[3,512,1024]{2,1,0:T(8,128)(2,1)} %project.1.q_ref.k_ref.v_ref), custom_call_target="tpu_custom_call" | custom-call | flops 1 | bytes 1 | tf_op jit(solution)/shard_map/attend_fwd/pallas_call | solution.py:485
  98.5 1.8 copy.28
  106.2 1.7 collective-permute-done.19.refs_7_.refs_11_
  108.5 1.5 collective-permute-start.21
  110.0 11.1 %collective-permute-done.22.refs_3_.refs_7_ = bf16[128,2560]{1,0:T(8,128)(2,1)S(1)} collective-permute-done((bf16[128,2560]{1,0:T(8,128)(2,1)}, bf16[128,2560]{1,0:T(8,128)(2,1)S(1)}, u32[]{:S(2)}, u32[]{:S(2)}) %collective-permute-start.22) | collective-permute-done | bytes 655392 | tf_op jit(solution)/shard_map/ppermute | solution.py:916
  122.3 2.5 collective-permute-done.24.refs_8_.refs_12_
  125.0 1.6 copy-done.3
  127.8 4.4 %join_heads.1 = (f32[512,1024]{1,0:T(8,128)S(1)}, bf16[512,1024]{1,0:T(8,128)(2,1)S(1)}, bf16[1024,512]{1,0:T(8,128)(2,1)S(1)}) custom-call(bf16[512,1024]{1,0:T(8,128)(2,1)} %get-tuple-element.261.attn_ref.refs_6_, bf16[512,1024]{1,0:T(8,128)(2,1)S(1)} %copy-done.11, f32[1,1024]{1,0:T(1,128)S(1)} %get-tuple-element.388.bias_ref, ...), custom_call_target="tpu_custom_call" | custom-call | flops 1 | bytes 1 | tf_op jit(solution)/shard_map/join_heads/pallas_call | solution.py:515
  133.6 11.4 %expand.1 = (bf16[512,4096]{1,0:T(8,128)(2,1)S(1)}, bf16[512,4096]{1,0:T(8,128)(2,1)}) custom-call(bf16[512,1024]{1,0:T(8,128)(2,1)S(1)} %get-tuple-element.226.h_ref, f32[1,4096]{1,0:T(1,128)S(1)} %bitcast.54, bf16[256,2560]{1,0:T(8,128)(2,1)S(1)} %copy-done.4, bf16[256,2560]{1,0:T(8,128)(2,1)S(1)} %collective-permute-done.15.refs_1_.refs_5_, ...), custom_call_target="tpu_custom_call" | custom-call | flops 1 | bytes 1 | tf_op jit(solution)/shard_map/expand/pallas_call | solution.py:543
  147.3 1.5 collective-permute-start.27
  148.9 11.2 %collective-permute-done.26.refs_3_.refs_8_ = bf16[128,2048]{1,0:T(8,128)(2,1)S(1)} collective-permute-done((bf16[128,2048]{1,0:T(8,128)(2,1)S(1)}, bf16[128,2048]{1,0:T(8,128)(2,1)S(1)}, u32[]{:S(2)}, u32[]{:S(2)}) %collective-permute-start.26) | collective-permute-done | bytes 524320 | tf_op jit(solution)/shard_map/ppermute | solution.py:916
  162.4 8.2 %grad_fc2.1 = (bf16[256,2048]{1,0:T(8,128)(2,1)S(1)}, bf16[256,2048]{1,0:T(8,128)(2,1)S(1)}, bf16[128,2048]{1,0:T(8,128)(2,1)S(1)}, bf16[256,2048]{1,0:T(8,128)(2,1)S(1)}, bf16[128,2048]{1,0:T(8,128)(2,1)S(1)}) custom-call(bf16[1024,512]{1,0:T(8,128)(2,1)S(1)} %copy-done.14, bf16[1024,512]{1,0:T(8,128)(2,1)} %collective-permute-done.12.refs_1_, ...), custom_call_target="tpu_custom_call" | custom-call | flops 1 | bytes 1 | tf_op jit(solution)/shard_map/grad_fc2/pallas_call | solution.py:849
  174.6 1.5 collective-permute-start.37
  176.2 10.2 %hidden_back.1 = (bf16[512,4096]{1,0:T(8,128)(2,1)}, f32[1,4096]{1,0:T(1,128)}) custom-call(bf16[512,1024]{1,0:T(8,128)(2,1)} %copy-done.12, bf16[512,4096]{1,0:T(8,128)(2,1)} %get-tuple-element.249.slope_ref, bf16[256,2048]{1,0:T(8,128)(2,1)} %all-gather.5.cloned.1.call-done.refs_0_.refs_5_, bf16[256,2048]{1,0:T(8,128)(2,1)} %copy-done.26, ...), custom_call_target="tpu_custom_call" | custom-call | flops 1 | bytes 1 | tf_op jit(solution)/shard_map/hidden_back/pallas_call | solution.py:571
  186.5 12.8 %second_back.1 = (f32[512,1024]{1,0:T(8,128)}, bf16[512,1024]{1,0:T(8,128)(2,1)}, bf16[512,512]{1,0:T(8,128)(2,1)}, bf16[512,512]{1,0:T(8,128)(2,1)}, f32[4,1024]{1,0:T(4,128)}) custom-call(bf16[512,4096]{1,0:T(8,128)(2,1)} %get-tuple-element.265.refs_0_.refs_2_, f32[512,1024]{1,0:T(8,128)} %copy-done.9, bf16[512,1024]{1,0:T(8,128)(2,1)} %copy-done.12, ...), custom_call_target="tpu_custom_call" | custom-call | flops 1 | bytes 1 | tf_op jit(solution)/shard_map/second_back/pallas_call | solution.py:635
  200.3 3.0 add_mid.3
  206.1 4.9 %heads_back.1.g_ref = bf16[512,1024]{1,0:T(8,128)(2,1)} custom-call(bf16[512,1024]{1,0:T(8,128)(2,1)} %get-tuple-element.267.da_ref, bf16[256,2560]{1,0:T(8,128)(2,1)} %all-gather.3.cloned.1.call-done.refs_0_.refs_4_, bf16[256,2560]{1,0:T(8,128)(2,1)} %copy-done.1, bf16[256,2560]{1,0:T(8,128)(2,1)} %copy-done.2, bf16[128,2560]{1,0:T(8,128)(2,1)} %copy-done.6, ...), custom_call_target="tpu_custom_call" | custom-call | flops 1 | bytes 1 | tf_op jit(solution)/shard_map/heads_back/pallas_call | solution.py:593
  211.8 13.8 %grad_two.1 = (bf16[256,2560]{1,0:T(8,128)(2,1)}, bf16[256,2560]{1,0:T(8,128)(2,1)}, bf16[128,2560]{1,0:T(8,128)(2,1)}, bf16[256,2560]{1,0:T(8,128)(2,1)}, bf16[128,2560]{1,0:T(8,128)(2,1)}) custom-call(bf16[1024,512]{1,0:T(8,128)(2,1)} %copy-done.15, bf16[512,512]{1,0:T(8,128)(2,1)} %copy-done.45, bf16[512,4096]{1,0:T(8,128)(2,1)} %get-tuple-element.265.refs_0_.refs_2_, ...), custom_call_target="tpu_custom_call" | custom-call | flops 1 | bytes 1 | tf_op jit(solution)/shard_map/grad_two/pallas_call | solution.py:849
  227.0 3.5 add_last.3
  230.4 16.9 %attend_bwd.1 = (bf16[3,512,1024]{2,1,0:T(8,128)(2,1)}, f32[1,1024]{1,0:T(1,128)}, f32[1,1024]{1,0:T(1,128)}) custom-call(bf16[3,512,1024]{2,1,0:T(8,128)(2,1)} %project.1.q_ref.k_ref.v_ref, bf16[3,512,1024]{2,1,0:T(8,128)(2,1)} %project.1.q_ref.k_ref.v_ref, bf16[3,512,1024]{2,1,0:T(8,128)(2,1)} %project.1.q_ref.k_ref.v_ref, ...), custom_call_target="tpu_custom_call" | custom-call | flops 1 | bytes 1 | tf_op jit(solution)/shard_map/attend_bwd/pallas_call | solution.py:783
  247.4 11.1 %first_back.1 = (bf16[256,1024]{1,0:T(8,128)(2,1)}, bf16[256,1024]{1,0:T(8,128)(2,1)}, f32[2,1024]{1,0:T(2,128)}) custom-call(bf16[3,512,1024]{2,1,0:T(8,128)(2,1)} %get-tuple-element.300.refs_0_.refs_2_, bf16[512,1024]{1,0:T(8,128)(2,1)} %copy-done.10, f32[512,1024]{1,0:T(8,128)} %get-tuple-element.296.refs_2_, f32[1,1024]{1,0:T(1,128)} %copy-done.22, ...), custom_call_target="tpu_custom_call" | custom-call | flops 1 | bytes 1 | tf_op jit(solution)/shard_map/first_back/pallas_call | solution.py:635
  258.9 3.3 add_mid.4
  265.0 1.9 fusion
  268.3 2.5 collective-permute-start.48
  270.8 11.8 %grad_qkv.1 = (bf16[256,1280]{1,0:T(8,128)(2,1)}, bf16[256,1280]{1,0:T(8,128)(2,1)}, bf16[128,1280]{1,0:T(8,128)(2,1)}, bf16[256,1280]{1,0:T(8,128)(2,1)}, bf16[...) custom-call(bf16[1024,512]{1,0:T(8,128)(2,1)} %copy-done.16, bf16[1024,512]{1,0:T(8,128)(2,1)} %collective-permute-done.12.refs_1_, ...), custom_call_target="tpu_custom_call" | custom-call | flops 1 | bytes 1 | tf_op jit(solution)/shard_map/grad_qkv/pallas_call | solution.py:849
  282.7 4.1 %add_last.4 = bf16[256,2560]{1,0:T(8,128)(2,1)} custom-call(bf16[256,2560]{1,0:T(8,128)(2,1)} %get-tuple-element.289.k00_ref, bf16[256,2560]{1,0:T(8,128)(2,1)} %collective-permute-done.42.rx_ref, bf16[256,2560]{1,0:T(8,128)(2,1)} %collective-permute-done.43.ry_ref, bf16[128,2560]{1,0:T(8,128)(2,1)} %collective-permute-done.46.y2_ref, ...), custom_call_target="tpu_custom_call" | custom-call | flops 1 | bytes 1 | tf_op jit(solution)/shard_map/add_last/pallas_call | solution.py:869
  288.2 4.9 %all-to-all-start = ((bf16[4,256,256]{2,1,0:T(8,128)(2,1)}), bf16[4,256,256]{2,1,0:T(8,128)(2,1)S(1)}, u32[]{:S(2)}, u32[]{:S(2)}) async-start(bf16[4,256,256]{2,1,0:T(8,128)(2,1)} %bitcast.22), calls=%async_computation | async-start | bytes 1048576 | tf_op jit(solution)/shard_map/all_to_all | solution.py:907
  293.8 10.2 %collective-permute-done.49.rx_ref = bf16[256,1280]{1,0:T(8,128)(2,1)S(1)} collective-permute-done((bf16[256,1280]{1,0:T(8,128)(2,1)S(1)}, bf16[256,1280]{1,0:T(8,128)(2,1)S(1)}, u32[]{:S(2)}, u32[]{:S(2)}) %collective-permute-start.49) | collective-permute-done | bytes 655392 | tf_op jit(solution)/shard_map/ppermute | solution.py:916
  305.7 2.4 add_mid.5
  312.1 11.5 %layer_out.1 = (bf16[256,1024]{1,0:T(8,128)(2,1)}, bf16[256,1024]{1,0:T(8,128)(2,1)}) custom-call(bf16[512,4096]{1,0:T(8,128)(2,1)} %copy-done.5, f32[512,1024]{1,0:T(8,128)} %copy-done.9, f32[1,1024]{1,0:T(1,128)} %get-tuple-element.385.refs_2_, f32[1,1024]{1,0:T(1,128)} %copy-done.23, bf16[1024,1024]{1,0:T(8,128)(2,1)} %copy-done, ...), custom_call_target="tpu_custom_call" | custom-call | flops 1 | bytes 1 | tf_op jit(solution)/shard_map/layer_out/pallas_call | solution.py:635
  324.5 2.8 add_last.5
  329.5 2.2 collective-permute-start.56
  331.7 3.5 all-to-all-start.1
  335.2 5.6 %collective-permute-done.55 = bf16[128,256]{1,0:T(8,128)(2,1)S(1)} collective-permute-done((bf16[128,256]{1,0:T(8,128)(2,1)S(1)}, bf16[128,256]{1,0:T(8,128)(2,1)S(1)}, u32[]{:S(2)}, u32[]{:S(2)}) %collective-permute-start.55) | collective-permute-done | bytes 65568 | tf_op jit(solution)/shard_map/ppermute | solution.py:916
  (324 shorter events, 72.7 us)
Async XLA Ops:
  7.2 51.3 %all-gather.3.cloned.1.call-start = ((), (), s32[]{:S(2)}) async-start(), calls=%async_computation.4 | async-start | bytes 1638400 | tf_op jit(solution)/shard_map/all_gather | solution.py:911
  16.1 20.1 %collective-permute-start.3 = (bf16[64,1536]{1,0:T(8,128)(2,1)S(1)}, bf16[64,1536]{1,0:T(8,128)(2,1)S(1)}, u32[]{:S(2)}, u32[]{:S(2)}) collective-permute-start(bf16[64,1536]{1,0:T(8,128)(2,1)S(1)} %bitcast.59), channel_id=1, source_target_pairs={{16,0},{17,1},{18,2},{19,3},{20,4},{21,5},{22,6},{23,7},{24,8},{25... | collective-permute-start | bytes 589832 | tf_op jit(solution)/shard_map/ppermute | solution.py:893
  16.1 20.1 %collective-permute-start.4 = (bf16[64,1536]{1,0:T(8,128)(2,1)S(1)}, bf16[64,1536]{1,0:T(8,128)(2,1)S(1)}, u32[]{:S(2)}, u32[]{:S(2)}) collective-permute-start(bf16[64,1536]{1,0:T(8,128)(2,1)S(1)} %bitcast.60), channel_id=1, source_target_pairs={{24,0},{25,1},{26,2},{27,3},{28,4},{29,5},{30,6},{31,7},{0,8},{1,9... | collective-permute-start | bytes 589832 | tf_op jit(solution)/shard_map/ppermute | solution.py:893
  17.1 26.6 %collective-permute-start = (bf16[512,1024]{1,0:T(8,128)(2,1)}, bf16[512,1024]{1,0:T(8,128)(2,1)}, u32[]{:S(2)}, u32[]{:S(2)}) collective-permute-start(bf16[512,1024]{1,0:T(8,128)(2,1)} %pad_maximum_fusion), channel_id=1, source_target_pairs={{1,0},{0,1},{3,2},{2,3},{5,4},{4,5},{7,6},{6,7},{9,8},{8,9},{11,10... | collective-permute-start | bytes 3145736 | tf_op jit(solution)/shard_map/ppermute | solution.py:916
  18.6 25.1 %collective-permute-start.1 = (f32[24,128]{1,0:T(8,128)S(1)}, f32[24,128]{1,0:T(8,128)S(1)}, u32[]{:S(2)}, u32[]{:S(2)}) collective-permute-start(f32[24,128]{1,0:T(8,128)S(1)} %maximum_bitcast_fusion.1), channel_id=1, source_target_pairs={{1,0},{0,1},{3,2},{2,3},{5,4},{4,5},{7,6},{6,7},{9,8},{8,9},{11,10... | collective-permute-start | bytes 36872 | tf_op jit(solution)/shard_map/ppermute | solution.py:916
  20.0 85.5 %all-gather.5.cloned.1.call-start = ((), (), s32[]{:S(2)}) async-start(), calls=%async_computation.5 | async-start | bytes 1310720 | tf_op jit(solution)/shard_map/all_gather | solution.py:911
  36.2 22.2 %collective-permute-start.5 = (bf16[256,1536]{1,0:T(8,128)(2,1)S(1)}, bf16[256,1536]{1,0:T(8,128)(2,1)S(1)}, u32[]{:S(2)}, u32[]{:S(2)}) collective-permute-start(bf16[256,1536]{1,0:T(8,128)(2,1)S(1)} %constant_dynamic-update-slice_fusion.refs_0_.refs_5_), channel_id=1, source_target_pairs={{1,0},{0,1},{3,2},{2,3},{5,4},{4,5},{7,6},{6,7},{9,8},{8,9},{11,10... | collective-permute-start | bytes 2359304 | tf_op jit(solution)/shard_map/ppermute | solution.py:916
  37.9 20.6 %collective-permute-start.6 = (bf16[256,1536]{1,0:T(8,128)(2,1)S(1)}, bf16[256,1536]{1,0:T(8,128)(2,1)}, u32[]{:S(2)}, u32[]{:S(2)}) collective-permute-start(bf16[256,1536]{1,0:T(8,128)(2,1)S(1)} %constant_dynamic-update-slice_fusion.refs_0_.refs_5_), channel_id=1, source_target_pairs={{4,0},{5,1},{6,2},{7,3},{0,4},{1,5},{2,6},{3,7},{12,8},{13,9},{14,... | collective-permute-start | bytes 2359304 | tf_op jit(solution)/shard_map/ppermute | solution.py:919
  60.2 12.0 %collective-permute-start.7 = (bf16[128,1536]{1,0:T(8,128)(2,1)S(1)}, bf16[128,1536]{1,0:T(8,128)(2,1)S(1)}, u32[]{:S(2)}, u32[]{:S(2)}) collective-permute-start(bf16[128,1536]{1,0:T(8,128)(2,1)S(1)} %slice.156), channel_id=1, source_target_pairs={{1,0},{0,1},{3,2},{2,3},{5,4},{4,5},{7,6},{6,7},{9,8},{8,9},{11,10... | collective-permute-start | bytes 1179656 | tf_op jit(solution)/shard_map/ppermute | solution.py:916
  61.7 12.1 %collective-permute-start.8 = (bf16[128,1536]{1,0:T(8,128)(2,1)S(1)}, bf16[128,1536]{1,0:T(8,128)(2,1)}, u32[]{:S(2)}, u32[]{:S(2)}) collective-permute-start(bf16[128,1536]{1,0:T(8,128)(2,1)S(1)} %slice.157), channel_id=1, source_target_pairs={{4,0},{5,1},{6,2},{7,3},{0,4},{1,5},{2,6},{3,7},{12,8},{13,9},{14,... | collective-permute-start | bytes 1179656 | tf_op jit(solution)/shard_map/ppermute | solution.py:919
  63.3 37.0 %collective-permute-start.15 = (bf16[256,2560]{1,0:T(8,128)(2,1)}, bf16[256,2560]{1,0:T(8,128)(2,1)S(1)}, u32[]{:S(2)}, u32[]{:S(2)}) collective-permute-start(bf16[256,2560]{1,0:T(8,128)(2,1)} %all-gather.3.cloned.1.call-done.refs_0_.refs_4_), channel_id=1, source_target_pairs={{1,0},{0,1},{3,2},{2,3},{5,4},{4,5},{7,6},{6,7},{9,8},{8,9},{11,10... | collective-permute-start | bytes 3932168 | tf_op jit(solution)/shard_map/ppermute | solution.py:916
  64.8 36.2 %collective-permute-start.16 = (bf16[256,2560]{1,0:T(8,128)(2,1)}, bf16[256,2560]{1,0:T(8,128)(2,1)S(1)}, u32[]{:S(2)}, u32[]{:S(2)}) collective-permute-start(bf16[256,2560]{1,0:T(8,128)(2,1)} %all-gather.3.cloned.1.call-done.refs_0_.refs_4_), channel_id=1, source_target_pairs={{4,0},{5,1},{6,2},{7,3},{0,4},{1,5},{2,6},{3,7},{12,8},{13,9},{14,... | collective-permute-start | bytes 3932168 | tf_op jit(solution)/shard_map/ppermute | solution.py:919
  74.4 266.5 %reduce-scatter.5.cloned.1.call-start = ((), (), s32[]{:S(2)}) async-start(), calls=%async_computation.7 | async-start | bytes 1310720 | tf_op jit(solution)/shard_map/reduce_scatter | solution.py:902
  103.3 17.7 %collective-permute-start.22 = (bf16[128,2560]{1,0:T(8,128)(2,1)}, bf16[128,2560]{1,0:T(8,128)(2,1)S(1)}, u32[]{:S(2)}, u32[]{:S(2)}) collective-permute-start(bf16[128,2560]{1,0:T(8,128)(2,1)} %slice.163), channel_id=1, source_target_pairs={{1,0},{0,1},{3,2},{2,3},{5,4},{4,5},{7,6},{6,7},{9,8},{8,9},{11,10... | collective-permute-start | bytes 1966088 | tf_op jit(solution)/shard_map/ppermute | solution.py:916
  103.9 17.9 %collective-permute-start.23 = (bf16[128,2560]{1,0:T(8,128)(2,1)}, bf16[128,2560]{1,0:T(8,128)(2,1)}, u32[]{:S(2)}, u32[]{:S(2)}) collective-permute-start(bf16[128,2560]{1,0:T(8,128)(2,1)} %slice.164), channel_id=1, source_target_pairs={{4,0},{5,1},{6,2},{7,3},{0,4},{1,5},{2,6},{3,7},{12,8},{13,9},{14,... | collective-permute-start | bytes 1966088 | tf_op jit(solution)/shard_map/ppermute | solution.py:919
  107.9 37.0 %collective-permute-start.20 = (bf16[256,2048]{1,0:T(8,128)(2,1)}, bf16[256,2048]{1,0:T(8,128)(2,1)S(1)}, u32[]{:S(2)}, u32[]{:S(2)}) collective-permute-start(bf16[256,2048]{1,0:T(8,128)(2,1)} %all-gather.5.cloned.1.call-done.refs_0_.refs_5_), channel_id=1, source_target_pairs={{1,0},{0,1},{3,2},{2,3},{5,4},{4,5},{7,6},{6,7},{9,8},{8,9},{11,10... | collective-permute-start | bytes 3145736 | tf_op jit(solution)/shard_map/ppermute | solution.py:916
  108.5 36.5 %collective-permute-start.21 = (bf16[256,2048]{1,0:T(8,128)(2,1)}, bf16[256,2048]{1,0:T(8,128)(2,1)S(1)}, u32[]{:S(2)}, u32[]{:S(2)}) collective-permute-start(bf16[256,2048]{1,0:T(8,128)(2,1)} %all-gather.5.cloned.1.call-done.refs_0_.refs_5_), channel_id=1, source_target_pairs={{4,0},{5,1},{6,2},{7,3},{0,4},{1,5},{2,6},{3,7},{12,8},{13,9},{14,... | collective-permute-start | bytes 3145736 | tf_op jit(solution)/shard_map/ppermute | solution.py:919
  145.0 16.3 %collective-permute-start.28 = (bf16[512,4096]{1,0:T(8,128)(2,1)S(1)}, bf16[512,4096]{1,0:T(8,128)(2,1)S(1)}, u32[]{:S(2)}, u32[]{:S(2)}) collective-permute-start(bf16[512,4096]{1,0:T(8,128)(2,1)S(1)} %get-tuple-element.335.refs_2_.refs_0_), channel_id=1, source_target_pairs={{2,0},{3,1},{0,2},{1,3},{6,4},{7,5},{4,6},{5,7},{10,8},{11,9},{8,1... | collective-permute-start | bytes 12582920 | tf_op jit(solution)/shard_map/ppermute | solution.py:922
  145.2 16.0 %collective-permute-start.29 = (bf16[256,2048]{1,0:T(8,128)(2,1)S(1)}, bf16[256,2048]{1,0:T(8,128)(2,1)S(1)}, u32[]{:S(2)}, u32[]{:S(2)}) collective-permute-start(bf16[256,2048]{1,0:T(8,128)(2,1)S(1)} %copy-done.30), channel_id=1, source_target_pairs={{2,0},{3,1},{0,2},{1,3},{6,4},{7,5},{4,6},{5,7},{10,8},{11,9},{8,1... | collective-permute-start | bytes 3145736 | tf_op jit(solution)/shard_map/ppermute | solution.py:922
  145.6 15.7 %collective-permute-start.30 = (bf16[256,2048]{1,0:T(8,128)(2,1)S(1)}, bf16[256,2048]{1,0:T(8,128)(2,1)S(1)}, u32[]{:S(2)}, u32[]{:S(2)}) collective-permute-start(bf16[256,2048]{1,0:T(8,128)(2,1)S(1)} %collective-permute-done.20.refs_1_.refs_6_), channel_id=1, source_target_pairs={{2,0},{3,1},{0,2},{1,3},{6,4},{7,5},{4,6},{5,7},{10,8},{11,9},{8,1... | collective-permute-start | bytes 3145736 | tf_op jit(solution)/shard_map/ppermute | solution.py:922
  145.8 14.3 %collective-permute-start.26 = (bf16[128,2048]{1,0:T(8,128)(2,1)S(1)}, bf16[128,2048]{1,0:T(8,128)(2,1)S(1)}, u32[]{:S(2)}, u32[]{:S(2)}) collective-permute-start(bf16[128,2048]{1,0:T(8,128)(2,1)S(1)} %slice.166), channel_id=1, source_target_pairs={{1,0},{0,1},{3,2},{2,3},{5,4},{4,5},{7,6},{6,7},{9,8},{8,9},{11,10... | collective-permute-start | bytes 1572872 | tf_op jit(solution)/shard_map/ppermute | solution.py:916
  147.3 13.9 %collective-permute-start.27 = (bf16[128,2048]{1,0:T(8,128)(2,1)S(1)}, bf16[128,2048]{1,0:T(8,128)(2,1)S(1)}, u32[]{:S(2)}, u32[]{:S(2)}) collective-permute-start(bf16[128,2048]{1,0:T(8,128)(2,1)S(1)} %slice.167), channel_id=1, source_target_pairs={{4,0},{5,1},{6,2},{7,3},{0,4},{1,5},{2,6},{3,7},{12,8},{13,9},{14,... | collective-permute-start | bytes 1572872 | tf_op jit(solution)/shard_map/ppermute | solution.py:919
  161.3 12.0 %collective-permute-start.31 = (bf16[256,2048]{1,0:T(8,128)(2,1)S(1)}, bf16[256,2048]{1,0:T(8,128)(2,1)S(1)}, u32[]{:S(2)}, u32[]{:S(2)}) collective-permute-start(bf16[256,2048]{1,0:T(8,128)(2,1)S(1)} %collective-permute-done.21.refs_2_.refs_7_), channel_id=1, source_target_pairs={{2,0},{3,1},{0,2},{1,3},{6,4},{7,5},{4,6},{5,7},{10,8},{11,9},{8,1... | collective-permute-start | bytes 3145736 | tf_op jit(solution)/shard_map/ppermute | solution.py:922
  161.3 11.9 %collective-permute-start.32 = (bf16[128,2048]{1,0:T(8,128)(2,1)S(1)}, bf16[128,2048]{1,0:T(8,128)(2,1)S(1)}, u32[]{:S(2)}, u32[]{:S(2)}) collective-permute-start(bf16[128,2048]{1,0:T(8,128)(2,1)S(1)} %collective-permute-done.26.refs_3_.refs_8_), channel_id=1, source_target_pairs={{2,0},{3,1},{0,2},{1,3},{6,4},{7,5},{4,6},{5,7},{10,8},{11,9},{8,1... | collective-permute-start | bytes 1572872 | tf_op jit(solution)/shard_map/ppermute | solution.py:922
  161.8 11.4 %collective-permute-start.33 = (bf16[128,2048]{1,0:T(8,128)(2,1)S(1)}, bf16[128,2048]{1,0:T(8,128)(2,1)S(1)}, u32[]{:S(2)}, u32[]{:S(2)}) collective-permute-start(bf16[128,2048]{1,0:T(8,128)(2,1)S(1)} %collective-permute-done.27.refs_4_.refs_9_), channel_id=1, source_target_pairs={{2,0},{3,1},{0,2},{1,3},{6,4},{7,5},{4,6},{5,7},{10,8},{11,9},{8,1... | collective-permute-start | bytes 1572872 | tf_op jit(solution)/shard_map/ppermute | solution.py:922
  174.0 25.2 %collective-permute-start.36 = (bf16[256,2048]{1,0:T(8,128)(2,1)S(1)}, bf16[256,2048]{1,0:T(8,128)(2,1)S(1)}, u32[]{:S(2)}, u32[]{:S(2)}) collective-permute-start(bf16[256,2048]{1,0:T(8,128)(2,1)S(1)} %get-tuple-element.262), channel_id=1, source_target_pairs={{1,0},{0,1},{3,2},{2,3},{5,4},{4,5},{7,6},{6,7},{9,8},{8,9},{11,10... | collective-permute-start | bytes 3145736 | tf_op jit(solution)/shard_map/ppermute | solution.py:916
  174.6 25.0 %collective-permute-start.37 = (bf16[256,2048]{1,0:T(8,128)(2,1)S(1)}, bf16[256,2048]{1,0:T(8,128)(2,1)}, u32[]{:S(2)}, u32[]{:S(2)}) collective-permute-start(bf16[256,2048]{1,0:T(8,128)(2,1)S(1)} %get-tuple-element.263), channel_id=1, source_target_pairs={{4,0},{5,1},{6,2},{7,3},{0,4},{1,5},{2,6},{3,7},{12,8},{13,9},{14,... | collective-permute-start | bytes 3145736 | tf_op jit(solution)/shard_map/ppermute | solution.py:919
  176.1 23.4 %collective-permute-start.35 = (bf16[512,1024]{1,0:T(8,128)(2,1)}, bf16[512,1024]{1,0:T(8,128)(2,1)}, u32[]{:S(2)}, u32[]{:S(2)}) collective-permute-start(bf16[512,1024]{1,0:T(8,128)(2,1)} %get-tuple-element.261.attn_ref.refs_6_), channel_id=1, source_target_pairs={{2,0},{3,1},{0,2},{1,3},{6,4},{7,5},{4,6},{5,7},{10,8},{11,9},{8,1... | collective-permute-start | bytes 3145736 | tf_op jit(solution)/shard_map/ppermute | solution.py:922
  199.6 11.4 %collective-permute-start.38 = (bf16[512,4096]{1,0:T(8,128)(2,1)}, bf16[512,4096]{1,0:T(8,128)(2,1)}, u32[]{:S(2)}, u32[]{:S(2)}) collective-permute-start(bf16[512,4096]{1,0:T(8,128)(2,1)} %get-tuple-element.265.refs_0_.refs_2_), channel_id=1, source_target_pairs={{2,0},{3,1},{0,2},{1,3},{6,4},{7,5},{4,6},{5,7},{10,8},{11,9},{8,1... | collective-permute-start | bytes 12582920 | tf_op jit(solution)/shard_map/ppermute | solution.py:922
  203.3 22.3 %collective-permute-start.40 = (bf16[128,2048]{1,0:T(8,128)(2,1)}, bf16[128,2048]{1,0:T(8,128)(2,1)S(1)}, u32[]{:S(2)}, u32[]{:S(2)}) collective-permute-start(bf16[128,2048]{1,0:T(8,128)(2,1)} %get-tuple-element.280), channel_id=1, source_target_pairs={{4,0},{5,1},{6,2},{7,3},{0,4},{1,5},{2,6},{3,7},{12,8},{13,9},{14,... | collective-permute-start | bytes 1572872 | tf_op jit(solution)/shard_map/ppermute | solution.py:919
  204.7 20.9 %collective-permute-start.41 = (bf16[128,2048]{1,0:T(8,128)(2,1)}, bf16[128,2048]{1,0:T(8,128)(2,1)S(1)}, u32[]{:S(2)}, u32[]{:S(2)}) collective-permute-start(bf16[128,2048]{1,0:T(8,128)(2,1)} %get-tuple-element.281), channel_id=1, source_target_pairs={{1,0},{0,1},{3,2},{2,3},{5,4},{4,5},{7,6},{6,7},{9,8},{8,9},{11,10... | collective-permute-start | bytes 1572872 | tf_op jit(solution)/shard_map/ppermute | solution.py:916
  225.6 32.9 %collective-permute-start.42 = (bf16[256,2560]{1,0:T(8,128)(2,1)}, bf16[256,2560]{1,0:T(8,128)(2,1)}, u32[]{:S(2)}, u32[]{:S(2)}) collective-permute-start(bf16[256,2560]{1,0:T(8,128)(2,1)} %get-tuple-element.286), channel_id=1, source_target_pairs={{1,0},{0,1},{3,2},{2,3},{5,4},{4,5},{7,6},{6,7},{9,8},{8,9},{11,10... | collective-permute-start | bytes 3932168 | tf_op jit(solution)/shard_map/ppermute | solution.py:916
  226.3 32.2 %collective-permute-start.43 = (bf16[256,2560]{1,0:T(8,128)(2,1)}, bf16[256,2560]{1,0:T(8,128)(2,1)}, u32[]{:S(2)}, u32[]{:S(2)}) collective-permute-start(bf16[256,2560]{1,0:T(8,128)(2,1)} %get-tuple-element.287), channel_id=1, source_target_pairs={{4,0},{5,1},{6,2},{7,3},{0,4},{1,5},{2,6},{3,7},{12,8},{13,9},{14,... | collective-permute-start | bytes 3932168 | tf_op jit(solution)/shard_map/ppermute | solution.py:919
  258.7 82.2 %reduce-scatter.3.cloned.1.call-start = ((), (), s32[]{:S(2)}) async-start(), calls=%async_computation.6 | async-start | bytes 1638400 | tf_op jit(solution)/shard_map/reduce_scatter | solution.py:902
  262.2 20.4 %collective-permute-start.46 = (bf16[128,2560]{1,0:T(8,128)(2,1)}, bf16[128,2560]{1,0:T(8,128)(2,1)}, u32[]{:S(2)}, u32[]{:S(2)}) collective-permute-start(bf16[128,2560]{1,0:T(8,128)(2,1)} %get-tuple-element.304), channel_id=1, source_target_pairs={{4,0},{5,1},{6,2},{7,3},{0,4},{1,5},{2,6},{3,7},{12,8},{13,9},{14,... | collective-permute-start | bytes 1966088 | tf_op jit(solution)/shard_map/ppermute | solution.py:919
  263.6 19.0 %collective-permute-start.47 = (bf16[128,2560]{1,0:T(8,128)(2,1)}, bf16[128,2560]{1,0:T(8,128)(2,1)}, u32[]{:S(2)}, u32[]{:S(2)}) collective-permute-start(bf16[128,2560]{1,0:T(8,128)(2,1)} %get-tuple-element.305), channel_id=1, source_target_pairs={{1,0},{0,1},{3,2},{2,3},{5,4},{4,5},{7,6},{6,7},{9,8},{8,9},{11,10... | collective-permute-start | bytes 1966088 | tf_op jit(solution)/shard_map/ppermute | solution.py:916
  268.3 14.4 %collective-permute-start.48 = (f32[96,128]{1,0:T(8,128)S(1)}, f32[96,128]{1,0:T(8,128)S(1)}, u32[]{:S(2)}, u32[]{:S(2)}) collective-permute-start(f32[96,128]{1,0:T(8,128)S(1)} %fusion.39), channel_id=1, source_target_pairs={{8,0},{9,1},{10,2},{11,3},{12,4},{13,5},{14,6},{15,7},{0,8},{1,9},... | collective-permute-start | bytes 147464 | tf_op jit(solution)/shard_map/ppermute | solution.py:926
  286.9 17.1 %collective-permute-start.49 = (bf16[256,1280]{1,0:T(8,128)(2,1)S(1)}, bf16[256,1280]{1,0:T(8,128)(2,1)S(1)}, u32[]{:S(2)}, u32[]{:S(2)}) collective-permute-start(bf16[256,1280]{1,0:T(8,128)(2,1)S(1)} %copy-done.64), channel_id=1, source_target_pairs={{1,0},{0,1},{3,2},{2,3},{5,4},{4,5},{7,6},{6,7},{9,8},{8,9},{11,10... | collective-permute-start | bytes 1966088 | tf_op jit(solution)/shard_map/ppermute | solution.py:916
  287.6 16.4 %collective-permute-start.50 = (bf16[256,1280]{1,0:T(8,128)(2,1)S(1)}, bf16[256,1280]{1,0:T(8,128)(2,1)S(1)}, u32[]{:S(2)}, u32[]{:S(2)}) collective-permute-start(bf16[256,1280]{1,0:T(8,128)(2,1)S(1)} %copy-done.63), channel_id=1, source_target_pairs={{4,0},{5,1},{6,2},{7,3},{0,4},{1,5},{2,6},{3,7},{12,8},{13,9},{14,... | collective-permute-start | bytes 1966088 | tf_op jit(solution)/shard_map/ppermute | solution.py:919
  288.2 39.8 %all-to-all-start = ((bf16[4,256,256]{2,1,0:T(8,128)(2,1)}), bf16[4,256,256]{2,1,0:T(8,128)(2,1)S(1)}, u32[]{:S(2)}, u32[]{:S(2)}) async-start(bf16[4,256,256]{2,1,0:T(8,128)(2,1)} %bitcast.22), calls=%async_computation | async-start | bytes 1048576 | tf_op jit(solution)/shard_map/all_to_all | solution.py:907
  293.1 14.9 %collective-permute-start.51 = (f32[96,128]{1,0:T(8,128)S(1)}, f32[96,128]{1,0:T(8,128)S(1)}, u32[]{:S(2)}, u32[]{:S(2)}) collective-permute-start(f32[96,128]{1,0:T(8,128)S(1)} %add.178), channel_id=1, source_target_pairs={{1,0},{0,1},{3,2},{2,3},{5,4},{4,5},{7,6},{6,7},{9,8},{8,9},{11,10... | collective-permute-start | bytes 147464 | tf_op jit(solution)/shard_map/ppermute | solution.py:916
  308.1 15.5 %collective-permute-start.52 = (bf16[128,1280]{1,0:T(8,128)(2,1)}, bf16[128,1280]{1,0:T(8,128)(2,1)S(1)}, u32[]{:S(2)}, u32[]{:S(2)}) collective-permute-start(bf16[128,1280]{1,0:T(8,128)(2,1)} %get-tuple-element.338), channel_id=1, source_target_pairs={{4,0},{5,1},{6,2},{7,3},{0,4},{1,5},{2,6},{3,7},{12,8},{13,9},{14,... | collective-permute-start | bytes 983048 | tf_op jit(solution)/shard_map/ppermute | solution.py:919
  308.8 14.9 %collective-permute-start.53 = (bf16[128,1280]{1,0:T(8,128)(2,1)}, bf16[128,1280]{1,0:T(8,128)(2,1)S(1)}, u32[]{:S(2)}, u32[]{:S(2)}) collective-permute-start(bf16[128,1280]{1,0:T(8,128)(2,1)} %get-tuple-element.339), channel_id=1, source_target_pairs={{1,0},{0,1},{3,2},{2,3},{5,4},{4,5},{7,6},{6,7},{9,8},{8,9},{11,10... | collective-permute-start | bytes 983048 | tf_op jit(solution)/shard_map/ppermute | solution.py:916
  309.3 18.0 %collective-permute-start.54 = (f32[96,128]{1,0:T(8,128)S(1)}, f32[96,128]{1,0:T(8,128)S(1)}, u32[]{:S(2)}, u32[]{:S(2)}) collective-permute-start(f32[96,128]{1,0:T(8,128)S(1)} %add.179), channel_id=1, source_target_pairs={{4,0},{5,1},{6,2},{7,3},{0,4},{1,5},{2,6},{3,7},{12,8},{13,9},{14,... | collective-permute-start | bytes 147464 | tf_op jit(solution)/shard_map/ppermute | solution.py:919
  310.8 30.1 %collective-permute-start.58 = (bf16[256,1024]{1,0:T(8,128)(2,1)}, bf16[256,1024]{1,0:T(8,128)(2,1)S(1)}, u32[]{:S(2)}, u32[]{:S(2)}) collective-permute-start(bf16[256,1024]{1,0:T(8,128)(2,1)} %get-tuple-element.350), channel_id=1, source_target_pairs={{1,0},{0,1},{3,2},{2,3},{5,4},{4,5},{7,6},{6,7},{9,8},{8,9},{11,10... | collective-permute-start | bytes 1572872 | tf_op jit(solution)/shard_map/ppermute | solution.py:916
  327.3 13.6 %collective-permute-start.57 = (bf16[256,1024]{1,0:T(8,128)(2,1)}, bf16[256,1024]{1,0:T(8,128)(2,1)S(1)}, u32[]{:S(2)}, u32[]{:S(2)}) collective-permute-start(bf16[256,1024]{1,0:T(8,128)(2,1)} %get-tuple-element.349), channel_id=1, source_target_pairs={{1,0},{0,1},{3,2},{2,3},{5,4},{4,5},{7,6},{6,7},{9,8},{8,9},{11,10... | collective-permute-start | bytes 1572872 | tf_op jit(solution)/shard_map/ppermute | solution.py:916
  328.1 12.7 %collective-permute-start.55 = (bf16[128,256]{1,0:T(8,128)(2,1)S(1)}, bf16[128,256]{1,0:T(8,128)(2,1)S(1)}, u32[]{:S(2)}, u32[]{:S(2)}) collective-permute-start(bf16[128,256]{1,0:T(8,128)(2,1)S(1)} %slice.211), channel_id=1, source_target_pairs={{1,0},{0,1},{3,2},{2,3},{5,4},{4,5},{7,6},{6,7},{9,8},{8,9},{11,10... | collective-permute-start | bytes 196616 | tf_op jit(solution)/shard_map/ppermute | solution.py:916
  331.7 19.7 %all-to-all-start.1 = ((bf16[4,64,1280]{2,1,0:T(8,128)(2,1)}), bf16[4,64,1280]{2,1,0:T(8,128)(2,1)S(1)}, u32[]{:S(2)}, u32[]{:S(2)}) async-start(bf16[4,64,1280]{2,1,0:T(8,128)(2,1)} %bitcast.55), calls=%async_computation.3 | async-start | bytes 1310720 | tf_op jit(solution)/shard_map/all_to_all | solution.py:907
  (87 other events, 779.6 us)
Sparse Core Ops, SparseCore 0:
  20.1 34.0 all-gather.2
  74.5 29.4 all-gather.4
  258.8 29.5 reduce-scatter.4
  290.7 36.5 reduce-scatter.2

commit v7 on v6

--- a/solution.py
+++ b/solution.py
@@ -1063,23 +1063,21 @@
     other_two, along_three = after((), other_two, along_three)
 
     near_three = links.x(along_three), links.y(along_three)
+    other_three = [links.c(along_three)]
     far_two = after(other_two, far_two)
     other_two += [links.c(piece) for piece in far_two]
     w_two = [along_two, *near_two, *far_two, *other_two]
     y, h2, h2_t = join_heads(attn, x, w_two, hidden_here, outs[0], gains[1], shifts[1])
     hidden, slope = expand(h2, w_two, fc1_biases, hidden_here)
-    near_three, hidden, slope, h2_t, along_three = after(
-        (), near_three, hidden, slope, h2_t, along_three
+    near_three, other_three, hidden, slope, h2_t = after(
+        (), near_three, other_three, hidden, slope, h2_t
     )
 
     far_three = start_far(links, near_three)
     twin_hidden = links.c(hidden)
-    other_three = [links.c(piece) for piece in (along_three, near_three[0])]
-    far_three, twin_hidden, other_three, near_three, h2_sent, attn_sent = after(
-        (), far_three, twin_hidden, other_three, near_three, h2_t[half:], attn
-    )
-
-    quarter = width // 8
+    other_three += [links.c(near_three[0])]
+    twin_attn = links.c(attn)
+
     stack = lambda one, two: jnp.concatenate([one[...], two[...]], axis=0)
     join = lambda one, two: jnp.concatenate([one[...], two[...]], axis=1)
     tiles = hidden_here // TILE
@@ -1132,28 +1130,24 @@
 
     home_fc2, home_two, home_qkv = Home(links), Home(links), Home(links)
 
+    pieces = grad_fc2()
+    far_three, other_three, near_three, twin_attn, pieces, h2_sent = after(
+        (), far_three, other_three, near_three, twin_attn, pieces, h2_t[half:]
+    )
+
+    home_fc2.first(pieces)
     other_three += [links.c(piece) for piece in (near_three[1], *far_three)]
-    twin_h2 = links.c(h2_sent)
-    pieces = grad_fc2()
-    pieces, other_three, twin_h2, attn_sent = after(
-        (), pieces, other_three, twin_h2, attn_sent
-    )
     w_fc2 = [along_three, *near_three, *far_three, *other_three]
-
-    home_fc2.first(pieces)
-    twin_attn = links.c(attn_sent)
     du, fc1b_sum = hidden_back(e, slope, w_fc2)
     mid, da, da_t, da_t_far, second_sums = second_back(du, w_two, hidden_here, y, e, gains[1])
     enter_window(da, home_fc2)
-    du, da, da_t, da_t_far, twin_attn = after(
-        home_fc2.x_got, du, da, da_t, da_t_far, twin_attn
-    )
+    du, da, da_t, da_t_far = after(home_fc2.x_got, du, da, da_t, da_t_far)
 
     twin_du = links.c(du)
-    twin_da = links.c(da_t_far)
+    twin_da, twin_h2 = links.c(da_t_far), links.c(h2_sent)
     home_fc2.second(*home_fc2.middle())
     d_heads = heads_back(da, w_two, hidden_here)
-    twin_du, twin_da = after(d_heads, twin_du, twin_da)
+    twin_du, twin_da, twin_h2 = after(d_heads, twin_du, twin_da, twin_h2)
     pieces = grad_two()
     pieces, d_heads, home_fc2.y_last, home_fc2.x_last = after(
         (), pieces, d_heads, home_fc2.y_last, home_fc2.x_last
@@ -1198,39 +1192,42 @@
     small = small + small_got
     small_got = links.x(small)
     moved = home_two.last(pieces, True)
-    enter_window(moved, home_qkv)
-    moved, small, small_got, hidden_out, grad_sent_rows = after(
-        (), home_qkv.middle(), small, small_got, hidden, grad_sent_rows
+    out_near, out_sent = layer_out(after(moved, hidden), w_fc2, y, outs[1], live, order_b)
+    enter_window(out_near, home_qkv)
+    moved, small, small_got, out_sent, grad_sent_rows = after(
+        (), home_qkv.middle(), small, small_got, out_sent, grad_sent_rows
     )
 
     home_qkv.second(*moved)
     grad_got = links.x(grad_sent_rows)
     small = small + small_got
     small_got = links.y(small)
-    out_near, out_sent = layer_out(hidden_out, w_fc2, y, outs[1], live, order_b)
-    moved = home_qkv.last(out_near, False)
+    moved = home_qkv.last((), False)
     moved, out_sent, small, small_got = after((), moved, out_sent, small, small_got)
 
     by_z = jnp.sum(after(moved, by_z).astype(f32), axis=0)
-    v_got = links.x(by_z[quarter:].astype(bf16))
+    by_z = by_z.reshape(2, 2, block, -1)
+    v_got = links.y(by_z[:, 1].astype(bf16).reshape(2 * block, -1))
     out_got = links.x(out_sent)
     small = small + small_got
     bit = 2
     while bit < links.nz:
         small = small + links.flip(small, bit)
         bit *= 2
-    by_x = by_z[:quarter] + v_got.astype(f32)
-    by_x, small, out_got, grad_got, home_two.home, home_fc2.home = after(
-        (), by_x, small, out_got, grad_got, home_two.home, home_fc2.home
-    )
-    v_got = links.y(by_x[block:].astype(bf16))
-    g_v = (by_x[:block] + v_got.astype(f32)) * grad_scale
+    by_y = by_z[:, 0].reshape(2 * block, -1) + v_got.astype(f32)
+    by_y, small, grad_got, home_two.home, home_fc2.home = after(
+        (), by_y, small, grad_got, home_two.home, home_fc2.home
+    )
+    v_got = links.x(by_y[block:].astype(bf16))
+    g_v = (by_y[:block] + v_got.astype(f32)) * grad_scale
     small = small.reshape(-1) * grad_scale
     sums = small[: 6 * width].reshape(6, width)
     own = lambda first, size: lax.dynamic_slice_in_dim(small, first + t * size, size, 0)
-    g_qkv = home_qkv.value(g_v, grad_scale)
     g_fc2 = home_fc2.value(moved, grad_scale)
     g_two = home_two.value(moved, grad_scale)
+    g_fc2, g_proj, g_fc1 = g_fc2.T, g_two[:, hidden_here:].T, g_two[:, :hidden_here]
+    g_v, g_fc2, g_proj, g_fc1, out_got = after((), g_v, g_fc2, g_proj, g_fc1, out_got)
+    g_qkv = home_qkv.value(g_v, grad_scale)
 
     def both_slots(near, got):
         return jnp.where(t == 0, jnp.stack([near, got]), jnp.stack([got, near]))
@@ -1241,10 +1238,10 @@
         jnp.concatenate([g_qkv, g_v], axis=1).reshape(block, 3, heads_cols),
         own(6 * width, heads_cols),
         own(6 * width + 2 * heads_cols, heads_cols),
-        g_two[:, hidden_here:].T,
-        g_two[:, :hidden_here],
+        g_proj,
+        g_fc1,
         own(6 * width + 4 * heads_cols, hidden_here),
-        g_fc2.T,
+        g_fc2,
         sums[0:2],
         sums[2:4],
         sums[4:6],

time: 366 us -> 360 us (0.984)
  waiting for transfers between devices: 80.3 us -> 70.4 us
    ppermute x18, waiting for transfers between devices: 51.6 us -> 37.9 us  [x(): return lax.ppermute(rows, AXES, self.across)]
    ppermute x3, waiting for transfers between devices: 14.9 us -> 7.55 us  [from_z(): return lax.ppermute(rows, AXES, shift)]
    ppermute x23, waiting for transfers between devices: 9.06 us -> 14.1 us  [c(): return lax.ppermute(rows, AXES, self.twin)]
    ppermute x14, waiting for transfers between devices: 4.53 us -> 8.4 us  [y(): return lax.ppermute(rows, AXES, self.beside)]
    unnamed x138 -> x140, local copies, waits for them, and re-layouts: 12.8 us -> 15 us
  transfers between devices with their start and end apart: 66 -> 66, of which waited for: 21 -> 23; matrix products, arithmetic and copies ran while one was open for 7% -> 7% of each run, Pallas kernels for 44% -> 45%
where the time goes in v7:
time: 360 us; the launch traced here: 353 us
  Pallas kernels  159 us (44%)
  waiting for transfers between devices  70.4 us (20%)
  starting transfers between devices  62.5 us (17%)
  local copies, waits for them, and re-layouts  32.1 us (9%)
  between operations  16.1 us (4%)
  other arithmetic  9.75 us (3%)
    ppermute x18, waiting for transfers between devices, x(): return lax.ppermute(rows, AXES, self.across)  37.9 us
    pallas_call x3, Pallas kernels, contract_back(): kernel_call(body, name, (2 * load.tiles,), rows_specs + [pl.BlockSpec(mem...  35.5 us
    pallas_call x3, Pallas kernels, both_sides(): kernel_call(body, name, (2 * tiles,), specs, out_specs, shapes)(*args)  33.9 us
    pallas_call x6, Pallas kernels, small_call(): kernel_call(body, name, (1,), [whole(a.shape) for a in args], out_specs,...  19 us
    ppermute x18, starting transfers between devices, x(): return lax.ppermute(rows, AXES, self.across)  19 us
    pallas_call x1, Pallas kernels, attend_bwd(): kernel_call(attend_back_kernel, 'attend_bwd', (width // PAIR,), [head_spe...  16.9 us
    ppermute x14, starting transfers between devices, y(): return lax.ppermute(rows, AXES, self.beside)  16.8 us
    unnamed x140, local copies, waits for them, and re-layouts  15 us
  transfers between devices with their start and end apart: 66, of which 23 were waited for; matrix products, arithmetic and copies ran while one was open for 7% of the time, Pallas kernels for 45%

profile of v7, /device:TPU:0, one launch (start us, length us, event | category | flops | bytes accessed | tf_op | source)
XLA Modules:
  0.0 352.7 jit_solution(15824316568613053059)
XLA Ops:
  8.2 1.7 dynamic-slice_bitcast_fusion.1
  11.0 3.0 collective-permute-start.2
  14.0 2.6 collective-permute-start.1
  18.0 1.6 collective-permute-start.6
  22.0 5.9 %collective-permute-done = bf16[64,1536]{1,0:T(8,128)(2,1)S(1)} collective-permute-done((bf16[64,1536]{1,0:T(8,128)(2,1)S(1)}, bf16[64,1536]{1,0:T(8,128)(2,1)S(1)}, u32[]{:S(2)}, u32[]{:S(2)}) %collective-permute-start) | collective-permute-done | bytes 196640 | tf_op jit(solution)/shard_map/ppermute | solution.py:893
  28.0 1.6 collective-permute-done.1
  29.7 1.6 collective-permute-start.4
  36.0 10.9 %collective-permute-done.5 = bf16[512,1024]{1,0:T(8,128)(2,1)} collective-permute-done((bf16[512,1024]{1,0:T(8,128)(2,1)}, bf16[512,1024]{1,0:T(8,128)(2,1)}, u32[]{:S(2)}, u32[]{:S(2)}) %collective-permute-start.5) | collective-permute-done | bytes 1048608 | tf_op jit(solution)/shard_map/ppermute | solution.py:916
  50.5 1.7 enter.1
  54.3 7.1 %collective-permute-done.3.refs_1_.refs_6_ = bf16[256,1536]{1,0:T(8,128)(2,1)} collective-permute-done((bf16[256,1536]{1,0:T(8,128)(2,1)S(1)}, bf16[256,1536]{1,0:T(8,128)(2,1)}, u32[]{:S(2)}, u32[]{:S(2)}) %collective-permute-start.3) | collective-permute-done | bytes 786464 | tf_op jit(solution)/shard_map/ppermute | solution.py:916
  65.9 1.5 collective-permute-start.11
  68.1 6.9 %collective-permute-done.12.refs_3_.refs_8_ = bf16[128,1536]{1,0:T(8,128)(2,1)S(1)} collective-permute-done((bf16[128,1536]{1,0:T(8,128)(2,1)S(1)}, bf16[128,1536]{1,0:T(8,128)(2,1)S(1)}, u32[]{:S(2)}, u32[]{:S(2)}) %collective-permute-start.12) | collective-permute-done | bytes 393248 | tf_op jit(solution)/shard_map/ppermute | solution.py:916
  77.4 2.0 collective-permute-done.15.refs_8_.refs_13_
  80.0 8.3 %project.1.q_ref.k_ref.v_ref = bf16[3,512,1024]{2,1,0:T(8,128)(2,1)} custom-call(bf16[512,1024]{1,0:T(8,128)(2,1)} %copy-done.19, f32[2,1,1536]{2,1,0:T(1,128)} %broadcast_in_dim.23.bias_ref, bf16[256,1536]{1,0:T(8,128)(2,1)} %copy-done.26, bf16[256,1536]{1,0:T(8,128)(2,1)} %collective-permute-done.3.refs_1_.refs_6_, bf16[256,1536]{1,0:T(8,128)(2,1)} %copy-done.29, ...), custom_call_target="tpu_custom_call" | custom-call | flops 1 | bytes 1 | tf_op jit(solution)/shard_map/project/pallas_call | solution.py:445
  88.3 12.3 %attend_fwd.1 = (bf16[512,1024]{1,0:T(8,128)(2,1)}, f32[512,128]{1,0:T(8,128)}) custom-call(bf16[3,512,1024]{2,1,0:T(8,128)(2,1)} %project.1.q_ref.k_ref.v_ref, bf16[3,512,1024]{2,1,0:T(8,128)(2,1)} %project.1.q_ref.k_ref.v_ref, bf16[3,512,1024]{2,1,0:T(8,128)(2,1)} %project.1.q_ref.k_ref.v_ref), custom_call_target="tpu_custom_call" | custom-call | flops 1 | bytes 1 | tf_op jit(solution)/shard_map/attend_fwd/pallas_call | solution.py:485
  100.6 1.8 copy.31
  110.2 1.5 collective-permute-start.21
  113.1 10.4 %collective-permute-done.23.refs_3_.refs_7_ = bf16[128,2560]{1,0:T(8,128)(2,1)S(1)} collective-permute-done((bf16[128,2560]{1,0:T(8,128)(2,1)}, bf16[128,2560]{1,0:T(8,128)(2,1)S(1)}, u32[]{:S(2)}, u32[]{:S(2)}) %collective-permute-start.23) | collective-permute-done | bytes 655392 | tf_op jit(solution)/shard_map/ppermute | solution.py:916
  125.4 2.5 collective-permute-done.25.refs_8_.refs_12_
  128.2 1.6 copy-done.3
  132.2 3.1 join_heads.1
  136.7 11.4 %expand.1 = (bf16[512,4096]{1,0:T(8,128)(2,1)S(1)}, bf16[512,4096]{1,0:T(8,128)(2,1)}) custom-call(bf16[512,1024]{1,0:T(8,128)(2,1)S(1)} %get-tuple-element.222.h_ref, f32[1,4096]{1,0:T(1,128)S(1)} %bitcast.58, bf16[256,2560]{1,0:T(8,128)(2,1)S(1)} %copy-done.4, bf16[256,2560]{1,0:T(8,128)(2,1)S(1)} %collective-permute-done.10.refs_1_.refs_5_, ...), custom_call_target="tpu_custom_call" | custom-call | flops 1 | bytes 1 | tf_op jit(solution)/shard_map/expand/pallas_call | solution.py:543
  149.0 1.6 collective-permute-start.28
  152.1 3.3 collective-permute-done.31.refs_3_
  155.4 8.2 %grad_fc2.1 = (bf16[256,2048]{1,0:T(8,128)(2,1)S(1)}, bf16[256,2048]{1,0:T(8,128)(2,1)S(1)}, bf16[128,2048]{1,0:T(8,128)(2,1)S(1)}, bf16[256,2048]{1,0:T(8,128)(2,1)S(1)}, bf16[128,2048]{1,0:T(8,128)(2,1)S(1)}) custom-call(bf16[1024,512]{1,0:T(8,128)(2,1)S(1)} %copy-done.15, bf16[1024,512]{1,0:T(8,128)(2,1)} %collective-permute-done.14.refs_1_, ...), custom_call_target="tpu_custom_call" | custom-call | flops 1 | bytes 1 | tf_op jit(solution)/shard_map/grad_fc2/pallas_call | solution.py:849
  173.6 10.2 %hidden_back.1 = (bf16[512,4096]{1,0:T(8,128)(2,1)}, f32[1,4096]{1,0:T(1,128)}) custom-call(bf16[512,1024]{1,0:T(8,128)(2,1)} %copy-done.13, bf16[512,4096]{1,0:T(8,128)(2,1)} %get-tuple-element.228.slope_ref, bf16[256,2048]{1,0:T(8,128)(2,1)} %all-gather.5.cloned.1.call-done.refs_0_.refs_5_, bf16[256,2048]{1,0:T(8,128)(2,1)} %copy-done.28, ...), custom_call_target="tpu_custom_call" | custom-call | flops 1 | bytes 1 | tf_op jit(solution)/shard_map/hidden_back/pallas_call | solution.py:571
  183.8 12.8 %second_back.1 = (f32[512,1024]{1,0:T(8,128)}, bf16[512,1024]{1,0:T(8,128)(2,1)}, bf16[512,512]{1,0:T(8,128)(2,1)}, bf16[512,512]{1,0:T(8,128)(2,1)}, f32[4,1024]{1,0:T(4,128)}) custom-call(bf16[512,4096]{1,0:T(8,128)(2,1)} %get-tuple-element.252.refs_0_.refs_2_, f32[512,1024]{1,0:T(8,128)} %copy-done.9, bf16[512,1024]{1,0:T(8,128)(2,1)} %copy-done.13, ...), custom_call_target="tpu_custom_call" | custom-call | flops 1 | bytes 1 | tf_op jit(solution)/shard_map/second_back/pallas_call | solution.py:635
  197.6 3.0 add_mid.3
  202.5 4.9 %heads_back.1.g_ref = bf16[512,1024]{1,0:T(8,128)(2,1)} custom-call(bf16[512,1024]{1,0:T(8,128)(2,1)} %get-tuple-element.255.da_ref, bf16[256,2560]{1,0:T(8,128)(2,1)} %all-gather.3.cloned.1.call-done.refs_0_.refs_4_, bf16[256,2560]{1,0:T(8,128)(2,1)} %copy-done.2, bf16[256,2560]{1,0:T(8,128)(2,1)} %copy-done.1, bf16[128,2560]{1,0:T(8,128)(2,1)} %copy-done.6, ...), custom_call_target="tpu_custom_call" | custom-call | flops 1 | bytes 1 | tf_op jit(solution)/shard_map/heads_back/pallas_call | solution.py:593
  208.4 13.9 %grad_two.1 = (bf16[256,2560]{1,0:T(8,128)(2,1)}, bf16[256,2560]{1,0:T(8,128)(2,1)}, bf16[128,2560]{1,0:T(8,128)(2,1)}, bf16[256,2560]{1,0:T(8,128)(2,1)}, bf16[128,2560]{1,0:T(8,128)(2,1)}) custom-call(bf16[1024,512]{1,0:T(8,128)(2,1)} %copy-done.16, bf16[512,512]{1,0:T(8,128)(2,1)} %copy-done.47, bf16[512,4096]{1,0:T(8,128)(2,1)} %get-tuple-element.252.refs_0_.refs_2_, ...), custom_call_target="tpu_custom_call" | custom-call | flops 1 | bytes 1 | tf_op jit(solution)/shard_map/grad_two/pallas_call | solution.py:849
  224.5 3.5 add_last.3
  228.0 16.9 %attend_bwd.1 = (bf16[3,512,1024]{2,1,0:T(8,128)(2,1)}, f32[1,1024]{1,0:T(1,128)}, f32[1,1024]{1,0:T(1,128)}) custom-call(bf16[3,512,1024]{2,1,0:T(8,128)(2,1)} %project.1.q_ref.k_ref.v_ref, bf16[3,512,1024]{2,1,0:T(8,128)(2,1)} %project.1.q_ref.k_ref.v_ref, bf16[3,512,1024]{2,1,0:T(8,128)(2,1)} %project.1.q_ref.k_ref.v_ref, ...), custom_call_target="tpu_custom_call" | custom-call | flops 1 | bytes 1 | tf_op jit(solution)/shard_map/attend_bwd/pallas_call | solution.py:783
  245.0 11.1 %first_back.1 = (bf16[256,1024]{1,0:T(8,128)(2,1)}, bf16[256,1024]{1,0:T(8,128)(2,1)}, f32[2,1024]{1,0:T(2,128)}) custom-call(bf16[3,512,1024]{2,1,0:T(8,128)(2,1)} %get-tuple-element.290.refs_0_.refs_2_, bf16[512,1024]{1,0:T(8,128)(2,1)} %copy-done.11, f32[512,1024]{1,0:T(8,128)} %get-tuple-element.285.refs_2_, f32[1,1024]{1,0:T(1,128)} %copy-done.23, ...), custom_call_target="tpu_custom_call" | custom-call | flops 1 | bytes 1 | tf_op jit(solution)/shard_map/first_back/pallas_call | solution.py:635
  256.5 3.3 add_mid.4
  261.7 1.9 fusion
  265.0 4.7 %collective-permute-start.48 = (f32[96,128]{1,0:T(8,128)S(1)}, f32[96,128]{1,0:T(8,128)S(1)}, u32[]{:S(2)}, u32[]{:S(2)}) collective-permute-start(f32[96,128]{1,0:T(8,128)S(1)} %fusion.39), channel_id=1, source_target_pairs={{8,0},{9,1},{10,2},{11,3},{12,4},{13,5},{14,6},{15,7},{0,8},{1,9},... | collective-permute-start | bytes 147464 | tf_op jit(solution)/shard_map/ppermute | solution.py:926
  269.7 11.8 %grad_qkv.1 = (bf16[256,1280]{1,0:T(8,128)(2,1)}, bf16[256,1280]{1,0:T(8,128)(2,1)}, bf16[128,1280]{1,0:T(8,128)(2,1)}, bf16[256,1280]{1,0:T(8,128)(2,1)}, bf16[...) custom-call(bf16[1024,512]{1,0:T(8,128)(2,1)} %copy-done.17, bf16[1024,512]{1,0:T(8,128)(2,1)} %collective-permute-done.14.refs_1_, ...), custom_call_target="tpu_custom_call" | custom-call | flops 1 | bytes 1 | tf_op jit(solution)/shard_map/grad_qkv/pallas_call | solution.py:849
  281.5 4.1 %add_last.4 = bf16[256,2560]{1,0:T(8,128)(2,1)} custom-call(bf16[256,2560]{1,0:T(8,128)(2,1)} %get-tuple-element.271.k00_ref, bf16[256,2560]{1,0:T(8,128)(2,1)} %collective-permute-done.42.rx_ref, bf16[256,2560]{1,0:T(8,128)(2,1)} %collective-permute-done.43.ry_ref, bf16[128,2560]{1,0:T(8,128)(2,1)} %collective-permute-done.46.y2_ref, ...), custom_call_target="tpu_custom_call" | custom-call | flops 1 | bytes 1 | tf_op jit(solution)/shard_map/add_last/pallas_call | solution.py:869
  287.6 3.5 all-to-all-start
  292.1 11.6 %layer_out.1 = (bf16[256,1024]{1,0:T(8,128)(2,1)}, bf16[256,1024]{1,0:T(8,128)(2,1)}) custom-call(bf16[512,4096]{1,0:T(8,128)(2,1)} %copy-done.5, f32[512,1024]{1,0:T(8,128)} %copy-done.9, f32[1,1024]{1,0:T(1,128)} %get-tuple-element.391.refs_2_, f32[1,1024]{1,0:T(1,128)} %copy-done.24, bf16[1024,1024]{1,0:T(8,128)(2,1)} %copy-done, ...), custom_call_target="tpu_custom_call" | custom-call | flops 1 | bytes 1 | tf_op jit(solution)/shard_map/layer_out/pallas_call | solution.py:635
  304.7 2.4 add_mid.5
  311.1 5.4 %collective-permute-done.52.y2_ref = bf16[128,1280]{1,0:T(8,128)(2,1)S(1)} collective-permute-done((bf16[128,1280]{1,0:T(8,128)(2,1)}, bf16[128,1280]{1,0:T(8,128)(2,1)S(1)}, u32[]{:S(2)}, u32[]{:S(2)}) %collective-permute-start.52) | collective-permute-done | bytes 327712 | tf_op jit(solution)/shard_map/ppermute | solution.py:919
  316.5 2.6 collective-permute-done.53.x2_ref
  319.9 2.8 add_last.5
  323.7 2.8 collective-permute-start.56
  326.5 3.6 %all-to-all-start.1 = ((bf16[4,64,1280]{2,1,0:T(8,128)(2,1)}), bf16[4,64,1280]{2,1,0:T(8,128)(2,1)S(1)}, u32[]{:S(2)}, u32[]{:S(2)}) async-start(bf16[4,64,1280]{2,1,0:T(8,128)(2,1)} %bitcast.59), calls=%async_computation.3 | async-start | bytes 1310720 | tf_op jit(solution)/shard_map/all_to_all | solution.py:907
  332.4 1.8 multiply_bitcast_fusion.1
  341.4 2.3 all-to-all-done.1
  (327 shorter events, 81.7 us)
Async XLA Ops:
  7.2 54.2 %all-gather.3.cloned.1.call-start = ((), (), s32[]{:S(2)}) async-start(), calls=%async_computation.4 | async-start | bytes 1638400 | tf_op jit(solution)/shard_map/all_gather | solution.py:911
  11.0 18.6 %collective-permute-start.2 = (bf16[64,1536]{1,0:T(8,128)(2,1)S(1)}, bf16[64,1536]{1,0:T(8,128)(2,1)S(1)}, u32[]{:S(2)}, u32[]{:S(2)}) collective-permute-start(bf16[64,1536]{1,0:T(8,128)(2,1)S(1)} %bitcast.64), channel_id=1, source_target_pairs={{24,0},{25,1},{26,2},{27,3},{28,4},{29,5},{30,6},{31,7},{0,8},{1,9... | collective-permute-start | bytes 589832 | tf_op jit(solution)/shard_map/ppermute | solution.py:893
  14.0 15.6 %collective-permute-start.1 = (bf16[64,1536]{1,0:T(8,128)(2,1)S(1)}, bf16[64,1536]{1,0:T(8,128)(2,1)S(1)}, u32[]{:S(2)}, u32[]{:S(2)}) collective-permute-start(bf16[64,1536]{1,0:T(8,128)(2,1)S(1)} %bitcast.65), channel_id=1, source_target_pairs={{16,0},{17,1},{18,2},{19,3},{20,4},{21,5},{22,6},{23,7},{24,8},{25... | collective-permute-start | bytes 589832 | tf_op jit(solution)/shard_map/ppermute | solution.py:893
  16.6 11.3 %collective-permute-start = (bf16[64,1536]{1,0:T(8,128)(2,1)S(1)}, bf16[64,1536]{1,0:T(8,128)(2,1)S(1)}, u32[]{:S(2)}, u32[]{:S(2)}) collective-permute-start(bf16[64,1536]{1,0:T(8,128)(2,1)S(1)} %bitcast.66), channel_id=1, source_target_pairs={{8,0},{9,1},{10,2},{11,3},{12,4},{13,5},{14,6},{15,7},{16,8},{17,9... | collective-permute-start | bytes 589832 | tf_op jit(solution)/shard_map/ppermute | solution.py:893
  18.0 18.0 %collective-permute-start.6 = (f32[24,128]{1,0:T(8,128)S(1)}, f32[24,128]{1,0:T(8,128)S(1)}, u32[]{:S(2)}, u32[]{:S(2)}) collective-permute-start(f32[24,128]{1,0:T(8,128)S(1)} %maximum_bitcast_fusion.1), channel_id=1, source_target_pairs={{1,0},{0,1},{3,2},{2,3},{5,4},{4,5},{7,6},{6,7},{9,8},{8,9},{11,10... | collective-permute-start | bytes 36872 | tf_op jit(solution)/shard_map/ppermute | solution.py:916
  20.3 88.2 %all-gather.5.cloned.1.call-start = ((), (), s32[]{:S(2)}) async-start(), calls=%async_computation.5 | async-start | bytes 1310720 | tf_op jit(solution)/shard_map/all_gather | solution.py:911
  20.4 26.5 %collective-permute-start.5 = (bf16[512,1024]{1,0:T(8,128)(2,1)}, bf16[512,1024]{1,0:T(8,128)(2,1)}, u32[]{:S(2)}, u32[]{:S(2)}) collective-permute-start(bf16[512,1024]{1,0:T(8,128)(2,1)} %pad_maximum_fusion), channel_id=1, source_target_pairs={{1,0},{0,1},{3,2},{2,3},{5,4},{4,5},{7,6},{6,7},{9,8},{8,9},{11,10... | collective-permute-start | bytes 3145736 | tf_op jit(solution)/shard_map/ppermute | solution.py:916
  29.7 24.6 %collective-permute-start.4 = (bf16[256,1536]{1,0:T(8,128)(2,1)S(1)}, bf16[256,1536]{1,0:T(8,128)(2,1)S(1)}, u32[]{:S(2)}, u32[]{:S(2)}) collective-permute-start(bf16[256,1536]{1,0:T(8,128)(2,1)S(1)} %constant_dynamic-update-slice_fusion.refs_0_.refs_5_), channel_id=1, source_target_pairs={{4,0},{5,1},{6,2},{7,3},{0,4},{1,5},{2,6},{3,7},{12,8},{13,9},{14,... | collective-permute-start | bytes 2359304 | tf_op jit(solution)/shard_map/ppermute | solution.py:919
  31.2 30.1 %collective-permute-start.3 = (bf16[256,1536]{1,0:T(8,128)(2,1)S(1)}, bf16[256,1536]{1,0:T(8,128)(2,1)}, u32[]{:S(2)}, u32[]{:S(2)}) collective-permute-start(bf16[256,1536]{1,0:T(8,128)(2,1)S(1)} %constant_dynamic-update-slice_fusion.refs_0_.refs_5_), channel_id=1, source_target_pairs={{1,0},{0,1},{3,2},{2,3},{5,4},{4,5},{7,6},{6,7},{9,8},{8,9},{11,10... | collective-permute-start | bytes 2359304 | tf_op jit(solution)/shard_map/ppermute | solution.py:916
  63.0 12.0 %collective-permute-start.12 = (bf16[128,1536]{1,0:T(8,128)(2,1)S(1)}, bf16[128,1536]{1,0:T(8,128)(2,1)S(1)}, u32[]{:S(2)}, u32[]{:S(2)}) collective-permute-start(bf16[128,1536]{1,0:T(8,128)(2,1)S(1)} %slice.158), channel_id=1, source_target_pairs={{1,0},{0,1},{3,2},{2,3},{5,4},{4,5},{7,6},{6,7},{9,8},{8,9},{11,10... | collective-permute-start | bytes 1179656 | tf_op jit(solution)/shard_map/ppermute | solution.py:916
  63.8 12.1 %collective-permute-start.13 = (bf16[128,1536]{1,0:T(8,128)(2,1)S(1)}, bf16[128,1536]{1,0:T(8,128)(2,1)}, u32[]{:S(2)}, u32[]{:S(2)}) collective-permute-start(bf16[128,1536]{1,0:T(8,128)(2,1)S(1)} %slice.159), channel_id=1, source_target_pairs={{4,0},{5,1},{6,2},{7,3},{0,4},{1,5},{2,6},{3,7},{12,8},{13,9},{14,... | collective-permute-start | bytes 1179656 | tf_op jit(solution)/shard_map/ppermute | solution.py:919
  65.9 37.1 %collective-permute-start.11 = (bf16[256,2560]{1,0:T(8,128)(2,1)}, bf16[256,2560]{1,0:T(8,128)(2,1)S(1)}, u32[]{:S(2)}, u32[]{:S(2)}) collective-permute-start(bf16[256,2560]{1,0:T(8,128)(2,1)} %all-gather.3.cloned.1.call-done.refs_0_.refs_4_), channel_id=1, source_target_pairs={{4,0},{5,1},{6,2},{7,3},{0,4},{1,5},{2,6},{3,7},{12,8},{13,9},{14,... | collective-permute-start | bytes 3932168 | tf_op jit(solution)/shard_map/ppermute | solution.py:919
  67.5 35.6 %collective-permute-start.10 = (bf16[256,2560]{1,0:T(8,128)(2,1)}, bf16[256,2560]{1,0:T(8,128)(2,1)S(1)}, u32[]{:S(2)}, u32[]{:S(2)}) collective-permute-start(bf16[256,2560]{1,0:T(8,128)(2,1)} %all-gather.3.cloned.1.call-done.refs_0_.refs_4_), channel_id=1, source_target_pairs={{1,0},{0,1},{3,2},{2,3},{5,4},{4,5},{7,6},{6,7},{9,8},{8,9},{11,10... | collective-permute-start | bytes 3932168 | tf_op jit(solution)/shard_map/ppermute | solution.py:916
  76.4 255.1 %reduce-scatter.5.cloned.1.call-start = ((), (), s32[]{:S(2)}) async-start(), calls=%async_computation.7 | async-start | bytes 1310720 | tf_op jit(solution)/shard_map/reduce_scatter | solution.py:902
  105.6 17.8 %collective-permute-start.23 = (bf16[128,2560]{1,0:T(8,128)(2,1)}, bf16[128,2560]{1,0:T(8,128)(2,1)S(1)}, u32[]{:S(2)}, u32[]{:S(2)}) collective-permute-start(bf16[128,2560]{1,0:T(8,128)(2,1)} %slice.163), channel_id=1, source_target_pairs={{1,0},{0,1},{3,2},{2,3},{5,4},{4,5},{7,6},{6,7},{9,8},{8,9},{11,10... | collective-permute-start | bytes 1966088 | tf_op jit(solution)/shard_map/ppermute | solution.py:916
  107.0 17.9 %collective-permute-start.24 = (bf16[128,2560]{1,0:T(8,128)(2,1)}, bf16[128,2560]{1,0:T(8,128)(2,1)}, u32[]{:S(2)}, u32[]{:S(2)}) collective-permute-start(bf16[128,2560]{1,0:T(8,128)(2,1)} %slice.164), channel_id=1, source_target_pairs={{4,0},{5,1},{6,2},{7,3},{0,4},{1,5},{2,6},{3,7},{12,8},{13,9},{14,... | collective-permute-start | bytes 1966088 | tf_op jit(solution)/shard_map/ppermute | solution.py:919
  110.0 38.1 %collective-permute-start.22 = (bf16[256,2048]{1,0:T(8,128)(2,1)}, bf16[256,2048]{1,0:T(8,128)(2,1)S(1)}, u32[]{:S(2)}, u32[]{:S(2)}) collective-permute-start(bf16[256,2048]{1,0:T(8,128)(2,1)} %all-gather.5.cloned.1.call-done.refs_0_.refs_5_), channel_id=1, source_target_pairs={{2,0},{3,1},{0,2},{1,3},{6,4},{7,5},{4,6},{5,7},{10,8},{11,9},{8,1... | collective-permute-start | bytes 3145736 | tf_op jit(solution)/shard_map/ppermute | solution.py:922
  110.2 38.0 %collective-permute-start.21 = (bf16[256,2048]{1,0:T(8,128)(2,1)}, bf16[256,2048]{1,0:T(8,128)(2,1)S(1)}, u32[]{:S(2)}, u32[]{:S(2)}) collective-permute-start(bf16[256,2048]{1,0:T(8,128)(2,1)} %all-gather.5.cloned.1.call-done.refs_0_.refs_5_), channel_id=1, source_target_pairs={{4,0},{5,1},{6,2},{7,3},{0,4},{1,5},{2,6},{3,7},{12,8},{13,9},{14,... | collective-permute-start | bytes 3145736 | tf_op jit(solution)/shard_map/ppermute | solution.py:919
  111.7 36.5 %collective-permute-start.20 = (bf16[256,2048]{1,0:T(8,128)(2,1)}, bf16[256,2048]{1,0:T(8,128)(2,1)S(1)}, u32[]{:S(2)}, u32[]{:S(2)}) collective-permute-start(bf16[256,2048]{1,0:T(8,128)(2,1)} %all-gather.5.cloned.1.call-done.refs_0_.refs_5_), channel_id=1, source_target_pairs={{1,0},{0,1},{3,2},{2,3},{5,4},{4,5},{7,6},{6,7},{9,8},{8,9},{11,10... | collective-permute-start | bytes 3145736 | tf_op jit(solution)/shard_map/ppermute | solution.py:916
  148.4 17.8 %collective-permute-start.30 = (bf16[512,1024]{1,0:T(8,128)(2,1)S(1)}, bf16[512,1024]{1,0:T(8,128)(2,1)S(1)}, u32[]{:S(2)}, u32[]{:S(2)}) collective-permute-start(bf16[512,1024]{1,0:T(8,128)(2,1)S(1)} %copy-done.10), channel_id=1, source_target_pairs={{2,0},{3,1},{0,2},{1,3},{6,4},{7,5},{4,6},{5,7},{10,8},{11,9},{8,1... | collective-permute-start | bytes 3145736 | tf_op jit(solution)/shard_map/ppermute | solution.py:922
  148.7 17.5 %collective-permute-start.29 = (bf16[256,2048]{1,0:T(8,128)(2,1)S(1)}, bf16[256,2048]{1,0:T(8,128)(2,1)S(1)}, u32[]{:S(2)}, u32[]{:S(2)}) collective-permute-start(bf16[256,2048]{1,0:T(8,128)(2,1)S(1)} %collective-permute-done.20.refs_1_.refs_6_), channel_id=1, source_target_pairs={{2,0},{3,1},{0,2},{1,3},{6,4},{7,5},{4,6},{5,7},{10,8},{11,9},{8,1... | collective-permute-start | bytes 3145736 | tf_op jit(solution)/shard_map/ppermute | solution.py:922
  149.0 17.2 %collective-permute-start.28 = (bf16[128,2048]{1,0:T(8,128)(2,1)S(1)}, bf16[128,2048]{1,0:T(8,128)(2,1)S(1)}, u32[]{:S(2)}, u32[]{:S(2)}) collective-permute-start(bf16[128,2048]{1,0:T(8,128)(2,1)S(1)} %slice.167), channel_id=1, source_target_pairs={{4,0},{5,1},{6,2},{7,3},{0,4},{1,5},{2,6},{3,7},{12,8},{13,9},{14,... | collective-permute-start | bytes 1572872 | tf_op jit(solution)/shard_map/ppermute | solution.py:919
  150.6 15.7 %collective-permute-start.27 = (bf16[128,2048]{1,0:T(8,128)(2,1)S(1)}, bf16[128,2048]{1,0:T(8,128)(2,1)S(1)}, u32[]{:S(2)}, u32[]{:S(2)}) collective-permute-start(bf16[128,2048]{1,0:T(8,128)(2,1)S(1)} %slice.166), channel_id=1, source_target_pairs={{1,0},{0,1},{3,2},{2,3},{5,4},{4,5},{7,6},{6,7},{9,8},{8,9},{11,10... | collective-permute-start | bytes 1572872 | tf_op jit(solution)/shard_map/ppermute | solution.py:916
  167.9 28.8 %collective-permute-start.35 = (bf16[256,2048]{1,0:T(8,128)(2,1)S(1)}, bf16[256,2048]{1,0:T(8,128)(2,1)S(1)}, u32[]{:S(2)}, u32[]{:S(2)}) collective-permute-start(bf16[256,2048]{1,0:T(8,128)(2,1)S(1)} %get-tuple-element.249), channel_id=1, source_target_pairs={{1,0},{0,1},{3,2},{2,3},{5,4},{4,5},{7,6},{6,7},{9,8},{8,9},{11,10... | collective-permute-start | bytes 3145736 | tf_op jit(solution)/shard_map/ppermute | solution.py:916
  168.6 28.1 %collective-permute-start.36 = (bf16[256,2048]{1,0:T(8,128)(2,1)S(1)}, bf16[256,2048]{1,0:T(8,128)(2,1)}, u32[]{:S(2)}, u32[]{:S(2)}) collective-permute-start(bf16[256,2048]{1,0:T(8,128)(2,1)S(1)} %get-tuple-element.250), channel_id=1, source_target_pairs={{4,0},{5,1},{6,2},{7,3},{0,4},{1,5},{2,6},{3,7},{12,8},{13,9},{14,... | collective-permute-start | bytes 3145736 | tf_op jit(solution)/shard_map/ppermute | solution.py:919
  196.7 10.7 %collective-permute-start.37 = (bf16[512,4096]{1,0:T(8,128)(2,1)}, bf16[512,4096]{1,0:T(8,128)(2,1)}, u32[]{:S(2)}, u32[]{:S(2)}) collective-permute-start(bf16[512,4096]{1,0:T(8,128)(2,1)} %get-tuple-element.252.refs_0_.refs_2_), channel_id=1, source_target_pairs={{2,0},{3,1},{0,2},{1,3},{6,4},{7,5},{4,6},{5,7},{10,8},{11,9},{8,1... | collective-permute-start | bytes 12582920 | tf_op jit(solution)/shard_map/ppermute | solution.py:922
  196.9 10.5 %collective-permute-start.39 = (bf16[512,512]{1,0:T(8,128)(2,1)S(1)}, bf16[512,512]{1,0:T(8,128)(2,1)S(1)}, u32[]{:S(2)}, u32[]{:S(2)}) collective-permute-start(bf16[512,512]{1,0:T(8,128)(2,1)S(1)} %copy-done.49), channel_id=1, source_target_pairs={{2,0},{3,1},{0,2},{1,3},{6,4},{7,5},{4,6},{5,7},{10,8},{11,9},{8,1... | collective-permute-start | bytes 1572872 | tf_op jit(solution)/shard_map/ppermute | solution.py:922
  197.3 10.1 %collective-permute-start.38 = (bf16[512,512]{1,0:T(8,128)(2,1)}, bf16[512,512]{1,0:T(8,128)(2,1)S(1)}, u32[]{:S(2)}, u32[]{:S(2)}) collective-permute-start(bf16[512,512]{1,0:T(8,128)(2,1)} %get-tuple-element.253), channel_id=1, source_target_pairs={{2,0},{3,1},{0,2},{1,3},{6,4},{7,5},{4,6},{5,7},{10,8},{11,9},{8,1... | collective-permute-start | bytes 1572872 | tf_op jit(solution)/shard_map/ppermute | solution.py:922
  200.6 21.6 %collective-permute-start.40 = (bf16[128,2048]{1,0:T(8,128)(2,1)}, bf16[128,2048]{1,0:T(8,128)(2,1)S(1)}, u32[]{:S(2)}, u32[]{:S(2)}) collective-permute-start(bf16[128,2048]{1,0:T(8,128)(2,1)} %get-tuple-element.269), channel_id=1, source_target_pairs={{4,0},{5,1},{6,2},{7,3},{0,4},{1,5},{2,6},{3,7},{12,8},{13,9},{14,... | collective-permute-start | bytes 1572872 | tf_op jit(solution)/shard_map/ppermute | solution.py:919
  201.3 21.0 %collective-permute-start.41 = (bf16[128,2048]{1,0:T(8,128)(2,1)}, bf16[128,2048]{1,0:T(8,128)(2,1)S(1)}, u32[]{:S(2)}, u32[]{:S(2)}) collective-permute-start(bf16[128,2048]{1,0:T(8,128)(2,1)} %get-tuple-element.270), channel_id=1, source_target_pairs={{1,0},{0,1},{3,2},{2,3},{5,4},{4,5},{7,6},{6,7},{9,8},{8,9},{11,10... | collective-permute-start | bytes 1572872 | tf_op jit(solution)/shard_map/ppermute | solution.py:916
  222.3 33.8 %collective-permute-start.42 = (bf16[256,2560]{1,0:T(8,128)(2,1)}, bf16[256,2560]{1,0:T(8,128)(2,1)}, u32[]{:S(2)}, u32[]{:S(2)}) collective-permute-start(bf16[256,2560]{1,0:T(8,128)(2,1)} %get-tuple-element.272), channel_id=1, source_target_pairs={{1,0},{0,1},{3,2},{2,3},{5,4},{4,5},{7,6},{6,7},{9,8},{8,9},{11,10... | collective-permute-start | bytes 3932168 | tf_op jit(solution)/shard_map/ppermute | solution.py:916
  223.2 32.9 %collective-permute-start.43 = (bf16[256,2560]{1,0:T(8,128)(2,1)}, bf16[256,2560]{1,0:T(8,128)(2,1)}, u32[]{:S(2)}, u32[]{:S(2)}) collective-permute-start(bf16[256,2560]{1,0:T(8,128)(2,1)} %get-tuple-element.273), channel_id=1, source_target_pairs={{4,0},{5,1},{6,2},{7,3},{0,4},{1,5},{2,6},{3,7},{12,8},{13,9},{14,... | collective-permute-start | bytes 3932168 | tf_op jit(solution)/shard_map/ppermute | solution.py:919
  256.1 8.8 %collective-permute-start.44 = (bf16[3,512,1024]{2,1,0:T(8,128)(2,1)S(1)}, bf16[3,512,1024]{2,1,0:T(8,128)(2,1)}, u32[]{:S(2)}, u32[]{:S(2)}) collective-permute-start(bf16[3,512,1024]{2,1,0:T(8,128)(2,1)S(1)} %copy-done.25), channel_id=1, source_target_pairs={{2,0},{3,1},{0,2},{1,3},{6,4},{7,5},{4,6},{5,7},{10,8},{11,9},{8,1... | collective-permute-start | bytes 9437192 | tf_op jit(solution)/shard_map/ppermute | solution.py:922
  256.3 75.1 %reduce-scatter.3.cloned.1.call-start = ((), (), s32[]{:S(2)}) async-start(), calls=%async_computation.6 | async-start | bytes 1638400 | tf_op jit(solution)/shard_map/reduce_scatter | solution.py:902
  259.8 21.7 %collective-permute-start.46 = (bf16[128,2560]{1,0:T(8,128)(2,1)}, bf16[128,2560]{1,0:T(8,128)(2,1)}, u32[]{:S(2)}, u32[]{:S(2)}) collective-permute-start(bf16[128,2560]{1,0:T(8,128)(2,1)} %get-tuple-element.293), channel_id=1, source_target_pairs={{4,0},{5,1},{6,2},{7,3},{0,4},{1,5},{2,6},{3,7},{12,8},{13,9},{14,... | collective-permute-start | bytes 1966088 | tf_op jit(solution)/shard_map/ppermute | solution.py:919
  260.5 21.0 %collective-permute-start.47 = (bf16[128,2560]{1,0:T(8,128)(2,1)}, bf16[128,2560]{1,0:T(8,128)(2,1)}, u32[]{:S(2)}, u32[]{:S(2)}) collective-permute-start(bf16[128,2560]{1,0:T(8,128)(2,1)} %get-tuple-element.294), channel_id=1, source_target_pairs={{1,0},{0,1},{3,2},{2,3},{5,4},{4,5},{7,6},{6,7},{9,8},{8,9},{11,10... | collective-permute-start | bytes 1966088 | tf_op jit(solution)/shard_map/ppermute | solution.py:916
  265.0 16.5 %collective-permute-start.48 = (f32[96,128]{1,0:T(8,128)S(1)}, f32[96,128]{1,0:T(8,128)S(1)}, u32[]{:S(2)}, u32[]{:S(2)}) collective-permute-start(f32[96,128]{1,0:T(8,128)S(1)} %fusion.39), channel_id=1, source_target_pairs={{8,0},{9,1},{10,2},{11,3},{12,4},{13,5},{14,6},{15,7},{0,8},{1,9},... | collective-permute-start | bytes 147464 | tf_op jit(solution)/shard_map/ppermute | solution.py:926
  285.7 17.9 %collective-permute-start.49 = (bf16[256,1280]{1,0:T(8,128)(2,1)S(1)}, bf16[256,1280]{1,0:T(8,128)(2,1)S(1)}, u32[]{:S(2)}, u32[]{:S(2)}) collective-permute-start(bf16[256,1280]{1,0:T(8,128)(2,1)S(1)} %copy-done.64), channel_id=1, source_target_pairs={{1,0},{0,1},{3,2},{2,3},{5,4},{4,5},{7,6},{6,7},{9,8},{8,9},{11,10... | collective-permute-start | bytes 1966088 | tf_op jit(solution)/shard_map/ppermute | solution.py:916
  287.2 16.5 %collective-permute-start.50 = (bf16[256,1280]{1,0:T(8,128)(2,1)S(1)}, bf16[256,1280]{1,0:T(8,128)(2,1)S(1)}, u32[]{:S(2)}, u32[]{:S(2)}) collective-permute-start(bf16[256,1280]{1,0:T(8,128)(2,1)S(1)} %copy-done.63), channel_id=1, source_target_pairs={{4,0},{5,1},{6,2},{7,3},{0,4},{1,5},{2,6},{3,7},{12,8},{13,9},{14,... | collective-permute-start | bytes 1966088 | tf_op jit(solution)/shard_map/ppermute | solution.py:919
  287.6 35.0 %all-to-all-start = ((bf16[4,256,256]{2,1,0:T(8,128)(2,1)}), bf16[4,256,256]{2,1,0:T(8,128)(2,1)S(1)}, u32[]{:S(2)}, u32[]{:S(2)}) async-start(bf16[4,256,256]{2,1,0:T(8,128)(2,1)} %bitcast.22), calls=%async_computation | async-start | bytes 1048576 | tf_op jit(solution)/shard_map/all_to_all | solution.py:907
  291.1 16.0 %collective-permute-start.51 = (f32[96,128]{1,0:T(8,128)S(1)}, f32[96,128]{1,0:T(8,128)S(1)}, u32[]{:S(2)}, u32[]{:S(2)}) collective-permute-start(f32[96,128]{1,0:T(8,128)S(1)} %add.178), channel_id=1, source_target_pairs={{1,0},{0,1},{3,2},{2,3},{5,4},{4,5},{7,6},{6,7},{9,8},{8,9},{11,10... | collective-permute-start | bytes 147464 | tf_op jit(solution)/shard_map/ppermute | solution.py:916
  307.1 9.4 %collective-permute-start.52 = (bf16[128,1280]{1,0:T(8,128)(2,1)}, bf16[128,1280]{1,0:T(8,128)(2,1)S(1)}, u32[]{:S(2)}, u32[]{:S(2)}) collective-permute-start(bf16[128,1280]{1,0:T(8,128)(2,1)} %get-tuple-element.328), channel_id=1, source_target_pairs={{4,0},{5,1},{6,2},{7,3},{0,4},{1,5},{2,6},{3,7},{12,8},{13,9},{14,... | collective-permute-start | bytes 983048 | tf_op jit(solution)/shard_map/ppermute | solution.py:919
  308.3 10.9 %collective-permute-start.53 = (bf16[128,1280]{1,0:T(8,128)(2,1)}, bf16[128,1280]{1,0:T(8,128)(2,1)S(1)}, u32[]{:S(2)}, u32[]{:S(2)}) collective-permute-start(bf16[128,1280]{1,0:T(8,128)(2,1)} %get-tuple-element.329), channel_id=1, source_target_pairs={{1,0},{0,1},{3,2},{2,3},{5,4},{4,5},{7,6},{6,7},{9,8},{8,9},{11,10... | collective-permute-start | bytes 983048 | tf_op jit(solution)/shard_map/ppermute | solution.py:916
  309.7 21.7 %collective-permute-start.57 = (bf16[256,1024]{1,0:T(8,128)(2,1)}, bf16[256,1024]{1,0:T(8,128)(2,1)S(1)}, u32[]{:S(2)}, u32[]{:S(2)}) collective-permute-start(bf16[256,1024]{1,0:T(8,128)(2,1)} %get-tuple-element.339), channel_id=1, source_target_pairs={{1,0},{0,1},{3,2},{2,3},{5,4},{4,5},{7,6},{6,7},{9,8},{8,9},{11,10... | collective-permute-start | bytes 1572872 | tf_op jit(solution)/shard_map/ppermute | solution.py:916
  310.3 12.3 %collective-permute-start.54 = (f32[96,128]{1,0:T(8,128)S(1)}, f32[96,128]{1,0:T(8,128)S(1)}, u32[]{:S(2)}, u32[]{:S(2)}) collective-permute-start(f32[96,128]{1,0:T(8,128)S(1)} %add.179), channel_id=1, source_target_pairs={{4,0},{5,1},{6,2},{7,3},{0,4},{1,5},{2,6},{3,7},{12,8},{13,9},{14,... | collective-permute-start | bytes 147464 | tf_op jit(solution)/shard_map/ppermute | solution.py:919
  326.5 17.2 %all-to-all-start.1 = ((bf16[4,64,1280]{2,1,0:T(8,128)(2,1)}), bf16[4,64,1280]{2,1,0:T(8,128)(2,1)S(1)}, u32[]{:S(2)}, u32[]{:S(2)}) async-start(bf16[4,64,1280]{2,1,0:T(8,128)(2,1)} %bitcast.59), calls=%async_computation.3 | async-start | bytes 1310720 | tf_op jit(solution)/shard_map/all_to_all | solution.py:907
  330.1 11.2 %collective-permute-start.59 = (bf16[256,1024]{1,0:T(8,128)(2,1)S(1)}, bf16[256,1024]{1,0:T(8,128)(2,1)S(1)}, u32[]{:S(2)}, u32[]{:S(2)}) collective-permute-start(bf16[256,1024]{1,0:T(8,128)(2,1)S(1)} %copy-done.65), channel_id=1, source_target_pairs={{1,0},{0,1},{3,2},{2,3},{5,4},{4,5},{7,6},{6,7},{9,8},{8,9},{11,10... | collective-permute-start | bytes 1572872 | tf_op jit(solution)/shard_map/ppermute | solution.py:916
  331.5 9.8 %collective-permute-start.58 = (bf16[64,256]{1,0:T(8,128)(2,1)S(1)}, bf16[64,256]{1,0:T(8,128)(2,1)S(1)}, u32[]{:S(2)}, u32[]{:S(2)}) collective-permute-start(bf16[64,256]{1,0:T(8,128)(2,1)S(1)} %slice.211), channel_id=1, source_target_pairs={{1,0},{0,1},{3,2},{2,3},{5,4},{4,5},{7,6},{6,7},{9,8},{8,9},{11,10... | collective-permute-start | bytes 98312 | tf_op jit(solution)/shard_map/ppermute | solution.py:916
  (88 other events, 712.2 us)
Sparse Core Ops, SparseCore 0:
  20.4 34.5 all-gather.2
  76.5 29.2 all-gather.4
  256.4 29.4 reduce-scatter.4
  288.2 37.5 reduce-scatter.2
